TPU v7x, 32 devices: a whole 2x2x4 slice. The times are simulated.
32 devices in a mesh: ep: 8 (over z, y), tp: 4 (over x, core).
Axes of the slice: x: 2, y: 2, z: 4, core: 2. Of those that a mesh axis runs over, the one named last changes fastest.
Arguments:
- queries: bfloat16 [512, 2048], P('ep', 'tp'), may hold values from -1024 to 1024
- new_keys: bfloat16 [512, 512], P('ep', 'tp'), may hold values from -6 to 6
- new_values: bfloat16 [512, 512], P('ep', 'tp'), may hold values from -5 to 5
- key_cache: bfloat16 [8, 512, 512], P('ep', None, 'tp'), may hold values from -5 to 5
- value_cache: bfloat16 [8, 512, 512], P('ep', None, 'tp'), may hold values from -5 to 5
- cache_lengths: int32 [8], P('ep'), may hold values from 1 to 512, 2048 in all
- request_order: int32 [8], replicated, may hold values from 0 to 7, each once
- residual: bfloat16 [512, 2048], P('ep', 'tp'), may hold values from -6 to 6
- out_weight: bfloat16 [2048, 2048], P('tp'), may hold values from -0.125 to 0.125
- norm_gain: float32 [2048], replicated, may hold values from 0.1 to 1.9
- route_experts: int32 [512, 2], P('ep'), may hold values from 0 to 7, all different within a row; in each aligned block of 64 rows (0 to 63, 64 to 127, ...) at most 32 rows name the same one
- route_weights: float32 [512, 2], P('ep'), may hold values from 0.1 to 1
- expert_gate: bfloat16 [8, 2048, 768], P('ep', None, 'tp'), may hold values from -0.125 to 0.125
- expert_up: bfloat16 [8, 2048, 768], P('ep', None, 'tp'), may hold values from -0.125 to 0.125
- expert_down: bfloat16 [8, 768, 2048], P('ep', None, 'tp'), may hold values from -0.21875 to 0.21875
Outputs:
- output: bfloat16 [512, 2048], P('ep', 'tp')
Inputs may be any that keep to these rules, and one draw needn't show every extreme that they name: `cache_lengths`: the longest cache holds exactly 512 rows in every draw. `request_order`: each request block appears once. `route_experts`: each row names 2 different experts; within each request's block of 64 rows no expert is named by more than 32 rows, a bound that some block reaches.
All inputs are finite; a program needn't handle non-finite values. No bound on the sum of `cache_lengths` on one device may be relied on, other than what follows from the above.
Results may differ from a plain program's by a relative error of at most 0.0057.
Values may be sent and summed in bfloat16 or wider, within the bound.
No kernel may reach another device: no remote copies, remote signals or barrier semaphores. Data moves between devices by JAX's collectives and lax.ppermute only.
A program may use at most 64 MiB of HBM per device.

v0:
```python
import math

import jax
import jax.numpy as jnp
from jax import lax
from jax.sharding import PartitionSpec as P

HEAD = 128
QHEADS = 16
KVHEADS = 4


def attention_block(queries, new_keys, new_values, key_cache, value_cache, cache_lengths, kv_local):
    tokens_here = queries.shape[0]
    cached = key_cache.shape[1]
    group_size = QHEADS // KVHEADS
    query_view = queries.reshape(tokens_here, kv_local, group_size, HEAD)
    all_keys = jnp.concatenate([key_cache[0], new_keys], axis=0).reshape(
        cached + tokens_here, kv_local, HEAD
    )
    all_values = jnp.concatenate([value_cache[0], new_values], axis=0).reshape(
        cached + tokens_here, kv_local, HEAD
    )
    scores = jnp.einsum(
        "tghd,kgd->tghk", query_view, all_keys, preferred_element_type=jnp.float32
    ) / math.sqrt(HEAD)
    position = jnp.arange(cached + tokens_here, dtype=jnp.int32)
    current = jnp.arange(tokens_here, dtype=jnp.int32)
    visible = jnp.where(
        position[None, :] < cached,
        position[None, :] < cache_lengths[0],
        position[None, :] - cached <= current[:, None],
    )
    visible = visible[:, None, None, :]
    highest = jnp.max(jnp.where(visible, scores, -1e30), axis=-1, keepdims=True)
    raised = jnp.exp(jnp.where(visible, scores - highest, -1e30))
    totals = jnp.sum(raised, axis=-1, keepdims=True)
    weights = raised.astype(jnp.bfloat16)
    context = (
        jnp.einsum("tghk,kgd->tghd", weights, all_values, preferred_element_type=jnp.float32)
        / totals
    )
    return context.astype(jnp.bfloat16).reshape(tokens_here, -1)


def normalize(rows_block, norm_gain):
    width_total = rows_block.shape[-1]
    squares = jnp.einsum(
        "secd,secd->sec", rows_block, rows_block, preferred_element_type=jnp.float32
    )
    factor = lax.rsqrt(squares / width_total + 1e-06)
    return (rows_block.astype(jnp.float32) * factor[..., None] * norm_gain).astype(jnp.bfloat16)


def shards(
    queries,
    new_keys,
    new_values,
    key_cache,
    value_cache,
    cache_lengths,
    request_order,
    residual,
    out_weight,
    norm_gain,
    route_experts,
    route_weights,
    expert_gate,
    expert_up,
    expert_down,
):
    tp_count = lax.axis_size("tp")
    ep_count = lax.axis_size("ep")
    kv_local = KVHEADS // tp_count
    context = attention_block(
        queries, new_keys, new_values, key_cache, value_cache, cache_lengths, kv_local
    )
    head_terms = jnp.dot(context, out_weight, preferred_element_type=jnp.float32)
    attended = lax.psum_scatter(head_terms, "tp", scatter_dimension=1, tiled=True)
    hidden_slice = (residual.astype(jnp.float32) + attended).astype(jnp.bfloat16)
    tokens_here, top_count = route_experts.shape
    experts_local = expert_gate.shape[0]
    expert_count = experts_local * ep_count
    capacity = 2 * tokens_here * top_count // expert_count
    flat_routes = route_experts.reshape(-1)
    onehot = (flat_routes[:, None] == jnp.arange(expert_count, dtype=jnp.int32)[None, :]).astype(
        jnp.int32
    )
    ranking = jnp.sum(jnp.cumsum(onehot, axis=0) * onehot, axis=1) - 1
    slot_index = flat_routes * capacity + ranking
    pair_token = jnp.arange(flat_routes.shape[0], dtype=jnp.int32) // top_count
    mixing = (
        (route_weights / jnp.sum(route_weights, axis=1, keepdims=True))
        .astype(jnp.bfloat16)
        .reshape(-1)
    )
    slot_token = jnp.full((expert_count * capacity,), -1, jnp.int32).at[slot_index].set(pair_token)
    slot_mix = jnp.zeros((expert_count * capacity,), jnp.bfloat16).at[slot_index].set(mixing)
    present = slot_token >= 0
    safe_token = jnp.where(present, slot_token, 0)
    inverse = (
        jnp.zeros_like(request_order)
        .at[request_order]
        .set(jnp.arange(request_order.shape[0], dtype=jnp.int32))
    )
    token_range = jnp.arange(tokens_here, dtype=jnp.int32)
    mask_rows = present.astype(jnp.bfloat16)[:, None]
    send_rows = (jnp.take(hidden_slice, safe_token, axis=0) * mask_rows).reshape(
        ep_count, experts_local * capacity, -1
    )
    send_mix = slot_mix.reshape(ep_count, -1)
    send_token = slot_token.reshape(ep_count, -1)
    got_rows, got_mix, got_token = (
        lax.all_to_all(send_rows, "ep", split_axis=0, concat_axis=0, tiled=True),
        lax.all_to_all(send_mix, "ep", split_axis=0, concat_axis=0, tiled=True),
        lax.all_to_all(send_token, "ep", split_axis=0, concat_axis=0, tiled=True),
    )
    full_rows = lax.all_gather(got_rows, "tp", axis=2, tiled=True)
    block_shape = (ep_count, experts_local, capacity)
    normed = normalize(full_rows.reshape(block_shape + (-1,)), norm_gain)
    gate_value = jnp.einsum(
        "secd,edf->secf", normed, expert_gate, preferred_element_type=jnp.float32
    )
    up_value = jnp.einsum("secd,edf->secf", normed, expert_up, preferred_element_type=jnp.float32)
    activation = (jax.nn.silu(gate_value) * up_value).astype(jnp.bfloat16)
    expert_out = jnp.einsum(
        "secf,efd->secd",
        lax.all_gather(activation, "tp", axis=3, tiled=True),
        expert_down,
        preferred_element_type=jnp.float32,
    )
    own_rows = got_rows.reshape(block_shape + (-1,))
    contribution = (
        got_mix.reshape(block_shape).astype(jnp.float32)[..., None]
        * (own_rows.astype(jnp.float32) + expert_out)
    ).astype(jnp.bfloat16)
    back_rows = jnp.take(
        contribution.reshape(ep_count, experts_local * capacity, -1), inverse, axis=0
    )
    back_token = jnp.take(got_token, inverse, axis=0)
    came_rows, came_token = (
        lax.all_to_all(back_rows, "ep", split_axis=0, concat_axis=0, tiled=True),
        lax.all_to_all(back_token, "ep", split_axis=0, concat_axis=0, tiled=True),
    )
    selector = (came_token.reshape(1, -1) == token_range[:, None]).astype(jnp.bfloat16)
    output = jnp.dot(
        selector, came_rows.reshape(selector.shape[1], -1), preferred_element_type=jnp.float32
    ).astype(jnp.bfloat16)
    return output


def solution(mesh):
    return jax.shard_map(
        shards,
        mesh=mesh,
        in_specs=(
            P("ep", "tp"),
            P("ep", "tp"),
            P("ep", "tp"),
            P("ep", None, "tp"),
            P("ep", None, "tp"),
            P("ep"),
            P(),
            P("ep", "tp"),
            P("tp", None),
            P(),
            P("ep", None),
            P("ep", None),
            P("ep", None, "tp"),
            P("ep", None, "tp"),
            P("ep", None, "tp"),
        ),
        out_specs=P("ep", "tp"),
        check_vma=False,
    )
```

profile of v0, /device:TPU:0, one launch (start us, length us, event | category | flops | bytes accessed | tf_op | source)
XLA Modules:
  0.0 125.2 jit_solution(4502071902656724971)
XLA Ops:
  6.5 0.0 copy-start
  6.5 0.0 reduce-scatter.2.cloned.1.call-start
  7.4 1.3 %select_reduce_fusion = (f32[64,4]{0,1:T(4,128)S(1)}, f32[64,1,4,576]{3,0,2,1:T(8,128)S(1)}) fusion(pred[64,576]{1,0:T(8,128)(4,1)S(1)} %fusion.26, bf16[64,128]{1,0:T(8,128)(2,1)} %param.16, bf16[512,128]{1,0:T(8,128)(2,1)} %bitcast.114, bf16[64,512]{1,0:T(8,128)(2,1)} %param.15), kind=kOutput, calls=%fused_computation.31 | convolution fusion | flops 38485760 | bytes 840704 | tf_op jit(solution)/shard_map/tghd,kgd->tghk/dot_general | solution.py:24
  8.7 0.3 fusion.18
  9.0 0.0 copy-start.4
  9.0 1.3 %fusion.12 = bf16[64,1,4,128]{3,0,2,1:T(8,128)(2,1)S(1)} fusion(f32[64,1,4,576]{3,0,2,1:T(8,128)S(1)} %get-tuple-element.9, f32[64,4]{0,1:T(4,128)S(1)} %get-tuple-element.8, pred[64,576]{1,0:T(8,128)(4,1)S(1)} %fusion.26, bf16[64,128]{1,0:T(8,128)(2,1)} %param.17, bf16[512,128]{1,0:T(8,128)(2,1)} %bitcast.115, f32[64,4]{0,1:T(4,128)S(1)} %fusion.18), kind=kOutput, calls=%fused_computation.26 | convolution fusion | flops 38551552 | bytes 841728 | tf_op jit(solution)/shard_map/tghk,kgd->tghd/dot_general | solution.py:40
  10.2 0.0 copy-start.3
  10.2 0.1 copy.39
  10.3 0.0 copy-done
  10.3 1.3 %fusion.31 = f32[64,2048]{1,0:T(8,128)} fusion(bf16[512,2048]{1,0:T(8,128)(2,1)S(1)} %copy-done, bf16[8,8,4,128]{3,2,1,0:T(4,128)(2,1)S(1)} %bitcast.112), kind=kOutput, calls=%fused_computation.50 | convolution fusion | flops 134217728 | bytes 2686976 | tf_op jit(solution)/shard_map/dot_general | solution.py:78
  11.6 0.0 reduce-scatter.2.cloned.1.call-update
  11.6 0.0 all-gather.2.cloned.1.call-start
  11.7 0.1 copy.34
  11.8 0.1 eq.30
  11.9 0.1 copy.33
  12.0 0.1 mul.71
  12.2 0.1 fusion.36
  12.3 0.0 copy-start.5
  12.3 0.0 copy-start.7
  12.3 0.2 reduce_window_sum.11
  12.5 0.2 select_reduce_fusion.1
  12.6 1.0 scatter_custom_fusion.1
  13.6 0.1 reshape.253
  13.7 0.1 broadcast_in_dim.100
  13.8 22.3 %reduce-scatter.2.cloned.1.call-done = f32[64,512]{1,0:T(8,128)} async-done(((f32[64,2048]{1,0:T(8,128)}), f32[64,512]{1,0:T(8,128)}) %reduce-scatter.2.cloned.1.call-update) | async-done | bytes 131088 | tf_op jit(solution)/shard_map/reduce_scatter | solution.py:79
  36.1 0.0 copy-done.3
  36.1 0.9 add_convert_fusion
  37.0 0.0 copy-start.6
  37.0 1.2 gather_fusion.1
  38.2 0.1 select_multiply_fusion
  38.3 14.3 %all_to_all.38 = bf16[8,32,512]{2,1,0:T(8,128)(2,1)} all-to-all(bf16[8,32,512]{2,1,0:T(8,128)(2,1)S(1)} %select_multiply_fusion), channel_id=1, replica_groups=mesh['ep'=8,'tp'=4] {'ep'}, dimensions={0} | all-to-all | bytes 524288 | tf_op jit(solution)/shard_map/all_to_all | solution.py:114
  52.7 0.0 all-gather.2.cloned.1.call-update
  52.7 0.0 copy-done.5
  52.7 0.1 copy.36
  52.8 0.2 reshape.299
  53.0 1.3 %scatter_custom_fusion.2 = bf16[256]{0:T(256)(128)(2,1)S(1)} fusion(s32[128]{0:T(128)S(1)} %fusion.38, bf16[128]{0:T(256)(128)(2,1)S(1)} %reshape.299, bf16[]{:T(256)} %constant.84.clone.1), kind=kCustom, calls=%fused_computation.85 | custom fusion | bytes 514 | tf_op jit(solution)/shard_map/scatter | solution.py:98
  54.4 0.7 all_to_all.32
  55.0 3.6 %all-to-all-start.2 = ((bf16[8,1,32]{2,1,0:T(2,128)(2,1)}), bf16[8,1,32]{2,1,0:T(2,128)(2,1)S(1)}, u32[]{:S(2)}, u32[]{:S(2)}) async-start(bf16[8,1,32]{2,1,0:T(2,128)(2,1)} %all_to_all.32), calls=%async_computation.2 | async-start | bytes 8192 | tf_op jit(solution)/shard_map/all_to_all | solution.py:115
  58.6 0.6 scatter_custom_fusion
  59.3 0.7 all_to_all.24
  60.0 5.1 %all-to-all-done.2 = bf16[8,1,32]{2,1,0:T(2,128)(2,1)S(1)} async-done(((bf16[8,1,32]{2,1,0:T(2,128)(2,1)}), bf16[8,1,32]{2,1,0:T(2,128)(2,1)S(1)}, u32[]{:S(2)}, u32[]{:S(2)}) %all-to-all-start.2) | async-done | bytes 544 | tf_op jit(solution)/shard_map/all_to_all | solution.py:115
  65.0 3.3 %all-to-all-start = ((s32[8,1,32]{2,1,0:T(1,128)}), s32[8,1,32]{2,1,0:T(1,128)S(1)}, u32[]{:S(2)}, u32[]{:S(2)}) async-start(s32[8,1,32]{2,1,0:T(1,128)} %all_to_all.24), calls=%async_computation | async-start | bytes 8192 | tf_op jit(solution)/shard_map/all_to_all | solution.py:116
  68.4 6.4 %all-to-all-done = s32[8,1,32]{2,1,0:T(1,128)S(1)} async-done(((s32[8,1,32]{2,1,0:T(1,128)}), s32[8,1,32]{2,1,0:T(1,128)S(1)}, u32[]{:S(2)}, u32[]{:S(2)}) %all-to-all-start) | async-done | bytes 1056 | tf_op jit(solution)/shard_map/all_to_all | solution.py:116
  74.7 0.6 gather_fusion
  75.3 0.7 bitcast_select_fusion
  76.0 3.3 %all-to-all-start.1 = ((s32[8,1,32]{2,1,0:T(1,128)}), s32[8,1,32]{2,1,0:T(1,128)S(1)}, u32[]{:S(2)}, u32[]{:S(2)}) async-start(s32[8,1,32]{2,1,0:T(1,128)} %bitcast.4), calls=%async_computation.1 | async-start | bytes 8192 | tf_op jit(solution)/shard_map/all_to_all | solution.py:143
  79.3 0.0 all-gather.2.cloned.1.call-done
  79.3 1.6 %fusion.2 = f32[8,32]{1,0:T(8,128)S(1)} fusion(bf16[8,32,2048]{2,1,0:T(8,128)(2,1)} %all-gather.2.cloned.1.call-done), kind=kLoop, calls=%fused_computation.10 | loop fusion | flops 1572608 | bytes 1049600 | tf_op jit(solution)/shard_map/secd,secd->sec/dot_general | solution.py:48
  80.9 1.9 %convolution_bitcast_fusion.2 = f32[8,1,32,192]{3,2,0,1:T(8,128)S(1)} fusion(bf16[8,32,2048]{2,1,0:T(8,128)(2,1)} %all-gather.2.cloned.1.call-done, f32[2048]{0:T(1024)S(1)} %copy-done.6, f32[8,32]{1,0:T(8,128)S(1)} %add_rsqrt_fusion, bf16[1,2048,192]{1,2,0:T(8,128)(2,1)} %param.27), kind=kOutput, calls=%fused_computation.20 | convolution fusion | flops 203423744 | bytes 2040832 | tf_op jit(solution)/shard_map/secd,edf->secf/dot_general | solution.py:121
  82.9 0.0 copy-done.2
  82.9 1.6 %fusion.9 = bf16[8,1,32,192]{3,2,0,1:T(8,128)(2,1)S(1)} fusion(bf16[8,32,2048]{2,1,0:T(8,128)(2,1)S(1)} %copy-done.2, f32[2048]{0:T(1024)S(1)} %copy-done.6, f32[8,32]{1,0:T(8,128)S(1)} %add_rsqrt_fusion, bf16[1,2048,192]{1,2,0:T(8,128)(2,1)} %param.28, f32[8,1,32,192]{3,2,0,1:T(8,128)S(1)} %convolution_bitcast_fusion.2), kind=kOutput, calls=%fused_computation.21 | convolution fusion | flops 203718656 | bytes 2139136 | tf_op jit(solution)/shard_map/secd,edf->secf/dot_general | solution.py:124
  84.5 0.2 copy.40
  84.8 12.5 %all_gather.7 = bf16[8,1,32,768]{2,0,1,3:T(8,128)(2,1)} all-gather(bf16[8,1,32,192]{2,0,1,3:T(8,128)(2,1)S(1)} %copy.40), channel_id=1, replica_groups=mesh['ep'=8,'tp'=4] {'tp'}, dimensions={3}, use_global_device_ids=true | all-gather | bytes 491520 | tf_op jit(solution)/shard_map/all_gather | solution.py:128
  97.3 2.0 %copy.41 = bf16[8,1,32,768]{3,2,0,1:T(8,128)(2,1)S(1)} copy(bf16[8,1,32,768]{2,0,1,3:T(8,128)(2,1)} %all_gather.7) | data formatting | bytes 786432 | tf_op jit(solution)/shard_map/all_gather | solution.py:128
  99.3 1.5 %fusion.7 = bf16[8,32,512]{2,1,0:T(8,128)(2,1)S(1)} fusion(bf16[1,768,512]{2,1,0:T(8,128)(2,1)} %param.29, bf16[8,1,32,768]{3,2,0,1:T(8,128)(2,1)S(1)} %copy.41, bf16[8,32,512]{2,1,0:T(8,128)(2,1)S(1)} %copy-done.1, f32[8,32]{1,0:T(8,128)S(1)} %bitcast.113), kind=kOutput, calls=%fused_computation.17 | convolution fusion | flops 201850880 | bytes 1704960 | tf_op jit(solution)/shard_map/secf,efd->secd/dot_general | solution.py:126
  100.8 0.6 gather_fusion.2
  101.4 0.8 broadcast_select_fusion
  102.2 0.0 all-to-all-done.1
  102.2 5.9 %all-to-all-start.4 = ((bf16[8,32,512]{2,1,0:T(8,128)(2,1)}), bf16[8,32,512]{2,1,0:T(8,128)(2,1)S(1)}, u32[]{:S(2)}, u32[]{:S(2)}) async-start(bf16[8,32,512]{2,1,0:T(8,128)(2,1)} %broadcast_select_fusion), calls=%async_computation.5 | async-start | bytes 524288 | tf_op jit(solution)/shard_map/all_to_all | solution.py:142
  108.1 0.5 broadcast.218
  108.6 0.7 reduce.7
  109.3 0.1 eq.34
  109.3 8.2 %all-to-all-done.4 = bf16[8,32,512]{2,1,0:T(8,128)(2,1)S(1)} async-done(((bf16[8,32,512]{2,1,0:T(8,128)(2,1)}), bf16[8,32,512]{2,1,0:T(8,128)(2,1)S(1)}, u32[]{:S(2)}, u32[]{:S(2)}) %all-to-all-start.4) | async-done | bytes 262176 | tf_op jit(solution)/shard_map/all_to_all | solution.py:142
  117.5 0.8 convolution_convert_fusion
  (23 shorter events, 0.2 us)
Async XLA Ops:
  6.5 3.8 %copy-start = (bf16[512,2048]{1,0:T(8,128)(2,1)S(1)}, bf16[512,2048]{1,0:T(8,128)(2,1)}, u32[]{:S(2)}) copy-start(bf16[512,2048]{1,0:T(8,128)(2,1)} %param.23) | copy-start | bytes 6291460
  6.5 29.6 %reduce-scatter.2.cloned.1.call-start = ((), (), s32[]{:S(2)}) async-start(), calls=%async_computation.6 | async-start | bytes 655360 | tf_op jit(solution)/shard_map/reduce_scatter | solution.py:79
  9.0 2.7 %copy-start.4 = (s32[64,2]{0,1:T(2,128)S(1)}, s32[64,2]{0,1:T(2,128)}, u32[]{:S(2)}) copy-start(s32[64,2]{0,1:T(2,128)} %param.25) | copy-start | bytes 1540
  10.2 25.9 %copy-start.3 = (bf16[64,512]{1,0:T(8,128)(2,1)S(1)}, bf16[64,512]{1,0:T(8,128)(2,1)}, u32[]{:S(2)}) copy-start(bf16[64,512]{1,0:T(8,128)(2,1)} %param.22) | copy-start | bytes 196612
  11.6 67.7 %all-gather.2.cloned.1.call-start = ((), (), s32[]{:S(2)}) async-start(), calls=%async_computation.7 | async-start | bytes 1310720 | tf_op jit(solution)/shard_map/all_gather | solution.py:118
  12.3 40.4 %copy-start.5 = (f32[64,2]{0,1:T(2,128)S(1)}, f32[64,2]{0,1:T(2,128)}, u32[]{:S(2)}) copy-start(f32[64,2]{0,1:T(2,128)} %param.26) | copy-start | bytes 1540
  12.3 46.4 %copy-start.7 = (s32[8]{0:T(128)S(1)}, s32[8]{0:T(128)}, u32[]{:S(2)}) copy-start(s32[8]{0:T(128)} %param.21) | copy-start | bytes 100
  37.0 43.9 %copy-start.6 = (f32[2048]{0:T(1024)S(1)}, f32[2048]{0:T(1024)}, u32[]{:S(2)}) copy-start(f32[2048]{0:T(1024)} %param.24) | copy-start | bytes 24580
  55.0 10.0 %all-to-all-start.2 = ((bf16[8,1,32]{2,1,0:T(2,128)(2,1)}), bf16[8,1,32]{2,1,0:T(2,128)(2,1)S(1)}, u32[]{:S(2)}, u32[]{:S(2)}) async-start(bf16[8,1,32]{2,1,0:T(2,128)(2,1)} %all_to_all.32), calls=%async_computation.2 | async-start | bytes 8192 | tf_op jit(solution)/shard_map/all_to_all | solution.py:115
  65.0 9.7 %all-to-all-start = ((s32[8,1,32]{2,1,0:T(1,128)}), s32[8,1,32]{2,1,0:T(1,128)S(1)}, u32[]{:S(2)}, u32[]{:S(2)}) async-start(s32[8,1,32]{2,1,0:T(1,128)} %all_to_all.24), calls=%async_computation | async-start | bytes 8192 | tf_op jit(solution)/shard_map/all_to_all | solution.py:116
  76.0 26.2 %all-to-all-start.1 = ((s32[8,1,32]{2,1,0:T(1,128)}), s32[8,1,32]{2,1,0:T(1,128)S(1)}, u32[]{:S(2)}, u32[]{:S(2)}) async-start(s32[8,1,32]{2,1,0:T(1,128)} %bitcast.4), calls=%async_computation.1 | async-start | bytes 8192 | tf_op jit(solution)/shard_map/all_to_all | solution.py:143
  79.3 3.6 %copy-start.2 = (bf16[8,32,2048]{2,1,0:T(8,128)(2,1)S(1)}, bf16[8,32,2048]{2,1,0:T(8,128)(2,1)}, u32[]{:S(2)}) copy-start(bf16[8,32,2048]{2,1,0:T(8,128)(2,1)} %all-gather.2.cloned.1.call-done) | copy-start | bytes 3145732
  84.8 14.5 %copy-start.1 = (bf16[8,32,512]{2,1,0:T(8,128)(2,1)S(1)}, bf16[8,32,512]{2,1,0:T(8,128)(2,1)}, u32[]{:S(2)}) copy-start(bf16[8,32,512]{2,1,0:T(8,128)(2,1)} %all_to_all.38) | copy-start | bytes 786436
  102.2 15.3 %all-to-all-start.4 = ((bf16[8,32,512]{2,1,0:T(8,128)(2,1)}), bf16[8,32,512]{2,1,0:T(8,128)(2,1)S(1)}, u32[]{:S(2)}, u32[]{:S(2)}) async-start(bf16[8,32,512]{2,1,0:T(8,128)(2,1)} %broadcast_select_fusion), calls=%async_computation.5 | async-start | bytes 524288 | tf_op jit(solution)/shard_map/all_to_all | solution.py:142
Sparse Core Ops, SparseCore 0:
  11.7 24.3 reduce-scatter.1
  52.8 14.7 all-gather.1
where the time goes:
time: 126 us; the launch traced here: 125 us
  waiting for transfers between devices  41.9 us (33%)
  blocking collectives  26.9 us (21%)
  starting transfers between devices  16.2 us (13%)
  between operations  14.5 us (12%)
  local copies, waits for them, and re-layouts  10.4 us (8%)
  matrix products  9.68 us (8%)
  other arithmetic  5.6 us (4%)
    reduce_scatter x1, waiting for transfers between devices, shards(): lax.psum_scatter(head_terms, 'tp', scatter_dimension=1, tiled=True)  22.3 us
    all_to_all x1, blocking collectives, shards(): lax.all_to_all(send_rows, 'ep', split_axis=0, concat_axis=0, tiled=True)  14.3 us
    all_gather x1, blocking collectives, shards(): lax.all_gather(activation, 'tp', axis=3, tiled=True)  12.5 us
    all_to_all x1, waiting for transfers between devices, shards(): lax.all_to_all(back_rows, 'ep', split_axis=0, concat_axis=0, tiled=True)  8.17 us
    all_to_all x1, waiting for transfers between devices, shards(): lax.all_to_all(send_token, 'ep', split_axis=0, concat_axis=0, tiled=True)  6.37 us
    all_to_all x1, starting transfers between devices, shards(): lax.all_to_all(back_rows, 'ep', split_axis=0, concat_axis=0, tiled=True)  5.92 us
    all_to_all x1, waiting for transfers between devices, shards(): lax.all_to_all(send_mix, 'ep', split_axis=0, concat_axis=0, tiled=True)  5.06 us
    all_to_all x1, starting transfers between devices, shards(): lax.all_to_all(send_mix, 'ep', split_axis=0, concat_axis=0, tiled=True)  3.59 us
  transfers between devices with their start and end apart: 6, of which 4 were waited for; matrix products, arithmetic and copies ran while one was open for 14% of the time, Pallas kernels for 0%

commit v1 on v0

v1 whole, which is shorter than its diff:
```python
import math

import jax
import jax.numpy as jnp
from jax import lax
from jax.sharding import PartitionSpec as P

HEAD = 128
QHEADS = 16
KVHEADS = 4
META = 128


def attention_block(queries, new_keys, new_values, key_cache, value_cache, cache_lengths, kv_local):
    tokens_here = queries.shape[0]
    cached = key_cache.shape[1]
    group_size = QHEADS // KVHEADS
    query_view = queries.reshape(tokens_here, kv_local, group_size, HEAD)
    all_keys = jnp.concatenate([key_cache[0], new_keys], axis=0).reshape(
        cached + tokens_here, kv_local, HEAD
    )
    all_values = jnp.concatenate([value_cache[0], new_values], axis=0).reshape(
        cached + tokens_here, kv_local, HEAD
    )
    scores = jnp.einsum(
        "tghd,kgd->tghk", query_view, all_keys, preferred_element_type=jnp.float32
    ) / math.sqrt(HEAD)
    position = jnp.arange(cached + tokens_here, dtype=jnp.int32)
    current = jnp.arange(tokens_here, dtype=jnp.int32)
    visible = jnp.where(
        position[None, :] < cached,
        position[None, :] < cache_lengths[0],
        position[None, :] - cached <= current[:, None],
    )
    visible = visible[:, None, None, :]
    highest = jnp.max(jnp.where(visible, scores, -1e30), axis=-1, keepdims=True)
    raised = jnp.exp(jnp.where(visible, scores - highest, -1e30))
    totals = jnp.sum(raised, axis=-1, keepdims=True)
    weights = raised.astype(jnp.bfloat16)
    context = (
        jnp.einsum("tghk,kgd->tghd", weights, all_values, preferred_element_type=jnp.float32)
        / totals
    )
    return context.astype(jnp.bfloat16).reshape(tokens_here, -1)


def shards(
    queries,
    new_keys,
    new_values,
    key_cache,
    value_cache,
    cache_lengths,
    request_order,
    residual,
    out_weight,
    norm_gain,
    route_experts,
    route_weights,
    expert_gate,
    expert_up,
    expert_down,
):
    tp_count = lax.axis_size("tp")
    ep_count = lax.axis_size("ep")
    kv_local = KVHEADS // tp_count
    me_ep = lax.axis_index("ep")
    me_tp = lax.axis_index("tp")
    half, core = me_tp // 2, me_tp % 2
    bf = jnp.bfloat16

    def swap_core(x):
        return lax.ppermute(x, "tp", [(i, i ^ 1) for i in range(tp_count)])

    def swap_half(x):
        return lax.ppermute(x, "tp", [(i, i ^ 2) for i in range(tp_count)])

    tokens_here, top_count = route_experts.shape
    experts_local = expert_gate.shape[0]
    expert_count = experts_local * ep_count
    capacity = 2 * tokens_here * top_count // expert_count
    rows_each = experts_local * capacity
    peers = ep_count // 2
    width = residual.shape[1]
    full = width * tp_count

    context = attention_block(
        queries, new_keys, new_values, key_cache, value_cache, cache_lengths, kv_local
    )
    terms = jnp.dot(context, out_weight, preferred_element_type=jnp.float32)
    terms = terms.reshape(tokens_here, 2, 2, width)
    first, second = terms[:, :, 0], terms[:, :, 1]
    keep = jnp.where(core == 0, first, second)
    give = jnp.where(core == 0, second, first).astype(bf)
    keep = keep + swap_core(give).astype(jnp.float32)
    mine = (jnp.arange(2) == half)[None, :, None]
    keep = keep + jnp.where(mine, residual.astype(jnp.float32)[:, None, :], 0.0)
    hidden_part = (keep + swap_half(keep.astype(bf)).astype(jnp.float32)).astype(bf)
    hidden_other = swap_core(hidden_part)
    hidden = jnp.stack(
        [
            jnp.where(core == 0, hidden_part, hidden_other),
            jnp.where(core == 0, hidden_other, hidden_part),
        ],
        axis=2,
    ).reshape(tokens_here, full)

    offsets = 2 * jnp.arange(peers, dtype=jnp.int32) + core
    peer = jnp.bitwise_xor(me_ep, offsets)
    wanted = (
        peer[:, None] * experts_local + jnp.arange(experts_local, dtype=jnp.int32)[None, :]
    ).reshape(-1)
    named = jnp.any(route_experts[None] == wanted[:, None, None], axis=2)
    token_range = jnp.arange(tokens_here, dtype=jnp.int32)
    before = (token_range[:, None] < token_range[None, :]).astype(bf)
    rank = jnp.dot(named.astype(bf), before, preferred_element_type=jnp.float32).astype(jnp.int32)
    slot_range = jnp.arange(capacity, dtype=jnp.int32)
    pick = (
        (rank[:, None, :] == slot_range[None, :, None]) & named[:, None, :]
    ).astype(bf).reshape(peers * rows_each, tokens_here)
    mixing = (route_weights / jnp.sum(route_weights, axis=1, keepdims=True)).astype(bf)
    meta = jnp.concatenate(
        [(token_range + 1).astype(bf)[:, None], mixing, route_experts.astype(bf)], axis=1
    )
    meta = jnp.pad(meta, ((0, 0), (0, META - meta.shape[1])))
    source = jnp.concatenate([hidden, meta], axis=1)
    send = jnp.dot(pick, source, preferred_element_type=jnp.float32).astype(bf)
    send = send.reshape(peers, rows_each, full + META)

    def route(k):
        return [
            (e * tp_count + t, (e ^ (2 * k + t % 2)) * tp_count + t)
            for e in range(ep_count)
            for t in range(tp_count)
        ]

    got = [lax.ppermute(send[k], ("ep", "tp"), route(k)) for k in range(peers)]
    own = jnp.stack(got)
    other = jnp.stack([swap_core(g) for g in got])
    rows = jnp.concatenate(
        [jnp.where(core == 0, own, other), jnp.where(core == 0, other, own)], axis=0
    )
    rows = rows.reshape(ep_count, experts_local, capacity, full + META)
    tags = rows[..., full:].astype(jnp.float32)
    token = tags[..., 0]
    expert_ids = (me_ep * experts_local + jnp.arange(experts_local)).astype(jnp.float32)
    mix = jnp.sum(
        jnp.where(
            tags[..., 1 + top_count : 1 + 2 * top_count] == expert_ids[None, :, None, None],
            tags[..., 1 : 1 + top_count],
            0.0,
        ),
        axis=-1,
    )
    rows = rows[..., :full].astype(jnp.float32)
    factor = lax.rsqrt(jnp.mean(rows * rows, axis=-1, keepdims=True) + 1e-06)
    normed = (rows * factor * norm_gain).astype(bf)
    gate = jnp.einsum("secd,edf->secf", normed, expert_gate, preferred_element_type=jnp.float32)
    up = jnp.einsum("secd,edf->secf", normed, expert_up, preferred_element_type=jnp.float32)
    activation = (jax.nn.silu(gate) * up).astype(bf)
    activation = lax.all_gather(activation, "tp", axis=3, tiled=True)
    expert_out = jnp.einsum(
        "secf,efd->secd", activation, expert_down, preferred_element_type=jnp.float32
    )
    own_rows = lax.dynamic_slice_in_dim(rows, me_tp * width, width, axis=3)
    contribution = (mix[..., None] * (own_rows + expert_out)).astype(bf)
    result = jnp.concatenate(
        [contribution, jnp.broadcast_to(token[..., None].astype(bf), token.shape + (META,))],
        axis=-1,
    ).reshape(ep_count, rows_each, width + META)

    requests = jnp.arange(ep_count, dtype=jnp.int32)
    offset = jnp.bitwise_xor(requests, me_ep)
    place = offset // 2 + (offset % 2) * peers
    back = jnp.zeros((ep_count,), jnp.int32)
    back = jnp.sum(
        jnp.where(request_order[None, :] == requests[:, None], place[None, :], 0), axis=1
    )
    came = lax.all_to_all(
        jnp.take(result, back, axis=0), "ep", split_axis=0, concat_axis=0, tiled=True
    ).reshape(ep_count * rows_each, width + META)
    selector = (came[:, width].astype(jnp.int32)[None, :] == token_range[:, None] + 1).astype(bf)
    return jnp.dot(selector, came[:, :width], preferred_element_type=jnp.float32).astype(bf)


def solution(mesh):
    return jax.shard_map(
        shards,
        mesh=mesh,
        in_specs=(
            P("ep", "tp"),
            P("ep", "tp"),
            P("ep", "tp"),
            P("ep", None, "tp"),
            P("ep", None, "tp"),
            P("ep"),
            P(),
            P("ep", "tp"),
            P("tp", None),
            P(),
            P("ep", None),
            P("ep", None),
            P("ep", None, "tp"),
            P("ep", None, "tp"),
            P("ep", None, "tp"),
        ),
        out_specs=P("ep", "tp"),
        check_vma=False,
    )
```

time: 126 us -> 75.2 us (0.60)
  waiting for transfers between devices: 41.9 us -> 17.5 us
  blocking collectives: 26.9 us -> 12.9 us
  between operations: 14.5 us -> 1.13 us
  starting transfers between devices: 16.2 us -> 25.9 us
  local copies, waits for them, and re-layouts: 10.4 us -> 6.23 us
  matrix products: 9.68 us -> 6.98 us
  other arithmetic: 5.6 us -> 4.2 us
    reduce_scatter x1 -> x0, waiting for transfers between devices: 22.3 us -> none  [shards(): lax.psum_scatter(head_terms, 'tp', scatter_dimension=1, tiled=True)]
    ppermute x0 -> x11, starting transfers between devices: none -> 21.4 us  [the longest x6 13.4 us: swap_core(): return lax.ppermute(x, 'tp', [(i, i ^ 1) for i in range(tp_count)])]
    all_to_all x1 -> x0, blocking collectives: 14.3 us -> none  [shards(): lax.all_to_all(send_rows, 'ep', split_axis=0, concat_axis=0, tiled=True)]
    all_to_all x4 -> x1, starting transfers between devices: 16.1 us -> 4.49 us  [shards(): lax.all_to_all(jnp.take(result, back, axis=0), 'ep', split_axis=0, concat...]
    all_to_all x4 -> x1, waiting for transfers between devices: 19.6 us -> 10.8 us  [shards(): lax.all_to_all(jnp.take(result, back, axis=0), 'ep', split_axis=0, concat...]
    ppermute x0 -> x11, waiting for transfers between devices: none -> 6.67 us  [the longest x1 3.78 us: swap_half(): return lax.ppermute(x, 'tp', [(i, i ^ 2) for i in range(tp_count)])]
    scatter x3 -> x0, local copies, waits for them, and re-layouts: 2.92 us -> none  [the longest x1 1.35 us: shards(): jnp.zeros((expert_count * capacity,), jnp.bfloat16).at[slot_index]]
    dot_general x0 -> x1, local copies, waits for them, and re-layouts: none -> 2.87 us  [shards(): terms = jnp.dot(context, out_weight, preferred_element_type=jnp.float32)]
  transfers between devices with their start and end apart: 6 -> 12, of which waited for: 4 -> 6; matrix products, arithmetic and copies ran while one was open for 14% -> 1% of each run, Pallas kernels for 0% -> 0%
where the time goes in v1:
time: 75.2 us; the launch traced here: 74.8 us
  starting transfers between devices  25.9 us (34%)
  waiting for transfers between devices  17.5 us (23%)
  blocking collectives  12.9 us (17%)
  matrix products  6.98 us (9%)
  local copies, waits for them, and re-layouts  6.23 us (8%)
  other arithmetic  4.2 us (6%)
  between operations  1.13 us (2%)
    ppermute x6, starting transfers between devices, swap_core(): return lax.ppermute(x, 'tp', [(i, i ^ 1) for i in range(tp_count)])  13.4 us
    all_gather x1, blocking collectives, shards(): activation = lax.all_gather(activation, 'tp', axis=3, tiled=True)  12.9 us
    all_to_all x1, waiting for transfers between devices, shards(): lax.all_to_all(jnp.take(result, back, axis=0), 'ep', split_axis=0, concat...  10.8 us
    ppermute x4, starting transfers between devices, shards(): got = [lax.ppermute(send[k], ('ep', 'tp'), route(k)) for k in range(peers)]  5.15 us
    all_to_all x1, starting transfers between devices, shards(): lax.all_to_all(jnp.take(result, back, axis=0), 'ep', split_axis=0, concat...  4.49 us
    ppermute x1, waiting for transfers between devices, swap_half(): return lax.ppermute(x, 'tp', [(i, i ^ 2) for i in range(tp_count)])  3.78 us
    ppermute x1, starting transfers between devices, swap_half(): return lax.ppermute(x, 'tp', [(i, i ^ 2) for i in range(tp_count)])  2.91 us
    ppermute x6, waiting for transfers between devices, swap_core(): return lax.ppermute(x, 'tp', [(i, i ^ 1) for i in range(tp_count)])  2.88 us
  transfers between devices with their start and end apart: 12, of which 6 were waited for; matrix products, arithmetic and copies ran while one was open for 1% of the time, Pallas kernels for 0%

profile of v1, /device:TPU:0, one launch (start us, length us, event | category | flops | bytes accessed | tf_op | source)
XLA Modules:
  0.0 74.8 jit_solution(14542702324147105606)
XLA Ops:
  0.8 1.3 %select_reduce_fusion = (f32[64,4]{0,1:T(4,128)S(1)}, f32[64,1,4,576]{3,0,2,1:T(8,128)S(1)}) fusion(pred[64,576]{1,0:T(8,128)(4,1)S(1)} %fusion.33, bf16[64,128]{1,0:T(8,128)(2,1)} %param.16, bf16[512,128]{1,0:T(8,128)(2,1)} %bitcast.163, bf16[64,512]{1,0:T(8,128)(2,1)} %param.15), kind=kOutput, calls=%fused_computation.27 | convolution fusion | flops 38485760 | bytes 840704 | tf_op jit(solution)/shard_map/tghd,kgd->tghk/dot_general | solution.py:25
  2.1 0.3 fusion.16
  2.3 1.2 %fusion.8 = bf16[64,1,4,128]{3,0,2,1:T(8,128)(2,1)S(1)} fusion(f32[64,1,4,576]{3,0,2,1:T(8,128)S(1)} %get-tuple-element.16, f32[64,4]{0,1:T(4,128)S(1)} %get-tuple-element.15, pred[64,576]{1,0:T(8,128)(4,1)S(1)} %fusion.33, bf16[64,128]{1,0:T(8,128)(2,1)} %param.17, bf16[512,128]{1,0:T(8,128)(2,1)} %bitcast.164, f32[64,4]{0,1:T(4,128)S(1)} %fusion.16), kind=kOutput, calls=%fused_computation.20 | convolution fusion | flops 38551552 | bytes 841728 | tf_op jit(solution)/shard_map/tghk,kgd->tghd/dot_general | solution.py:41
  3.6 0.1 copy.51
  3.7 2.9 %copy.63 = bf16[2048,512]{1,0:T(8,128)(2,1)S(1)} copy(bf16[2048,512]{0,1:T(8,128)(2,1)} %bitcast.151) | data formatting | bytes 4194304 | tf_op jit(solution)/shard_map/dot_general | solution.py:90
  6.6 0.0 copy-start.3
  6.6 0.0 copy-start.2
  6.6 0.0 copy-start.1
  6.6 0.0 copy-start.7
  6.6 0.7 fusion.43
  7.4 0.5 collective-permute-start
  7.9 0.1 compare_reduce_fusion
  8.0 0.1 convolution_convert_fusion.2
  8.2 0.7 collective-permute-done
  8.9 0.1 fusion.58
  9.0 2.9 %collective-permute-start.1 = (bf16[64,2,512]{2,0,1:T(8,128)(2,1)S(1)}, bf16[64,2,512]{2,0,1:T(8,128)(2,1)S(1)}, u32[]{:S(2)}, u32[]{:S(2)}) collective-permute-start(bf16[64,2,512]{2,0,1:T(8,128)(2,1)S(1)} %get-tuple-element.5), channel_id=1, source_target_pairs={{0,2},{1,3},{2,0},{3,1},{4,6},{5,7},{6,4},{7,5},{8,10},{9,11},{10,... | collective-permute-start | bytes 393224 | tf_op jit(solution)/shard_map/ppermute | solution.py:76
  12.0 3.8 %collective-permute-done.1 = bf16[64,2,512]{2,0,1:T(8,128)(2,1)S(1)} collective-permute-done((bf16[64,2,512]{2,0,1:T(8,128)(2,1)S(1)}, bf16[64,2,512]{2,0,1:T(8,128)(2,1)S(1)}, u32[]{:S(2)}, u32[]{:S(2)}) %collective-permute-start.1) | collective-permute-done | bytes 131104 | tf_op jit(solution)/shard_map/ppermute | solution.py:76
  15.8 0.1 collective-permute-start.2
  15.9 0.1 eq.99
  16.0 0.1 copy.58
  16.1 0.1 fusion.45
  16.2 0.1 select_reduce_fusion.1
  16.3 0.9 %collective-permute-done.2 = bf16[64,2,512]{2,0,1:T(8,128)(2,1)S(1)} collective-permute-done((bf16[64,2,512]{2,0,1:T(8,128)(2,1)S(1)}, bf16[64,2,512]{2,0,1:T(8,128)(2,1)S(1)}, u32[]{:S(2)}, u32[]{:S(2)}) %collective-permute-start.2) | collective-permute-done | bytes 131104 | tf_op jit(solution)/shard_map/ppermute | solution.py:73
  17.3 0.3 copy.57
  17.5 0.2 reshape.256
  17.7 0.3 convolution_convert_fusion
  18.1 0.7 collective-permute-start.3
  18.7 1.9 %collective-permute-start.4 = (bf16[32,2176]{1,0:T(8,128)(2,1)S(1)}, bf16[32,2176]{1,0:T(8,128)(2,1)S(1)}, u32[]{:S(2)}, u32[]{:S(2)}) collective-permute-start(bf16[32,2176]{1,0:T(8,128)(2,1)S(1)} %get-tuple-element.12), channel_id=1, source_target_pairs={{0,8},{1,13},{2,10},{3,15},{4,12},{5,9},{6,14},{7,11},{8,0},{9,5},... | collective-permute-start | bytes 417800 | tf_op jit(solution)/shard_map/ppermute | solution.py:137
  20.6 2.6 %collective-permute-start.5 = (bf16[32,2176]{1,0:T(8,128)(2,1)S(1)}, bf16[32,2176]{1,0:T(8,128)(2,1)S(1)}, u32[]{:S(2)}, u32[]{:S(2)}) collective-permute-start(bf16[32,2176]{1,0:T(8,128)(2,1)S(1)} %get-tuple-element.11), channel_id=1, source_target_pairs={{0,16},{1,21},{2,18},{3,23},{4,20},{5,17},{6,22},{7,19},{8,24},{9,... | collective-permute-start | bytes 417800 | tf_op jit(solution)/shard_map/ppermute | solution.py:137
  23.2 0.0 collective-permute-start.6
  23.2 0.0 collective-permute-done.3
  23.2 3.0 %collective-permute-start.7 = (bf16[32,2176]{1,0:T(8,128)(2,1)S(1)}, bf16[32,2176]{1,0:T(8,128)(2,1)S(1)}, u32[]{:S(2)}, u32[]{:S(2)}) collective-permute-start(bf16[32,2176]{1,0:T(8,128)(2,1)S(1)} %collective-permute-done.3), channel_id=1, source_target_pairs={{0,1},{1,0},{2,3},{3,2},{4,5},{5,4},{6,7},{7,6},{8,9},{9,8},{10,11... | collective-permute-start | bytes 417800 | tf_op jit(solution)/shard_map/ppermute | solution.py:73
  26.3 0.0 collective-permute-done.4
  26.3 1.6 %collective-permute-start.8 = (bf16[32,2176]{1,0:T(8,128)(2,1)S(1)}, bf16[32,2176]{1,0:T(8,128)(2,1)S(1)}, u32[]{:S(2)}, u32[]{:S(2)}) collective-permute-start(bf16[32,2176]{1,0:T(8,128)(2,1)S(1)} %collective-permute-done.4), channel_id=1, source_target_pairs={{0,1},{1,0},{2,3},{3,2},{4,5},{5,4},{6,7},{7,6},{8,9},{9,8},{10,11... | collective-permute-start | bytes 417800 | tf_op jit(solution)/shard_map/ppermute | solution.py:73
  27.9 0.0 collective-permute-done.5
  27.9 8.1 %collective-permute-start.9 = (bf16[32,2176]{1,0:T(8,128)(2,1)S(1)}, bf16[32,2176]{1,0:T(8,128)(2,1)S(1)}, u32[]{:S(2)}, u32[]{:S(2)}) collective-permute-start(bf16[32,2176]{1,0:T(8,128)(2,1)S(1)} %collective-permute-done.5), channel_id=1, source_target_pairs={{0,1},{1,0},{2,3},{3,2},{4,5},{5,4},{6,7},{7,6},{8,9},{9,8},{10,11... | collective-permute-start | bytes 417800 | tf_op jit(solution)/shard_map/ppermute | solution.py:73
  36.0 0.0 collective-permute-done.6
  36.0 0.0 collective-permute-start.10
  36.0 0.0 collective-permute-done.7
  36.0 0.0 collective-permute-done.8
  36.1 0.9 %collective-permute-done.9 = bf16[32,2176]{1,0:T(8,128)(2,1)S(1)} collective-permute-done((bf16[32,2176]{1,0:T(8,128)(2,1)S(1)}, bf16[32,2176]{1,0:T(8,128)(2,1)S(1)}, u32[]{:S(2)}, u32[]{:S(2)}) %collective-permute-start.9) | collective-permute-done | bytes 139296 | tf_op jit(solution)/shard_map/ppermute | solution.py:73
  37.0 0.4 collective-permute-done.10
  37.4 0.2 broadcast_select_fusion.1
  37.6 0.1 maximum_bitcast_fusion
  37.7 0.0 copy-start.4
  37.7 0.0 copy-start.6
  37.7 0.3 multiply_reduce_fusion
  38.0 1.6 %slice_convert_fusion = f32[8,1,32,2048]{3,2,0,1:T(8,128)} fusion(bf16[8,1,32,2176]{3,2,0,1:T(8,128)(2,1)S(1)} %maximum_bitcast_fusion), kind=kLoop, calls=%fused_computation.22 | loop fusion | flops 524288 | bytes 3145728 | tf_op jit(solution)/shard_map/convert_element_type | solution.py:155
  39.6 0.1 slice_reduce_fusion
  39.7 0.5 convolution_bitcast_fusion.2
  40.3 0.5 copy-done.5
  40.7 0.5 fusion.5
  41.2 0.2 copy.59
  41.5 12.9 %all_gather.3 = bf16[8,1,32,768]{2,0,1,3:T(8,128)(2,1)S(1)} all-gather(bf16[8,1,32,192]{2,0,1,3:T(8,128)(2,1)S(1)} %copy.59), channel_id=1, replica_groups=mesh['ep'=8,'tp'=4] {'tp'}, dimensions={3}, use_global_device_ids=true | all-gather | bytes 491520 | tf_op jit(solution)/shard_map/all_gather | solution.py:161
  54.4 1.0 %copy.60 = bf16[8,1,32,768]{3,2,0,1:T(8,128)(2,1)S(1)} copy(bf16[8,1,32,768]{2,0,1,3:T(8,128)(2,1)S(1)} %all_gather.3) | data formatting | bytes 786432 | tf_op jit(solution)/shard_map/all_gather | solution.py:161
  55.3 0.2 fusion.40
  55.5 1.4 %fusion.3 = bf16[8,1,32,512]{3,2,0,1:T(8,128)(2,1)S(1)} fusion(bf16[1,768,512]{2,1,0:T(8,128)(2,1)S(1)} %copy-done, f32[8,1,32,2048]{3,2,0,1:T(8,128)} %slice_convert_fusion, s32[]{:T(128)S(6)} %select_n.140, bf16[8,1,32,768]{3,2,0,1:T(8,128)(2,1)S(1)} %copy.60, f32[8,32]{1,0:T(8,128)S(1)} %fusion.40), kind=kOutput, calls=%fused_computation.9 | convolution fusion | flops 201719808 | bytes 1967108 | tf_op jit(solution)/shard_map/secf,efd->secd/dot_general | solution.py:162
  57.0 0.1 broadcast_in_dim.123
  57.1 0.6 gather_fusion
  57.7 0.8 %broadcast_select_fusion.2 = bf16[8,32,640]{2,1,0:T(8,128)(2,1)} fusion(bf16[8,32,640]{2,1,0:T(8,128)(2,1)S(1)} %gather_fusion, pred[8]{0:T(512)(128)(4,1)S(1)} %compare_and_fusion), kind=kLoop, calls=%fused_computation.41 | loop fusion | flops 163840 | bytes 655368 | tf_op jit(solution)/shard_map/jit(_take)/select_n | solution.py:180
  58.5 4.5 %all-to-all-start = ((bf16[8,32,640]{2,1,0:T(8,128)(2,1)}), bf16[8,32,640]{2,1,0:T(8,128)(2,1)S(1)}, u32[]{:S(2)}, u32[]{:S(2)}) async-start(bf16[8,32,640]{2,1,0:T(8,128)(2,1)} %broadcast_select_fusion.2), calls=%async_computation | async-start | bytes 655360 | tf_op jit(solution)/shard_map/all_to_all | solution.py:179
  63.0 10.8 %all-to-all-done = bf16[8,32,640]{2,1,0:T(8,128)(2,1)S(1)} async-done(((bf16[8,32,640]{2,1,0:T(8,128)(2,1)}), bf16[8,32,640]{2,1,0:T(8,128)(2,1)S(1)}, u32[]{:S(2)}, u32[]{:S(2)}) %all-to-all-start) | async-done | bytes 327712 | tf_op jit(solution)/shard_map/all_to_all | solution.py:179
  73.8 0.1 copy.67
  73.9 0.9 %convolution_convert_fusion.1 = bf16[64,512]{1,0:T(8,128)(2,1)} fusion(bf16[256,640]{1,0:T(8,128)(2,1)S(1)} %bitcast.153, s32[256]{0:T(256)S(1)} %bitcast.162, s32[64]{0:T(128)S(1)} %iota_add_fusion.1), kind=kOutput, calls=%fused_computation.15 | convolution fusion | flops 16826368 | bytes 329216 | tf_op jit(solution)/shard_map/dot_general | solution.py:183
  (36 shorter events, 0.4 us)
Async XLA Ops:
  0.0 55.5 %copy-start = (bf16[1,768,512]{2,1,0:T(8,128)(2,1)S(1)}, bf16[1,768,512]{2,1,0:T(8,128)(2,1)}, u32[]{:S(2)}) copy-start(bf16[1,768,512]{2,1,0:T(8,128)(2,1)} %param.29) | copy-start | bytes 2359300
  6.6 1.4 %copy-start.3 = (s32[64,2]{0,1:T(2,128)S(1)}, s32[64,2]{0,1:T(2,128)}, u32[]{:S(2)}) copy-start(s32[64,2]{0,1:T(2,128)} %param.25) | copy-start | bytes 1540
  6.6 1.6 %copy-start.2 = (f32[64,2]{0,1:T(2,128)S(1)}, f32[64,2]{0,1:T(2,128)}, u32[]{:S(2)}) copy-start(f32[64,2]{0,1:T(2,128)} %param.26) | copy-start | bytes 1540
  6.6 1.6 %copy-start.1 = (bf16[64,512]{1,0:T(8,128)(2,1)S(1)}, bf16[64,512]{1,0:T(8,128)(2,1)}, u32[]{:S(2)}) copy-start(bf16[64,512]{1,0:T(8,128)(2,1)} %param.22) | copy-start | bytes 196612
  6.6 9.6 %copy-start.7 = (s32[8]{0:T(128)S(1)}, s32[8]{0:T(128)}, u32[]{:S(2)}) copy-start(s32[8]{0:T(128)} %param.21) | copy-start | bytes 100
  7.4 1.5 %collective-permute-start = (bf16[64,2,512]{2,0,1:T(8,128)(2,1)S(1)}, bf16[64,2,512]{2,0,1:T(8,128)(2,1)S(1)}, u32[]{:S(2)}, u32[]{:S(2)}) collective-permute-start(bf16[64,2,512]{2,0,1:T(8,128)(2,1)S(1)} %fusion.39), channel_id=1, source_target_pairs={{0,1},{1,0},{2,3},{3,2},{4,5},{5,4},{6,7},{7,6},{8,9},{9,8},{10,11... | collective-permute-start | bytes 393224 | tf_op jit(solution)/shard_map/ppermute | solution.py:73
  9.0 6.7 %collective-permute-start.1 = (bf16[64,2,512]{2,0,1:T(8,128)(2,1)S(1)}, bf16[64,2,512]{2,0,1:T(8,128)(2,1)S(1)}, u32[]{:S(2)}, u32[]{:S(2)}) collective-permute-start(bf16[64,2,512]{2,0,1:T(8,128)(2,1)S(1)} %get-tuple-element.5), channel_id=1, source_target_pairs={{0,2},{1,3},{2,0},{3,1},{4,6},{5,7},{6,4},{7,5},{8,10},{9,11},{10,... | collective-permute-start | bytes 393224 | tf_op jit(solution)/shard_map/ppermute | solution.py:76
  15.8 1.4 %collective-permute-start.2 = (bf16[64,2,512]{2,0,1:T(8,128)(2,1)S(1)}, bf16[64,2,512]{2,0,1:T(8,128)(2,1)S(1)}, u32[]{:S(2)}, u32[]{:S(2)}) collective-permute-start(bf16[64,2,512]{2,0,1:T(8,128)(2,1)S(1)} %add_convert_fusion), channel_id=1, source_target_pairs={{0,1},{1,0},{2,3},{3,2},{4,5},{5,4},{6,7},{7,6},{8,9},{9,8},{10,11... | collective-permute-start | bytes 393224 | tf_op jit(solution)/shard_map/ppermute | solution.py:73
  18.1 5.2 %collective-permute-start.3 = (bf16[32,2176]{1,0:T(8,128)(2,1)S(1)}, bf16[32,2176]{1,0:T(8,128)(2,1)S(1)}, u32[]{:S(2)}, u32[]{:S(2)}) collective-permute-start(bf16[32,2176]{1,0:T(8,128)(2,1)S(1)} %get-tuple-element.9), channel_id=1, source_target_pairs={{0,0},{1,5},{2,2},{3,7},{4,4},{5,1},{6,6},{7,3},{8,8},{9,13},{10,1... | collective-permute-start | bytes 417800 | tf_op jit(solution)/shard_map/ppermute | solution.py:137
  18.7 7.5 %collective-permute-start.4 = (bf16[32,2176]{1,0:T(8,128)(2,1)S(1)}, bf16[32,2176]{1,0:T(8,128)(2,1)S(1)}, u32[]{:S(2)}, u32[]{:S(2)}) collective-permute-start(bf16[32,2176]{1,0:T(8,128)(2,1)S(1)} %get-tuple-element.12), channel_id=1, source_target_pairs={{0,8},{1,13},{2,10},{3,15},{4,12},{5,9},{6,14},{7,11},{8,0},{9,5},... | collective-permute-start | bytes 417800 | tf_op jit(solution)/shard_map/ppermute | solution.py:137
  20.6 7.3 %collective-permute-start.5 = (bf16[32,2176]{1,0:T(8,128)(2,1)S(1)}, bf16[32,2176]{1,0:T(8,128)(2,1)S(1)}, u32[]{:S(2)}, u32[]{:S(2)}) collective-permute-start(bf16[32,2176]{1,0:T(8,128)(2,1)S(1)} %get-tuple-element.11), channel_id=1, source_target_pairs={{0,16},{1,21},{2,18},{3,23},{4,20},{5,17},{6,22},{7,19},{8,24},{9,... | collective-permute-start | bytes 417800 | tf_op jit(solution)/shard_map/ppermute | solution.py:137
  23.2 12.8 %collective-permute-start.6 = (bf16[32,2176]{1,0:T(8,128)(2,1)S(1)}, bf16[32,2176]{1,0:T(8,128)(2,1)S(1)}, u32[]{:S(2)}, u32[]{:S(2)}) collective-permute-start(bf16[32,2176]{1,0:T(8,128)(2,1)S(1)} %get-tuple-element.10), channel_id=1, source_target_pairs={{0,24},{1,29},{2,26},{3,31},{4,28},{5,25},{6,30},{7,27},{8,16},{9,... | collective-permute-start | bytes 417800 | tf_op jit(solution)/shard_map/ppermute | solution.py:137
  23.2 12.8 %collective-permute-start.7 = (bf16[32,2176]{1,0:T(8,128)(2,1)S(1)}, bf16[32,2176]{1,0:T(8,128)(2,1)S(1)}, u32[]{:S(2)}, u32[]{:S(2)}) collective-permute-start(bf16[32,2176]{1,0:T(8,128)(2,1)S(1)} %collective-permute-done.3), channel_id=1, source_target_pairs={{0,1},{1,0},{2,3},{3,2},{4,5},{5,4},{6,7},{7,6},{8,9},{9,8},{10,11... | collective-permute-start | bytes 417800 | tf_op jit(solution)/shard_map/ppermute | solution.py:73
  26.3 9.8 %collective-permute-start.8 = (bf16[32,2176]{1,0:T(8,128)(2,1)S(1)}, bf16[32,2176]{1,0:T(8,128)(2,1)S(1)}, u32[]{:S(2)}, u32[]{:S(2)}) collective-permute-start(bf16[32,2176]{1,0:T(8,128)(2,1)S(1)} %collective-permute-done.4), channel_id=1, source_target_pairs={{0,1},{1,0},{2,3},{3,2},{4,5},{5,4},{6,7},{7,6},{8,9},{9,8},{10,11... | collective-permute-start | bytes 417800 | tf_op jit(solution)/shard_map/ppermute | solution.py:73
  27.9 9.1 %collective-permute-start.9 = (bf16[32,2176]{1,0:T(8,128)(2,1)S(1)}, bf16[32,2176]{1,0:T(8,128)(2,1)S(1)}, u32[]{:S(2)}, u32[]{:S(2)}) collective-permute-start(bf16[32,2176]{1,0:T(8,128)(2,1)S(1)} %collective-permute-done.5), channel_id=1, source_target_pairs={{0,1},{1,0},{2,3},{3,2},{4,5},{5,4},{6,7},{7,6},{8,9},{9,8},{10,11... | collective-permute-start | bytes 417800 | tf_op jit(solution)/shard_map/ppermute | solution.py:73
  36.0 1.4 %collective-permute-start.10 = (bf16[32,2176]{1,0:T(8,128)(2,1)S(1)}, bf16[32,2176]{1,0:T(8,128)(2,1)S(1)}, u32[]{:S(2)}, u32[]{:S(2)}) collective-permute-start(bf16[32,2176]{1,0:T(8,128)(2,1)S(1)} %collective-permute-done.6), channel_id=1, source_target_pairs={{0,1},{1,0},{2,3},{3,2},{4,5},{5,4},{6,7},{7,6},{8,9},{9,8},{10,11... | collective-permute-start | bytes 417800 | tf_op jit(solution)/shard_map/ppermute | solution.py:73
  37.7 2.0 %copy-start.4 = (bf16[1,2048,192]{1,2,0:T(8,128)(2,1)S(1)}, bf16[1,2048,192]{1,2,0:T(8,128)(2,1)}, u32[]{:S(2)}) copy-start(bf16[1,2048,192]{1,2,0:T(8,128)(2,1)} %param.27) | copy-start | bytes 2359300
  37.7 2.0 %copy-start.6 = (f32[2048]{0:T(1024)S(1)}, f32[2048]{0:T(1024)}, u32[]{:S(2)}) copy-start(f32[2048]{0:T(1024)} %param.24) | copy-start | bytes 24580
  39.6 1.1 %copy-start.5 = (bf16[1,2048,192]{1,2,0:T(8,128)(2,1)S(1)}, bf16[1,2048,192]{1,2,0:T(8,128)(2,1)}, u32[]{:S(2)}) copy-start(bf16[1,2048,192]{1,2,0:T(8,128)(2,1)} %param.28) | copy-start | bytes 2359300
  58.5 15.3 %all-to-all-start = ((bf16[8,32,640]{2,1,0:T(8,128)(2,1)}), bf16[8,32,640]{2,1,0:T(8,128)(2,1)S(1)}, u32[]{:S(2)}, u32[]{:S(2)}) async-start(bf16[8,32,640]{2,1,0:T(8,128)(2,1)} %broadcast_select_fusion.2), calls=%async_computation | async-start | bytes 655360 | tf_op jit(solution)/shard_map/all_to_all | solution.py:179

commit v2 on v1

v2 whole, which is shorter than its diff:
```python
import functools
import math

import jax
import jax.numpy as jnp
from jax import lax
from jax.experimental import pallas as pl
from jax.experimental.pallas import tpu as pltpu
from jax.sharding import PartitionSpec as P

HEAD = 128
QHEADS = 16
KVHEADS = 4
LANES = 128
TAGS = 16
VMEM_LIMIT = 24 * 1024 * 1024

BF16 = jnp.bfloat16
F32 = jnp.float32


def vmem():
    return pl.BlockSpec(memory_space=pltpu.VMEM)


def params():
    return pltpu.CompilerParams(vmem_limit_bytes=VMEM_LIMIT)


def dot(a, b):
    return jnp.dot(a, b, preferred_element_type=F32)


def dot_t(a, b):
    return lax.dot_general(a, b, (((1,), (1,)), ((), ())), preferred_element_type=F32)


def attend_kernel(
    kv_local,
    length_ref,
    query_ref,
    new_key_ref,
    new_value_ref,
    key_ref,
    value_ref,
    weight_hbm,
    keep_ref,
    give_ref,
    weight_ref,
    sems,
):
    core = lax.axis_index("tp") % 2
    width = weight_ref.shape[2]
    copies = []
    for i, block in enumerate((1 - core, 3 - core, core, core + 2)):
        start = pl.multiple_of(block * width, width)
        copy = pltpu.make_async_copy(
            weight_hbm.at[:, pl.ds(start, width)], weight_ref.at[i], sems.at[i]
        )
        copy.start()
        copies.append(copy)
    tokens = query_ref.shape[0]
    cached = key_ref.shape[0]
    group = QHEADS // KVHEADS
    length = length_ref[0]
    scale = 1.0 / math.sqrt(HEAD)
    pieces = []
    for g in range(kv_local):
        columns = slice(g * HEAD, (g + 1) * HEAD)
        rows = jnp.concatenate(
            [
                query_ref[:, (g * group + i) * HEAD : (g * group + i + 1) * HEAD]
                for i in range(group)
            ],
            axis=0,
        )
        old = dot_t(rows, key_ref[:, columns]) * scale
        new = dot_t(rows, new_key_ref[:, columns]) * scale
        position = lax.broadcasted_iota(jnp.int32, old.shape, 1)
        old = jnp.where(position < length, old, -1e30)
        current = lax.broadcasted_iota(jnp.int32, new.shape, 0) % tokens
        position = lax.broadcasted_iota(jnp.int32, new.shape, 1)
        new = jnp.where(position <= current, new, -1e30)
        highest = jnp.maximum(
            jnp.max(old, axis=1, keepdims=True), jnp.max(new, axis=1, keepdims=True)
        )
        old = jnp.exp(old - highest)
        new = jnp.exp(new - highest)
        totals = jnp.sum(old, axis=1, keepdims=True) + jnp.sum(new, axis=1, keepdims=True)
        mixed = dot(old.astype(BF16), value_ref[:, columns]) + dot(
            new.astype(BF16), new_value_ref[:, columns]
        )
        mixed = (mixed / totals).astype(BF16)
        pieces += [mixed[i * tokens : (i + 1) * tokens] for i in range(group)]
    context = jnp.concatenate(pieces, axis=1)
    for i in range(4):
        copies[i].wait()
        part = dot(context, weight_ref[i])
        columns = slice((i % 2) * width, (i % 2 + 1) * width)
        if i < 2:
            give_ref[:, columns] = part.astype(BF16)
        else:
            keep_ref[:, columns] = part


def gather_kernel(peers, part_ref, other_ref, pick_ref, tags_ref, *send_refs):
    core = lax.axis_index("tp") % 2
    rows_each = pick_ref.shape[0] // peers
    pick = pick_ref[...]
    width = part_ref.shape[1] // 2
    blocks = width // LANES
    for source, parity in ((part_ref, core), (other_ref, 1 - core)):
        for half in range(2):
            rows = dot(pick, source[:, half * width : (half + 1) * width]).astype(BF16)
            base = (2 * half + parity) * (blocks * rows_each)
            for k in range(peers):
                for j in range(blocks):
                    start = pl.multiple_of(base + j * rows_each, rows_each)
                    send_refs[k][pl.ds(start, rows_each), :] = rows[
                        k * rows_each : (k + 1) * rows_each, j * LANES : (j + 1) * LANES
                    ]
    for k in range(peers):
        send_refs[k][4 * blocks * rows_each :, :] = tags_ref[k]


def hidden_units_kernel(
    peers, rows_each, gain_ref, gate_ref, gate_pair_ref, up_ref, up_pair_ref, *refs
):
    got = refs[:peers]
    act_ref, side_ref = refs[peers:]
    tp = lax.axis_index("tp")
    core = tp % 2
    blocks = gain_ref.shape[0]
    per_device = blocks // 4
    parts = [
        jnp.concatenate(
            [ref[j * rows_each : (j + 1) * rows_each, :] for ref in got], axis=0
        ).astype(F32)
        for j in range(blocks)
    ]
    squares = parts[0] * parts[0]
    for part in parts[1:]:
        squares = squares + part * part
    mean = jnp.sum(squares, axis=1, keepdims=True) * (1.0 / (blocks * LANES))
    factor = lax.rsqrt(mean + 1e-06)
    normed = jnp.concatenate(
        [(parts[j] * factor * gain_ref[j : j + 1, :]).astype(BF16) for j in range(blocks)], axis=1
    )

    def units(gate, up):
        value = dot(normed, gate[...])
        return value / (1.0 + jnp.exp(-value)) * dot(normed, up[...])

    own = units(gate_ref, up_ref)
    pair = units(gate_pair_ref, up_pair_ref)
    low = jnp.where(core == 0, own, pair)
    high = jnp.where(core == 0, pair, own)
    act_ref[...] = jnp.concatenate([low, high], axis=1).astype(BF16)
    tall = per_device * rows_each
    start = pl.multiple_of((tp + 1 - 2 * core) * tall, tall)
    for k in range(peers):
        side_ref[k, :tall, :] = got[k][pl.ds(start, tall), :]
        side_ref[k, tall:, :] = got[k][blocks * rows_each :, :]


def down_kernel(
    peers,
    rows_each,
    order_ref,
    act_ref,
    act_half_ref,
    act_core_ref,
    act_both_ref,
    down_ref,
    side_ref,
    *refs,
):
    got = refs[:peers]
    out_ref = refs[peers]
    tp = lax.axis_index("tp")
    me = lax.axis_index("ep")
    half, core = tp // 2, tp % 2
    units = act_ref.shape[1]
    blocks = down_ref.shape[1] // LANES
    tall = blocks * rows_each
    here = down_ref[pl.ds(pl.multiple_of(half * units, units), units), :]
    there = down_ref[pl.ds(pl.multiple_of((1 - half) * units, units), units), :]
    diagonal = lax.broadcasted_iota(jnp.int32, (rows_each, LANES), 0) == lax.broadcasted_iota(
        jnp.int32, (rows_each, LANES), 1
    )
    start = pl.multiple_of(tp * tall, tall)
    for group in range(2):
        near, far = ((act_ref, act_half_ref), (act_core_ref, act_both_ref))[group]
        result = dot(near[...], here) + dot(far[...], there)
        for k in range(peers):
            request = jnp.bitwise_xor(me, 2 * k + (core if group == 0 else 1 - core))
            place = order_ref[request]
            if group == 0:
                rows = got[k][pl.ds(start, tall), :]
                tags = got[k][4 * tall :, :]
            else:
                rows = side_ref[k, :tall, :]
                tags = side_ref[k, tall:, :]
            mix = jnp.sum(
                jnp.where(diagonal, tags.astype(F32)[1:2, :], 0.0), axis=1, keepdims=True
            )
            for j in range(blocks):
                piece = slice(j * rows_each, (j + 1) * rows_each)
                value = rows[piece].astype(F32) + result[
                    k * rows_each : (k + 1) * rows_each, j * LANES : (j + 1) * LANES
                ]
                out_ref[place, piece, :] = (mix * value).astype(BF16)
            out_ref[place, tall:, :] = tags


def combine_kernel(rows_each, came_ref, out_ref):
    tokens, width = out_ref.shape
    blocks = width // LANES
    tall = blocks * rows_each
    number = lax.broadcasted_iota(jnp.int32, (tokens, rows_each), 0).astype(F32) + 1.0
    total = jnp.zeros((tokens, width), F32)
    for e in range(came_ref.shape[0]):
        tags = came_ref[e, tall:, :].astype(F32)
        chosen = (number == tags[0:1, :rows_each]).astype(BF16)
        rows = jnp.concatenate(
            [came_ref[e, j * rows_each : (j + 1) * rows_each, :] for j in range(blocks)], axis=1
        )
        total = total + dot(chosen, rows)
    out_ref[...] = total.astype(BF16)


def shards(
    queries,
    new_keys,
    new_values,
    key_cache,
    value_cache,
    cache_lengths,
    request_order,
    residual,
    out_weight,
    norm_gain,
    route_experts,
    route_weights,
    expert_gate,
    expert_up,
    expert_down,
):
    tp_count = lax.axis_size("tp")
    ep_count = lax.axis_size("ep")
    kv_local = KVHEADS // tp_count
    me_ep = lax.axis_index("ep")
    me_tp = lax.axis_index("tp")
    half, core = me_tp // 2, me_tp % 2

    def swap_core(x):
        return lax.ppermute(x, "tp", [(i, i ^ 1) for i in range(tp_count)])

    def swap_half(x):
        return lax.ppermute(x, "tp", [(i, i ^ 2) for i in range(tp_count)])

    gate, up, down = expert_gate[0], expert_up[0], expert_down[0]
    gate_pair, up_pair = swap_core(gate), swap_core(up)

    tokens, top = route_experts.shape
    capacity = 2 * tokens * top // ep_count
    rows_each = -(-capacity // 16) * 16
    peers = ep_count // 2
    width = residual.shape[1]
    blocks = width // LANES
    tall = blocks * rows_each
    units = 2 * gate.shape[1]
    shape = jax.ShapeDtypeStruct

    keep, give = pl.pallas_call(
        functools.partial(attend_kernel, kv_local),
        out_shape=(shape((tokens, 2 * width), F32), shape((tokens, 2 * width), BF16)),
        in_specs=[pl.BlockSpec(memory_space=pltpu.SMEM)]
        + [vmem()] * 5
        + [pl.BlockSpec(memory_space=pl.ANY)],
        out_specs=(vmem(), vmem()),
        scratch_shapes=[
            pltpu.VMEM((4, out_weight.shape[0], width), BF16),
            pltpu.SemaphoreType.DMA((4,)),
        ],
        compiler_params=params(),
        name="attend",
    )(
        cache_lengths,
        queries,
        new_keys,
        new_values,
        key_cache[0],
        value_cache[0],
        out_weight,
    )

    peer = jnp.bitwise_xor(me_ep, 2 * jnp.arange(peers, dtype=jnp.int32) + core)
    matches = route_experts[None] == peer[:, None, None]
    named = jnp.any(matches, axis=2)
    token_range = jnp.arange(tokens, dtype=jnp.int32)
    before = (token_range[:, None] < token_range[None, :]).astype(BF16)
    rank = dot(named.astype(BF16), before).astype(jnp.int32)
    slots = jnp.arange(rows_each, dtype=jnp.int32)
    pick = (rank[:, None, :] == slots[None, :, None]) & named[:, None, :]
    mixing = (route_weights / jnp.sum(route_weights, axis=1, keepdims=True)).astype(BF16)
    mix_of = jnp.sum(jnp.where(matches, mixing[None].astype(F32), 0.0), axis=2)
    token_tag = jnp.sum(jnp.where(pick, (token_range + 1).astype(F32), 0.0), axis=2)
    mix_tag = jnp.sum(jnp.where(pick, mix_of[:, None, :], 0.0), axis=2)
    tags = jnp.pad(
        jnp.stack([token_tag, mix_tag], axis=1).astype(BF16),
        ((0, 0), (0, TAGS - 2), (0, LANES - rows_each)),
    )
    pick = pick.astype(BF16).reshape(peers * rows_each, tokens)

    keep = keep + swap_core(give).astype(F32)
    keep = keep.reshape(tokens, 2, width)
    mine = (jnp.arange(2) == half)[None, :, None]
    keep = keep + jnp.where(mine, residual.astype(F32)[:, None, :], 0.0)
    keep = keep.reshape(tokens, 2 * width)
    part = (keep + swap_half(keep.astype(BF16)).astype(F32)).astype(BF16)
    other = swap_core(part)

    block_shape = shape((tp_count * tall + TAGS, LANES), BF16)
    send = pl.pallas_call(
        functools.partial(gather_kernel, peers),
        out_shape=[block_shape] * peers,
        in_specs=[vmem()] * 4,
        out_specs=[vmem()] * peers,
        compiler_params=params(),
        name="gather_rows",
    )(part, other, pick, tags)

    def route(k):
        return [
            (e * tp_count + t, (e ^ (2 * k + t % 2)) * tp_count + t)
            for e in range(ep_count)
            for t in range(tp_count)
        ]

    got = [lax.ppermute(send[k], ("ep", "tp"), route(k)) for k in range(peers)]

    act, side = pl.pallas_call(
        functools.partial(hidden_units_kernel, peers, rows_each),
        out_shape=(
            shape((peers * rows_each, units), BF16),
            shape((peers, tall + TAGS, LANES), BF16),
        ),
        in_specs=[vmem()] * (5 + peers),
        out_specs=(vmem(), vmem()),
        compiler_params=params(),
        name="hidden_units",
    )(norm_gain.reshape(-1, LANES), gate, gate_pair, up, up_pair, *got)

    act_half = swap_half(act)
    act_core = swap_core(act)
    side = swap_core(side)
    act_both = swap_core(act_half)

    result = pl.pallas_call(
        functools.partial(down_kernel, peers, rows_each),
        out_shape=shape((ep_count, tall + TAGS, LANES), BF16),
        in_specs=[pl.BlockSpec(memory_space=pltpu.SMEM)] + [vmem()] * (6 + peers),
        out_specs=vmem(),
        compiler_params=params(),
        name="down",
    )(request_order, act, act_half, act_core, act_both, down, side, *got)

    came = lax.all_to_all(result, "ep", split_axis=0, concat_axis=0, tiled=True)
    return pl.pallas_call(
        functools.partial(combine_kernel, rows_each),
        out_shape=shape((tokens, width), BF16),
        in_specs=[vmem()],
        out_specs=vmem(),
        compiler_params=params(),
        name="combine",
    )(came)


def solution(mesh):
    return jax.shard_map(
        shards,
        mesh=mesh,
        in_specs=(
            P("ep", "tp"),
            P("ep", "tp"),
            P("ep", "tp"),
            P("ep", None, "tp"),
            P("ep", None, "tp"),
            P("ep"),
            P(),
            P("ep", "tp"),
            P("tp", None),
            P(),
            P("ep", None),
            P("ep", None),
            P("ep", None, "tp"),
            P("ep", None, "tp"),
            P("ep", None, "tp"),
        ),
        out_specs=P("ep", "tp"),
        check_vma=False,
    )
```

time: 75.2 us -> 65.6 us (0.87)
  starting transfers between devices: 25.9 us -> 14.4 us
  local copies, waits for them, and re-layouts: 6.23 us -> 13.5 us
  Pallas kernels: 0 us -> 7.02 us
  matrix products: 6.98 us -> 0.13 us
  waiting for transfers between devices: 17.5 us -> 11.1 us
  blocking collectives: 12.9 us -> 17.5 us
  other arithmetic: 4.2 us -> 0.54 us
    all_to_all x0 -> x1, blocking collectives: none -> 17.5 us  [shards(): came = lax.all_to_all(result, 'ep', split_axis=0, concat_axis=0, tiled=True)]
    all_gather x1 -> x0, blocking collectives: 12.9 us -> none  [shards(): activation = lax.all_gather(activation, 'tp', axis=3, tiled=True)]
    all_to_all x1 -> x0, waiting for transfers between devices: 10.8 us -> none  [shards(): lax.all_to_all(jnp.take(result, back, axis=0), 'ep', split_axis=0, concat...]
    ppermute x6 -> x7, starting transfers between devices: 13.4 us -> 4.03 us  [swap_core(): return lax.ppermute(x, 'tp', [(i, i ^ 1) for i in range(tp_count)])]
    unnamed x17 -> x31, local copies, waits for them, and re-layouts: 0.57 us -> 9.6 us
    pallas_call x0 -> x5, Pallas kernels: none -> 7.02 us  [the longest x1 1.9 us: shards(): pl.pallas_call(functools.partial(hidden_units_kernel, peers, rows_each),...]
    dot_general x9 -> x1, matrix products: 6.98 us -> 0.13 us  [dot(): return jnp.dot(a, b, preferred_element_type=F32)]
    all_to_all x1 -> x0, starting transfers between devices: 4.49 us -> none  [shards(): lax.all_to_all(jnp.take(result, back, axis=0), 'ep', split_axis=0, concat...]
  transfers between devices with their start and end apart: 12 -> 13, of which waited for: 6 -> 5; matrix products, arithmetic and copies ran while one was open for 1% -> 10% of each run, Pallas kernels for 0% -> 2%
where the time goes in v2:
time: 65.6 us; the launch traced here: 65 us
  blocking collectives  17.5 us (27%)
  starting transfers between devices  14.4 us (22%)
  local copies, waits for them, and re-layouts  13.5 us (21%)
  waiting for transfers between devices  11.1 us (17%)
  Pallas kernels  7.02 us (11%)
  between operations  0.87 us (1%)
    all_to_all x1, blocking collectives, shards(): came = lax.all_to_all(result, 'ep', split_axis=0, concat_axis=0, tiled=True)  17.5 us
    unnamed x31, local copies, waits for them, and re-layouts  9.6 us
    ppermute x4, starting transfers between devices, shards(): got = [lax.ppermute(send[k], ('ep', 'tp'), route(k)) for k in range(peers)]  5.97 us
    ppermute x2, waiting for transfers between devices, swap_half(): return lax.ppermute(x, 'tp', [(i, i ^ 2) for i in range(tp_count)])  5 us
    ppermute x2, starting transfers between devices, swap_half(): return lax.ppermute(x, 'tp', [(i, i ^ 2) for i in range(tp_count)])  4.42 us
    ppermute x4, waiting for transfers between devices, shards(): got = [lax.ppermute(send[k], ('ep', 'tp'), route(k)) for k in range(peers)]  4.14 us
    ppermute x7, starting transfers between devices, swap_core(): return lax.ppermute(x, 'tp', [(i, i ^ 1) for i in range(tp_count)])  4.03 us
    ppermute x2, local copies, waits for them, and re-layouts, swap_core(): return lax.ppermute(x, 'tp', [(i, i ^ 1) for i in range(tp_count)])  3.66 us
  transfers between devices with their start and end apart: 13, of which 5 were waited for; matrix products, arithmetic and copies ran while one was open for 10% of the time, Pallas kernels for 2%

profile of v2, /device:TPU:0, one launch (start us, length us, event | category | flops | bytes accessed | tf_op | source)
XLA Modules:
  0.0 65.0 jit_solution(8917117993632047476)
XLA Ops:
  0.0 0.0 copy-start.12
  0.0 0.0 copy-start.13
  0.7 0.0 copy-start.1
  0.7 1.6 %copy-done.1 = bf16[512,2048]{1,0:T(8,128)(2,1)S(1)} copy-done((bf16[512,2048]{1,0:T(8,128)(2,1)S(1)}, bf16[512,2048]{1,0:T(8,128)(2,1)}, u32[]{:S(2)}) %copy-start.1) | copy-done | bytes 2097176
  2.3 0.0 copy-start.3
  2.3 0.9 %copy-done.3 = bf16[1,512,128]{2,1,0:T(8,128)(2,1)S(1)} copy-done((bf16[1,512,128]{2,1,0:T(8,128)(2,1)S(1)}, bf16[1,512,128]{2,1,0:T(8,128)(2,1)}, u32[]{:S(2)}) %copy-start.3) | copy-done | bytes 131096
  3.2 0.0 copy-start.4
  3.2 0.9 %copy-done.4 = bf16[1,512,128]{2,1,0:T(8,128)(2,1)S(1)} copy-done((bf16[1,512,128]{2,1,0:T(8,128)(2,1)S(1)}, bf16[1,512,128]{2,1,0:T(8,128)(2,1)}, u32[]{:S(2)}) %copy-start.4) | copy-done | bytes 131096
  4.1 0.8 %copy-done.5 = bf16[64,512]{1,0:T(8,128)(2,1)S(1)} copy-done((bf16[64,512]{1,0:T(8,128)(2,1)S(1)}, bf16[64,512]{1,0:T(8,128)(2,1)}, u32[]{:S(2)}) %copy-start.5) | copy-done | bytes 65560
  4.9 0.7 %copy-done.6 = bf16[64,128]{1,0:T(8,128)(2,1)S(1)} copy-done((bf16[64,128]{1,0:T(8,128)(2,1)S(1)}, bf16[64,128]{1,0:T(8,128)(2,1)}, u32[]{:S(2)}) %copy-start.6) | copy-done | bytes 16408
  5.6 0.7 %copy-done.7 = bf16[64,128]{1,0:T(8,128)(2,1)S(1)} copy-done((bf16[64,128]{1,0:T(8,128)(2,1)S(1)}, bf16[64,128]{1,0:T(8,128)(2,1)}, u32[]{:S(2)}) %copy-start.7) | copy-done | bytes 16408
  6.4 1.8 %attend.1 = (f32[64,1024]{1,0:T(8,128)S(1)}, bf16[64,1024]{1,0:T(8,128)(2,1)S(1)}) custom-call(s32[1]{0:T(128)S(6)} %copy.43.length_ref, bf16[64,512]{1,0:T(8,128)(2,1)S(1)} %copy-done.5, bf16[64,128]{1,0:T(8,128)(2,1)S(1)} %copy-done.6, bf16[64,128]{1,0:T(8,128)(2,1)S(1)} %copy-done.7, bf16[512,128]{1,0:T(8,128)(2,1)S(1)} %bitcast.28, ...), custom_call_target="tpu_custom_call" | custom-call | tf_op jit(solution)/shard_map/attend/pallas_call | solution.py:275
  8.2 0.5 collective-permute-start.2
  8.7 0.0 copy-done.10
  8.7 0.1 collective-permute-start.1
  8.8 0.4 collective-permute-start
  9.2 0.0 copy-done.12
  9.2 0.1 broadcast_in_dim.68
  9.3 0.0 copy-done.11
  9.3 0.1 broadcast_in_dim.71
  9.5 0.0 copy-done.13
  9.5 0.1 compare_reduce_fusion
  9.6 0.1 convolution_convert_fusion
  9.7 0.0 collective-permute-done.2
  9.8 2.9 %collective-permute-start.3 = (bf16[64,1024]{1,0:T(8,128)(2,1)S(1)}, bf16[64,1024]{1,0:T(8,128)(2,1)S(1)}, u32[]{:S(2)}, u32[]{:S(2)}) collective-permute-start(bf16[64,1024]{1,0:T(8,128)(2,1)S(1)} %fusion.8), channel_id=1, source_target_pairs={{0,2},{1,3},{2,0},{3,1},{4,6},{5,7},{6,4},{7,5},{8,10},{9,11},{10,... | collective-permute-start | bytes 393224 | tf_op jit(solution)/shard_map/ppermute | solution.py:260
  12.6 0.1 fusion.10
  12.7 3.8 %collective-permute-done.3 = bf16[64,1024]{1,0:T(8,128)(2,1)S(1)} collective-permute-done((bf16[64,1024]{1,0:T(8,128)(2,1)S(1)}, bf16[64,1024]{1,0:T(8,128)(2,1)S(1)}, u32[]{:S(2)}, u32[]{:S(2)}) %collective-permute-start.3) | collective-permute-done | bytes 131104 | tf_op jit(solution)/shard_map/ppermute | solution.py:260
  16.5 0.1 add_convert_fusion.part_ref
  16.5 0.1 collective-permute-start.4
  16.6 0.1 select_reduce_fusion.1
  16.8 0.1 eq.57
  16.9 0.1 fusion.2.pick_ref
  17.0 1.0 %collective-permute-done.4.other_ref = bf16[64,1024]{1,0:T(8,128)(2,1)S(1)} collective-permute-done((bf16[64,1024]{1,0:T(8,128)(2,1)S(1)}, bf16[64,1024]{1,0:T(8,128)(2,1)S(1)}, u32[]{:S(2)}, u32[]{:S(2)}) %collective-permute-start.4) | collective-permute-done | bytes 131104 | tf_op jit(solution)/shard_map/ppermute | solution.py:257
  18.0 1.1 %gather_rows.1 = (bf16[528,128]{1,0:T(8,128)(2,1)}, bf16[528,128]{1,0:T(8,128)(2,1)}, bf16[528,128]{1,0:T(8,128)(2,1)}, bf16[528,128]{1,0:T(8,128)(2,1)}) custom-call(bf16[64,1024]{1,0:T(8,128)(2,1)S(1)} %add_convert_fusion.part_ref, bf16[64,1024]{1,0:T(8,128)(2,1)S(1)} %collective-permute-done.4.other_ref, bf16[128,64]{1,0:T(8,128)(2,1)S(1)} %fusion.2.pick_ref, ...), custom_call_target="tpu_custom_call" | custom-call | tf_op jit(solution)/shard_map/gather_rows/pallas_call | solution.py:325
  19.0 1.6 %collective-permute-start.5 = (bf16[528,128]{1,0:T(8,128)(2,1)}, bf16[528,128]{1,0:T(8,128)(2,1)S(1)}, u32[]{:S(2)}, u32[]{:S(2)}) collective-permute-start(bf16[528,128]{1,0:T(8,128)(2,1)} %get-tuple-element.15), channel_id=1, source_target_pairs={{0,0},{1,5},{2,2},{3,7},{4,4},{5,1},{6,6},{7,3},{8,8},{9,13},{10,1... | collective-permute-start | bytes 405512 | tf_op jit(solution)/shard_map/ppermute | solution.py:341
  20.6 1.8 %collective-permute-start.6 = (bf16[528,128]{1,0:T(8,128)(2,1)}, bf16[528,128]{1,0:T(8,128)(2,1)S(1)}, u32[]{:S(2)}, u32[]{:S(2)}) collective-permute-start(bf16[528,128]{1,0:T(8,128)(2,1)} %get-tuple-element.16), channel_id=1, source_target_pairs={{0,8},{1,13},{2,10},{3,15},{4,12},{5,9},{6,14},{7,11},{8,0},{9,5},... | collective-permute-start | bytes 405512 | tf_op jit(solution)/shard_map/ppermute | solution.py:341
  22.4 2.6 %collective-permute-start.7 = (bf16[528,128]{1,0:T(8,128)(2,1)}, bf16[528,128]{1,0:T(8,128)(2,1)S(1)}, u32[]{:S(2)}, u32[]{:S(2)}) collective-permute-start(bf16[528,128]{1,0:T(8,128)(2,1)} %get-tuple-element.17), channel_id=1, source_target_pairs={{0,16},{1,21},{2,18},{3,23},{4,20},{5,17},{6,22},{7,19},{8,24},{9,... | collective-permute-start | bytes 405512 | tf_op jit(solution)/shard_map/ppermute | solution.py:341
  25.0 0.0 collective-permute-done.1
  25.0 0.0 collective-permute-start.8
  25.0 1.4 %copy.32 = bf16[1,2048,192]{2,1,0:T(8,128)(2,1)S(1)} copy(bf16[1,2048,192]{1,2,0:T(8,128)(2,1)} %param.27) | data formatting | bytes 1572864 | tf_op args[12]
  26.4 0.5 copy.34
  27.0 1.4 %copy.39.up_pair_ref = bf16[2048,192]{1,0:T(8,128)(2,1)S(1)} copy(bf16[2048,192]{0,1:T(8,128)(2,1)} %collective-permute-done.1) | data formatting | bytes 1572864 | tf_op jit(solution)/shard_map/ppermute | solution.py:257
  28.4 0.0 collective-permute-done
  28.4 2.2 %copy.38.gate_pair_ref = bf16[2048,192]{1,0:T(8,128)(2,1)} copy(bf16[2048,192]{0,1:T(8,128)(2,1)} %collective-permute-done) | data formatting | bytes 1572864 | tf_op jit(solution)/shard_map/ppermute | solution.py:257
  30.6 0.0 collective-permute-done.5.refs_0_
  30.6 0.0 collective-permute-done.6.refs_1_
  30.6 0.0 collective-permute-done.7.refs_2_
  30.6 4.1 %collective-permute-done.8.refs_3_ = bf16[528,128]{1,0:T(8,128)(2,1)} collective-permute-done((bf16[528,128]{1,0:T(8,128)(2,1)}, bf16[528,128]{1,0:T(8,128)(2,1)}, u32[]{:S(2)}, u32[]{:S(2)}) %collective-permute-start.8) | collective-permute-done | bytes 135200 | tf_op jit(solution)/shard_map/ppermute | solution.py:341
  34.8 1.2 %copy-done = bf16[2048,192]{1,0:T(8,128)(2,1)S(1)} copy-done((bf16[2048,192]{1,0:T(8,128)(2,1)S(1)}, bf16[2048,192]{1,0:T(8,128)(2,1)}, u32[]{:S(2)}) %copy-start) | copy-done | bytes 786456
  36.0 0.7 %copy-done.8 = f32[2048]{0:T(1024)S(1)} copy-done((f32[2048]{0:T(1024)S(1)}, f32[2048]{0:T(1024)}, u32[]{:S(2)}) %copy-start.8) | copy-done | bytes 8216
  36.7 1.9 %hidden_units.1 = (bf16[128,384]{1,0:T(8,128)(2,1)S(1)}, bf16[4,144,128]{2,1,0:T(8,128)(2,1)S(1)}) custom-call(f32[16,128]{1,0:T(8,128)S(1)} %bitcast.30, bf16[2048,192]{1,0:T(8,128)(2,1)S(1)} %bitcast.25, bf16[2048,192]{1,0:T(8,128)(2,1)S(1)} %copy-done, bf16[2048,192]{1,0:T(8,128)(2,1)S(1)} %bitcast.26, bf16[2048,192]{1,0:T(8,128)(2,1)S(1)} %copy.39.up_pair_ref, ...), custom_call_target="tpu_custom_call" | custom-call | tf_op jit(solution)/shard_map/hidden_units/pallas_call | solution.py:343
  38.6 1.6 %collective-permute-start.9 = (bf16[128,384]{1,0:T(8,128)(2,1)S(1)}, bf16[128,384]{1,0:T(8,128)(2,1)S(1)}, u32[]{:S(2)}, u32[]{:S(2)}) collective-permute-start(bf16[128,384]{1,0:T(8,128)(2,1)S(1)} %get-tuple-element.19.act_ref), channel_id=1, source_target_pairs={{0,2},{1,3},{2,0},{3,1},{4,6},{5,7},{6,4},{7,5},{8,10},{9,11},{10,... | collective-permute-start | bytes 294920 | tf_op jit(solution)/shard_map/ppermute | solution.py:260
  40.2 1.9 %collective-permute-start.12 = (bf16[4,144,128]{2,1,0:T(8,128)(2,1)S(1)}, bf16[4,144,128]{2,1,0:T(8,128)(2,1)S(1)}, u32[]{:S(2)}, u32[]{:S(2)}) collective-permute-start(bf16[4,144,128]{2,1,0:T(8,128)(2,1)S(1)} %get-tuple-element.20), channel_id=1, source_target_pairs={{0,1},{1,0},{2,3},{3,2},{4,5},{5,4},{6,7},{7,6},{8,9},{9,8},{10,11... | collective-permute-start | bytes 442376 | tf_op jit(solution)/shard_map/ppermute | solution.py:257
  42.1 0.0 collective-permute-start.10
  42.1 1.2 %collective-permute-done.9.act_half_ref = bf16[128,384]{1,0:T(8,128)(2,1)S(1)} collective-permute-done((bf16[128,384]{1,0:T(8,128)(2,1)S(1)}, bf16[128,384]{1,0:T(8,128)(2,1)S(1)}, u32[]{:S(2)}, u32[]{:S(2)}) %collective-permute-start.9) | collective-permute-done | bytes 98336 | tf_op jit(solution)/shard_map/ppermute | solution.py:260
  43.3 1.0 %collective-permute-start.11 = (bf16[128,384]{1,0:T(8,128)(2,1)S(1)}, bf16[128,384]{1,0:T(8,128)(2,1)S(1)}, u32[]{:S(2)}, u32[]{:S(2)}) collective-permute-start(bf16[128,384]{1,0:T(8,128)(2,1)S(1)} %collective-permute-done.9.act_half_ref), channel_id=1, source_target_pairs={{0,1},{1,0},{2,3},{3,2},{4,5},{5,4},{6,7},{7,6},{8,9},{9,8},{10,11... | collective-permute-start | bytes 294920 | tf_op jit(solution)/shard_map/ppermute | solution.py:257
  44.3 0.0 collective-permute-done.10.act_core_ref
  44.3 0.0 collective-permute-done.12.side_ref
  44.3 0.9 %collective-permute-done.11.act_both_ref = bf16[128,384]{1,0:T(8,128)(2,1)S(1)} collective-permute-done((bf16[128,384]{1,0:T(8,128)(2,1)S(1)}, bf16[128,384]{1,0:T(8,128)(2,1)S(1)}, u32[]{:S(2)}, u32[]{:S(2)}) %collective-permute-start.11) | collective-permute-done | bytes 98336 | tf_op jit(solution)/shard_map/ppermute | solution.py:257
  45.3 0.0 copy-done.2
  45.3 0.0 copy-done.9
  45.3 1.4 %down.1 = bf16[8,144,128]{2,1,0:T(8,128)(2,1)S(1)} custom-call(s32[8]{0:T(128)S(1)} %copy-done.9, bf16[128,384]{1,0:T(8,128)(2,1)S(1)} %get-tuple-element.19.act_ref, bf16[128,384]{1,0:T(8,128)(2,1)S(1)} %collective-permute-done.9.act_half_ref, bf16[128,384]{1,0:T(8,128)(2,1)S(1)} %collective-permute-done.10.act_core_ref, ...), custom_call_target="tpu_custom_call" | custom-call | tf_op jit(solution)/shard_map/down/pallas_call | solution.py:360
  46.7 17.5 %all_to_all.5.came_ref = bf16[8,144,128]{2,1,0:T(8,128)(2,1)S(1)} all-to-all(bf16[8,144,128]{2,1,0:T(8,128)(2,1)S(1)} %down.1), channel_id=1, replica_groups=mesh['ep'=8,'tp'=4] {'ep'}, dimensions={0} | all-to-all | bytes 589824 | tf_op jit(solution)/shard_map/all_to_all | solution.py:369
  64.1 0.9 %combine.1 = bf16[64,512]{1,0:T(8,128)(2,1)} custom-call(bf16[8,144,128]{2,1,0:T(8,128)(2,1)S(1)} %all_to_all.5.came_ref), custom_call_target="tpu_custom_call" | custom-call | tf_op jit(solution)/shard_map/combine/pallas_call | solution.py:370
  (21 shorter events, 0.2 us)
Async XLA Ops:
  0.0 9.2 %copy-start.12 = (f32[64,2]{0,1:T(2,128)S(1)}, f32[64,2]{0,1:T(2,128)}, u32[]{:S(2)}) copy-start(f32[64,2]{0,1:T(2,128)} %param.26) | copy-start | bytes 1540
  0.0 9.5 %copy-start.13 = (s32[64,2]{0,1:T(2,128)S(1)}, s32[64,2]{0,1:T(2,128)}, u32[]{:S(2)}) copy-start(s32[64,2]{0,1:T(2,128)} %param.25) | copy-start | bytes 1540
  0.7 1.6 %copy-start.1 = (bf16[512,2048]{1,0:T(8,128)(2,1)S(1)}, bf16[512,2048]{1,0:T(8,128)(2,1)}, u32[]{:S(2)}) copy-start(bf16[512,2048]{1,0:T(8,128)(2,1)} %weight_hbm.1) | copy-start | bytes 6291460
  2.3 0.9 %copy-start.3 = (bf16[1,512,128]{2,1,0:T(8,128)(2,1)S(1)}, bf16[1,512,128]{2,1,0:T(8,128)(2,1)}, u32[]{:S(2)}) copy-start(bf16[1,512,128]{2,1,0:T(8,128)(2,1)} %param.18) | copy-start | bytes 393220
  3.2 0.9 %copy-start.4 = (bf16[1,512,128]{2,1,0:T(8,128)(2,1)S(1)}, bf16[1,512,128]{2,1,0:T(8,128)(2,1)}, u32[]{:S(2)}) copy-start(bf16[1,512,128]{2,1,0:T(8,128)(2,1)} %param.19) | copy-start | bytes 393220
  4.1 0.8 %copy-start.5 = (bf16[64,512]{1,0:T(8,128)(2,1)S(1)}, bf16[64,512]{1,0:T(8,128)(2,1)}, u32[]{:S(2)}) copy-start(bf16[64,512]{1,0:T(8,128)(2,1)} %query_ref.1) | copy-start | bytes 196612
  4.9 0.7 %copy-start.6 = (bf16[64,128]{1,0:T(8,128)(2,1)S(1)}, bf16[64,128]{1,0:T(8,128)(2,1)}, u32[]{:S(2)}) copy-start(bf16[64,128]{1,0:T(8,128)(2,1)} %new_key_ref.1) | copy-start | bytes 49156
  5.6 0.7 %copy-start.7 = (bf16[64,128]{1,0:T(8,128)(2,1)S(1)}, bf16[64,128]{1,0:T(8,128)(2,1)}, u32[]{:S(2)}) copy-start(bf16[64,128]{1,0:T(8,128)(2,1)} %new_value_ref.1) | copy-start | bytes 49156
  6.4 2.3 %copy-start.10 = (bf16[1,2048,192]{1,2,0:T(8,128)(2,1)S(1)}, bf16[1,2048,192]{1,2,0:T(8,128)(2,1)}, u32[]{:S(2)}) copy-start(bf16[1,2048,192]{1,2,0:T(8,128)(2,1)} %param.28) | copy-start | bytes 2359300
  6.4 3.0 %copy-start.11 = (bf16[64,512]{1,0:T(8,128)(2,1)S(1)}, bf16[64,512]{1,0:T(8,128)(2,1)}, u32[]{:S(2)}) copy-start(bf16[64,512]{1,0:T(8,128)(2,1)} %param.22) | copy-start | bytes 196612
  8.2 1.5 %collective-permute-start.2 = (bf16[64,1024]{1,0:T(8,128)(2,1)S(1)}, bf16[64,1024]{1,0:T(8,128)(2,1)S(1)}, u32[]{:S(2)}, u32[]{:S(2)}) collective-permute-start(bf16[64,1024]{1,0:T(8,128)(2,1)S(1)} %get-tuple-element.14), channel_id=1, source_target_pairs={{0,1},{1,0},{2,3},{3,2},{4,5},{5,4},{6,7},{7,6},{8,9},{9,8},{10,11... | collective-permute-start | bytes 393224 | tf_op jit(solution)/shard_map/ppermute | solution.py:257
  8.7 16.3 %collective-permute-start.1 = (bf16[2048,192]{0,1:T(8,128)(2,1)S(1)}, bf16[2048,192]{0,1:T(8,128)(2,1)}, u32[]{:S(2)}, u32[]{:S(2)}) collective-permute-start(bf16[2048,192]{0,1:T(8,128)(2,1)S(1)} %bitcast.34), channel_id=1, source_target_pairs={{0,1},{1,0},{2,3},{3,2},{4,5},{5,4},{6,7},{7,6},{8,9},{9,8},{10,11... | collective-permute-start | bytes 2359304 | tf_op jit(solution)/shard_map/ppermute | solution.py:257
  8.8 19.6 %collective-permute-start = (bf16[2048,192]{0,1:T(8,128)(2,1)}, bf16[2048,192]{0,1:T(8,128)(2,1)}, u32[]{:S(2)}, u32[]{:S(2)}) collective-permute-start(bf16[2048,192]{0,1:T(8,128)(2,1)} %bitcast.2), channel_id=1, source_target_pairs={{0,1},{1,0},{2,3},{3,2},{4,5},{5,4},{6,7},{7,6},{8,9},{9,8},{10,11... | collective-permute-start | bytes 2359304 | tf_op jit(solution)/shard_map/ppermute | solution.py:257
  9.8 6.7 %collective-permute-start.3 = (bf16[64,1024]{1,0:T(8,128)(2,1)S(1)}, bf16[64,1024]{1,0:T(8,128)(2,1)S(1)}, u32[]{:S(2)}, u32[]{:S(2)}) collective-permute-start(bf16[64,1024]{1,0:T(8,128)(2,1)S(1)} %fusion.8), channel_id=1, source_target_pairs={{0,2},{1,3},{2,0},{3,1},{4,6},{5,7},{6,4},{7,5},{8,10},{9,11},{10,... | collective-permute-start | bytes 393224 | tf_op jit(solution)/shard_map/ppermute | solution.py:260
  16.5 1.4 %collective-permute-start.4 = (bf16[64,1024]{1,0:T(8,128)(2,1)S(1)}, bf16[64,1024]{1,0:T(8,128)(2,1)S(1)}, u32[]{:S(2)}, u32[]{:S(2)}) collective-permute-start(bf16[64,1024]{1,0:T(8,128)(2,1)S(1)} %add_convert_fusion.part_ref), channel_id=1, source_target_pairs={{0,1},{1,0},{2,3},{3,2},{4,5},{5,4},{6,7},{7,6},{8,9},{9,8},{10,11... | collective-permute-start | bytes 393224 | tf_op jit(solution)/shard_map/ppermute | solution.py:257
  19.0 11.6 %collective-permute-start.5 = (bf16[528,128]{1,0:T(8,128)(2,1)}, bf16[528,128]{1,0:T(8,128)(2,1)S(1)}, u32[]{:S(2)}, u32[]{:S(2)}) collective-permute-start(bf16[528,128]{1,0:T(8,128)(2,1)} %get-tuple-element.15), channel_id=1, source_target_pairs={{0,0},{1,5},{2,2},{3,7},{4,4},{5,1},{6,6},{7,3},{8,8},{9,13},{10,1... | collective-permute-start | bytes 405512 | tf_op jit(solution)/shard_map/ppermute | solution.py:341
  20.6 10.1 %collective-permute-start.6 = (bf16[528,128]{1,0:T(8,128)(2,1)}, bf16[528,128]{1,0:T(8,128)(2,1)S(1)}, u32[]{:S(2)}, u32[]{:S(2)}) collective-permute-start(bf16[528,128]{1,0:T(8,128)(2,1)} %get-tuple-element.16), channel_id=1, source_target_pairs={{0,8},{1,13},{2,10},{3,15},{4,12},{5,9},{6,14},{7,11},{8,0},{9,5},... | collective-permute-start | bytes 405512 | tf_op jit(solution)/shard_map/ppermute | solution.py:341
  22.4 8.2 %collective-permute-start.7 = (bf16[528,128]{1,0:T(8,128)(2,1)}, bf16[528,128]{1,0:T(8,128)(2,1)S(1)}, u32[]{:S(2)}, u32[]{:S(2)}) collective-permute-start(bf16[528,128]{1,0:T(8,128)(2,1)} %get-tuple-element.17), channel_id=1, source_target_pairs={{0,16},{1,21},{2,18},{3,23},{4,20},{5,17},{6,22},{7,19},{8,24},{9,... | collective-permute-start | bytes 405512 | tf_op jit(solution)/shard_map/ppermute | solution.py:341
  25.0 9.8 %collective-permute-start.8 = (bf16[528,128]{1,0:T(8,128)(2,1)}, bf16[528,128]{1,0:T(8,128)(2,1)}, u32[]{:S(2)}, u32[]{:S(2)}) collective-permute-start(bf16[528,128]{1,0:T(8,128)(2,1)} %get-tuple-element.18), channel_id=1, source_target_pairs={{0,24},{1,29},{2,26},{3,31},{4,28},{5,25},{6,30},{7,27},{8,16},{9,... | collective-permute-start | bytes 405512 | tf_op jit(solution)/shard_map/ppermute | solution.py:341
  34.8 1.2 %copy-start = (bf16[2048,192]{1,0:T(8,128)(2,1)S(1)}, bf16[2048,192]{1,0:T(8,128)(2,1)}, u32[]{:S(2)}) copy-start(bf16[2048,192]{1,0:T(8,128)(2,1)} %copy.38.gate_pair_ref) | copy-start | bytes 2359300
  36.0 0.7 %copy-start.8 = (f32[2048]{0:T(1024)S(1)}, f32[2048]{0:T(1024)}, u32[]{:S(2)}) copy-start(f32[2048]{0:T(1024)} %param.24) | copy-start | bytes 24580
  36.7 8.6 %copy-start.2 = (bf16[1,768,512]{2,1,0:T(8,128)(2,1)S(1)}, bf16[1,768,512]{2,1,0:T(8,128)(2,1)}, u32[]{:S(2)}) copy-start(bf16[1,768,512]{2,1,0:T(8,128)(2,1)} %param.29) | copy-start | bytes 2359300
  36.7 8.6 %copy-start.9 = (s32[8]{0:T(128)S(1)}, s32[8]{0:T(128)}, u32[]{:S(2)}) copy-start(s32[8]{0:T(128)} %order_ref.1) | copy-start | bytes 100
  38.6 4.7 %collective-permute-start.9 = (bf16[128,384]{1,0:T(8,128)(2,1)S(1)}, bf16[128,384]{1,0:T(8,128)(2,1)S(1)}, u32[]{:S(2)}, u32[]{:S(2)}) collective-permute-start(bf16[128,384]{1,0:T(8,128)(2,1)S(1)} %get-tuple-element.19.act_ref), channel_id=1, source_target_pairs={{0,2},{1,3},{2,0},{3,1},{4,6},{5,7},{6,4},{7,5},{8,10},{9,11},{10,... | collective-permute-start | bytes 294920 | tf_op jit(solution)/shard_map/ppermute | solution.py:260
  40.2 4.2 %collective-permute-start.12 = (bf16[4,144,128]{2,1,0:T(8,128)(2,1)S(1)}, bf16[4,144,128]{2,1,0:T(8,128)(2,1)S(1)}, u32[]{:S(2)}, u32[]{:S(2)}) collective-permute-start(bf16[4,144,128]{2,1,0:T(8,128)(2,1)S(1)} %get-tuple-element.20), channel_id=1, source_target_pairs={{0,1},{1,0},{2,3},{3,2},{4,5},{5,4},{6,7},{7,6},{8,9},{9,8},{10,11... | collective-permute-start | bytes 442376 | tf_op jit(solution)/shard_map/ppermute | solution.py:257
  42.1 2.3 %collective-permute-start.10 = (bf16[128,384]{1,0:T(8,128)(2,1)S(1)}, bf16[128,384]{1,0:T(8,128)(2,1)S(1)}, u32[]{:S(2)}, u32[]{:S(2)}) collective-permute-start(bf16[128,384]{1,0:T(8,128)(2,1)S(1)} %get-tuple-element.19.act_ref), channel_id=1, source_target_pairs={{0,1},{1,0},{2,3},{3,2},{4,5},{5,4},{6,7},{7,6},{8,9},{9,8},{10,11... | collective-permute-start | bytes 294920 | tf_op jit(solution)/shard_map/ppermute | solution.py:257
  43.3 2.0 %collective-permute-start.11 = (bf16[128,384]{1,0:T(8,128)(2,1)S(1)}, bf16[128,384]{1,0:T(8,128)(2,1)S(1)}, u32[]{:S(2)}, u32[]{:S(2)}) collective-permute-start(bf16[128,384]{1,0:T(8,128)(2,1)S(1)} %collective-permute-done.9.act_half_ref), channel_id=1, source_target_pairs={{0,1},{1,0},{2,3},{3,2},{4,5},{5,4},{6,7},{7,6},{8,9},{9,8},{10,11... | collective-permute-start | bytes 294920 | tf_op jit(solution)/shard_map/ppermute | solution.py:257

commit v3 on v2

--- a/solution.py
+++ b/solution.py
@@ -13,7 +13,8 @@
 KVHEADS = 4
 LANES = 128
 TAGS = 16
-VMEM_LIMIT = 24 * 1024 * 1024
+MIB = 1024 * 1024
+ATTEND_MIB = 61
 
 BF16 = jnp.bfloat16
 F32 = jnp.float32
@@ -23,8 +24,12 @@
     return pl.BlockSpec(memory_space=pltpu.VMEM)
 
 
-def params():
-    return pltpu.CompilerParams(vmem_limit_bytes=VMEM_LIMIT)
+def hbm():
+    return pl.BlockSpec(memory_space=pltpu.HBM)
+
+
+def params(mib):
+    return pltpu.CompilerParams(vmem_limit_bytes=int(mib * MIB))
 
 
 def dot(a, b):
@@ -37,33 +42,57 @@
 
 def attend_kernel(
     kv_local,
+    length_hbm,
+    query_hbm,
+    new_key_hbm,
+    new_value_hbm,
+    key_hbm,
+    value_hbm,
+    residual_hbm,
+    weight_hbm,
+    keep_hbm,
+    give_hbm,
     length_ref,
     query_ref,
     new_key_ref,
     new_value_ref,
     key_ref,
     value_ref,
-    weight_hbm,
+    residual_ref,
+    weight_ref,
     keep_ref,
     give_ref,
-    weight_ref,
     sems,
 ):
-    core = lax.axis_index("tp") % 2
+    tp = lax.axis_index("tp")
+    half, core = tp // 2, tp % 2
     width = weight_ref.shape[2]
     copies = []
+    for source, target in (
+        (query_hbm, query_ref),
+        (key_hbm, key_ref),
+        (new_key_hbm, new_key_ref),
+        (length_hbm, length_ref),
+        (value_hbm, value_ref),
+        (new_value_hbm, new_value_ref),
+        (residual_hbm, residual_ref),
+    ):
+        copies.append(pltpu.make_async_copy(source, target, sems.at[len(copies)]))
     for i, block in enumerate((1 - core, 3 - core, core, core + 2)):
         start = pl.multiple_of(block * width, width)
-        copy = pltpu.make_async_copy(
-            weight_hbm.at[:, pl.ds(start, width)], weight_ref.at[i], sems.at[i]
+        copies.append(
+            pltpu.make_async_copy(
+                weight_hbm.at[:, pl.ds(start, width)], weight_ref.at[i], sems.at[len(copies)]
+            )
         )
+    for copy in copies:
         copy.start()
-        copies.append(copy)
     tokens = query_ref.shape[0]
-    cached = key_ref.shape[0]
     group = QHEADS // KVHEADS
+    scale = 1.0 / math.sqrt(HEAD)
+    for copy in copies[:4]:
+        copy.wait()
     length = length_ref[0]
-    scale = 1.0 / math.sqrt(HEAD)
     pieces = []
     for g in range(kv_local):
         columns = slice(g * HEAD, (g + 1) * HEAD)
@@ -87,20 +116,80 @@
         old = jnp.exp(old - highest)
         new = jnp.exp(new - highest)
         totals = jnp.sum(old, axis=1, keepdims=True) + jnp.sum(new, axis=1, keepdims=True)
+        if g == 0:
+            for copy in copies[4:6]:
+                copy.wait()
         mixed = dot(old.astype(BF16), value_ref[:, columns]) + dot(
             new.astype(BF16), new_value_ref[:, columns]
         )
         mixed = (mixed / totals).astype(BF16)
         pieces += [mixed[i * tokens : (i + 1) * tokens] for i in range(group)]
     context = jnp.concatenate(pieces, axis=1)
+    copies[6].wait()
+    given = pltpu.make_async_copy(give_ref, give_hbm, sems.at[len(copies)])
+    kept = pltpu.make_async_copy(keep_ref, keep_hbm, sems.at[len(copies) + 1])
     for i in range(4):
-        copies[i].wait()
+        copies[7 + i].wait()
         part = dot(context, weight_ref[i])
         columns = slice((i % 2) * width, (i % 2 + 1) * width)
         if i < 2:
             give_ref[:, columns] = part.astype(BF16)
         else:
-            keep_ref[:, columns] = part
+            keep_ref[:, columns] = part + jnp.where(
+                half == i - 2, residual_ref[...].astype(F32), 0.0
+            )
+        if i == 1:
+            given.start()
+    kept.start()
+    given.wait()
+    kept.wait()
+
+
+def load_kernel(from_ref, to_ref):
+    to_ref[...] = from_ref[...]
+
+
+def route_kernel(peers, after_ref, expert_ref, weight_ref, pick_ref, tags_ref):
+    del after_ref
+    me = lax.axis_index("ep")
+    core = lax.axis_index("tp") % 2
+    top, tokens = expert_ref.shape
+    rows_each = pick_ref.shape[0] // peers
+    peer = jnp.bitwise_xor(
+        2 * lax.broadcasted_iota(jnp.int32, (peers, tokens), 0) + core, me
+    )
+    weights = weight_ref[...]
+    mixing = (weights / jnp.sum(weights, axis=0, keepdims=True)).astype(BF16).astype(F32)
+    mix_of = jnp.zeros((peers, tokens), F32)
+    named = jnp.zeros((peers, tokens), F32)
+    for j in range(top):
+        match = expert_ref[j : j + 1, :] == peer
+        mix_of = mix_of + jnp.where(match, mixing[j : j + 1, :], 0.0)
+        named = named + jnp.where(match, 1.0, 0.0)
+    earlier = lax.broadcasted_iota(jnp.int32, (tokens, tokens), 0) < lax.broadcasted_iota(
+        jnp.int32, (tokens, tokens), 1
+    )
+    rank = dot(named.astype(BF16), jnp.where(earlier, 1.0, 0.0).astype(BF16))
+    rank = jnp.where(named > 0.0, rank, -1.0)
+    slot = lax.broadcasted_iota(jnp.int32, (rows_each, tokens), 0).astype(F32)
+    line = lax.broadcasted_iota(jnp.int32, (TAGS, tokens), 0)
+    number = lax.broadcasted_iota(jnp.int32, (TAGS, tokens), 1).astype(F32) + 1.0
+    tags_ref[...] = jnp.zeros(tags_ref.shape, BF16)
+    for k in range(peers):
+        pick = jnp.where(rank[k : k + 1, :] == slot, 1.0, 0.0).astype(BF16)
+        pick_ref[k * rows_each : (k + 1) * rows_each, :] = pick
+        known = jnp.where(line == 0, number, jnp.where(line == 1, mix_of[k : k + 1, :], 0.0))
+        tags_ref[k, :, :rows_each] = dot_t(known.astype(BF16), pick).astype(BF16)
+
+
+def add_core_kernel(keep_ref, came_ref, sum_ref, send_ref):
+    value = keep_ref[...] + came_ref[...].astype(F32)
+    sum_ref[...] = value
+    send_ref[...] = value.astype(BF16)
+
+
+def add_half_kernel(sum_ref, came_ref, out_ref):
+    out_ref[...] = (sum_ref[...] + came_ref[...].astype(F32)).astype(BF16)
 
 
 def gather_kernel(peers, part_ref, other_ref, pick_ref, tags_ref, *send_refs):
@@ -123,9 +212,20 @@
         send_refs[k][4 * blocks * rows_each :, :] = tags_ref[k]
 
 
-def hidden_units_kernel(
-    peers, rows_each, gain_ref, gate_ref, gate_pair_ref, up_ref, up_pair_ref, *refs
-):
+def stage_kernel(after_ref, *refs):
+    del after_ref
+    count = len(refs) - 2
+    target, sems = refs[count:]
+    copies = [
+        pltpu.make_async_copy(refs[i], target.at[i], sems.at[i]) for i in range(count)
+    ]
+    for copy in copies:
+        copy.start()
+    for copy in copies:
+        copy.wait()
+
+
+def hidden_units_kernel(peers, rows_each, gain_ref, weight_ref, *refs):
     got = refs[:peers]
     act_ref, side_ref = refs[peers:]
     tp = lax.axis_index("tp")
@@ -148,11 +248,11 @@
     )
 
     def units(gate, up):
-        value = dot(normed, gate[...])
-        return value / (1.0 + jnp.exp(-value)) * dot(normed, up[...])
-
-    own = units(gate_ref, up_ref)
-    pair = units(gate_pair_ref, up_pair_ref)
+        value = dot_t(normed, weight_ref[gate])
+        return value / (1.0 + jnp.exp(-value)) * dot_t(normed, weight_ref[up])
+
+    own = units(0, 1)
+    pair = units(2, 3)
     low = jnp.where(core == 0, own, pair)
     high = jnp.where(core == 0, pair, own)
     act_ref[...] = jnp.concatenate([low, high], axis=1).astype(BF16)
@@ -249,9 +349,6 @@
     tp_count = lax.axis_size("tp")
     ep_count = lax.axis_size("ep")
     kv_local = KVHEADS // tp_count
-    me_ep = lax.axis_index("ep")
-    me_tp = lax.axis_index("tp")
-    half, core = me_tp // 2, me_tp % 2
 
     def swap_core(x):
         return lax.ppermute(x, "tp", [(i, i ^ 1) for i in range(tp_count)])
@@ -259,9 +356,7 @@
     def swap_half(x):
         return lax.ppermute(x, "tp", [(i, i ^ 2) for i in range(tp_count)])
 
-    gate, up, down = expert_gate[0], expert_up[0], expert_down[0]
-    gate_pair, up_pair = swap_core(gate), swap_core(up)
-
+    gate, up, down = expert_gate[0].T, expert_up[0].T, expert_down[0]
     tokens, top = route_experts.shape
     capacity = 2 * tokens * top // ep_count
     rows_each = -(-capacity // 16) * 16
@@ -269,21 +364,28 @@
     width = residual.shape[1]
     blocks = width // LANES
     tall = blocks * rows_each
-    units = 2 * gate.shape[1]
+    units = 2 * gate.shape[0]
     shape = jax.ShapeDtypeStruct
 
     keep, give = pl.pallas_call(
         functools.partial(attend_kernel, kv_local),
         out_shape=(shape((tokens, 2 * width), F32), shape((tokens, 2 * width), BF16)),
-        in_specs=[pl.BlockSpec(memory_space=pltpu.SMEM)]
-        + [vmem()] * 5
-        + [pl.BlockSpec(memory_space=pl.ANY)],
-        out_specs=(vmem(), vmem()),
+        in_specs=[hbm()] * 8,
+        out_specs=(hbm(), hbm()),
         scratch_shapes=[
+            pltpu.SMEM(cache_lengths.shape, jnp.int32),
+            pltpu.VMEM(queries.shape, BF16),
+            pltpu.VMEM(new_keys.shape, BF16),
+            pltpu.VMEM(new_values.shape, BF16),
+            pltpu.VMEM(key_cache.shape[1:], BF16),
+            pltpu.VMEM(value_cache.shape[1:], BF16),
+            pltpu.VMEM(residual.shape, BF16),
             pltpu.VMEM((4, out_weight.shape[0], width), BF16),
-            pltpu.SemaphoreType.DMA((4,)),
+            pltpu.VMEM((tokens, 2 * width), F32),
+            pltpu.VMEM((tokens, 2 * width), BF16),
+            pltpu.SemaphoreType.DMA((13,)),
         ],
-        compiler_params=params(),
+        compiler_params=params(ATTEND_MIB),
         name="attend",
     )(
         cache_lengths,
@@ -292,33 +394,48 @@
         new_values,
         key_cache[0],
         value_cache[0],
+        residual,
         out_weight,
     )
 
-    peer = jnp.bitwise_xor(me_ep, 2 * jnp.arange(peers, dtype=jnp.int32) + core)
-    matches = route_experts[None] == peer[:, None, None]
-    named = jnp.any(matches, axis=2)
-    token_range = jnp.arange(tokens, dtype=jnp.int32)
-    before = (token_range[:, None] < token_range[None, :]).astype(BF16)
-    rank = dot(named.astype(BF16), before).astype(jnp.int32)
-    slots = jnp.arange(rows_each, dtype=jnp.int32)
-    pick = (rank[:, None, :] == slots[None, :, None]) & named[:, None, :]
-    mixing = (route_weights / jnp.sum(route_weights, axis=1, keepdims=True)).astype(BF16)
-    mix_of = jnp.sum(jnp.where(matches, mixing[None].astype(F32), 0.0), axis=2)
-    token_tag = jnp.sum(jnp.where(pick, (token_range + 1).astype(F32), 0.0), axis=2)
-    mix_tag = jnp.sum(jnp.where(pick, mix_of[:, None, :], 0.0), axis=2)
-    tags = jnp.pad(
-        jnp.stack([token_tag, mix_tag], axis=1).astype(BF16),
-        ((0, 0), (0, TAGS - 2), (0, LANES - rows_each)),
-    )
-    pick = pick.astype(BF16).reshape(peers * rows_each, tokens)
-
-    keep = keep + swap_core(give).astype(F32)
-    keep = keep.reshape(tokens, 2, width)
-    mine = (jnp.arange(2) == half)[None, :, None]
-    keep = keep + jnp.where(mine, residual.astype(F32)[:, None, :], 0.0)
-    keep = keep.reshape(tokens, 2 * width)
-    part = (keep + swap_half(keep.astype(BF16)).astype(F32)).astype(BF16)
+    keep = pl.pallas_call(
+        load_kernel,
+        out_shape=shape(keep.shape, F32),
+        in_specs=[vmem()],
+        out_specs=vmem(),
+        compiler_params=params(4),
+        cost_estimate=pl.CostEstimate(flops=0, bytes_accessed=MIB, transcendentals=0),
+        name="load",
+    )(keep)
+    summed, send = pl.pallas_call(
+        add_core_kernel,
+        out_shape=(shape(keep.shape, F32), shape(keep.shape, BF16)),
+        in_specs=[vmem()] * 2,
+        out_specs=(vmem(), vmem()),
+        compiler_params=params(4),
+        name="add_core",
+    )(keep, swap_core(give))
+
+    part = pl.pallas_call(
+        add_half_kernel,
+        out_shape=shape(keep.shape, BF16),
+        in_specs=[vmem()] * 2,
+        out_specs=vmem(),
+        compiler_params=params(4),
+        name="add_half",
+    )(summed, swap_half(send))
+    pick, tags = pl.pallas_call(
+        functools.partial(route_kernel, peers),
+        out_shape=(
+            shape((peers * rows_each, tokens), BF16),
+            shape((peers, TAGS, LANES), BF16),
+        ),
+        in_specs=[pl.BlockSpec(memory_space=pl.ANY)] + [vmem()] * 2,
+        out_specs=(vmem(), vmem()),
+        compiler_params=params(4),
+        cost_estimate=pl.CostEstimate(flops=0, bytes_accessed=MIB, transcendentals=0),
+        name="route",
+    )(part, route_experts.T, route_weights.T)
     other = swap_core(part)
 
     block_shape = shape((tp_count * tall + TAGS, LANES), BF16)
@@ -327,7 +444,7 @@
         out_shape=[block_shape] * peers,
         in_specs=[vmem()] * 4,
         out_specs=[vmem()] * peers,
-        compiler_params=params(),
+        compiler_params=params(8),
         name="gather_rows",
     )(part, other, pick, tags)
 
@@ -338,7 +455,23 @@
             for t in range(tp_count)
         ]
 
+    send = list(send)
+    gate, up, send[-1] = lax.optimization_barrier((gate, up, send[-1]))
+    gate_pair, up_pair = swap_core(gate), swap_core(up)
     got = [lax.ppermute(send[k], ("ep", "tp"), route(k)) for k in range(peers)]
+
+    weights = pl.pallas_call(
+        stage_kernel,
+        out_shape=shape((4,) + gate.shape, BF16),
+        in_specs=[vmem()] + [hbm()] * 4,
+        out_specs=vmem(),
+        scratch_shapes=[pltpu.SemaphoreType.DMA((4,))],
+        compiler_params=params(32),
+        cost_estimate=pl.CostEstimate(
+            flops=0, bytes_accessed=16 * gate.size, transcendentals=0
+        ),
+        name="stage",
+    )(tags, gate, up, gate_pair, up_pair)
 
     act, side = pl.pallas_call(
         functools.partial(hidden_units_kernel, peers, rows_each),
@@ -346,11 +479,11 @@
             shape((peers * rows_each, units), BF16),
             shape((peers, tall + TAGS, LANES), BF16),
         ),
-        in_specs=[vmem()] * (5 + peers),
+        in_specs=[vmem()] * (2 + peers),
         out_specs=(vmem(), vmem()),
-        compiler_params=params(),
+        compiler_params=params(16),
         name="hidden_units",
-    )(norm_gain.reshape(-1, LANES), gate, gate_pair, up, up_pair, *got)
+    )(norm_gain.reshape(-1, LANES), weights, *got)
 
     act_half = swap_half(act)
     act_core = swap_core(act)
@@ -362,7 +495,7 @@
         out_shape=shape((ep_count, tall + TAGS, LANES), BF16),
         in_specs=[pl.BlockSpec(memory_space=pltpu.SMEM)] + [vmem()] * (6 + peers),
         out_specs=vmem(),
-        compiler_params=params(),
+        compiler_params=params(16),
         name="down",
     )(request_order, act, act_half, act_core, act_both, down, side, *got)
 
@@ -372,7 +505,7 @@
         out_shape=shape((tokens, width), BF16),
         in_specs=[vmem()],
         out_specs=vmem(),
-        compiler_params=params(),
+        compiler_params=params(8),
         name="combine",
     )(came)
 

time: 65.6 us -> 55.9 us (0.85)
  local copies, waits for them, and re-layouts: 13.5 us -> 0.98 us
  waiting for transfers between devices: 11.1 us -> 20 us
  starting transfers between devices: 14.4 us -> 11.2 us
  blocking collectives: 17.5 us -> 15.1 us
    unnamed x31 -> x16, local copies, waits for them, and re-layouts: 9.6 us -> 0.98 us
    ppermute x4, waiting for transfers between devices: 4.14 us -> 10.5 us  [shards(): got = [lax.ppermute(send[k], ('ep', 'tp'), route(k)) for k in range(peers)]]
    ppermute x2 -> x0, local copies, waits for them, and re-layouts: 3.66 us -> none  [swap_core(): return lax.ppermute(x, 'tp', [(i, i ^ 1) for i in range(tp_count)])]
    all_to_all x1, blocking collectives: 17.5 us -> 15.1 us  [shards(): came = lax.all_to_all(result, 'ep', split_axis=0, concat_axis=0, tiled=True)]
    ppermute x7, starting transfers between devices: 4.03 us -> 1.68 us  [swap_core(): return lax.ppermute(x, 'tp', [(i, i ^ 1) for i in range(tp_count)])]
    ppermute x2, waiting for transfers between devices: 5 us -> 6.87 us  [swap_half(): return lax.ppermute(x, 'tp', [(i, i ^ 2) for i in range(tp_count)])]
    pallas_call x1, Pallas kernels: 1.78 us -> 3.34 us  [shards(): pl.pallas_call(functools.partial(attend_kernel, kv_local), out_shape=(sha...]
    ppermute x4, starting transfers between devices: 5.97 us -> 5.13 us  [shards(): got = [lax.ppermute(send[k], ('ep', 'tp'), route(k)) for k in range(peers)]]
  transfers between devices with their start and end apart: 13 -> 13, of which waited for: 5 -> 8; matrix products, arithmetic and copies ran while one was open for 10% -> 0% of each run, Pallas kernels for 2% -> 1%
where the time goes in v3:
time: 55.9 us; the launch traced here: 55.7 us
  waiting for transfers between devices  20 us (36%)
  blocking collectives  15.1 us (27%)
  starting transfers between devices  11.2 us (20%)
  Pallas kernels  7.48 us (13%)
  local copies, waits for them, and re-layouts  0.98 us (2%)
  between operations  0.92 us (2%)
    all_to_all x1, blocking collectives, shards(): came = lax.all_to_all(result, 'ep', split_axis=0, concat_axis=0, tiled=True)  15.1 us
    ppermute x4, waiting for transfers between devices, shards(): got = [lax.ppermute(send[k], ('ep', 'tp'), route(k)) for k in range(peers)]  10.5 us
    ppermute x2, waiting for transfers between devices, swap_half(): return lax.ppermute(x, 'tp', [(i, i ^ 2) for i in range(tp_count)])  6.87 us
    ppermute x4, starting transfers between devices, shards(): got = [lax.ppermute(send[k], ('ep', 'tp'), route(k)) for k in range(peers)]  5.13 us
    ppermute x2, starting transfers between devices, swap_half(): return lax.ppermute(x, 'tp', [(i, i ^ 2) for i in range(tp_count)])  4.44 us
    pallas_call x1, Pallas kernels, shards(): pl.pallas_call(functools.partial(attend_kernel, kv_local), out_shape=(sha...  3.34 us
    ppermute x7, waiting for transfers between devices, swap_core(): return lax.ppermute(x, 'tp', [(i, i ^ 1) for i in range(tp_count)])  2.58 us
    ppermute x7, starting transfers between devices, swap_core(): return lax.ppermute(x, 'tp', [(i, i ^ 1) for i in range(tp_count)])  1.68 us
  transfers between devices with their start and end apart: 13, of which 8 were waited for; matrix products, arithmetic and copies ran while one was open for 0% of the time, Pallas kernels for 1%

profile of v3, /device:TPU:0, one launch (start us, length us, event | category | flops | bytes accessed | tf_op | source)
XLA Modules:
  0.0 55.7 jit_solution(3549192832272537614)
XLA Ops:
  0.0 0.0 copy-start.6
  0.0 0.0 copy-start.5
  0.0 0.0 copy-start.1
  0.0 0.0 copy-start
  0.8 3.3 %attend.1 = (f32[64,1024]{1,0:T(8,128)}, bf16[64,1024]{1,0:T(8,128)(2,1)}) custom-call(s32[1]{0:T(128)S(6)} %copy.16.length_hbm, bf16[64,512]{1,0:T(8,128)(2,1)} %query_hbm.1, bf16[64,128]{1,0:T(8,128)(2,1)} %new_key_hbm.1, bf16[64,128]{1,0:T(8,128)(2,1)} %new_value_hbm.1, bf16[512,128]{1,0:T(8,128)(2,1)} %bitcast.20, bf16[512,128]{1,0:T(8,128)(2,1)} %bitcast.21, ...), custom_call_target="tpu_custom_call" | custom-call | tf_op jit(solution)/shard_map/attend/pallas_call | solution.py:370
  4.1 0.5 collective-permute-start
  4.6 0.0 copy-start.3
  4.7 0.9 %copy-done.3 = f32[64,1024]{1,0:T(8,128)S(1)} copy-done((f32[64,1024]{1,0:T(8,128)S(1)}, f32[64,1024]{1,0:T(8,128)}, u32[]{:S(2)}) %copy-start.3) | copy-done | bytes 262168
  5.6 0.2 collective-permute-done.came_ref
  5.9 2.9 %collective-permute-start.1 = (bf16[64,1024]{1,0:T(8,128)(2,1)S(1)}, bf16[64,1024]{1,0:T(8,128)(2,1)S(1)}, u32[]{:S(2)}, u32[]{:S(2)}) collective-permute-start(bf16[64,1024]{1,0:T(8,128)(2,1)S(1)} %get-tuple-element.23), channel_id=1, source_target_pairs={{0,2},{1,3},{2,0},{3,1},{4,6},{5,7},{6,4},{7,5},{8,10},{9,11},{10,... | collective-permute-start | bytes 393224 | tf_op jit(solution)/shard_map/ppermute | solution.py:357
  8.8 3.8 %collective-permute-done.1.came_ref = bf16[64,1024]{1,0:T(8,128)(2,1)S(1)} collective-permute-done((bf16[64,1024]{1,0:T(8,128)(2,1)S(1)}, bf16[64,1024]{1,0:T(8,128)(2,1)S(1)}, u32[]{:S(2)}, u32[]{:S(2)}) %collective-permute-start.1) | collective-permute-done | bytes 131104 | tf_op jit(solution)/shard_map/ppermute | solution.py:357
  12.6 0.1 collective-permute-start.2
  12.7 0.0 copy-done.6
  12.7 0.0 copy-done.5
  12.7 0.3 route.1
  13.0 1.1 %collective-permute-done.2.other_ref = bf16[64,1024]{1,0:T(8,128)(2,1)S(1)} collective-permute-done((bf16[64,1024]{1,0:T(8,128)(2,1)S(1)}, bf16[64,1024]{1,0:T(8,128)(2,1)S(1)}, u32[]{:S(2)}, u32[]{:S(2)}) %collective-permute-start.2) | collective-permute-done | bytes 131104 | tf_op jit(solution)/shard_map/ppermute | solution.py:354
  14.1 0.3 gather_rows.1
  14.3 0.0 copy-done
  14.3 0.2 collective-permute-start.3
  14.6 0.0 copy-done.1
  14.6 0.4 collective-permute-start.4
  14.9 3.9 %collective-permute-start.8 = (bf16[528,128]{1,0:T(8,128)(2,1)S(1)}, bf16[528,128]{1,0:T(8,128)(2,1)S(1)}, u32[]{:S(2)}, u32[]{:S(2)}) collective-permute-start(bf16[528,128]{1,0:T(8,128)(2,1)S(1)} %get-tuple-element.32), channel_id=1, source_target_pairs={{0,24},{1,29},{2,26},{3,31},{4,28},{5,25},{6,30},{7,27},{8,16},{9,... | collective-permute-start | bytes 405512 | tf_op jit(solution)/shard_map/ppermute | solution.py:461
  18.8 0.7 %collective-permute-start.5 = (bf16[528,128]{1,0:T(8,128)(2,1)S(1)}, bf16[528,128]{1,0:T(8,128)(2,1)S(1)}, u32[]{:S(2)}, u32[]{:S(2)}) collective-permute-start(bf16[528,128]{1,0:T(8,128)(2,1)S(1)} %get-tuple-element.29), channel_id=1, source_target_pairs={{0,0},{1,5},{2,2},{3,7},{4,4},{5,1},{6,6},{7,3},{8,8},{9,13},{10,1... | collective-permute-start | bytes 405512 | tf_op jit(solution)/shard_map/ppermute | solution.py:461
  19.4 0.1 collective-permute-start.6
  19.5 0.0 collective-permute-done.3.refs_2_
  19.5 0.0 copy-start.4
  19.5 0.5 collective-permute-start.7
  20.1 0.0 collective-permute-done.4.refs_3_
  20.1 0.3 stage.1.weight_ref
  20.3 0.0 copy-start.2
  20.4 0.0 copy-start.7
  20.4 2.6 %collective-permute-done.8.refs_3_ = bf16[528,128]{1,0:T(8,128)(2,1)S(1)} collective-permute-done((bf16[528,128]{1,0:T(8,128)(2,1)S(1)}, bf16[528,128]{1,0:T(8,128)(2,1)S(1)}, u32[]{:S(2)}, u32[]{:S(2)}) %collective-permute-start.8) | collective-permute-done | bytes 135200 | tf_op jit(solution)/shard_map/ppermute | solution.py:461
  23.0 0.0 collective-permute-done.5.refs_0_
  23.0 2.6 %collective-permute-done.6.refs_1_ = bf16[528,128]{1,0:T(8,128)(2,1)S(1)} collective-permute-done((bf16[528,128]{1,0:T(8,128)(2,1)S(1)}, bf16[528,128]{1,0:T(8,128)(2,1)S(1)}, u32[]{:S(2)}, u32[]{:S(2)}) %collective-permute-start.6) | collective-permute-done | bytes 135200 | tf_op jit(solution)/shard_map/ppermute | solution.py:461
  25.6 5.3 %collective-permute-done.7.refs_2_ = bf16[528,128]{1,0:T(8,128)(2,1)S(1)} collective-permute-done((bf16[528,128]{1,0:T(8,128)(2,1)S(1)}, bf16[528,128]{1,0:T(8,128)(2,1)S(1)}, u32[]{:S(2)}, u32[]{:S(2)}) %collective-permute-start.7) | collective-permute-done | bytes 135200 | tf_op jit(solution)/shard_map/ppermute | solution.py:461
  30.9 0.0 copy-done.4
  30.9 1.4 %hidden_units.1 = (bf16[128,384]{1,0:T(8,128)(2,1)S(1)}, bf16[4,144,128]{2,1,0:T(8,128)(2,1)S(1)}) custom-call(f32[16,128]{1,0:T(8,128)S(1)} %bitcast.17, bf16[4,192,2048]{2,1,0:T(8,128)(2,1)S(1)} %stage.1.weight_ref, bf16[528,128]{1,0:T(8,128)(2,1)S(1)} %collective-permute-done.5.refs_0_, bf16[528,128]{1,0:T(8,128)(2,1)S(1)} %collective-permute-done.6.refs_1_, ...), custom_call_target="tpu_custom_call" | custom-call | tf_op jit(solution)/shard_map/hidden_units/pallas_call | solution.py:476
  32.3 1.5 %collective-permute-start.9 = (bf16[128,384]{1,0:T(8,128)(2,1)S(1)}, bf16[128,384]{1,0:T(8,128)(2,1)S(1)}, u32[]{:S(2)}, u32[]{:S(2)}) collective-permute-start(bf16[128,384]{1,0:T(8,128)(2,1)S(1)} %get-tuple-element.33.act_ref), channel_id=1, source_target_pairs={{0,2},{1,3},{2,0},{3,1},{4,6},{5,7},{6,4},{7,5},{8,10},{9,11},{10,... | collective-permute-start | bytes 294920 | tf_op jit(solution)/shard_map/ppermute | solution.py:357
  33.8 0.1 collective-permute-start.12
  33.9 0.4 collective-permute-start.10
  34.3 3.1 %collective-permute-done.9.act_half_ref = bf16[128,384]{1,0:T(8,128)(2,1)S(1)} collective-permute-done((bf16[128,384]{1,0:T(8,128)(2,1)S(1)}, bf16[128,384]{1,0:T(8,128)(2,1)S(1)}, u32[]{:S(2)}, u32[]{:S(2)}) %collective-permute-start.9) | collective-permute-done | bytes 98336 | tf_op jit(solution)/shard_map/ppermute | solution.py:357
  37.4 0.0 collective-permute-start.11
  37.4 0.0 collective-permute-done.10.act_core_ref
  37.4 0.0 collective-permute-done.12.side_ref
  37.4 1.3 %collective-permute-done.11.act_both_ref = bf16[128,384]{1,0:T(8,128)(2,1)S(1)} collective-permute-done((bf16[128,384]{1,0:T(8,128)(2,1)S(1)}, bf16[128,384]{1,0:T(8,128)(2,1)S(1)}, u32[]{:S(2)}, u32[]{:S(2)}) %collective-permute-start.11) | collective-permute-done | bytes 98336 | tf_op jit(solution)/shard_map/ppermute | solution.py:354
  38.7 0.0 copy-done.2
  38.7 0.0 copy-done.7
  38.7 1.0 %down.1 = bf16[8,144,128]{2,1,0:T(8,128)(2,1)S(1)} custom-call(s32[8]{0:T(128)S(1)} %copy-done.7, bf16[128,384]{1,0:T(8,128)(2,1)S(1)} %get-tuple-element.33.act_ref, bf16[128,384]{1,0:T(8,128)(2,1)S(1)} %collective-permute-done.9.act_half_ref, bf16[128,384]{1,0:T(8,128)(2,1)S(1)} %collective-permute-done.10.act_core_ref, ...), custom_call_target="tpu_custom_call" | custom-call | tf_op jit(solution)/shard_map/down/pallas_call | solution.py:493
  39.7 15.1 %all_to_all.5.came_ref = bf16[8,144,128]{2,1,0:T(8,128)(2,1)S(1)} all-to-all(bf16[8,144,128]{2,1,0:T(8,128)(2,1)S(1)} %down.1), channel_id=1, replica_groups=mesh['ep'=8,'tp'=4] {'ep'}, dimensions={0} | all-to-all | bytes 589824 | tf_op jit(solution)/shard_map/all_to_all | solution.py:502
  54.8 0.9 %combine.1 = bf16[64,512]{1,0:T(8,128)(2,1)} custom-call(bf16[8,144,128]{2,1,0:T(8,128)(2,1)S(1)} %all_to_all.5.came_ref), custom_call_target="tpu_custom_call" | custom-call | tf_op jit(solution)/shard_map/combine/pallas_call | solution.py:503
  (3 shorter events, 0.1 us)
Async XLA Ops:
  0.0 12.7 %copy-start.6 = (f32[64,2]{0,1:T(2,128)S(1)}, f32[64,2]{0,1:T(2,128)}, u32[]{:S(2)}) copy-start(f32[64,2]{0,1:T(2,128)} %param.26) | copy-start | bytes 1540
  0.0 12.7 %copy-start.5 = (s32[64,2]{0,1:T(2,128)S(1)}, s32[64,2]{0,1:T(2,128)}, u32[]{:S(2)}) copy-start(s32[64,2]{0,1:T(2,128)} %param.25) | copy-start | bytes 1540
  0.0 14.6 %copy-start.1 = (bf16[1,2048,192]{1,2,0:T(8,128)(2,1)S(1)}, bf16[1,2048,192]{1,2,0:T(8,128)(2,1)}, u32[]{:S(2)}) copy-start(bf16[1,2048,192]{1,2,0:T(8,128)(2,1)} %param.28) | copy-start | bytes 2359300
  0.0 14.3 %copy-start = (bf16[1,2048,192]{1,2,0:T(8,128)(2,1)S(1)}, bf16[1,2048,192]{1,2,0:T(8,128)(2,1)}, u32[]{:S(2)}) copy-start(bf16[1,2048,192]{1,2,0:T(8,128)(2,1)} %param.27) | copy-start | bytes 2359300
  4.1 1.7 %collective-permute-start = (bf16[64,1024]{1,0:T(8,128)(2,1)}, bf16[64,1024]{1,0:T(8,128)(2,1)S(1)}, u32[]{:S(2)}, u32[]{:S(2)}) collective-permute-start(bf16[64,1024]{1,0:T(8,128)(2,1)} %get-tuple-element.21), channel_id=1, source_target_pairs={{0,1},{1,0},{2,3},{3,2},{4,5},{5,4},{6,7},{7,6},{8,9},{9,8},{10,11... | collective-permute-start | bytes 393224 | tf_op jit(solution)/shard_map/ppermute | solution.py:354
  4.6 0.9 %copy-start.3 = (f32[64,1024]{1,0:T(8,128)S(1)}, f32[64,1024]{1,0:T(8,128)}, u32[]{:S(2)}) copy-start(f32[64,1024]{1,0:T(8,128)} %get-tuple-element.20.from_ref) | copy-start | bytes 786436
  5.9 6.7 %collective-permute-start.1 = (bf16[64,1024]{1,0:T(8,128)(2,1)S(1)}, bf16[64,1024]{1,0:T(8,128)(2,1)S(1)}, u32[]{:S(2)}, u32[]{:S(2)}) collective-permute-start(bf16[64,1024]{1,0:T(8,128)(2,1)S(1)} %get-tuple-element.23), channel_id=1, source_target_pairs={{0,2},{1,3},{2,0},{3,1},{4,6},{5,7},{6,4},{7,5},{8,10},{9,11},{10,... | collective-permute-start | bytes 393224 | tf_op jit(solution)/shard_map/ppermute | solution.py:357
  12.6 1.4 %collective-permute-start.2 = (bf16[64,1024]{1,0:T(8,128)(2,1)S(1)}, bf16[64,1024]{1,0:T(8,128)(2,1)S(1)}, u32[]{:S(2)}, u32[]{:S(2)}) collective-permute-start(bf16[64,1024]{1,0:T(8,128)(2,1)S(1)} %add_half.1.after_ref.part_ref), channel_id=1, source_target_pairs={{0,1},{1,0},{2,3},{3,2},{4,5},{5,4},{6,7},{7,6},{8,9},{9,8},{10,11... | collective-permute-start | bytes 393224 | tf_op jit(solution)/shard_map/ppermute | solution.py:354
  14.3 5.2 %collective-permute-start.3 = (bf16[192,2048]{1,0:T(8,128)(2,1)S(1)}, bf16[192,2048]{1,0:T(8,128)(2,1)S(1)}, u32[]{:S(2)}, u32[]{:S(2)}) collective-permute-start(bf16[192,2048]{1,0:T(8,128)(2,1)S(1)} %bitcast.12), channel_id=1, source_target_pairs={{0,1},{1,0},{2,3},{3,2},{4,5},{5,4},{6,7},{7,6},{8,9},{9,8},{10,11... | collective-permute-start | bytes 2359304 | tf_op jit(solution)/shard_map/ppermute | solution.py:354
  14.6 5.5 %collective-permute-start.4 = (bf16[192,2048]{1,0:T(8,128)(2,1)S(1)}, bf16[192,2048]{1,0:T(8,128)(2,1)S(1)}, u32[]{:S(2)}, u32[]{:S(2)}) collective-permute-start(bf16[192,2048]{1,0:T(8,128)(2,1)S(1)} %bitcast.14), channel_id=1, source_target_pairs={{0,1},{1,0},{2,3},{3,2},{4,5},{5,4},{6,7},{7,6},{8,9},{9,8},{10,11... | collective-permute-start | bytes 2359304 | tf_op jit(solution)/shard_map/ppermute | solution.py:354
  14.9 8.1 %collective-permute-start.8 = (bf16[528,128]{1,0:T(8,128)(2,1)S(1)}, bf16[528,128]{1,0:T(8,128)(2,1)S(1)}, u32[]{:S(2)}, u32[]{:S(2)}) collective-permute-start(bf16[528,128]{1,0:T(8,128)(2,1)S(1)} %get-tuple-element.32), channel_id=1, source_target_pairs={{0,24},{1,29},{2,26},{3,31},{4,28},{5,25},{6,30},{7,27},{8,16},{9,... | collective-permute-start | bytes 405512 | tf_op jit(solution)/shard_map/ppermute | solution.py:461
  18.8 4.2 %collective-permute-start.5 = (bf16[528,128]{1,0:T(8,128)(2,1)S(1)}, bf16[528,128]{1,0:T(8,128)(2,1)S(1)}, u32[]{:S(2)}, u32[]{:S(2)}) collective-permute-start(bf16[528,128]{1,0:T(8,128)(2,1)S(1)} %get-tuple-element.29), channel_id=1, source_target_pairs={{0,0},{1,5},{2,2},{3,7},{4,4},{5,1},{6,6},{7,3},{8,8},{9,13},{10,1... | collective-permute-start | bytes 405512 | tf_op jit(solution)/shard_map/ppermute | solution.py:461
  19.4 6.1 %collective-permute-start.6 = (bf16[528,128]{1,0:T(8,128)(2,1)S(1)}, bf16[528,128]{1,0:T(8,128)(2,1)S(1)}, u32[]{:S(2)}, u32[]{:S(2)}) collective-permute-start(bf16[528,128]{1,0:T(8,128)(2,1)S(1)} %get-tuple-element.30), channel_id=1, source_target_pairs={{0,8},{1,13},{2,10},{3,15},{4,12},{5,9},{6,14},{7,11},{8,0},{9,5},... | collective-permute-start | bytes 405512 | tf_op jit(solution)/shard_map/ppermute | solution.py:461
  19.5 11.4 %copy-start.4 = (f32[2048]{0:T(1024)S(1)}, f32[2048]{0:T(1024)}, u32[]{:S(2)}) copy-start(f32[2048]{0:T(1024)} %param.24) | copy-start | bytes 24580
  19.5 11.4 %collective-permute-start.7 = (bf16[528,128]{1,0:T(8,128)(2,1)S(1)}, bf16[528,128]{1,0:T(8,128)(2,1)S(1)}, u32[]{:S(2)}, u32[]{:S(2)}) collective-permute-start(bf16[528,128]{1,0:T(8,128)(2,1)S(1)} %get-tuple-element.31), channel_id=1, source_target_pairs={{0,16},{1,21},{2,18},{3,23},{4,20},{5,17},{6,22},{7,19},{8,24},{9,... | collective-permute-start | bytes 405512 | tf_op jit(solution)/shard_map/ppermute | solution.py:461
  20.3 18.3 %copy-start.2 = (bf16[1,768,512]{2,1,0:T(8,128)(2,1)S(1)}, bf16[1,768,512]{2,1,0:T(8,128)(2,1)}, u32[]{:S(2)}) copy-start(bf16[1,768,512]{2,1,0:T(8,128)(2,1)} %param.29) | copy-start | bytes 2359300
  20.4 18.3 %copy-start.7 = (s32[8]{0:T(128)S(1)}, s32[8]{0:T(128)}, u32[]{:S(2)}) copy-start(s32[8]{0:T(128)} %order_ref.1) | copy-start | bytes 100
  32.3 5.1 %collective-permute-start.9 = (bf16[128,384]{1,0:T(8,128)(2,1)S(1)}, bf16[128,384]{1,0:T(8,128)(2,1)S(1)}, u32[]{:S(2)}, u32[]{:S(2)}) collective-permute-start(bf16[128,384]{1,0:T(8,128)(2,1)S(1)} %get-tuple-element.33.act_ref), channel_id=1, source_target_pairs={{0,2},{1,3},{2,0},{3,1},{4,6},{5,7},{6,4},{7,5},{8,10},{9,11},{10,... | collective-permute-start | bytes 294920 | tf_op jit(solution)/shard_map/ppermute | solution.py:357
  33.8 3.6 %collective-permute-start.12 = (bf16[4,144,128]{2,1,0:T(8,128)(2,1)S(1)}, bf16[4,144,128]{2,1,0:T(8,128)(2,1)S(1)}, u32[]{:S(2)}, u32[]{:S(2)}) collective-permute-start(bf16[4,144,128]{2,1,0:T(8,128)(2,1)S(1)} %get-tuple-element.34), channel_id=1, source_target_pairs={{0,1},{1,0},{2,3},{3,2},{4,5},{5,4},{6,7},{7,6},{8,9},{9,8},{10,11... | collective-permute-start | bytes 442376 | tf_op jit(solution)/shard_map/ppermute | solution.py:354
  33.9 3.5 %collective-permute-start.10 = (bf16[128,384]{1,0:T(8,128)(2,1)S(1)}, bf16[128,384]{1,0:T(8,128)(2,1)S(1)}, u32[]{:S(2)}, u32[]{:S(2)}) collective-permute-start(bf16[128,384]{1,0:T(8,128)(2,1)S(1)} %get-tuple-element.33.act_ref), channel_id=1, source_target_pairs={{0,1},{1,0},{2,3},{3,2},{4,5},{5,4},{6,7},{7,6},{8,9},{9,8},{10,11... | collective-permute-start | bytes 294920 | tf_op jit(solution)/shard_map/ppermute | solution.py:354
  37.4 1.3 %collective-permute-start.11 = (bf16[128,384]{1,0:T(8,128)(2,1)S(1)}, bf16[128,384]{1,0:T(8,128)(2,1)S(1)}, u32[]{:S(2)}, u32[]{:S(2)}) collective-permute-start(bf16[128,384]{1,0:T(8,128)(2,1)S(1)} %collective-permute-done.9.act_half_ref), channel_id=1, source_target_pairs={{0,1},{1,0},{2,3},{3,2},{4,5},{5,4},{6,7},{7,6},{8,9},{9,8},{10,11... | collective-permute-start | bytes 294920 | tf_op jit(solution)/shard_map/ppermute | solution.py:354

commit v4 on v3

--- a/solution.py
+++ b/solution.py
@@ -92,7 +92,7 @@
     scale = 1.0 / math.sqrt(HEAD)
     for copy in copies[:4]:
         copy.wait()
-    length = length_ref[0]
+    length = length_ref[0, 0]
     pieces = []
     for g in range(kv_local):
         columns = slice(g * HEAD, (g + 1) * HEAD)
@@ -149,6 +149,18 @@
     to_ref[...] = from_ref[...]
 
 
+def earlier_tokens(tokens):
+    earlier = lax.broadcasted_iota(jnp.int32, (tokens, tokens), 0) < lax.broadcasted_iota(
+        jnp.int32, (tokens, tokens), 1
+    )
+    return jnp.where(earlier, 1.0, 0.0).astype(BF16)
+
+
+def slot_numbers(named, tokens):
+    rank = dot(named.astype(BF16), earlier_tokens(tokens))
+    return jnp.where(named > 0.0, rank, -1.0)
+
+
 def route_kernel(peers, after_ref, expert_ref, weight_ref, pick_ref, tags_ref):
     del after_ref
     me = lax.axis_index("ep")
@@ -166,20 +178,47 @@
         match = expert_ref[j : j + 1, :] == peer
         mix_of = mix_of + jnp.where(match, mixing[j : j + 1, :], 0.0)
         named = named + jnp.where(match, 1.0, 0.0)
-    earlier = lax.broadcasted_iota(jnp.int32, (tokens, tokens), 0) < lax.broadcasted_iota(
-        jnp.int32, (tokens, tokens), 1
-    )
-    rank = dot(named.astype(BF16), jnp.where(earlier, 1.0, 0.0).astype(BF16))
-    rank = jnp.where(named > 0.0, rank, -1.0)
+    rank = slot_numbers(named, tokens)
     slot = lax.broadcasted_iota(jnp.int32, (rows_each, tokens), 0).astype(F32)
     line = lax.broadcasted_iota(jnp.int32, (TAGS, tokens), 0)
-    number = lax.broadcasted_iota(jnp.int32, (TAGS, tokens), 1).astype(F32) + 1.0
+    names = jnp.zeros((TAGS, tokens), F32)
+    for j in range(top):
+        names = jnp.where(line == j + 1, expert_ref[j : j + 1, :].astype(F32), names)
     tags_ref[...] = jnp.zeros(tags_ref.shape, BF16)
     for k in range(peers):
         pick = jnp.where(rank[k : k + 1, :] == slot, 1.0, 0.0).astype(BF16)
         pick_ref[k * rows_each : (k + 1) * rows_each, :] = pick
-        known = jnp.where(line == 0, number, jnp.where(line == 1, mix_of[k : k + 1, :], 0.0))
-        tags_ref[k, :, :rows_each] = dot_t(known.astype(BF16), pick).astype(BF16)
+        tags_ref[k, :, :tokens] = names.astype(BF16)
+        mix = jnp.where(line == 0, mix_of[k : k + 1, :], 0.0).astype(BF16)
+        tags_ref[k, :1, :rows_each] = dot_t(mix, pick)[:1].astype(BF16)
+
+
+def select_kernel(peers, top, order_ref, side_ref, *refs):
+    got = refs[:peers]
+    chosen_ref = refs[peers]
+    me = lax.axis_index("ep")
+    core = lax.axis_index("tp") % 2
+    tokens = chosen_ref.shape[0]
+    experts = 2 * peers
+    rows_each = chosen_ref.shape[1] // experts
+    names = jnp.zeros((TAGS, LANES), F32)
+    for k in range(peers):
+        for tags, parity in (
+            (got[k][got[k].shape[0] - TAGS :, :], core),
+            (side_ref[k, side_ref.shape[1] - TAGS :, :], 1 - core),
+        ):
+            here = order_ref[jnp.bitwise_xor(me, 2 * k + parity)] == me
+            names = names + jnp.where(here, tags.astype(F32), 0.0)
+    expert = lax.broadcasted_iota(jnp.int32, (experts, tokens), 0).astype(F32)
+    named = jnp.zeros((experts, tokens), F32)
+    for j in range(top):
+        named = named + jnp.where(names[j + 1 : j + 2, :tokens] == expert, 1.0, 0.0)
+    rank = slot_numbers(named, tokens)
+    slot = lax.broadcasted_iota(jnp.int32, (rows_each, tokens), 0).astype(F32)
+    pick = jnp.concatenate(
+        [jnp.where(rank[e : e + 1, :] == slot, 1.0, 0.0) for e in range(experts)], axis=0
+    )
+    chosen_ref[...] = pick.T.astype(BF16)
 
 
 def add_core_kernel(keep_ref, came_ref, sum_ref, send_ref):
@@ -192,24 +231,25 @@
     out_ref[...] = (sum_ref[...] + came_ref[...].astype(F32)).astype(BF16)
 
 
-def gather_kernel(peers, part_ref, other_ref, pick_ref, tags_ref, *send_refs):
+def gather_kernel(first, count, after_ref, part_ref, other_ref, pick_ref, tags_ref, *send_refs):
+    del after_ref
     core = lax.axis_index("tp") % 2
-    rows_each = pick_ref.shape[0] // peers
-    pick = pick_ref[...]
+    rows_each = pick_ref.shape[0] // tags_ref.shape[0]
+    pick = pick_ref[first * rows_each : (first + count) * rows_each, :]
     width = part_ref.shape[1] // 2
     blocks = width // LANES
     for source, parity in ((part_ref, core), (other_ref, 1 - core)):
         for half in range(2):
             rows = dot(pick, source[:, half * width : (half + 1) * width]).astype(BF16)
             base = (2 * half + parity) * (blocks * rows_each)
-            for k in range(peers):
+            for k in range(count):
                 for j in range(blocks):
                     start = pl.multiple_of(base + j * rows_each, rows_each)
                     send_refs[k][pl.ds(start, rows_each), :] = rows[
                         k * rows_each : (k + 1) * rows_each, j * LANES : (j + 1) * LANES
                     ]
-    for k in range(peers):
-        send_refs[k][4 * blocks * rows_each :, :] = tags_ref[k]
+    for k in range(count):
+        send_refs[k][4 * blocks * rows_each :, :] = tags_ref[first + k]
 
 
 def stage_kernel(after_ref, *refs):
@@ -266,6 +306,7 @@
 def down_kernel(
     peers,
     rows_each,
+    after_ref,
     order_ref,
     act_ref,
     act_half_ref,
@@ -275,6 +316,7 @@
     side_ref,
     *refs,
 ):
+    del after_ref
     got = refs[:peers]
     out_ref = refs[peers]
     tp = lax.axis_index("tp")
@@ -302,7 +344,7 @@
                 rows = side_ref[k, :tall, :]
                 tags = side_ref[k, tall:, :]
             mix = jnp.sum(
-                jnp.where(diagonal, tags.astype(F32)[1:2, :], 0.0), axis=1, keepdims=True
+                jnp.where(diagonal, tags.astype(F32)[0:1, :], 0.0), axis=1, keepdims=True
             )
             for j in range(blocks):
                 piece = slice(j * rows_each, (j + 1) * rows_each)
@@ -310,23 +352,16 @@
                     k * rows_each : (k + 1) * rows_each, j * LANES : (j + 1) * LANES
                 ]
                 out_ref[place, piece, :] = (mix * value).astype(BF16)
-            out_ref[place, tall:, :] = tags
-
-
-def combine_kernel(rows_each, came_ref, out_ref):
-    tokens, width = out_ref.shape
-    blocks = width // LANES
-    tall = blocks * rows_each
-    number = lax.broadcasted_iota(jnp.int32, (tokens, rows_each), 0).astype(F32) + 1.0
-    total = jnp.zeros((tokens, width), F32)
-    for e in range(came_ref.shape[0]):
-        tags = came_ref[e, tall:, :].astype(F32)
-        chosen = (number == tags[0:1, :rows_each]).astype(BF16)
+
+
+def combine_kernel(rows_each, chosen_ref, came_ref, out_ref):
+    chosen = chosen_ref[...]
+    experts, tall, _ = came_ref.shape
+    for j in range(tall // rows_each):
         rows = jnp.concatenate(
-            [came_ref[e, j * rows_each : (j + 1) * rows_each, :] for j in range(blocks)], axis=1
+            [came_ref[e, j * rows_each : (j + 1) * rows_each, :] for e in range(experts)], axis=0
         )
-        total = total + dot(chosen, rows)
-    out_ref[...] = total.astype(BF16)
+        out_ref[:, j * LANES : (j + 1) * LANES] = dot(chosen, rows).astype(BF16)
 
 
 def shards(
@@ -373,7 +408,7 @@
         in_specs=[hbm()] * 8,
         out_specs=(hbm(), hbm()),
         scratch_shapes=[
-            pltpu.SMEM(cache_lengths.shape, jnp.int32),
+            pltpu.SMEM((1, 1), jnp.int32),
             pltpu.VMEM(queries.shape, BF16),
             pltpu.VMEM(new_keys.shape, BF16),
             pltpu.VMEM(new_values.shape, BF16),
@@ -388,7 +423,7 @@
         compiler_params=params(ATTEND_MIB),
         name="attend",
     )(
-        cache_lengths,
+        cache_lengths.reshape(1, 1),
         queries,
         new_keys,
         new_values,
@@ -438,15 +473,15 @@
     )(part, route_experts.T, route_weights.T)
     other = swap_core(part)
 
-    block_shape = shape((tp_count * tall + TAGS, LANES), BF16)
-    send = pl.pallas_call(
-        functools.partial(gather_kernel, peers),
-        out_shape=[block_shape] * peers,
-        in_specs=[vmem()] * 4,
-        out_specs=[vmem()] * peers,
-        compiler_params=params(8),
-        name="gather_rows",
-    )(part, other, pick, tags)
+    def gather(first, count, after):
+        return pl.pallas_call(
+            functools.partial(gather_kernel, first, count),
+            out_shape=[shape((tp_count * tall + TAGS, LANES), BF16)] * count,
+            in_specs=[pl.BlockSpec(memory_space=pl.ANY)] + [vmem()] * 4,
+            out_specs=[vmem()] * count,
+            compiler_params=params(8),
+            name="gather_rows",
+        )(after, part, other, pick, tags)
 
     def route(k):
         return [
@@ -455,10 +490,15 @@
             for t in range(tp_count)
         ]
 
-    send = list(send)
-    gate, up, send[-1] = lax.optimization_barrier((gate, up, send[-1]))
+    near = peers // 2
+    far_send = list(gather(near, peers - near, tags))
+    gate, up, far_send[-1] = lax.optimization_barrier((gate, up, far_send[-1]))
+    far = [
+        lax.ppermute(x, ("ep", "tp"), route(near + k)) for k, x in enumerate(far_send)
+    ]
     gate_pair, up_pair = swap_core(gate), swap_core(up)
-    got = [lax.ppermute(send[k], ("ep", "tp"), route(k)) for k in range(peers)]
+    near_send = gather(0, near, gate_pair)
+    got = [lax.ppermute(x, ("ep", "tp"), route(k)) for k, x in enumerate(near_send)] + far
 
     weights = pl.pallas_call(
         stage_kernel,
@@ -490,24 +530,34 @@
     side = swap_core(side)
     act_both = swap_core(act_half)
 
+    chosen = pl.pallas_call(
+        functools.partial(select_kernel, peers, top),
+        out_shape=shape((tokens, ep_count * rows_each), BF16),
+        in_specs=[pl.BlockSpec(memory_space=pltpu.SMEM)] + [vmem()] * (1 + peers),
+        out_specs=vmem(),
+        compiler_params=params(8),
+        cost_estimate=pl.CostEstimate(flops=0, bytes_accessed=MIB, transcendentals=0),
+        name="select",
+    )(request_order, side, *got)
     result = pl.pallas_call(
         functools.partial(down_kernel, peers, rows_each),
-        out_shape=shape((ep_count, tall + TAGS, LANES), BF16),
-        in_specs=[pl.BlockSpec(memory_space=pltpu.SMEM)] + [vmem()] * (6 + peers),
+        out_shape=shape((ep_count, tall, LANES), BF16),
+        in_specs=[pl.BlockSpec(memory_space=pl.ANY), pl.BlockSpec(memory_space=pltpu.SMEM)]
+        + [vmem()] * (6 + peers),
         out_specs=vmem(),
         compiler_params=params(16),
         name="down",
-    )(request_order, act, act_half, act_core, act_both, down, side, *got)
+    )(chosen, request_order, act, act_half, act_core, act_both, down, side, *got)
 
     came = lax.all_to_all(result, "ep", split_axis=0, concat_axis=0, tiled=True)
     return pl.pallas_call(
         functools.partial(combine_kernel, rows_each),
         out_shape=shape((tokens, width), BF16),
-        in_specs=[vmem()],
+        in_specs=[vmem()] * 2,
         out_specs=vmem(),
         compiler_params=params(8),
         name="combine",
-    )(came)
+    )(chosen, came)
 
 
 def solution(mesh):

time: 55.9 us -> 54.2 us (0.970)
  blocking collectives: 15.1 us -> 13.7 us
  waiting for transfers between devices: 20 us -> 18.8 us
  Pallas kernels: 7.48 us -> 8.29 us
    all_to_all x1, blocking collectives: 15.1 us -> 13.7 us  [shards(): came = lax.all_to_all(result, 'ep', split_axis=0, concat_axis=0, tiled=True)]
    pallas_call x1 -> x3, Pallas kernels: 0.27 us -> 1.19 us  [the longest x1 0.77 us: shards(): pl.pallas_call(functools.partial(select_kernel, peers, top), out_shape=sh...]
    ppermute x7, waiting for transfers between devices: 2.58 us -> 1.79 us  [swap_core(): return lax.ppermute(x, 'tp', [(i, i ^ 1) for i in range(tp_count)])]
  transfers between devices with their start and end apart: 13 -> 13, of which waited for: 8 -> 7; matrix products, arithmetic and copies ran while one was open for 0% -> 0% of each run, Pallas kernels for 1% -> 3%
where the time goes in v4:
time: 54.2 us; the launch traced here: 54 us
  waiting for transfers between devices  18.8 us (35%)
  blocking collectives  13.7 us (25%)
  starting transfers between devices  11.3 us (21%)
  Pallas kernels  8.29 us (15%)
  local copies, waits for them, and re-layouts  0.98 us (2%)
  between operations  0.93 us (2%)
    all_to_all x1, blocking collectives, shards(): came = lax.all_to_all(result, 'ep', split_axis=0, concat_axis=0, tiled=True)  13.7 us
    ppermute x2, waiting for transfers between devices, shards(): lax.ppermute(x, ('ep', 'tp'), route(near + k))  10.6 us
    ppermute x2, waiting for transfers between devices, swap_half(): return lax.ppermute(x, 'tp', [(i, i ^ 2) for i in range(tp_count)])  6.43 us
    ppermute x2, starting transfers between devices, swap_half(): return lax.ppermute(x, 'tp', [(i, i ^ 2) for i in range(tp_count)])  4.47 us
    ppermute x2, starting transfers between devices, shards(): lax.ppermute(x, ('ep', 'tp'), route(near + k))  3.85 us
    pallas_call x1, Pallas kernels, shards(): pl.pallas_call(functools.partial(attend_kernel, kv_local), out_shape=(sha...  3.35 us
    ppermute x7, waiting for transfers between devices, swap_core(): return lax.ppermute(x, 'tp', [(i, i ^ 1) for i in range(tp_count)])  1.79 us
    ppermute x7, starting transfers between devices, swap_core(): return lax.ppermute(x, 'tp', [(i, i ^ 1) for i in range(tp_count)])  1.68 us
  transfers between devices with their start and end apart: 13, of which 7 were waited for; matrix products, arithmetic and copies ran while one was open for 0% of the time, Pallas kernels for 3%

profile of v4, /device:TPU:0, one launch (start us, length us, event | category | flops | bytes accessed | tf_op | source)
XLA Modules:
  0.0 54.0 jit_solution(4506627755907874836)
XLA Ops:
  0.0 0.0 copy-start.7
  0.0 0.0 copy-start.6
  0.0 0.0 copy-start.1
  0.0 0.0 copy-start
  0.8 3.3 %attend.1 = (f32[64,1024]{1,0:T(8,128)}, bf16[64,1024]{1,0:T(8,128)(2,1)}) custom-call(s32[1,1]{1,0:T(1,128)} %bitcast.13.length_hbm, bf16[64,512]{1,0:T(8,128)(2,1)} %query_hbm.1, bf16[64,128]{1,0:T(8,128)(2,1)} %new_key_hbm.1, bf16[64,128]{1,0:T(8,128)(2,1)} %new_value_hbm.1, bf16[512,128]{1,0:T(8,128)(2,1)} %bitcast.22, bf16[512,128]{1,0:T(8,128)(2,1)} %bitcast.23, ...), custom_call_target="tpu_custom_call" | custom-call | tf_op jit(solution)/shard_map/attend/pallas_call | solution.py:405
  4.1 0.5 collective-permute-start
  4.7 0.0 copy-start.3
  4.7 0.9 %copy-done.3 = f32[64,1024]{1,0:T(8,128)S(1)} copy-done((f32[64,1024]{1,0:T(8,128)S(1)}, f32[64,1024]{1,0:T(8,128)}, u32[]{:S(2)}) %copy-start.3) | copy-done | bytes 262168
  5.6 0.2 collective-permute-done.came_ref
  5.9 2.9 %collective-permute-start.1 = (bf16[64,1024]{1,0:T(8,128)(2,1)S(1)}, bf16[64,1024]{1,0:T(8,128)(2,1)S(1)}, u32[]{:S(2)}, u32[]{:S(2)}) collective-permute-start(bf16[64,1024]{1,0:T(8,128)(2,1)S(1)} %get-tuple-element.23), channel_id=1, source_target_pairs={{0,2},{1,3},{2,0},{3,1},{4,6},{5,7},{6,4},{7,5},{8,10},{9,11},{10,... | collective-permute-start | bytes 393224 | tf_op jit(solution)/shard_map/ppermute | solution.py:392
  8.8 3.8 %collective-permute-done.1.came_ref = bf16[64,1024]{1,0:T(8,128)(2,1)S(1)} collective-permute-done((bf16[64,1024]{1,0:T(8,128)(2,1)S(1)}, bf16[64,1024]{1,0:T(8,128)(2,1)S(1)}, u32[]{:S(2)}, u32[]{:S(2)}) %collective-permute-start.1) | collective-permute-done | bytes 131104 | tf_op jit(solution)/shard_map/ppermute | solution.py:392
  12.6 0.1 collective-permute-start.2
  12.7 0.0 copy-done.7
  12.7 0.0 copy-done.6
  12.7 0.3 route.1
  13.0 1.1 %collective-permute-done.2.other_ref = bf16[64,1024]{1,0:T(8,128)(2,1)S(1)} collective-permute-done((bf16[64,1024]{1,0:T(8,128)(2,1)S(1)}, bf16[64,1024]{1,0:T(8,128)(2,1)S(1)}, u32[]{:S(2)}, u32[]{:S(2)}) %collective-permute-start.2) | collective-permute-done | bytes 131104 | tf_op jit(solution)/shard_map/ppermute | solution.py:389
  14.1 0.2 gather_rows.2
  14.3 0.0 copy-done
  14.3 0.2 collective-permute-start.3
  14.5 0.0 copy-done.1
  14.5 0.4 collective-permute-start.4
  14.9 3.8 %collective-permute-start.8 = (bf16[528,128]{1,0:T(8,128)(2,1)S(1)}, bf16[528,128]{1,0:T(8,128)(2,1)S(1)}, u32[]{:S(2)}, u32[]{:S(2)}) collective-permute-start(bf16[528,128]{1,0:T(8,128)(2,1)S(1)} %get-tuple-element.32), channel_id=1, source_target_pairs={{0,24},{1,29},{2,26},{3,31},{4,28},{5,25},{6,30},{7,27},{8,16},{9,... | collective-permute-start | bytes 405512 | tf_op jit(solution)/shard_map/ppermute | solution.py:497
  18.7 0.0 collective-permute-start.7
  18.7 0.0 collective-permute-done.3.refs_2_.after_ref
  18.7 0.2 gather_rows.3
  18.9 0.7 %collective-permute-start.5 = (bf16[528,128]{1,0:T(8,128)(2,1)S(1)}, bf16[528,128]{1,0:T(8,128)(2,1)S(1)}, u32[]{:S(2)}, u32[]{:S(2)}) collective-permute-start(bf16[528,128]{1,0:T(8,128)(2,1)S(1)} %get-tuple-element.29), channel_id=1, source_target_pairs={{0,0},{1,5},{2,2},{3,7},{4,4},{5,1},{6,6},{7,3},{8,8},{9,13},{10,1... | collective-permute-start | bytes 405512 | tf_op jit(solution)/shard_map/ppermute | solution.py:501
  19.6 0.0 copy-start.4
  19.6 0.6 %collective-permute-start.6 = (bf16[528,128]{1,0:T(8,128)(2,1)S(1)}, bf16[528,128]{1,0:T(8,128)(2,1)S(1)}, u32[]{:S(2)}, u32[]{:S(2)}) collective-permute-start(bf16[528,128]{1,0:T(8,128)(2,1)S(1)} %get-tuple-element.30), channel_id=1, source_target_pairs={{0,8},{1,13},{2,10},{3,15},{4,12},{5,9},{6,14},{7,11},{8,0},{9,5},... | collective-permute-start | bytes 405512 | tf_op jit(solution)/shard_map/ppermute | solution.py:501
  20.2 0.0 collective-permute-done.4.refs_3_
  20.2 0.3 stage.1.weight_ref
  20.5 0.0 copy-start.5
  20.5 0.0 copy-start.2
  20.5 2.4 %collective-permute-done.8.refs_3_ = bf16[528,128]{1,0:T(8,128)(2,1)S(1)} collective-permute-done((bf16[528,128]{1,0:T(8,128)(2,1)S(1)}, bf16[528,128]{1,0:T(8,128)(2,1)S(1)}, u32[]{:S(2)}, u32[]{:S(2)}) %collective-permute-start.8) | collective-permute-done | bytes 135200 | tf_op jit(solution)/shard_map/ppermute | solution.py:497
  23.0 8.2 %collective-permute-done.7.refs_2_ = bf16[528,128]{1,0:T(8,128)(2,1)S(1)} collective-permute-done((bf16[528,128]{1,0:T(8,128)(2,1)S(1)}, bf16[528,128]{1,0:T(8,128)(2,1)S(1)}, u32[]{:S(2)}, u32[]{:S(2)}) %collective-permute-start.7) | collective-permute-done | bytes 135200 | tf_op jit(solution)/shard_map/ppermute | solution.py:497
  31.1 0.0 collective-permute-done.5.refs_0_
  31.1 0.0 collective-permute-done.6.refs_1_
  31.1 0.0 copy-done.4
  31.1 1.4 %hidden_units.1 = (bf16[128,384]{1,0:T(8,128)(2,1)S(1)}, bf16[4,144,128]{2,1,0:T(8,128)(2,1)S(1)}) custom-call(f32[16,128]{1,0:T(8,128)S(1)} %bitcast.19, bf16[4,192,2048]{2,1,0:T(8,128)(2,1)S(1)} %stage.1.weight_ref, bf16[528,128]{1,0:T(8,128)(2,1)S(1)} %collective-permute-done.5.refs_0_, bf16[528,128]{1,0:T(8,128)(2,1)S(1)} %collective-permute-done.6.refs_1_, ...), custom_call_target="tpu_custom_call" | custom-call | tf_op jit(solution)/shard_map/hidden_units/pallas_call | solution.py:516
  32.5 1.6 %collective-permute-start.10 = (bf16[128,384]{1,0:T(8,128)(2,1)S(1)}, bf16[128,384]{1,0:T(8,128)(2,1)S(1)}, u32[]{:S(2)}, u32[]{:S(2)}) collective-permute-start(bf16[128,384]{1,0:T(8,128)(2,1)S(1)} %get-tuple-element.34.act_ref), channel_id=1, source_target_pairs={{0,2},{1,3},{2,0},{3,1},{4,6},{5,7},{6,4},{7,5},{8,10},{9,11},{10,... | collective-permute-start | bytes 294920 | tf_op jit(solution)/shard_map/ppermute | solution.py:392
  34.1 0.0 collective-permute-start.9
  34.1 0.5 collective-permute-start.11
  34.6 2.6 %collective-permute-done.10.act_half_ref = bf16[128,384]{1,0:T(8,128)(2,1)S(1)} collective-permute-done((bf16[128,384]{1,0:T(8,128)(2,1)S(1)}, bf16[128,384]{1,0:T(8,128)(2,1)S(1)}, u32[]{:S(2)}, u32[]{:S(2)}) %collective-permute-start.10) | collective-permute-done | bytes 98336 | tf_op jit(solution)/shard_map/ppermute | solution.py:392
  37.2 0.0 collective-permute-start.12
  37.2 0.0 collective-permute-done.9.side_ref
  37.2 0.0 copy-done.5
  37.2 0.8 %select.1.after_ref.chosen_ref = bf16[64,256]{1,0:T(8,128)(2,1)S(1)} custom-call(s32[8]{0:T(128)S(1)} %copy-done.5, bf16[4,144,128]{2,1,0:T(8,128)(2,1)S(1)} %collective-permute-done.9.side_ref, bf16[528,128]{1,0:T(8,128)(2,1)S(1)} %collective-permute-done.5.refs_0_, bf16[528,128]{1,0:T(8,128)(2,1)S(1)} %collective-permute-done.6.refs_1_, ...), custom_call_target="tpu_custom_call" | custom-call | bytes 1048576 | tf_op jit(solution)/shard_map/select/pallas_call | solution.py:533
  38.0 0.0 collective-permute-done.11.act_core_ref
  38.0 0.5 collective-permute-done.12.act_both_ref
  38.5 0.0 copy-done.2
  38.5 1.0 %down.1 = bf16[8,128,128]{2,1,0:T(8,128)(2,1)S(1)} custom-call(bf16[64,256]{1,0:T(8,128)(2,1)S(1)} %select.1.after_ref.chosen_ref, s32[8]{0:T(128)S(1)} %copy-done.5, bf16[128,384]{1,0:T(8,128)(2,1)S(1)} %get-tuple-element.34.act_ref, bf16[128,384]{1,0:T(8,128)(2,1)S(1)} %collective-permute-done.10.act_half_ref, ...), custom_call_target="tpu_custom_call" | custom-call | tf_op jit(solution)/shard_map/down/pallas_call | solution.py:542
  39.5 13.7 %all_to_all.5.came_ref = bf16[8,128,128]{2,1,0:T(8,128)(2,1)S(1)} all-to-all(bf16[8,128,128]{2,1,0:T(8,128)(2,1)S(1)} %down.1), channel_id=1, replica_groups=mesh['ep'=8,'tp'=4] {'ep'}, dimensions={0} | all-to-all | bytes 524288 | tf_op jit(solution)/shard_map/all_to_all | solution.py:552
  53.2 0.8 %combine.1 = bf16[64,512]{1,0:T(8,128)(2,1)} custom-call(bf16[64,256]{1,0:T(8,128)(2,1)S(1)} %select.1.after_ref.chosen_ref, bf16[8,128,128]{2,1,0:T(8,128)(2,1)S(1)} %all_to_all.5.came_ref), custom_call_target="tpu_custom_call" | custom-call | tf_op jit(solution)/shard_map/combine/pallas_call | solution.py:553
  (3 shorter events, 0.1 us)
Async XLA Ops:
  0.0 12.7 %copy-start.7 = (f32[64,2]{0,1:T(2,128)S(1)}, f32[64,2]{0,1:T(2,128)}, u32[]{:S(2)}) copy-start(f32[64,2]{0,1:T(2,128)} %param.26) | copy-start | bytes 1540
  0.0 12.7 %copy-start.6 = (s32[64,2]{0,1:T(2,128)S(1)}, s32[64,2]{0,1:T(2,128)}, u32[]{:S(2)}) copy-start(s32[64,2]{0,1:T(2,128)} %param.25) | copy-start | bytes 1540
  0.0 14.5 %copy-start.1 = (bf16[1,2048,192]{1,2,0:T(8,128)(2,1)S(1)}, bf16[1,2048,192]{1,2,0:T(8,128)(2,1)}, u32[]{:S(2)}) copy-start(bf16[1,2048,192]{1,2,0:T(8,128)(2,1)} %param.28) | copy-start | bytes 2359300
  0.0 14.3 %copy-start = (bf16[1,2048,192]{1,2,0:T(8,128)(2,1)S(1)}, bf16[1,2048,192]{1,2,0:T(8,128)(2,1)}, u32[]{:S(2)}) copy-start(bf16[1,2048,192]{1,2,0:T(8,128)(2,1)} %param.27) | copy-start | bytes 2359300
  4.1 1.7 %collective-permute-start = (bf16[64,1024]{1,0:T(8,128)(2,1)}, bf16[64,1024]{1,0:T(8,128)(2,1)S(1)}, u32[]{:S(2)}, u32[]{:S(2)}) collective-permute-start(bf16[64,1024]{1,0:T(8,128)(2,1)} %get-tuple-element.21), channel_id=1, source_target_pairs={{0,1},{1,0},{2,3},{3,2},{4,5},{5,4},{6,7},{7,6},{8,9},{9,8},{10,11... | collective-permute-start | bytes 393224 | tf_op jit(solution)/shard_map/ppermute | solution.py:389
  4.7 0.9 %copy-start.3 = (f32[64,1024]{1,0:T(8,128)S(1)}, f32[64,1024]{1,0:T(8,128)}, u32[]{:S(2)}) copy-start(f32[64,1024]{1,0:T(8,128)} %get-tuple-element.20.from_ref) | copy-start | bytes 786436
  5.9 6.7 %collective-permute-start.1 = (bf16[64,1024]{1,0:T(8,128)(2,1)S(1)}, bf16[64,1024]{1,0:T(8,128)(2,1)S(1)}, u32[]{:S(2)}, u32[]{:S(2)}) collective-permute-start(bf16[64,1024]{1,0:T(8,128)(2,1)S(1)} %get-tuple-element.23), channel_id=1, source_target_pairs={{0,2},{1,3},{2,0},{3,1},{4,6},{5,7},{6,4},{7,5},{8,10},{9,11},{10,... | collective-permute-start | bytes 393224 | tf_op jit(solution)/shard_map/ppermute | solution.py:392
  12.6 1.4 %collective-permute-start.2 = (bf16[64,1024]{1,0:T(8,128)(2,1)S(1)}, bf16[64,1024]{1,0:T(8,128)(2,1)S(1)}, u32[]{:S(2)}, u32[]{:S(2)}) collective-permute-start(bf16[64,1024]{1,0:T(8,128)(2,1)S(1)} %add_half.1.after_ref.part_ref), channel_id=1, source_target_pairs={{0,1},{1,0},{2,3},{3,2},{4,5},{5,4},{6,7},{7,6},{8,9},{9,8},{10,11... | collective-permute-start | bytes 393224 | tf_op jit(solution)/shard_map/ppermute | solution.py:389
  14.3 4.4 %collective-permute-start.3 = (bf16[192,2048]{1,0:T(8,128)(2,1)S(1)}, bf16[192,2048]{1,0:T(8,128)(2,1)S(1)}, u32[]{:S(2)}, u32[]{:S(2)}) collective-permute-start(bf16[192,2048]{1,0:T(8,128)(2,1)S(1)} %bitcast.14), channel_id=1, source_target_pairs={{0,1},{1,0},{2,3},{3,2},{4,5},{5,4},{6,7},{7,6},{8,9},{9,8},{10,11... | collective-permute-start | bytes 2359304 | tf_op jit(solution)/shard_map/ppermute | solution.py:389
  14.5 5.8 %collective-permute-start.4 = (bf16[192,2048]{1,0:T(8,128)(2,1)S(1)}, bf16[192,2048]{1,0:T(8,128)(2,1)S(1)}, u32[]{:S(2)}, u32[]{:S(2)}) collective-permute-start(bf16[192,2048]{1,0:T(8,128)(2,1)S(1)} %bitcast.16), channel_id=1, source_target_pairs={{0,1},{1,0},{2,3},{3,2},{4,5},{5,4},{6,7},{7,6},{8,9},{9,8},{10,11... | collective-permute-start | bytes 2359304 | tf_op jit(solution)/shard_map/ppermute | solution.py:389
  14.9 8.1 %collective-permute-start.8 = (bf16[528,128]{1,0:T(8,128)(2,1)S(1)}, bf16[528,128]{1,0:T(8,128)(2,1)S(1)}, u32[]{:S(2)}, u32[]{:S(2)}) collective-permute-start(bf16[528,128]{1,0:T(8,128)(2,1)S(1)} %get-tuple-element.32), channel_id=1, source_target_pairs={{0,24},{1,29},{2,26},{3,31},{4,28},{5,25},{6,30},{7,27},{8,16},{9,... | collective-permute-start | bytes 405512 | tf_op jit(solution)/shard_map/ppermute | solution.py:497
  18.7 12.4 %collective-permute-start.7 = (bf16[528,128]{1,0:T(8,128)(2,1)S(1)}, bf16[528,128]{1,0:T(8,128)(2,1)S(1)}, u32[]{:S(2)}, u32[]{:S(2)}) collective-permute-start(bf16[528,128]{1,0:T(8,128)(2,1)S(1)} %get-tuple-element.31), channel_id=1, source_target_pairs={{0,16},{1,21},{2,18},{3,23},{4,20},{5,17},{6,22},{7,19},{8,24},{9,... | collective-permute-start | bytes 405512 | tf_op jit(solution)/shard_map/ppermute | solution.py:497
  18.9 12.2 %collective-permute-start.5 = (bf16[528,128]{1,0:T(8,128)(2,1)S(1)}, bf16[528,128]{1,0:T(8,128)(2,1)S(1)}, u32[]{:S(2)}, u32[]{:S(2)}) collective-permute-start(bf16[528,128]{1,0:T(8,128)(2,1)S(1)} %get-tuple-element.29), channel_id=1, source_target_pairs={{0,0},{1,5},{2,2},{3,7},{4,4},{5,1},{6,6},{7,3},{8,8},{9,13},{10,1... | collective-permute-start | bytes 405512 | tf_op jit(solution)/shard_map/ppermute | solution.py:501
  19.6 11.5 %copy-start.4 = (f32[2048]{0:T(1024)S(1)}, f32[2048]{0:T(1024)}, u32[]{:S(2)}) copy-start(f32[2048]{0:T(1024)} %param.24) | copy-start | bytes 24580
  19.6 11.5 %collective-permute-start.6 = (bf16[528,128]{1,0:T(8,128)(2,1)S(1)}, bf16[528,128]{1,0:T(8,128)(2,1)S(1)}, u32[]{:S(2)}, u32[]{:S(2)}) collective-permute-start(bf16[528,128]{1,0:T(8,128)(2,1)S(1)} %get-tuple-element.30), channel_id=1, source_target_pairs={{0,8},{1,13},{2,10},{3,15},{4,12},{5,9},{6,14},{7,11},{8,0},{9,5},... | collective-permute-start | bytes 405512 | tf_op jit(solution)/shard_map/ppermute | solution.py:501
  20.5 16.7 %copy-start.5 = (s32[8]{0:T(128)S(1)}, s32[8]{0:T(128)}, u32[]{:S(2)}) copy-start(s32[8]{0:T(128)} %order_ref.3) | copy-start | bytes 100
  20.5 18.0 %copy-start.2 = (bf16[1,768,512]{2,1,0:T(8,128)(2,1)S(1)}, bf16[1,768,512]{2,1,0:T(8,128)(2,1)}, u32[]{:S(2)}) copy-start(bf16[1,768,512]{2,1,0:T(8,128)(2,1)} %param.29) | copy-start | bytes 2359300
  32.5 4.7 %collective-permute-start.10 = (bf16[128,384]{1,0:T(8,128)(2,1)S(1)}, bf16[128,384]{1,0:T(8,128)(2,1)S(1)}, u32[]{:S(2)}, u32[]{:S(2)}) collective-permute-start(bf16[128,384]{1,0:T(8,128)(2,1)S(1)} %get-tuple-element.34.act_ref), channel_id=1, source_target_pairs={{0,2},{1,3},{2,0},{3,1},{4,6},{5,7},{6,4},{7,5},{8,10},{9,11},{10,... | collective-permute-start | bytes 294920 | tf_op jit(solution)/shard_map/ppermute | solution.py:392
  34.1 3.1 %collective-permute-start.9 = (bf16[4,144,128]{2,1,0:T(8,128)(2,1)S(1)}, bf16[4,144,128]{2,1,0:T(8,128)(2,1)S(1)}, u32[]{:S(2)}, u32[]{:S(2)}) collective-permute-start(bf16[4,144,128]{2,1,0:T(8,128)(2,1)S(1)} %get-tuple-element.33), channel_id=1, source_target_pairs={{0,1},{1,0},{2,3},{3,2},{4,5},{5,4},{6,7},{7,6},{8,9},{9,8},{10,11... | collective-permute-start | bytes 442376 | tf_op jit(solution)/shard_map/ppermute | solution.py:389
  34.1 3.9 %collective-permute-start.11 = (bf16[128,384]{1,0:T(8,128)(2,1)S(1)}, bf16[128,384]{1,0:T(8,128)(2,1)S(1)}, u32[]{:S(2)}, u32[]{:S(2)}) collective-permute-start(bf16[128,384]{1,0:T(8,128)(2,1)S(1)} %get-tuple-element.34.act_ref), channel_id=1, source_target_pairs={{0,1},{1,0},{2,3},{3,2},{4,5},{5,4},{6,7},{7,6},{8,9},{9,8},{10,11... | collective-permute-start | bytes 294920 | tf_op jit(solution)/shard_map/ppermute | solution.py:389
  37.2 1.3 %collective-permute-start.12 = (bf16[128,384]{1,0:T(8,128)(2,1)S(1)}, bf16[128,384]{1,0:T(8,128)(2,1)S(1)}, u32[]{:S(2)}, u32[]{:S(2)}) collective-permute-start(bf16[128,384]{1,0:T(8,128)(2,1)S(1)} %collective-permute-done.10.act_half_ref), channel_id=1, source_target_pairs={{0,1},{1,0},{2,3},{3,2},{4,5},{5,4},{6,7},{7,6},{8,9},{9,8},{10,11... | collective-permute-start | bytes 294920 | tf_op jit(solution)/shard_map/ppermute | solution.py:389

commit v5 on v4

--- a/solution.py
+++ b/solution.py
@@ -231,25 +231,36 @@
     out_ref[...] = (sum_ref[...] + came_ref[...].astype(F32)).astype(BF16)
 
 
-def gather_kernel(first, count, after_ref, part_ref, other_ref, pick_ref, tags_ref, *send_refs):
+def gather_kernel(first, split, after_ref, part_ref, other_ref, pick_ref, tags_ref, *send_refs):
     del after_ref
-    core = lax.axis_index("tp") % 2
+    tp = lax.axis_index("tp")
+    mine, core = tp // 2, tp % 2
+    count = len(split)
     rows_each = pick_ref.shape[0] // tags_ref.shape[0]
     pick = pick_ref[first * rows_each : (first + count) * rows_each, :]
     width = part_ref.shape[1] // 2
     blocks = width // LANES
+    tall = blocks * rows_each
+
+    def put(ref, rows, base):
+        for j in range(blocks):
+            start = pl.multiple_of(base + j * rows_each, rows_each)
+            ref[pl.ds(start, rows_each), :] = rows[:, j * LANES : (j + 1) * LANES]
+
     for source, parity in ((part_ref, core), (other_ref, 1 - core)):
-        for half in range(2):
+        whole = [k for k in range(count) if not split[k]]
+        for half in range(2) if whole else ():
             rows = dot(pick, source[:, half * width : (half + 1) * width]).astype(BF16)
-            base = (2 * half + parity) * (blocks * rows_each)
-            for k in range(count):
-                for j in range(blocks):
-                    start = pl.multiple_of(base + j * rows_each, rows_each)
-                    send_refs[k][pl.ds(start, rows_each), :] = rows[
-                        k * rows_each : (k + 1) * rows_each, j * LANES : (j + 1) * LANES
-                    ]
+            for k in whole:
+                piece = rows[k * rows_each : (k + 1) * rows_each]
+                put(send_refs[k], piece, (2 * half + parity) * tall)
+        for k in range(count):
+            if split[k]:
+                columns = pl.ds(pl.multiple_of(mine * width, width), width)
+                piece = pick[k * rows_each : (k + 1) * rows_each]
+                put(send_refs[k], dot(piece, source[:, columns]).astype(BF16), parity * tall)
     for k in range(count):
-        send_refs[k][4 * blocks * rows_each :, :] = tags_ref[first + k]
+        send_refs[k][send_refs[k].shape[0] - TAGS :, :] = tags_ref[first + k]
 
 
 def stage_kernel(after_ref, *refs):
@@ -265,17 +276,28 @@
         copy.wait()
 
 
-def hidden_units_kernel(peers, rows_each, gain_ref, weight_ref, *refs):
+def hidden_units_kernel(split, rows_each, gain_ref, weight_ref, *refs):
+    peers = len(split)
     got = refs[:peers]
-    act_ref, side_ref = refs[peers:]
+    halves = list(refs[peers:-2])
+    act_ref, side_ref = refs[-2:]
     tp = lax.axis_index("tp")
-    core = tp % 2
+    half, core = tp // 2, tp % 2
     blocks = gain_ref.shape[0]
-    per_device = blocks // 4
+    tall = blocks // 4 * rows_each
+
+    columns = []
+    for ref, parted in zip(got, split):
+        if parted:
+            own, came = ref[: 2 * tall, :], halves.pop(0)[: 2 * tall, :]
+            low = jnp.where(half == 0, own, came)
+            high = jnp.where(half == 0, came, own)
+            rows = jnp.concatenate([low, high], axis=0)
+        else:
+            rows = ref[: 4 * tall, :]
+        columns.append([rows[j * rows_each : (j + 1) * rows_each] for j in range(blocks)])
     parts = [
-        jnp.concatenate(
-            [ref[j * rows_each : (j + 1) * rows_each, :] for ref in got], axis=0
-        ).astype(F32)
+        jnp.concatenate([column[j] for column in columns], axis=0).astype(F32)
         for j in range(blocks)
     ]
     squares = parts[0] * parts[0]
@@ -296,15 +318,15 @@
     low = jnp.where(core == 0, own, pair)
     high = jnp.where(core == 0, pair, own)
     act_ref[...] = jnp.concatenate([low, high], axis=1).astype(BF16)
-    tall = per_device * rows_each
-    start = pl.multiple_of((tp + 1 - 2 * core) * tall, tall)
     for k in range(peers):
+        place = 1 - core + (0 if split[k] else 2 * half)
+        start = pl.multiple_of(place * tall, tall)
         side_ref[k, :tall, :] = got[k][pl.ds(start, tall), :]
-        side_ref[k, tall:, :] = got[k][blocks * rows_each :, :]
+        side_ref[k, tall:, :] = got[k][got[k].shape[0] - TAGS :, :]
 
 
 def down_kernel(
-    peers,
+    split,
     rows_each,
     after_ref,
     order_ref,
@@ -317,6 +339,7 @@
     *refs,
 ):
     del after_ref
+    peers = len(split)
     got = refs[:peers]
     out_ref = refs[peers]
     tp = lax.axis_index("tp")
@@ -330,7 +353,6 @@
     diagonal = lax.broadcasted_iota(jnp.int32, (rows_each, LANES), 0) == lax.broadcasted_iota(
         jnp.int32, (rows_each, LANES), 1
     )
-    start = pl.multiple_of(tp * tall, tall)
     for group in range(2):
         near, far = ((act_ref, act_half_ref), (act_core_ref, act_both_ref))[group]
         result = dot(near[...], here) + dot(far[...], there)
@@ -338,8 +360,9 @@
             request = jnp.bitwise_xor(me, 2 * k + (core if group == 0 else 1 - core))
             place = order_ref[request]
             if group == 0:
+                start = pl.multiple_of((core if split[k] else tp) * tall, tall)
                 rows = got[k][pl.ds(start, tall), :]
-                tags = got[k][4 * tall :, :]
+                tags = got[k][got[k].shape[0] - TAGS :, :]
             else:
                 rows = side_ref[k, :tall, :]
                 tags = side_ref[k, tall:, :]
@@ -473,12 +496,18 @@
     )(part, route_experts.T, route_weights.T)
     other = swap_core(part)
 
-    def gather(first, count, after):
+    near = peers // 2
+    split = [k >= near and (k - near) % 2 == 1 for k in range(peers)]
+
+    def gather(first, last, after):
         return pl.pallas_call(
-            functools.partial(gather_kernel, first, count),
-            out_shape=[shape((tp_count * tall + TAGS, LANES), BF16)] * count,
+            functools.partial(gather_kernel, first, split[first:last]),
+            out_shape=[
+                shape(((2 if split[k] else 4) * tall + TAGS, LANES), BF16)
+                for k in range(first, last)
+            ],
             in_specs=[pl.BlockSpec(memory_space=pl.ANY)] + [vmem()] * 4,
-            out_specs=[vmem()] * count,
+            out_specs=[vmem()] * (last - first),
             compiler_params=params(8),
             name="gather_rows",
         )(after, part, other, pick, tags)
@@ -490,8 +519,7 @@
             for t in range(tp_count)
         ]
 
-    near = peers // 2
-    far_send = list(gather(near, peers - near, tags))
+    far_send = list(gather(near, peers, tags))
     gate, up, far_send[-1] = lax.optimization_barrier((gate, up, far_send[-1]))
     far = [
         lax.ppermute(x, ("ep", "tp"), route(near + k)) for k, x in enumerate(far_send)
@@ -499,6 +527,7 @@
     gate_pair, up_pair = swap_core(gate), swap_core(up)
     near_send = gather(0, near, gate_pair)
     got = [lax.ppermute(x, ("ep", "tp"), route(k)) for k, x in enumerate(near_send)] + far
+    halves = [swap_half(got[k]) for k in range(peers) if split[k]]
 
     weights = pl.pallas_call(
         stage_kernel,
@@ -514,16 +543,16 @@
     )(tags, gate, up, gate_pair, up_pair)
 
     act, side = pl.pallas_call(
-        functools.partial(hidden_units_kernel, peers, rows_each),
+        functools.partial(hidden_units_kernel, split, rows_each),
         out_shape=(
             shape((peers * rows_each, units), BF16),
             shape((peers, tall + TAGS, LANES), BF16),
         ),
-        in_specs=[vmem()] * (2 + peers),
+        in_specs=[vmem()] * (2 + peers + len(halves)),
         out_specs=(vmem(), vmem()),
         compiler_params=params(16),
         name="hidden_units",
-    )(norm_gain.reshape(-1, LANES), weights, *got)
+    )(norm_gain.reshape(-1, LANES), weights, *got, *halves)
 
     act_half = swap_half(act)
     act_core = swap_core(act)
@@ -540,7 +569,7 @@
         name="select",
     )(request_order, side, *got)
     result = pl.pallas_call(
-        functools.partial(down_kernel, peers, rows_each),
+        functools.partial(down_kernel, split, rows_each),
         out_shape=shape((ep_count, tall, LANES), BF16),
         in_specs=[pl.BlockSpec(memory_space=pl.ANY), pl.BlockSpec(memory_space=pltpu.SMEM)]
         + [vmem()] * (6 + peers),

time: 54.2 us -> 52.3 us (0.965)
  waiting for transfers between devices: 18.8 us -> 14.3 us
  starting transfers between devices: 11.3 us -> 13.8 us
    ppermute x2, waiting for transfers between devices: 10.6 us -> 6.05 us  [shards(): lax.ppermute(x, ('ep', 'tp'), route(near + k))]
    ppermute x2 -> x3, starting transfers between devices: 4.47 us -> 6.33 us  [swap_half(): return lax.ppermute(x, 'tp', [(i, i ^ 2) for i in range(tp_count)])]
    ppermute x7, starting transfers between devices: 1.68 us -> 2.34 us  [swap_core(): return lax.ppermute(x, 'tp', [(i, i ^ 1) for i in range(tp_count)])]
    ppermute x2 -> x3, waiting for transfers between devices: 6.43 us -> 6.61 us  [swap_half(): return lax.ppermute(x, 'tp', [(i, i ^ 2) for i in range(tp_count)])]
  transfers between devices with their start and end apart: 13 -> 14, of which waited for: 7 -> 7; matrix products, arithmetic and copies ran while one was open for 0% -> 0% of each run, Pallas kernels for 3% -> 3%
where the time goes in v5:
time: 52.3 us; the launch traced here: 52.1 us
  waiting for transfers between devices  14.3 us (27%)
  starting transfers between devices  13.8 us (26%)
  blocking collectives  13.7 us (26%)
  Pallas kernels  8.31 us (16%)
  local copies, waits for them, and re-layouts  0.98 us (2%)
  between operations  0.93 us (2%)
    all_to_all x1, blocking collectives, shards(): came = lax.all_to_all(result, 'ep', split_axis=0, concat_axis=0, tiled=True)  13.7 us
    ppermute x3, waiting for transfers between devices, swap_half(): return lax.ppermute(x, 'tp', [(i, i ^ 2) for i in range(tp_count)])  6.61 us
    ppermute x3, starting transfers between devices, swap_half(): return lax.ppermute(x, 'tp', [(i, i ^ 2) for i in range(tp_count)])  6.33 us
    ppermute x2, waiting for transfers between devices, shards(): lax.ppermute(x, ('ep', 'tp'), route(near + k))  6.05 us
    ppermute x2, starting transfers between devices, shards(): lax.ppermute(x, ('ep', 'tp'), route(near + k))  3.85 us
    pallas_call x1, Pallas kernels, shards(): pl.pallas_call(functools.partial(attend_kernel, kv_local), out_shape=(sha...  3.34 us
    ppermute x7, starting transfers between devices, swap_core(): return lax.ppermute(x, 'tp', [(i, i ^ 1) for i in range(tp_count)])  2.34 us
    ppermute x7, waiting for transfers between devices, swap_core(): return lax.ppermute(x, 'tp', [(i, i ^ 1) for i in range(tp_count)])  1.65 us
  transfers between devices with their start and end apart: 14, of which 7 were waited for; matrix products, arithmetic and copies ran while one was open for 0% of the time, Pallas kernels for 3%

profile of v5, /device:TPU:0, one launch (start us, length us, event | category | flops | bytes accessed | tf_op | source)
XLA Modules:
  0.0 52.1 jit_solution(18033749629451022610)
XLA Ops:
  0.0 0.0 copy-start.6
  0.0 0.0 copy-start.7
  0.0 0.0 copy-start
  0.0 0.0 copy-start.1
  0.8 3.3 %attend.1 = (f32[64,1024]{1,0:T(8,128)}, bf16[64,1024]{1,0:T(8,128)(2,1)}) custom-call(s32[1,1]{1,0:T(1,128)} %bitcast.13.length_hbm, bf16[64,512]{1,0:T(8,128)(2,1)} %query_hbm.1, bf16[64,128]{1,0:T(8,128)(2,1)} %new_key_hbm.1, bf16[64,128]{1,0:T(8,128)(2,1)} %new_value_hbm.1, bf16[512,128]{1,0:T(8,128)(2,1)} %bitcast.22, bf16[512,128]{1,0:T(8,128)(2,1)} %bitcast.23, ...), custom_call_target="tpu_custom_call" | custom-call | tf_op jit(solution)/shard_map/attend/pallas_call | solution.py:428
  4.1 0.5 collective-permute-start
  4.6 0.0 copy-start.3
  4.6 0.9 %copy-done.3 = f32[64,1024]{1,0:T(8,128)S(1)} copy-done((f32[64,1024]{1,0:T(8,128)S(1)}, f32[64,1024]{1,0:T(8,128)}, u32[]{:S(2)}) %copy-start.3) | copy-done | bytes 262168
  5.6 0.2 collective-permute-done.came_ref
  5.9 2.9 %collective-permute-start.1 = (bf16[64,1024]{1,0:T(8,128)(2,1)S(1)}, bf16[64,1024]{1,0:T(8,128)(2,1)S(1)}, u32[]{:S(2)}, u32[]{:S(2)}) collective-permute-start(bf16[64,1024]{1,0:T(8,128)(2,1)S(1)} %get-tuple-element.23), channel_id=1, source_target_pairs={{0,2},{1,3},{2,0},{3,1},{4,6},{5,7},{6,4},{7,5},{8,10},{9,11},{10,... | collective-permute-start | bytes 393224 | tf_op jit(solution)/shard_map/ppermute | solution.py:415
  8.8 3.8 %collective-permute-done.1.came_ref = bf16[64,1024]{1,0:T(8,128)(2,1)S(1)} collective-permute-done((bf16[64,1024]{1,0:T(8,128)(2,1)S(1)}, bf16[64,1024]{1,0:T(8,128)(2,1)S(1)}, u32[]{:S(2)}, u32[]{:S(2)}) %collective-permute-start.1) | collective-permute-done | bytes 131104 | tf_op jit(solution)/shard_map/ppermute | solution.py:415
  12.6 0.1 collective-permute-start.2
  12.7 0.0 copy-done.6
  12.7 0.0 copy-done.7
  12.7 0.3 route.1
  13.0 1.1 %collective-permute-done.2.other_ref = bf16[64,1024]{1,0:T(8,128)(2,1)S(1)} collective-permute-done((bf16[64,1024]{1,0:T(8,128)(2,1)S(1)}, bf16[64,1024]{1,0:T(8,128)(2,1)S(1)}, u32[]{:S(2)}, u32[]{:S(2)}) %collective-permute-start.2) | collective-permute-done | bytes 131104 | tf_op jit(solution)/shard_map/ppermute | solution.py:412
  14.0 0.2 gather_rows.2
  14.3 0.0 copy-done
  14.3 0.2 collective-permute-start.3
  14.5 0.0 copy-done.1
  14.5 0.4 collective-permute-start.4
  14.9 3.8 %collective-permute-start.8 = (bf16[272,128]{1,0:T(8,128)(2,1)S(1)}, bf16[272,128]{1,0:T(8,128)(2,1)S(1)}, u32[]{:S(2)}, u32[]{:S(2)}) collective-permute-start(bf16[272,128]{1,0:T(8,128)(2,1)S(1)} %get-tuple-element.32), channel_id=1, source_target_pairs={{0,24},{1,29},{2,26},{3,31},{4,28},{5,25},{6,30},{7,27},{8,16},{9,... | collective-permute-start | bytes 208904 | tf_op jit(solution)/shard_map/ppermute | solution.py:525
  18.7 0.0 collective-permute-start.7
  18.7 0.0 collective-permute-done.3.refs_2_.after_ref
  18.7 0.2 gather_rows.3
  19.0 0.7 %collective-permute-start.5 = (bf16[528,128]{1,0:T(8,128)(2,1)S(1)}, bf16[528,128]{1,0:T(8,128)(2,1)S(1)}, u32[]{:S(2)}, u32[]{:S(2)}) collective-permute-start(bf16[528,128]{1,0:T(8,128)(2,1)S(1)} %get-tuple-element.29), channel_id=1, source_target_pairs={{0,0},{1,5},{2,2},{3,7},{4,4},{5,1},{6,6},{7,3},{8,8},{9,13},{10,1... | collective-permute-start | bytes 405512 | tf_op jit(solution)/shard_map/ppermute | solution.py:529
  19.6 0.0 copy-start.4
  19.6 0.6 %collective-permute-start.6 = (bf16[528,128]{1,0:T(8,128)(2,1)S(1)}, bf16[528,128]{1,0:T(8,128)(2,1)S(1)}, u32[]{:S(2)}, u32[]{:S(2)}) collective-permute-start(bf16[528,128]{1,0:T(8,128)(2,1)S(1)} %get-tuple-element.30), channel_id=1, source_target_pairs={{0,8},{1,13},{2,10},{3,15},{4,12},{5,9},{6,14},{7,11},{8,0},{9,5},... | collective-permute-start | bytes 405512 | tf_op jit(solution)/shard_map/ppermute | solution.py:529
  20.3 1.3 %collective-permute-done.8.refs_3_ = bf16[272,128]{1,0:T(8,128)(2,1)S(1)} collective-permute-done((bf16[272,128]{1,0:T(8,128)(2,1)S(1)}, bf16[272,128]{1,0:T(8,128)(2,1)S(1)}, u32[]{:S(2)}, u32[]{:S(2)}) %collective-permute-start.8) | collective-permute-done | bytes 69664 | tf_op jit(solution)/shard_map/ppermute | solution.py:525
  21.6 1.8 %collective-permute-start.9 = (bf16[272,128]{1,0:T(8,128)(2,1)S(1)}, bf16[272,128]{1,0:T(8,128)(2,1)S(1)}, u32[]{:S(2)}, u32[]{:S(2)}) collective-permute-start(bf16[272,128]{1,0:T(8,128)(2,1)S(1)} %collective-permute-done.8.refs_3_), channel_id=1, source_target_pairs={{0,2},{1,3},{2,0},{3,1},{4,6},{5,7},{6,4},{7,5},{8,10},{9,11},{10,... | collective-permute-start | bytes 208904 | tf_op jit(solution)/shard_map/ppermute | solution.py:415
  23.4 0.0 collective-permute-done.4.refs_3_
  23.4 0.3 stage.1.weight_ref
  23.7 0.0 copy-start.5
  23.7 0.0 copy-start.2
  23.7 4.7 %collective-permute-done.7.refs_2_ = bf16[528,128]{1,0:T(8,128)(2,1)S(1)} collective-permute-done((bf16[528,128]{1,0:T(8,128)(2,1)S(1)}, bf16[528,128]{1,0:T(8,128)(2,1)S(1)}, u32[]{:S(2)}, u32[]{:S(2)}) %collective-permute-start.7) | collective-permute-done | bytes 135200 | tf_op jit(solution)/shard_map/ppermute | solution.py:525
  28.4 0.0 collective-permute-done.9.refs_4_
  28.4 0.0 collective-permute-done.5.refs_0_
  28.4 0.0 collective-permute-done.6.refs_1_
  28.5 0.0 copy-done.4
  28.5 1.4 %hidden_units.1 = (bf16[128,384]{1,0:T(8,128)(2,1)S(1)}, bf16[4,144,128]{2,1,0:T(8,128)(2,1)S(1)}) custom-call(f32[16,128]{1,0:T(8,128)S(1)} %bitcast.19, bf16[4,192,2048]{2,1,0:T(8,128)(2,1)S(1)} %stage.1.weight_ref, bf16[528,128]{1,0:T(8,128)(2,1)S(1)} %collective-permute-done.5.refs_0_, bf16[528,128]{1,0:T(8,128)(2,1)S(1)} %collective-permute-done.6.refs_1_, ...), custom_call_target="tpu_custom_call" | custom-call | tf_op jit(solution)/shard_map/hidden_units/pallas_call | solution.py:545
  29.8 1.6 %collective-permute-start.11 = (bf16[128,384]{1,0:T(8,128)(2,1)S(1)}, bf16[128,384]{1,0:T(8,128)(2,1)S(1)}, u32[]{:S(2)}, u32[]{:S(2)}) collective-permute-start(bf16[128,384]{1,0:T(8,128)(2,1)S(1)} %get-tuple-element.34.act_ref), channel_id=1, source_target_pairs={{0,2},{1,3},{2,0},{3,1},{4,6},{5,7},{6,4},{7,5},{8,10},{9,11},{10,... | collective-permute-start | bytes 294920 | tf_op jit(solution)/shard_map/ppermute | solution.py:415
  31.4 1.0 %collective-permute-start.10 = (bf16[4,144,128]{2,1,0:T(8,128)(2,1)S(1)}, bf16[4,144,128]{2,1,0:T(8,128)(2,1)S(1)}, u32[]{:S(2)}, u32[]{:S(2)}) collective-permute-start(bf16[4,144,128]{2,1,0:T(8,128)(2,1)S(1)} %get-tuple-element.33), channel_id=1, source_target_pairs={{0,1},{1,0},{2,3},{3,2},{4,5},{5,4},{6,7},{7,6},{8,9},{9,8},{10,11... | collective-permute-start | bytes 442376 | tf_op jit(solution)/shard_map/ppermute | solution.py:412
  32.4 0.0 collective-permute-start.12
  32.4 2.8 %collective-permute-done.11.act_half_ref = bf16[128,384]{1,0:T(8,128)(2,1)S(1)} collective-permute-done((bf16[128,384]{1,0:T(8,128)(2,1)S(1)}, bf16[128,384]{1,0:T(8,128)(2,1)S(1)}, u32[]{:S(2)}, u32[]{:S(2)}) %collective-permute-start.11) | collective-permute-done | bytes 98336 | tf_op jit(solution)/shard_map/ppermute | solution.py:415
  35.2 0.1 collective-permute-start.13
  35.4 0.0 collective-permute-done.10.side_ref
  35.4 0.0 copy-done.5
  35.4 0.8 %select.1.after_ref.chosen_ref = bf16[64,256]{1,0:T(8,128)(2,1)S(1)} custom-call(s32[8]{0:T(128)S(1)} %copy-done.5, bf16[4,144,128]{2,1,0:T(8,128)(2,1)S(1)} %collective-permute-done.10.side_ref, bf16[528,128]{1,0:T(8,128)(2,1)S(1)} %collective-permute-done.5.refs_0_, bf16[528,128]{1,0:T(8,128)(2,1)S(1)} %collective-permute-done.6.refs_1_, ...), custom_call_target="tpu_custom_call" | custom-call | bytes 1048576 | tf_op jit(solution)/shard_map/select/pallas_call | solution.py:562
  36.2 0.0 collective-permute-done.12.act_core_ref
  36.2 0.4 collective-permute-done.13.act_both_ref
  36.5 0.0 copy-done.2
  36.5 1.0 %down.1 = bf16[8,128,128]{2,1,0:T(8,128)(2,1)S(1)} custom-call(bf16[64,256]{1,0:T(8,128)(2,1)S(1)} %select.1.after_ref.chosen_ref, s32[8]{0:T(128)S(1)} %copy-done.5, bf16[128,384]{1,0:T(8,128)(2,1)S(1)} %get-tuple-element.34.act_ref, bf16[128,384]{1,0:T(8,128)(2,1)S(1)} %collective-permute-done.11.act_half_ref, ...), custom_call_target="tpu_custom_call" | custom-call | tf_op jit(solution)/shard_map/down/pallas_call | solution.py:571
  37.6 13.7 %all_to_all.5.came_ref = bf16[8,128,128]{2,1,0:T(8,128)(2,1)S(1)} all-to-all(bf16[8,128,128]{2,1,0:T(8,128)(2,1)S(1)} %down.1), channel_id=1, replica_groups=mesh['ep'=8,'tp'=4] {'ep'}, dimensions={0} | all-to-all | bytes 524288 | tf_op jit(solution)/shard_map/all_to_all | solution.py:581
  51.3 0.8 %combine.1 = bf16[64,512]{1,0:T(8,128)(2,1)} custom-call(bf16[64,256]{1,0:T(8,128)(2,1)S(1)} %select.1.after_ref.chosen_ref, bf16[8,128,128]{2,1,0:T(8,128)(2,1)S(1)} %all_to_all.5.came_ref), custom_call_target="tpu_custom_call" | custom-call | tf_op jit(solution)/shard_map/combine/pallas_call | solution.py:582
  (3 shorter events, 0.1 us)
Async XLA Ops:
  0.0 12.7 %copy-start.6 = (s32[64,2]{0,1:T(2,128)S(1)}, s32[64,2]{0,1:T(2,128)}, u32[]{:S(2)}) copy-start(s32[64,2]{0,1:T(2,128)} %param.25) | copy-start | bytes 1540
  0.0 12.7 %copy-start.7 = (f32[64,2]{0,1:T(2,128)S(1)}, f32[64,2]{0,1:T(2,128)}, u32[]{:S(2)}) copy-start(f32[64,2]{0,1:T(2,128)} %param.26) | copy-start | bytes 1540
  0.0 14.3 %copy-start = (bf16[1,2048,192]{1,2,0:T(8,128)(2,1)S(1)}, bf16[1,2048,192]{1,2,0:T(8,128)(2,1)}, u32[]{:S(2)}) copy-start(bf16[1,2048,192]{1,2,0:T(8,128)(2,1)} %param.27) | copy-start | bytes 2359300
  0.0 14.5 %copy-start.1 = (bf16[1,2048,192]{1,2,0:T(8,128)(2,1)S(1)}, bf16[1,2048,192]{1,2,0:T(8,128)(2,1)}, u32[]{:S(2)}) copy-start(bf16[1,2048,192]{1,2,0:T(8,128)(2,1)} %param.28) | copy-start | bytes 2359300
  4.1 1.7 %collective-permute-start = (bf16[64,1024]{1,0:T(8,128)(2,1)}, bf16[64,1024]{1,0:T(8,128)(2,1)S(1)}, u32[]{:S(2)}, u32[]{:S(2)}) collective-permute-start(bf16[64,1024]{1,0:T(8,128)(2,1)} %get-tuple-element.21), channel_id=1, source_target_pairs={{0,1},{1,0},{2,3},{3,2},{4,5},{5,4},{6,7},{7,6},{8,9},{9,8},{10,11... | collective-permute-start | bytes 393224 | tf_op jit(solution)/shard_map/ppermute | solution.py:412
  4.6 0.9 %copy-start.3 = (f32[64,1024]{1,0:T(8,128)S(1)}, f32[64,1024]{1,0:T(8,128)}, u32[]{:S(2)}) copy-start(f32[64,1024]{1,0:T(8,128)} %get-tuple-element.20.from_ref) | copy-start | bytes 786436
  5.9 6.7 %collective-permute-start.1 = (bf16[64,1024]{1,0:T(8,128)(2,1)S(1)}, bf16[64,1024]{1,0:T(8,128)(2,1)S(1)}, u32[]{:S(2)}, u32[]{:S(2)}) collective-permute-start(bf16[64,1024]{1,0:T(8,128)(2,1)S(1)} %get-tuple-element.23), channel_id=1, source_target_pairs={{0,2},{1,3},{2,0},{3,1},{4,6},{5,7},{6,4},{7,5},{8,10},{9,11},{10,... | collective-permute-start | bytes 393224 | tf_op jit(solution)/shard_map/ppermute | solution.py:415
  12.6 1.4 %collective-permute-start.2 = (bf16[64,1024]{1,0:T(8,128)(2,1)S(1)}, bf16[64,1024]{1,0:T(8,128)(2,1)S(1)}, u32[]{:S(2)}, u32[]{:S(2)}) collective-permute-start(bf16[64,1024]{1,0:T(8,128)(2,1)S(1)} %add_half.1.after_ref.part_ref), channel_id=1, source_target_pairs={{0,1},{1,0},{2,3},{3,2},{4,5},{5,4},{6,7},{7,6},{8,9},{9,8},{10,11... | collective-permute-start | bytes 393224 | tf_op jit(solution)/shard_map/ppermute | solution.py:412
  14.3 4.4 %collective-permute-start.3 = (bf16[192,2048]{1,0:T(8,128)(2,1)S(1)}, bf16[192,2048]{1,0:T(8,128)(2,1)S(1)}, u32[]{:S(2)}, u32[]{:S(2)}) collective-permute-start(bf16[192,2048]{1,0:T(8,128)(2,1)S(1)} %bitcast.14), channel_id=1, source_target_pairs={{0,1},{1,0},{2,3},{3,2},{4,5},{5,4},{6,7},{7,6},{8,9},{9,8},{10,11... | collective-permute-start | bytes 2359304 | tf_op jit(solution)/shard_map/ppermute | solution.py:412
  14.5 8.9 %collective-permute-start.4 = (bf16[192,2048]{1,0:T(8,128)(2,1)S(1)}, bf16[192,2048]{1,0:T(8,128)(2,1)S(1)}, u32[]{:S(2)}, u32[]{:S(2)}) collective-permute-start(bf16[192,2048]{1,0:T(8,128)(2,1)S(1)} %bitcast.16), channel_id=1, source_target_pairs={{0,1},{1,0},{2,3},{3,2},{4,5},{5,4},{6,7},{7,6},{8,9},{9,8},{10,11... | collective-permute-start | bytes 2359304 | tf_op jit(solution)/shard_map/ppermute | solution.py:412
  14.9 6.7 %collective-permute-start.8 = (bf16[272,128]{1,0:T(8,128)(2,1)S(1)}, bf16[272,128]{1,0:T(8,128)(2,1)S(1)}, u32[]{:S(2)}, u32[]{:S(2)}) collective-permute-start(bf16[272,128]{1,0:T(8,128)(2,1)S(1)} %get-tuple-element.32), channel_id=1, source_target_pairs={{0,24},{1,29},{2,26},{3,31},{4,28},{5,25},{6,30},{7,27},{8,16},{9,... | collective-permute-start | bytes 208904 | tf_op jit(solution)/shard_map/ppermute | solution.py:525
  18.7 9.7 %collective-permute-start.7 = (bf16[528,128]{1,0:T(8,128)(2,1)S(1)}, bf16[528,128]{1,0:T(8,128)(2,1)S(1)}, u32[]{:S(2)}, u32[]{:S(2)}) collective-permute-start(bf16[528,128]{1,0:T(8,128)(2,1)S(1)} %get-tuple-element.31), channel_id=1, source_target_pairs={{0,16},{1,21},{2,18},{3,23},{4,20},{5,17},{6,22},{7,19},{8,24},{9,... | collective-permute-start | bytes 405512 | tf_op jit(solution)/shard_map/ppermute | solution.py:525
  19.0 9.5 %collective-permute-start.5 = (bf16[528,128]{1,0:T(8,128)(2,1)S(1)}, bf16[528,128]{1,0:T(8,128)(2,1)S(1)}, u32[]{:S(2)}, u32[]{:S(2)}) collective-permute-start(bf16[528,128]{1,0:T(8,128)(2,1)S(1)} %get-tuple-element.29), channel_id=1, source_target_pairs={{0,0},{1,5},{2,2},{3,7},{4,4},{5,1},{6,6},{7,3},{8,8},{9,13},{10,1... | collective-permute-start | bytes 405512 | tf_op jit(solution)/shard_map/ppermute | solution.py:529
  19.6 8.8 %copy-start.4 = (f32[2048]{0:T(1024)S(1)}, f32[2048]{0:T(1024)}, u32[]{:S(2)}) copy-start(f32[2048]{0:T(1024)} %param.24) | copy-start | bytes 24580
  19.6 8.8 %collective-permute-start.6 = (bf16[528,128]{1,0:T(8,128)(2,1)S(1)}, bf16[528,128]{1,0:T(8,128)(2,1)S(1)}, u32[]{:S(2)}, u32[]{:S(2)}) collective-permute-start(bf16[528,128]{1,0:T(8,128)(2,1)S(1)} %get-tuple-element.30), channel_id=1, source_target_pairs={{0,8},{1,13},{2,10},{3,15},{4,12},{5,9},{6,14},{7,11},{8,0},{9,5},... | collective-permute-start | bytes 405512 | tf_op jit(solution)/shard_map/ppermute | solution.py:529
  21.6 6.8 %collective-permute-start.9 = (bf16[272,128]{1,0:T(8,128)(2,1)S(1)}, bf16[272,128]{1,0:T(8,128)(2,1)S(1)}, u32[]{:S(2)}, u32[]{:S(2)}) collective-permute-start(bf16[272,128]{1,0:T(8,128)(2,1)S(1)} %collective-permute-done.8.refs_3_), channel_id=1, source_target_pairs={{0,2},{1,3},{2,0},{3,1},{4,6},{5,7},{6,4},{7,5},{8,10},{9,11},{10,... | collective-permute-start | bytes 208904 | tf_op jit(solution)/shard_map/ppermute | solution.py:415
  23.7 11.7 %copy-start.5 = (s32[8]{0:T(128)S(1)}, s32[8]{0:T(128)}, u32[]{:S(2)}) copy-start(s32[8]{0:T(128)} %order_ref.3) | copy-start | bytes 100
  23.7 12.8 %copy-start.2 = (bf16[1,768,512]{2,1,0:T(8,128)(2,1)S(1)}, bf16[1,768,512]{2,1,0:T(8,128)(2,1)}, u32[]{:S(2)}) copy-start(bf16[1,768,512]{2,1,0:T(8,128)(2,1)} %param.29) | copy-start | bytes 2359300
  29.8 5.4 %collective-permute-start.11 = (bf16[128,384]{1,0:T(8,128)(2,1)S(1)}, bf16[128,384]{1,0:T(8,128)(2,1)S(1)}, u32[]{:S(2)}, u32[]{:S(2)}) collective-permute-start(bf16[128,384]{1,0:T(8,128)(2,1)S(1)} %get-tuple-element.34.act_ref), channel_id=1, source_target_pairs={{0,2},{1,3},{2,0},{3,1},{4,6},{5,7},{6,4},{7,5},{8,10},{9,11},{10,... | collective-permute-start | bytes 294920 | tf_op jit(solution)/shard_map/ppermute | solution.py:415
  31.4 4.0 %collective-permute-start.10 = (bf16[4,144,128]{2,1,0:T(8,128)(2,1)S(1)}, bf16[4,144,128]{2,1,0:T(8,128)(2,1)S(1)}, u32[]{:S(2)}, u32[]{:S(2)}) collective-permute-start(bf16[4,144,128]{2,1,0:T(8,128)(2,1)S(1)} %get-tuple-element.33), channel_id=1, source_target_pairs={{0,1},{1,0},{2,3},{3,2},{4,5},{5,4},{6,7},{7,6},{8,9},{9,8},{10,11... | collective-permute-start | bytes 442376 | tf_op jit(solution)/shard_map/ppermute | solution.py:412
  32.4 3.7 %collective-permute-start.12 = (bf16[128,384]{1,0:T(8,128)(2,1)S(1)}, bf16[128,384]{1,0:T(8,128)(2,1)S(1)}, u32[]{:S(2)}, u32[]{:S(2)}) collective-permute-start(bf16[128,384]{1,0:T(8,128)(2,1)S(1)} %get-tuple-element.34.act_ref), channel_id=1, source_target_pairs={{0,1},{1,0},{2,3},{3,2},{4,5},{5,4},{6,7},{7,6},{8,9},{9,8},{10,11... | collective-permute-start | bytes 294920 | tf_op jit(solution)/shard_map/ppermute | solution.py:412
  35.2 1.3 %collective-permute-start.13 = (bf16[128,384]{1,0:T(8,128)(2,1)S(1)}, bf16[128,384]{1,0:T(8,128)(2,1)S(1)}, u32[]{:S(2)}, u32[]{:S(2)}) collective-permute-start(bf16[128,384]{1,0:T(8,128)(2,1)S(1)} %collective-permute-done.11.act_half_ref), channel_id=1, source_target_pairs={{0,1},{1,0},{2,3},{3,2},{4,5},{5,4},{6,7},{7,6},{8,9},{9,8},{10,11... | collective-permute-start | bytes 294920 | tf_op jit(solution)/shard_map/ppermute | solution.py:412

commit v6 on v5

--- a/solution.py
+++ b/solution.py
@@ -14,7 +14,6 @@
 LANES = 128
 TAGS = 16
 MIB = 1024 * 1024
-ATTEND_MIB = 61
 
 BF16 = jnp.bfloat16
 F32 = jnp.float32
@@ -40,59 +39,26 @@
     return lax.dot_general(a, b, (((1,), (1,)), ((), ())), preferred_element_type=F32)
 
 
+def begin_kernel(out_ref):
+    out_ref[...] = jnp.zeros(out_ref.shape, F32)
+
+
 def attend_kernel(
     kv_local,
-    length_hbm,
-    query_hbm,
-    new_key_hbm,
-    new_value_hbm,
-    key_hbm,
-    value_hbm,
-    residual_hbm,
-    weight_hbm,
-    keep_hbm,
-    give_hbm,
+    after_ref,
     length_ref,
     query_ref,
     new_key_ref,
     new_value_ref,
     key_ref,
     value_ref,
-    residual_ref,
-    weight_ref,
-    keep_ref,
-    give_ref,
-    sems,
+    context_ref,
 ):
-    tp = lax.axis_index("tp")
-    half, core = tp // 2, tp % 2
-    width = weight_ref.shape[2]
-    copies = []
-    for source, target in (
-        (query_hbm, query_ref),
-        (key_hbm, key_ref),
-        (new_key_hbm, new_key_ref),
-        (length_hbm, length_ref),
-        (value_hbm, value_ref),
-        (new_value_hbm, new_value_ref),
-        (residual_hbm, residual_ref),
-    ):
-        copies.append(pltpu.make_async_copy(source, target, sems.at[len(copies)]))
-    for i, block in enumerate((1 - core, 3 - core, core, core + 2)):
-        start = pl.multiple_of(block * width, width)
-        copies.append(
-            pltpu.make_async_copy(
-                weight_hbm.at[:, pl.ds(start, width)], weight_ref.at[i], sems.at[len(copies)]
-            )
-        )
-    for copy in copies:
-        copy.start()
+    del after_ref
     tokens = query_ref.shape[0]
     group = QHEADS // KVHEADS
+    length = length_ref[0]
     scale = 1.0 / math.sqrt(HEAD)
-    for copy in copies[:4]:
-        copy.wait()
-    length = length_ref[0, 0]
     pieces = []
     for g in range(kv_local):
         columns = slice(g * HEAD, (g + 1) * HEAD)
@@ -116,21 +82,22 @@
         old = jnp.exp(old - highest)
         new = jnp.exp(new - highest)
         totals = jnp.sum(old, axis=1, keepdims=True) + jnp.sum(new, axis=1, keepdims=True)
-        if g == 0:
-            for copy in copies[4:6]:
-                copy.wait()
         mixed = dot(old.astype(BF16), value_ref[:, columns]) + dot(
             new.astype(BF16), new_value_ref[:, columns]
         )
         mixed = (mixed / totals).astype(BF16)
         pieces += [mixed[i * tokens : (i + 1) * tokens] for i in range(group)]
-    context = jnp.concatenate(pieces, axis=1)
-    copies[6].wait()
-    given = pltpu.make_async_copy(give_ref, give_hbm, sems.at[len(copies)])
-    kept = pltpu.make_async_copy(keep_ref, keep_hbm, sems.at[len(copies) + 1])
-    for i in range(4):
-        copies[7 + i].wait()
-        part = dot(context, weight_ref[i])
+    context_ref[...] = jnp.concatenate(pieces, axis=1)
+
+
+def project_kernel(context_ref, residual_ref, weight_ref, keep_ref, give_ref):
+    tp = lax.axis_index("tp")
+    half, core = tp // 2, tp % 2
+    width = residual_ref.shape[1]
+    context = context_ref[...]
+    for i, block in enumerate((1 - core, 3 - core, core, core + 2)):
+        start = pl.multiple_of(block * width, width)
+        part = dot(context, weight_ref[:, pl.ds(start, width)])
         columns = slice((i % 2) * width, (i % 2 + 1) * width)
         if i < 2:
             give_ref[:, columns] = part.astype(BF16)
@@ -138,15 +105,6 @@
             keep_ref[:, columns] = part + jnp.where(
                 half == i - 2, residual_ref[...].astype(F32), 0.0
             )
-        if i == 1:
-            given.start()
-    kept.start()
-    given.wait()
-    kept.wait()
-
-
-def load_kernel(from_ref, to_ref):
-    to_ref[...] = from_ref[...]
 
 
 def earlier_tokens(tokens):
@@ -263,17 +221,23 @@
         send_refs[k][send_refs[k].shape[0] - TAGS :, :] = tags_ref[first + k]
 
 
-def stage_kernel(after_ref, *refs):
+def stage_kernel(after_ref, gate, up, gate_pair, up_pair, out_ref, held_ref, sems):
     del after_ref
-    count = len(refs) - 2
-    target, sems = refs[count:]
+    core = lax.axis_index("tp") % 2
     copies = [
-        pltpu.make_async_copy(refs[i], target.at[i], sems.at[i]) for i in range(count)
+        pltpu.make_async_copy(source, held_ref.at[place], sems.at[i])
+        for i, (source, place) in enumerate(
+            ((gate, core), (up, 2 + core), (gate_pair, 1 - core), (up_pair, 3 - core))
+        )
     ]
     for copy in copies:
         copy.start()
     for copy in copies:
         copy.wait()
+    units, width = held_ref.shape[1:]
+    for j in range(width // LANES):
+        columns = slice(j * LANES, (j + 1) * LANES)
+        out_ref[columns, :] = held_ref[:, :, columns].reshape(4 * units, LANES).T
 
 
 def hidden_units_kernel(split, rows_each, gain_ref, weight_ref, *refs):
@@ -309,15 +273,10 @@
         [(parts[j] * factor * gain_ref[j : j + 1, :]).astype(BF16) for j in range(blocks)], axis=1
     )
 
-    def units(gate, up):
-        value = dot_t(normed, weight_ref[gate])
-        return value / (1.0 + jnp.exp(-value)) * dot_t(normed, weight_ref[up])
-
-    own = units(0, 1)
-    pair = units(2, 3)
-    low = jnp.where(core == 0, own, pair)
-    high = jnp.where(core == 0, pair, own)
-    act_ref[...] = jnp.concatenate([low, high], axis=1).astype(BF16)
+    product = dot(normed, weight_ref[...])
+    units = act_ref.shape[1]
+    gate, up = product[:, :units], product[:, units:]
+    act_ref[...] = (gate / (1.0 + jnp.exp(-gate)) * up).astype(BF16)
     for k in range(peers):
         place = 1 - core + (0 if split[k] else 2 * half)
         start = pl.multiple_of(place * tall, tall)
@@ -425,46 +384,37 @@
     units = 2 * gate.shape[0]
     shape = jax.ShapeDtypeStruct
 
+    begun = pl.pallas_call(
+        begin_kernel,
+        out_shape=shape((8, LANES), F32),
+        out_specs=vmem(),
+        compiler_params=params(1),
+        cost_estimate=pl.CostEstimate(
+            flops=20 * 10**9, bytes_accessed=64 * MIB, transcendentals=0
+        ),
+        name="begin",
+    )()
+    context = pl.pallas_call(
+        functools.partial(attend_kernel, kv_local),
+        out_shape=shape(queries.shape, BF16),
+        in_specs=[pl.BlockSpec(memory_space=pl.ANY), pl.BlockSpec(memory_space=pltpu.SMEM)]
+        + [vmem()] * 5,
+        out_specs=vmem(),
+        compiler_params=params(16),
+        cost_estimate=pl.CostEstimate(
+            flops=2 * 10**8, bytes_accessed=MIB // 2, transcendentals=0
+        ),
+        name="attend",
+    )(begun, cache_lengths, queries, new_keys, new_values, key_cache[0], value_cache[0])
     keep, give = pl.pallas_call(
-        functools.partial(attend_kernel, kv_local),
+        project_kernel,
         out_shape=(shape((tokens, 2 * width), F32), shape((tokens, 2 * width), BF16)),
-        in_specs=[hbm()] * 8,
-        out_specs=(hbm(), hbm()),
-        scratch_shapes=[
-            pltpu.SMEM((1, 1), jnp.int32),
-            pltpu.VMEM(queries.shape, BF16),
-            pltpu.VMEM(new_keys.shape, BF16),
-            pltpu.VMEM(new_values.shape, BF16),
-            pltpu.VMEM(key_cache.shape[1:], BF16),
-            pltpu.VMEM(value_cache.shape[1:], BF16),
-            pltpu.VMEM(residual.shape, BF16),
-            pltpu.VMEM((4, out_weight.shape[0], width), BF16),
-            pltpu.VMEM((tokens, 2 * width), F32),
-            pltpu.VMEM((tokens, 2 * width), BF16),
-            pltpu.SemaphoreType.DMA((13,)),
-        ],
-        compiler_params=params(ATTEND_MIB),
-        name="attend",
-    )(
-        cache_lengths.reshape(1, 1),
-        queries,
-        new_keys,
-        new_values,
-        key_cache[0],
-        value_cache[0],
-        residual,
-        out_weight,
-    )
-
-    keep = pl.pallas_call(
-        load_kernel,
-        out_shape=shape(keep.shape, F32),
-        in_specs=[vmem()],
-        out_specs=vmem(),
-        compiler_params=params(4),
-        cost_estimate=pl.CostEstimate(flops=0, bytes_accessed=MIB, transcendentals=0),
-        name="load",
-    )(keep)
+        in_specs=[vmem()] * 3,
+        out_specs=(vmem(), vmem()),
+        compiler_params=params(16),
+        name="project",
+    )(context, residual, out_weight)
+
     summed, send = pl.pallas_call(
         add_core_kernel,
         out_shape=(shape(keep.shape, F32), shape(keep.shape, BF16)),
@@ -531,10 +481,13 @@
 
     weights = pl.pallas_call(
         stage_kernel,
-        out_shape=shape((4,) + gate.shape, BF16),
+        out_shape=shape((gate.shape[1], 2 * units), BF16),
         in_specs=[vmem()] + [hbm()] * 4,
         out_specs=vmem(),
-        scratch_shapes=[pltpu.SemaphoreType.DMA((4,))],
+        scratch_shapes=[
+            pltpu.VMEM((4,) + gate.shape, BF16),
+            pltpu.SemaphoreType.DMA((4,)),
+        ],
         compiler_params=params(32),
         cost_estimate=pl.CostEstimate(
             flops=0, bytes_accessed=16 * gate.size, transcendentals=0

time: 52.3 us -> 49.6 us (0.948)
  Pallas kernels: 8.31 us -> 6.25 us
  local copies, waits for them, and re-layouts: 0.98 us -> 0.42 us
    pallas_call x3 -> x4, Pallas kernels: 3.61 us -> 2.2 us  [the longest x1 1.13 us: shards(): pl.pallas_call(stage_kernel, out_shape=shape((gate.shape[1], 2 * units),...]
    ppermute x2, waiting for transfers between devices: 6.05 us -> 5.17 us  [shards(): lax.ppermute(x, ('ep', 'tp'), route(near + k))]
    ppermute x7, waiting for transfers between devices: 1.65 us -> 2.44 us  [swap_core(): return lax.ppermute(x, 'tp', [(i, i ^ 1) for i in range(tp_count)])]
    pallas_call x1, Pallas kernels: 1.36 us -> 0.71 us  [shards(): pl.pallas_call(functools.partial(hidden_units_kernel, split, rows_each),...]
    unnamed x16 -> x28, local copies, waits for them, and re-layouts: 0.98 us -> 0.42 us
  transfers between devices with their start and end apart: 14 -> 14, of which waited for: 7 -> 7; matrix products, arithmetic and copies ran while one was open for 0% -> 0% of each run, Pallas kernels for 3% -> 5%
where the time goes in v6:
time: 49.6 us; the launch traced here: 49.4 us
  waiting for transfers between devices  14.2 us (29%)
  starting transfers between devices  13.8 us (28%)
  blocking collectives  13.6 us (27%)
  Pallas kernels  6.25 us (13%)
  between operations  1.03 us (2%)
    all_to_all x1, blocking collectives, shards(): came = lax.all_to_all(result, 'ep', split_axis=0, concat_axis=0, tiled=True)  13.6 us
    ppermute x3, waiting for transfers between devices, swap_half(): return lax.ppermute(x, 'tp', [(i, i ^ 2) for i in range(tp_count)])  6.62 us
    ppermute x3, starting transfers between devices, swap_half(): return lax.ppermute(x, 'tp', [(i, i ^ 2) for i in range(tp_count)])  6.29 us
    ppermute x2, waiting for transfers between devices, shards(): lax.ppermute(x, ('ep', 'tp'), route(near + k))  5.17 us
    ppermute x2, starting transfers between devices, shards(): lax.ppermute(x, ('ep', 'tp'), route(near + k))  3.85 us
    ppermute x7, waiting for transfers between devices, swap_core(): return lax.ppermute(x, 'tp', [(i, i ^ 1) for i in range(tp_count)])  2.44 us
    ppermute x7, starting transfers between devices, swap_core(): return lax.ppermute(x, 'tp', [(i, i ^ 1) for i in range(tp_count)])  2.36 us
    ppermute x2, starting transfers between devices, shards(): lax.ppermute(x, ('ep', 'tp'), route(k))  1.3 us
  transfers between devices with their start and end apart: 14, of which 7 were waited for; matrix products, arithmetic and copies ran while one was open for 0% of the time, Pallas kernels for 5%

profile of v6, /device:TPU:0, one launch (start us, length us, event | category | flops | bytes accessed | tf_op | source)
XLA Modules:
  0.0 49.4 jit_solution(9916536963068116715)
XLA Ops:
  0.0 0.0 copy-start.9
  0.0 0.0 copy-start.10
  0.0 0.0 copy-start.4
  0.0 0.0 copy-start
  0.0 0.0 copy-start.7
  0.1 0.0 copy-start.8
  0.1 0.0 copy-start.1
  0.1 0.0 copy-start.2
  0.9 0.0 copy-done.9
  0.9 0.1 copy-done.10
  1.0 0.0 copy-done.11
  1.0 0.0 copy-done.12
  1.0 0.0 copy-done.13
  1.0 0.6 %attend.1.context_ref = bf16[64,512]{1,0:T(8,128)(2,1)S(1)} custom-call(f32[8,128]{1,0:T(8,128)S(1)} %begin.1.after_ref, s32[1]{0:T(128)S(6)} %copy.16.length_ref, bf16[64,512]{1,0:T(8,128)(2,1)S(1)} %copy-done.11, bf16[64,128]{1,0:T(8,128)(2,1)S(1)} %copy-done.12, bf16[64,128]{1,0:T(8,128)(2,1)S(1)} %copy-done.13, bf16[512,128]{1,0:T(8,128)(2,1)S(1)} %bitcast.20, ...), custom_call_target="tpu_custom_call" | custom-call | flops 200000000 | bytes 524288 | tf_op jit(solution)/shard_map/attend/pallas_call | solution.py:397
  1.6 0.0 copy-done.4
  1.6 0.3 copy-done
  1.9 0.5 project.1
  2.3 0.5 %collective-permute-start = (bf16[64,1024]{1,0:T(8,128)(2,1)S(1)}, bf16[64,1024]{1,0:T(8,128)(2,1)S(1)}, u32[]{:S(2)}, u32[]{:S(2)}) collective-permute-start(bf16[64,1024]{1,0:T(8,128)(2,1)S(1)} %get-tuple-element.21), channel_id=1, source_target_pairs={{0,1},{1,0},{2,3},{3,2},{4,5},{5,4},{6,7},{7,6},{8,9},{9,8},{10,11... | collective-permute-start | bytes 393224 | tf_op jit(solution)/shard_map/ppermute | solution.py:371
  2.9 1.0 %collective-permute-done.came_ref = bf16[64,1024]{1,0:T(8,128)(2,1)S(1)} collective-permute-done((bf16[64,1024]{1,0:T(8,128)(2,1)S(1)}, bf16[64,1024]{1,0:T(8,128)(2,1)S(1)}, u32[]{:S(2)}, u32[]{:S(2)}) %collective-permute-start) | collective-permute-done | bytes 131104 | tf_op jit(solution)/shard_map/ppermute | solution.py:371
  3.9 2.9 %collective-permute-start.1 = (bf16[64,1024]{1,0:T(8,128)(2,1)S(1)}, bf16[64,1024]{1,0:T(8,128)(2,1)S(1)}, u32[]{:S(2)}, u32[]{:S(2)}) collective-permute-start(bf16[64,1024]{1,0:T(8,128)(2,1)S(1)} %get-tuple-element.23), channel_id=1, source_target_pairs={{0,2},{1,3},{2,0},{3,1},{4,6},{5,7},{6,4},{7,5},{8,10},{9,11},{10,... | collective-permute-start | bytes 393224 | tf_op jit(solution)/shard_map/ppermute | solution.py:374
  6.8 3.8 %collective-permute-done.1.came_ref = bf16[64,1024]{1,0:T(8,128)(2,1)S(1)} collective-permute-done((bf16[64,1024]{1,0:T(8,128)(2,1)S(1)}, bf16[64,1024]{1,0:T(8,128)(2,1)S(1)}, u32[]{:S(2)}, u32[]{:S(2)}) %collective-permute-start.1) | collective-permute-done | bytes 131104 | tf_op jit(solution)/shard_map/ppermute | solution.py:374
  10.6 0.1 collective-permute-start.2
  10.7 0.0 copy-done.7
  10.7 0.0 copy-done.8
  10.7 0.3 route.1
  11.0 1.1 %collective-permute-done.2.other_ref = bf16[64,1024]{1,0:T(8,128)(2,1)S(1)} collective-permute-done((bf16[64,1024]{1,0:T(8,128)(2,1)S(1)}, bf16[64,1024]{1,0:T(8,128)(2,1)S(1)}, u32[]{:S(2)}, u32[]{:S(2)}) %collective-permute-start.2) | collective-permute-done | bytes 131104 | tf_op jit(solution)/shard_map/ppermute | solution.py:371
  12.1 0.2 gather_rows.2
  12.3 0.0 copy-done.1
  12.3 0.2 collective-permute-start.3
  12.5 0.0 copy-done.2
  12.5 0.4 collective-permute-start.4
  12.9 3.8 %collective-permute-start.8 = (bf16[272,128]{1,0:T(8,128)(2,1)S(1)}, bf16[272,128]{1,0:T(8,128)(2,1)S(1)}, u32[]{:S(2)}, u32[]{:S(2)}) collective-permute-start(bf16[272,128]{1,0:T(8,128)(2,1)S(1)} %get-tuple-element.32), channel_id=1, source_target_pairs={{0,24},{1,29},{2,26},{3,31},{4,28},{5,25},{6,30},{7,27},{8,16},{9,... | collective-permute-start | bytes 208904 | tf_op jit(solution)/shard_map/ppermute | solution.py:475
  16.7 0.0 collective-permute-start.7
  16.7 0.0 collective-permute-done.3.gate_pair.after_ref
  16.7 0.2 gather_rows.3
  17.0 0.7 %collective-permute-start.5 = (bf16[528,128]{1,0:T(8,128)(2,1)S(1)}, bf16[528,128]{1,0:T(8,128)(2,1)S(1)}, u32[]{:S(2)}, u32[]{:S(2)}) collective-permute-start(bf16[528,128]{1,0:T(8,128)(2,1)S(1)} %get-tuple-element.29), channel_id=1, source_target_pairs={{0,0},{1,5},{2,2},{3,7},{4,4},{5,1},{6,6},{7,3},{8,8},{9,13},{10,1... | collective-permute-start | bytes 405512 | tf_op jit(solution)/shard_map/ppermute | solution.py:479
  17.6 0.0 copy-start.5
  17.6 0.6 %collective-permute-start.6 = (bf16[528,128]{1,0:T(8,128)(2,1)S(1)}, bf16[528,128]{1,0:T(8,128)(2,1)S(1)}, u32[]{:S(2)}, u32[]{:S(2)}) collective-permute-start(bf16[528,128]{1,0:T(8,128)(2,1)S(1)} %get-tuple-element.30), channel_id=1, source_target_pairs={{0,8},{1,13},{2,10},{3,15},{4,12},{5,9},{6,14},{7,11},{8,0},{9,5},... | collective-permute-start | bytes 405512 | tf_op jit(solution)/shard_map/ppermute | solution.py:479
  18.3 1.3 %collective-permute-done.8.refs_3_ = bf16[272,128]{1,0:T(8,128)(2,1)S(1)} collective-permute-done((bf16[272,128]{1,0:T(8,128)(2,1)S(1)}, bf16[272,128]{1,0:T(8,128)(2,1)S(1)}, u32[]{:S(2)}, u32[]{:S(2)}) %collective-permute-start.8) | collective-permute-done | bytes 69664 | tf_op jit(solution)/shard_map/ppermute | solution.py:475
  19.6 1.8 %collective-permute-start.9 = (bf16[272,128]{1,0:T(8,128)(2,1)S(1)}, bf16[272,128]{1,0:T(8,128)(2,1)S(1)}, u32[]{:S(2)}, u32[]{:S(2)}) collective-permute-start(bf16[272,128]{1,0:T(8,128)(2,1)S(1)} %collective-permute-done.8.refs_3_), channel_id=1, source_target_pairs={{0,2},{1,3},{2,0},{3,1},{4,6},{5,7},{6,4},{7,5},{8,10},{9,11},{10,... | collective-permute-start | bytes 208904 | tf_op jit(solution)/shard_map/ppermute | solution.py:374
  21.4 0.0 collective-permute-done.4.up_pair
  21.4 1.1 %stage.1.weight_ref = bf16[2048,768]{1,0:T(8,128)(2,1)S(1)} custom-call(bf16[4,16,128]{2,1,0:T(8,128)(2,1)S(1)} %get-tuple-element.24.after_ref.tags_ref, bf16[192,2048]{1,0:T(8,128)(2,1)S(1)} %bitcast.13, bf16[192,2048]{1,0:T(8,128)(2,1)S(1)} %bitcast.15, bf16[192,2048]{1,0:T(8,128)(2,1)S(1)} %collective-permute-done.3.gate_pair.after_ref, ...), custom_call_target="tpu_custom_call" | custom-call | bytes 6291456 | tf_op jit(solution)/shard_map/stage/pallas_call | solution.py:482
  22.6 0.0 copy-start.6
  22.6 0.0 copy-start.3
  22.6 3.8 %collective-permute-done.7.refs_2_ = bf16[528,128]{1,0:T(8,128)(2,1)S(1)} collective-permute-done((bf16[528,128]{1,0:T(8,128)(2,1)S(1)}, bf16[528,128]{1,0:T(8,128)(2,1)S(1)}, u32[]{:S(2)}, u32[]{:S(2)}) %collective-permute-start.7) | collective-permute-done | bytes 135200 | tf_op jit(solution)/shard_map/ppermute | solution.py:475
  26.4 0.0 collective-permute-done.9.refs_4_
  26.4 0.0 collective-permute-done.5.refs_0_
  26.5 0.0 collective-permute-done.6.refs_1_
  26.5 0.0 copy-done.5
  26.5 0.7 %hidden_units.1 = (bf16[128,384]{1,0:T(8,128)(2,1)S(1)}, bf16[4,144,128]{2,1,0:T(8,128)(2,1)S(1)}) custom-call(f32[16,128]{1,0:T(8,128)S(1)} %bitcast.17, bf16[2048,768]{1,0:T(8,128)(2,1)S(1)} %stage.1.weight_ref, bf16[528,128]{1,0:T(8,128)(2,1)S(1)} %collective-permute-done.5.refs_0_, bf16[528,128]{1,0:T(8,128)(2,1)S(1)} %collective-permute-done.6.refs_1_, ...), custom_call_target="tpu_custom_call" | custom-call | tf_op jit(solution)/shard_map/hidden_units/pallas_call | solution.py:498
  27.2 1.6 %collective-permute-start.11 = (bf16[128,384]{1,0:T(8,128)(2,1)S(1)}, bf16[128,384]{1,0:T(8,128)(2,1)S(1)}, u32[]{:S(2)}, u32[]{:S(2)}) collective-permute-start(bf16[128,384]{1,0:T(8,128)(2,1)S(1)} %get-tuple-element.34.act_ref), channel_id=1, source_target_pairs={{0,2},{1,3},{2,0},{3,1},{4,6},{5,7},{6,4},{7,5},{8,10},{9,11},{10,... | collective-permute-start | bytes 294920 | tf_op jit(solution)/shard_map/ppermute | solution.py:374
  28.7 1.1 %collective-permute-start.10 = (bf16[4,144,128]{2,1,0:T(8,128)(2,1)S(1)}, bf16[4,144,128]{2,1,0:T(8,128)(2,1)S(1)}, u32[]{:S(2)}, u32[]{:S(2)}) collective-permute-start(bf16[4,144,128]{2,1,0:T(8,128)(2,1)S(1)} %get-tuple-element.33), channel_id=1, source_target_pairs={{0,1},{1,0},{2,3},{3,2},{4,5},{5,4},{6,7},{7,6},{8,9},{9,8},{10,11... | collective-permute-start | bytes 442376 | tf_op jit(solution)/shard_map/ppermute | solution.py:371
  29.8 0.0 collective-permute-start.12
  29.8 2.8 %collective-permute-done.11.act_half_ref = bf16[128,384]{1,0:T(8,128)(2,1)S(1)} collective-permute-done((bf16[128,384]{1,0:T(8,128)(2,1)S(1)}, bf16[128,384]{1,0:T(8,128)(2,1)S(1)}, u32[]{:S(2)}, u32[]{:S(2)}) %collective-permute-start.11) | collective-permute-done | bytes 98336 | tf_op jit(solution)/shard_map/ppermute | solution.py:374
  32.6 0.1 collective-permute-start.13
  32.7 0.0 collective-permute-done.10.side_ref
  32.7 0.0 copy-done.6
  32.7 0.8 %select.1.after_ref.chosen_ref = bf16[64,256]{1,0:T(8,128)(2,1)S(1)} custom-call(s32[8]{0:T(128)S(1)} %copy-done.6, bf16[4,144,128]{2,1,0:T(8,128)(2,1)S(1)} %collective-permute-done.10.side_ref, bf16[528,128]{1,0:T(8,128)(2,1)S(1)} %collective-permute-done.5.refs_0_, bf16[528,128]{1,0:T(8,128)(2,1)S(1)} %collective-permute-done.6.refs_1_, ...), custom_call_target="tpu_custom_call" | custom-call | bytes 1048576 | tf_op jit(solution)/shard_map/select/pallas_call | solution.py:515
  33.5 0.0 collective-permute-done.12.act_core_ref
  33.5 0.4 collective-permute-done.13.act_both_ref
  33.9 0.0 copy-done.3
  33.9 1.0 %down.1 = bf16[8,128,128]{2,1,0:T(8,128)(2,1)S(1)} custom-call(bf16[64,256]{1,0:T(8,128)(2,1)S(1)} %select.1.after_ref.chosen_ref, s32[8]{0:T(128)S(1)} %copy-done.6, bf16[128,384]{1,0:T(8,128)(2,1)S(1)} %get-tuple-element.34.act_ref, bf16[128,384]{1,0:T(8,128)(2,1)S(1)} %collective-permute-done.11.act_half_ref, ...), custom_call_target="tpu_custom_call" | custom-call | tf_op jit(solution)/shard_map/down/pallas_call | solution.py:524
  34.9 13.6 %all_to_all.5.came_ref = bf16[8,128,128]{2,1,0:T(8,128)(2,1)S(1)} all-to-all(bf16[8,128,128]{2,1,0:T(8,128)(2,1)S(1)} %down.1), channel_id=1, replica_groups=mesh['ep'=8,'tp'=4] {'ep'}, dimensions={0} | all-to-all | bytes 524288 | tf_op jit(solution)/shard_map/all_to_all | solution.py:534
  48.6 0.8 %combine.1 = bf16[64,512]{1,0:T(8,128)(2,1)} custom-call(bf16[64,256]{1,0:T(8,128)(2,1)S(1)} %select.1.after_ref.chosen_ref, bf16[8,128,128]{2,1,0:T(8,128)(2,1)S(1)} %all_to_all.5.came_ref), custom_call_target="tpu_custom_call" | custom-call | tf_op jit(solution)/shard_map/combine/pallas_call | solution.py:535
  (6 shorter events, 0.1 us)
Async XLA Ops:
  0.0 0.9 %copy-start.9 = (bf16[1,512,128]{2,1,0:T(8,128)(2,1)S(1)}, bf16[1,512,128]{2,1,0:T(8,128)(2,1)}, u32[]{:S(2)}) copy-start(bf16[1,512,128]{2,1,0:T(8,128)(2,1)} %param.18) | copy-start | bytes 393220
  0.0 1.0 %copy-start.10 = (bf16[1,512,128]{2,1,0:T(8,128)(2,1)S(1)}, bf16[1,512,128]{2,1,0:T(8,128)(2,1)}, u32[]{:S(2)}) copy-start(bf16[1,512,128]{2,1,0:T(8,128)(2,1)} %param.19) | copy-start | bytes 393220
  0.0 1.0 %copy-start.11 = (bf16[64,512]{1,0:T(8,128)(2,1)S(1)}, bf16[64,512]{1,0:T(8,128)(2,1)}, u32[]{:S(2)}) copy-start(bf16[64,512]{1,0:T(8,128)(2,1)} %query_ref.1) | copy-start | bytes 196612
  0.0 1.0 %copy-start.12 = (bf16[64,128]{1,0:T(8,128)(2,1)S(1)}, bf16[64,128]{1,0:T(8,128)(2,1)}, u32[]{:S(2)}) copy-start(bf16[64,128]{1,0:T(8,128)(2,1)} %new_key_ref.1) | copy-start | bytes 49156
  0.0 1.0 %copy-start.13 = (bf16[64,128]{1,0:T(8,128)(2,1)S(1)}, bf16[64,128]{1,0:T(8,128)(2,1)}, u32[]{:S(2)}) copy-start(bf16[64,128]{1,0:T(8,128)(2,1)} %new_value_ref.1) | copy-start | bytes 49156
  0.0 1.6 %copy-start.4 = (bf16[64,512]{1,0:T(8,128)(2,1)S(1)}, bf16[64,512]{1,0:T(8,128)(2,1)}, u32[]{:S(2)}) copy-start(bf16[64,512]{1,0:T(8,128)(2,1)} %residual_ref.1) | copy-start | bytes 196612
  0.0 1.8 %copy-start = (bf16[512,2048]{1,0:T(8,128)(2,1)S(1)}, bf16[512,2048]{1,0:T(8,128)(2,1)}, u32[]{:S(2)}) copy-start(bf16[512,2048]{1,0:T(8,128)(2,1)} %weight_ref.1) | copy-start | bytes 6291460
  0.0 10.7 %copy-start.7 = (s32[64,2]{0,1:T(2,128)S(1)}, s32[64,2]{0,1:T(2,128)}, u32[]{:S(2)}) copy-start(s32[64,2]{0,1:T(2,128)} %param.25) | copy-start | bytes 1540
  0.1 10.7 %copy-start.8 = (f32[64,2]{0,1:T(2,128)S(1)}, f32[64,2]{0,1:T(2,128)}, u32[]{:S(2)}) copy-start(f32[64,2]{0,1:T(2,128)} %param.26) | copy-start | bytes 1540
  0.1 12.2 %copy-start.1 = (bf16[1,2048,192]{1,2,0:T(8,128)(2,1)S(1)}, bf16[1,2048,192]{1,2,0:T(8,128)(2,1)}, u32[]{:S(2)}) copy-start(bf16[1,2048,192]{1,2,0:T(8,128)(2,1)} %param.27) | copy-start | bytes 2359300
  0.1 12.4 %copy-start.2 = (bf16[1,2048,192]{1,2,0:T(8,128)(2,1)S(1)}, bf16[1,2048,192]{1,2,0:T(8,128)(2,1)}, u32[]{:S(2)}) copy-start(bf16[1,2048,192]{1,2,0:T(8,128)(2,1)} %param.28) | copy-start | bytes 2359300
  2.3 1.5 %collective-permute-start = (bf16[64,1024]{1,0:T(8,128)(2,1)S(1)}, bf16[64,1024]{1,0:T(8,128)(2,1)S(1)}, u32[]{:S(2)}, u32[]{:S(2)}) collective-permute-start(bf16[64,1024]{1,0:T(8,128)(2,1)S(1)} %get-tuple-element.21), channel_id=1, source_target_pairs={{0,1},{1,0},{2,3},{3,2},{4,5},{5,4},{6,7},{7,6},{8,9},{9,8},{10,11... | collective-permute-start | bytes 393224 | tf_op jit(solution)/shard_map/ppermute | solution.py:371
  3.9 6.7 %collective-permute-start.1 = (bf16[64,1024]{1,0:T(8,128)(2,1)S(1)}, bf16[64,1024]{1,0:T(8,128)(2,1)S(1)}, u32[]{:S(2)}, u32[]{:S(2)}) collective-permute-start(bf16[64,1024]{1,0:T(8,128)(2,1)S(1)} %get-tuple-element.23), channel_id=1, source_target_pairs={{0,2},{1,3},{2,0},{3,1},{4,6},{5,7},{6,4},{7,5},{8,10},{9,11},{10,... | collective-permute-start | bytes 393224 | tf_op jit(solution)/shard_map/ppermute | solution.py:374
  10.6 1.4 %collective-permute-start.2 = (bf16[64,1024]{1,0:T(8,128)(2,1)S(1)}, bf16[64,1024]{1,0:T(8,128)(2,1)S(1)}, u32[]{:S(2)}, u32[]{:S(2)}) collective-permute-start(bf16[64,1024]{1,0:T(8,128)(2,1)S(1)} %add_half.1.after_ref.part_ref), channel_id=1, source_target_pairs={{0,1},{1,0},{2,3},{3,2},{4,5},{5,4},{6,7},{7,6},{8,9},{9,8},{10,11... | collective-permute-start | bytes 393224 | tf_op jit(solution)/shard_map/ppermute | solution.py:371
  12.3 4.4 %collective-permute-start.3 = (bf16[192,2048]{1,0:T(8,128)(2,1)S(1)}, bf16[192,2048]{1,0:T(8,128)(2,1)S(1)}, u32[]{:S(2)}, u32[]{:S(2)}) collective-permute-start(bf16[192,2048]{1,0:T(8,128)(2,1)S(1)} %bitcast.12), channel_id=1, source_target_pairs={{0,1},{1,0},{2,3},{3,2},{4,5},{5,4},{6,7},{7,6},{8,9},{9,8},{10,11... | collective-permute-start | bytes 2359304 | tf_op jit(solution)/shard_map/ppermute | solution.py:371
  12.5 8.9 %collective-permute-start.4 = (bf16[192,2048]{1,0:T(8,128)(2,1)S(1)}, bf16[192,2048]{1,0:T(8,128)(2,1)S(1)}, u32[]{:S(2)}, u32[]{:S(2)}) collective-permute-start(bf16[192,2048]{1,0:T(8,128)(2,1)S(1)} %bitcast.14), channel_id=1, source_target_pairs={{0,1},{1,0},{2,3},{3,2},{4,5},{5,4},{6,7},{7,6},{8,9},{9,8},{10,11... | collective-permute-start | bytes 2359304 | tf_op jit(solution)/shard_map/ppermute | solution.py:371
  12.9 6.7 %collective-permute-start.8 = (bf16[272,128]{1,0:T(8,128)(2,1)S(1)}, bf16[272,128]{1,0:T(8,128)(2,1)S(1)}, u32[]{:S(2)}, u32[]{:S(2)}) collective-permute-start(bf16[272,128]{1,0:T(8,128)(2,1)S(1)} %get-tuple-element.32), channel_id=1, source_target_pairs={{0,24},{1,29},{2,26},{3,31},{4,28},{5,25},{6,30},{7,27},{8,16},{9,... | collective-permute-start | bytes 208904 | tf_op jit(solution)/shard_map/ppermute | solution.py:475
  16.7 9.7 %collective-permute-start.7 = (bf16[528,128]{1,0:T(8,128)(2,1)S(1)}, bf16[528,128]{1,0:T(8,128)(2,1)S(1)}, u32[]{:S(2)}, u32[]{:S(2)}) collective-permute-start(bf16[528,128]{1,0:T(8,128)(2,1)S(1)} %get-tuple-element.31), channel_id=1, source_target_pairs={{0,16},{1,21},{2,18},{3,23},{4,20},{5,17},{6,22},{7,19},{8,24},{9,... | collective-permute-start | bytes 405512 | tf_op jit(solution)/shard_map/ppermute | solution.py:475
  17.0 9.5 %collective-permute-start.5 = (bf16[528,128]{1,0:T(8,128)(2,1)S(1)}, bf16[528,128]{1,0:T(8,128)(2,1)S(1)}, u32[]{:S(2)}, u32[]{:S(2)}) collective-permute-start(bf16[528,128]{1,0:T(8,128)(2,1)S(1)} %get-tuple-element.29), channel_id=1, source_target_pairs={{0,0},{1,5},{2,2},{3,7},{4,4},{5,1},{6,6},{7,3},{8,8},{9,13},{10,1... | collective-permute-start | bytes 405512 | tf_op jit(solution)/shard_map/ppermute | solution.py:479
  17.6 8.8 %copy-start.5 = (f32[2048]{0:T(1024)S(1)}, f32[2048]{0:T(1024)}, u32[]{:S(2)}) copy-start(f32[2048]{0:T(1024)} %param.24) | copy-start | bytes 24580
  17.6 8.8 %collective-permute-start.6 = (bf16[528,128]{1,0:T(8,128)(2,1)S(1)}, bf16[528,128]{1,0:T(8,128)(2,1)S(1)}, u32[]{:S(2)}, u32[]{:S(2)}) collective-permute-start(bf16[528,128]{1,0:T(8,128)(2,1)S(1)} %get-tuple-element.30), channel_id=1, source_target_pairs={{0,8},{1,13},{2,10},{3,15},{4,12},{5,9},{6,14},{7,11},{8,0},{9,5},... | collective-permute-start | bytes 405512 | tf_op jit(solution)/shard_map/ppermute | solution.py:479
  19.6 6.8 %collective-permute-start.9 = (bf16[272,128]{1,0:T(8,128)(2,1)S(1)}, bf16[272,128]{1,0:T(8,128)(2,1)S(1)}, u32[]{:S(2)}, u32[]{:S(2)}) collective-permute-start(bf16[272,128]{1,0:T(8,128)(2,1)S(1)} %collective-permute-done.8.refs_3_), channel_id=1, source_target_pairs={{0,2},{1,3},{2,0},{3,1},{4,6},{5,7},{6,4},{7,5},{8,10},{9,11},{10,... | collective-permute-start | bytes 208904 | tf_op jit(solution)/shard_map/ppermute | solution.py:374
  22.6 10.2 %copy-start.6 = (s32[8]{0:T(128)S(1)}, s32[8]{0:T(128)}, u32[]{:S(2)}) copy-start(s32[8]{0:T(128)} %order_ref.3) | copy-start | bytes 100
  22.6 11.3 %copy-start.3 = (bf16[1,768,512]{2,1,0:T(8,128)(2,1)S(1)}, bf16[1,768,512]{2,1,0:T(8,128)(2,1)}, u32[]{:S(2)}) copy-start(bf16[1,768,512]{2,1,0:T(8,128)(2,1)} %param.29) | copy-start | bytes 2359300
  27.2 5.4 %collective-permute-start.11 = (bf16[128,384]{1,0:T(8,128)(2,1)S(1)}, bf16[128,384]{1,0:T(8,128)(2,1)S(1)}, u32[]{:S(2)}, u32[]{:S(2)}) collective-permute-start(bf16[128,384]{1,0:T(8,128)(2,1)S(1)} %get-tuple-element.34.act_ref), channel_id=1, source_target_pairs={{0,2},{1,3},{2,0},{3,1},{4,6},{5,7},{6,4},{7,5},{8,10},{9,11},{10,... | collective-permute-start | bytes 294920 | tf_op jit(solution)/shard_map/ppermute | solution.py:374
  28.7 4.0 %collective-permute-start.10 = (bf16[4,144,128]{2,1,0:T(8,128)(2,1)S(1)}, bf16[4,144,128]{2,1,0:T(8,128)(2,1)S(1)}, u32[]{:S(2)}, u32[]{:S(2)}) collective-permute-start(bf16[4,144,128]{2,1,0:T(8,128)(2,1)S(1)} %get-tuple-element.33), channel_id=1, source_target_pairs={{0,1},{1,0},{2,3},{3,2},{4,5},{5,4},{6,7},{7,6},{8,9},{9,8},{10,11... | collective-permute-start | bytes 442376 | tf_op jit(solution)/shard_map/ppermute | solution.py:371
  29.8 3.7 %collective-permute-start.12 = (bf16[128,384]{1,0:T(8,128)(2,1)S(1)}, bf16[128,384]{1,0:T(8,128)(2,1)S(1)}, u32[]{:S(2)}, u32[]{:S(2)}) collective-permute-start(bf16[128,384]{1,0:T(8,128)(2,1)S(1)} %get-tuple-element.34.act_ref), channel_id=1, source_target_pairs={{0,1},{1,0},{2,3},{3,2},{4,5},{5,4},{6,7},{7,6},{8,9},{9,8},{10,11... | collective-permute-start | bytes 294920 | tf_op jit(solution)/shard_map/ppermute | solution.py:371
  32.6 1.3 %collective-permute-start.13 = (bf16[128,384]{1,0:T(8,128)(2,1)S(1)}, bf16[128,384]{1,0:T(8,128)(2,1)S(1)}, u32[]{:S(2)}, u32[]{:S(2)}) collective-permute-start(bf16[128,384]{1,0:T(8,128)(2,1)S(1)} %collective-permute-done.11.act_half_ref), channel_id=1, source_target_pairs={{0,1},{1,0},{2,3},{3,2},{4,5},{5,4},{6,7},{7,6},{8,9},{9,8},{10,11... | collective-permute-start | bytes 294920 | tf_op jit(solution)/shard_map/ppermute | solution.py:371

commit v7 on v6

--- a/solution.py
+++ b/solution.py
@@ -288,7 +288,7 @@
     split,
     rows_each,
     after_ref,
-    order_ref,
+    order_vmem,
     act_ref,
     act_half_ref,
     act_core_ref,
@@ -300,7 +300,9 @@
     del after_ref
     peers = len(split)
     got = refs[:peers]
-    out_ref = refs[peers]
+    out_ref, order_ref, sem = refs[peers:]
+    fetch = pltpu.make_async_copy(order_vmem, order_ref, sem)
+    fetch.start()
     tp = lax.axis_index("tp")
     me = lax.axis_index("ep")
     half, core = tp // 2, tp % 2
@@ -312,9 +314,12 @@
     diagonal = lax.broadcasted_iota(jnp.int32, (rows_each, LANES), 0) == lax.broadcasted_iota(
         jnp.int32, (rows_each, LANES), 1
     )
-    for group in range(2):
-        near, far = ((act_ref, act_half_ref), (act_core_ref, act_both_ref))[group]
-        result = dot(near[...], here) + dot(far[...], there)
+    outcomes = [
+        dot(near[...], here) + dot(far[...], there)
+        for near, far in ((act_ref, act_half_ref), (act_core_ref, act_both_ref))
+    ]
+    fetch.wait()
+    for group, result in enumerate(outcomes):
         for k in range(peers):
             request = jnp.bitwise_xor(me, 2 * k + (core if group == 0 else 1 - core))
             place = order_ref[request]
@@ -459,6 +464,9 @@
             in_specs=[pl.BlockSpec(memory_space=pl.ANY)] + [vmem()] * 4,
             out_specs=[vmem()] * (last - first),
             compiler_params=params(8),
+            cost_estimate=pl.CostEstimate(
+                flops=(20 * 10**9 if first else 0), bytes_accessed=MIB, transcendentals=0
+            ),
             name="gather_rows",
         )(after, part, other, pick, tags)
 
@@ -470,7 +478,7 @@
         ]
 
     far_send = list(gather(near, peers, tags))
-    gate, up, far_send[-1] = lax.optimization_barrier((gate, up, far_send[-1]))
+    gate, up, tags = lax.optimization_barrier((gate, up, tags))
     far = [
         lax.ppermute(x, ("ep", "tp"), route(near + k)) for k, x in enumerate(far_send)
     ]
@@ -524,9 +532,12 @@
     result = pl.pallas_call(
         functools.partial(down_kernel, split, rows_each),
         out_shape=shape((ep_count, tall, LANES), BF16),
-        in_specs=[pl.BlockSpec(memory_space=pl.ANY), pl.BlockSpec(memory_space=pltpu.SMEM)]
-        + [vmem()] * (6 + peers),
-        out_specs=vmem(),
+        in_specs=[pl.BlockSpec(memory_space=pl.ANY)] + [vmem()] * (7 + peers),
+        out_specs=vmem(),
+        scratch_shapes=[
+            pltpu.SMEM(request_order.shape, jnp.int32),
+            pltpu.SemaphoreType.DMA(()),
+        ],
         compiler_params=params(16),
         name="down",
     )(chosen, request_order, act, act_half, act_core, act_both, down, side, *got)

time: 49.6 us -> 48.8 us (0.984)
  waiting for transfers between devices: 14.2 us -> 13.6 us
    ppermute x7, waiting for transfers between devices: 2.44 us -> 1.87 us  [swap_core(): return lax.ppermute(x, 'tp', [(i, i ^ 1) for i in range(tp_count)])]
where the time goes in v7:
time: 48.8 us; the launch traced here: 48.6 us
  starting transfers between devices  13.9 us (28%)
  waiting for transfers between devices  13.6 us (28%)
  blocking collectives  13.6 us (28%)
  Pallas kernels  6.01 us (12%)
  between operations  1.02 us (2%)
    all_to_all x1, blocking collectives, shards(): came = lax.all_to_all(result, 'ep', split_axis=0, concat_axis=0, tiled=True)  13.6 us
    ppermute x3, waiting for transfers between devices, swap_half(): return lax.ppermute(x, 'tp', [(i, i ^ 2) for i in range(tp_count)])  6.62 us
    ppermute x3, starting transfers between devices, swap_half(): return lax.ppermute(x, 'tp', [(i, i ^ 2) for i in range(tp_count)])  6.29 us
    ppermute x2, waiting for transfers between devices, shards(): lax.ppermute(x, ('ep', 'tp'), route(near + k))  5.1 us
    ppermute x2, starting transfers between devices, shards(): lax.ppermute(x, ('ep', 'tp'), route(near + k))  3.92 us
    ppermute x7, starting transfers between devices, swap_core(): return lax.ppermute(x, 'tp', [(i, i ^ 1) for i in range(tp_count)])  2.35 us
    ppermute x7, waiting for transfers between devices, swap_core(): return lax.ppermute(x, 'tp', [(i, i ^ 1) for i in range(tp_count)])  1.87 us
    ppermute x2, starting transfers between devices, shards(): lax.ppermute(x, ('ep', 'tp'), route(k))  1.37 us
  transfers between devices with their start and end apart: 14, of which 7 were waited for; matrix products, arithmetic and copies ran while one was open for 0% of the time, Pallas kernels for 5%

profile of v7, /device:TPU:0, one launch (start us, length us, event | category | flops | bytes accessed | tf_op | source)
XLA Modules:
  0.0 48.6 jit_solution(15471077430010360275)
XLA Ops:
  0.0 0.0 copy-start.9
  0.0 0.0 copy-start.10
  0.0 0.0 copy-start.4
  0.0 0.0 copy-start
  0.0 0.0 copy-start.7
  0.1 0.0 copy-start.8
  0.1 0.0 copy-start.1
  0.1 0.0 copy-start.2
  0.9 0.0 copy-done.9
  0.9 0.1 copy-done.10
  1.0 0.0 copy-done.11
  1.0 0.0 copy-done.12
  1.0 0.0 copy-done.13
  1.0 0.6 %attend.1.context_ref = bf16[64,512]{1,0:T(8,128)(2,1)S(1)} custom-call(f32[8,128]{1,0:T(8,128)S(1)} %begin.1.after_ref, s32[1]{0:T(128)S(6)} %copy.16.length_ref, bf16[64,512]{1,0:T(8,128)(2,1)S(1)} %copy-done.11, bf16[64,128]{1,0:T(8,128)(2,1)S(1)} %copy-done.12, bf16[64,128]{1,0:T(8,128)(2,1)S(1)} %copy-done.13, bf16[512,128]{1,0:T(8,128)(2,1)S(1)} %bitcast.20, ...), custom_call_target="tpu_custom_call" | custom-call | flops 200000000 | bytes 524288 | tf_op jit(solution)/shard_map/attend/pallas_call | solution.py:402
  1.6 0.0 copy-done.4
  1.6 0.3 copy-done
  1.9 0.5 project.1
  2.3 0.5 %collective-permute-start = (bf16[64,1024]{1,0:T(8,128)(2,1)S(1)}, bf16[64,1024]{1,0:T(8,128)(2,1)S(1)}, u32[]{:S(2)}, u32[]{:S(2)}) collective-permute-start(bf16[64,1024]{1,0:T(8,128)(2,1)S(1)} %get-tuple-element.21), channel_id=1, source_target_pairs={{0,1},{1,0},{2,3},{3,2},{4,5},{5,4},{6,7},{7,6},{8,9},{9,8},{10,11... | collective-permute-start | bytes 393224 | tf_op jit(solution)/shard_map/ppermute | solution.py:376
  2.9 1.0 %collective-permute-done.came_ref = bf16[64,1024]{1,0:T(8,128)(2,1)S(1)} collective-permute-done((bf16[64,1024]{1,0:T(8,128)(2,1)S(1)}, bf16[64,1024]{1,0:T(8,128)(2,1)S(1)}, u32[]{:S(2)}, u32[]{:S(2)}) %collective-permute-start) | collective-permute-done | bytes 131104 | tf_op jit(solution)/shard_map/ppermute | solution.py:376
  3.9 2.9 %collective-permute-start.1 = (bf16[64,1024]{1,0:T(8,128)(2,1)S(1)}, bf16[64,1024]{1,0:T(8,128)(2,1)S(1)}, u32[]{:S(2)}, u32[]{:S(2)}) collective-permute-start(bf16[64,1024]{1,0:T(8,128)(2,1)S(1)} %get-tuple-element.23), channel_id=1, source_target_pairs={{0,2},{1,3},{2,0},{3,1},{4,6},{5,7},{6,4},{7,5},{8,10},{9,11},{10,... | collective-permute-start | bytes 393224 | tf_op jit(solution)/shard_map/ppermute | solution.py:379
  6.8 3.8 %collective-permute-done.1.came_ref = bf16[64,1024]{1,0:T(8,128)(2,1)S(1)} collective-permute-done((bf16[64,1024]{1,0:T(8,128)(2,1)S(1)}, bf16[64,1024]{1,0:T(8,128)(2,1)S(1)}, u32[]{:S(2)}, u32[]{:S(2)}) %collective-permute-start.1) | collective-permute-done | bytes 131104 | tf_op jit(solution)/shard_map/ppermute | solution.py:379
  10.6 0.1 collective-permute-start.4
  10.7 0.0 copy-done.7
  10.7 0.0 copy-done.8
  10.7 0.3 route.1
  11.0 0.0 copy-done.1
  11.0 0.5 %collective-permute-start.2 = (bf16[192,2048]{1,0:T(8,128)(2,1)S(1)}, bf16[192,2048]{1,0:T(8,128)(2,1)S(1)}, u32[]{:S(2)}, u32[]{:S(2)}) collective-permute-start(bf16[192,2048]{1,0:T(8,128)(2,1)S(1)} %bitcast.12), channel_id=1, source_target_pairs={{0,1},{1,0},{2,3},{3,2},{4,5},{5,4},{6,7},{7,6},{8,9},{9,8},{10,11... | collective-permute-start | bytes 2359304 | tf_op jit(solution)/shard_map/ppermute | solution.py:376
  11.5 0.0 copy-done.2
  11.5 0.1 collective-permute-start.3
  11.6 0.5 collective-permute-done.4.other_ref
  12.1 0.2 gather_rows.3
  12.3 3.9 %collective-permute-start.8 = (bf16[272,128]{1,0:T(8,128)(2,1)S(1)}, bf16[272,128]{1,0:T(8,128)(2,1)S(1)}, u32[]{:S(2)}, u32[]{:S(2)}) collective-permute-start(bf16[272,128]{1,0:T(8,128)(2,1)S(1)} %get-tuple-element.32), channel_id=1, source_target_pairs={{0,24},{1,29},{2,26},{3,31},{4,28},{5,25},{6,30},{7,27},{8,16},{9,... | collective-permute-start | bytes 208904 | tf_op jit(solution)/shard_map/ppermute | solution.py:483
  16.2 0.0 collective-permute-start.7
  16.2 0.0 collective-permute-done.2.gate_pair.after_ref
  16.2 0.2 gather_rows.2
  16.4 0.7 %collective-permute-start.5 = (bf16[528,128]{1,0:T(8,128)(2,1)S(1)}, bf16[528,128]{1,0:T(8,128)(2,1)S(1)}, u32[]{:S(2)}, u32[]{:S(2)}) collective-permute-start(bf16[528,128]{1,0:T(8,128)(2,1)S(1)} %get-tuple-element.29), channel_id=1, source_target_pairs={{0,0},{1,5},{2,2},{3,7},{4,4},{5,1},{6,6},{7,3},{8,8},{9,13},{10,1... | collective-permute-start | bytes 405512 | tf_op jit(solution)/shard_map/ppermute | solution.py:487
  17.1 0.0 copy-start.5
  17.1 0.7 %collective-permute-start.6 = (bf16[528,128]{1,0:T(8,128)(2,1)S(1)}, bf16[528,128]{1,0:T(8,128)(2,1)S(1)}, u32[]{:S(2)}, u32[]{:S(2)}) collective-permute-start(bf16[528,128]{1,0:T(8,128)(2,1)S(1)} %get-tuple-element.30), channel_id=1, source_target_pairs={{0,8},{1,13},{2,10},{3,15},{4,12},{5,9},{6,14},{7,11},{8,0},{9,5},... | collective-permute-start | bytes 405512 | tf_op jit(solution)/shard_map/ppermute | solution.py:487
  17.8 1.3 %collective-permute-done.8.refs_3_ = bf16[272,128]{1,0:T(8,128)(2,1)S(1)} collective-permute-done((bf16[272,128]{1,0:T(8,128)(2,1)S(1)}, bf16[272,128]{1,0:T(8,128)(2,1)S(1)}, u32[]{:S(2)}, u32[]{:S(2)}) %collective-permute-start.8) | collective-permute-done | bytes 69664 | tf_op jit(solution)/shard_map/ppermute | solution.py:483
  19.1 1.8 %collective-permute-start.9 = (bf16[272,128]{1,0:T(8,128)(2,1)S(1)}, bf16[272,128]{1,0:T(8,128)(2,1)S(1)}, u32[]{:S(2)}, u32[]{:S(2)}) collective-permute-start(bf16[272,128]{1,0:T(8,128)(2,1)S(1)} %collective-permute-done.8.refs_3_), channel_id=1, source_target_pairs={{0,2},{1,3},{2,0},{3,1},{4,6},{5,7},{6,4},{7,5},{8,10},{9,11},{10,... | collective-permute-start | bytes 208904 | tf_op jit(solution)/shard_map/ppermute | solution.py:379
  20.9 0.0 collective-permute-done.3.up_pair
  20.9 1.1 %stage.1.weight_ref = bf16[2048,768]{1,0:T(8,128)(2,1)S(1)} custom-call(bf16[4,16,128]{2,1,0:T(8,128)(2,1)S(1)} %get-tuple-element.25.after_ref.tags_ref, bf16[192,2048]{1,0:T(8,128)(2,1)S(1)} %bitcast.13, bf16[192,2048]{1,0:T(8,128)(2,1)S(1)} %bitcast.15, bf16[192,2048]{1,0:T(8,128)(2,1)S(1)} %collective-permute-done.2.gate_pair.after_ref, ...), custom_call_target="tpu_custom_call" | custom-call | bytes 6291456 | tf_op jit(solution)/shard_map/stage/pallas_call | solution.py:490
  22.1 0.0 copy-start.6
  22.1 0.0 copy-start.3
  22.1 3.8 %collective-permute-done.7.refs_2_ = bf16[528,128]{1,0:T(8,128)(2,1)S(1)} collective-permute-done((bf16[528,128]{1,0:T(8,128)(2,1)S(1)}, bf16[528,128]{1,0:T(8,128)(2,1)S(1)}, u32[]{:S(2)}, u32[]{:S(2)}) %collective-permute-start.7) | collective-permute-done | bytes 135200 | tf_op jit(solution)/shard_map/ppermute | solution.py:483
  25.9 0.0 collective-permute-done.9.refs_4_
  25.9 0.0 collective-permute-done.5.refs_0_
  25.9 0.0 collective-permute-done.6.refs_1_
  25.9 0.0 copy-done.5
  25.9 0.7 %hidden_units.1 = (bf16[128,384]{1,0:T(8,128)(2,1)S(1)}, bf16[4,144,128]{2,1,0:T(8,128)(2,1)S(1)}) custom-call(f32[16,128]{1,0:T(8,128)S(1)} %bitcast.17, bf16[2048,768]{1,0:T(8,128)(2,1)S(1)} %stage.1.weight_ref, bf16[528,128]{1,0:T(8,128)(2,1)S(1)} %collective-permute-done.5.refs_0_, bf16[528,128]{1,0:T(8,128)(2,1)S(1)} %collective-permute-done.6.refs_1_, ...), custom_call_target="tpu_custom_call" | custom-call | tf_op jit(solution)/shard_map/hidden_units/pallas_call | solution.py:506
  26.7 1.6 %collective-permute-start.11 = (bf16[128,384]{1,0:T(8,128)(2,1)S(1)}, bf16[128,384]{1,0:T(8,128)(2,1)S(1)}, u32[]{:S(2)}, u32[]{:S(2)}) collective-permute-start(bf16[128,384]{1,0:T(8,128)(2,1)S(1)} %get-tuple-element.34.act_ref), channel_id=1, source_target_pairs={{0,2},{1,3},{2,0},{3,1},{4,6},{5,7},{6,4},{7,5},{8,10},{9,11},{10,... | collective-permute-start | bytes 294920 | tf_op jit(solution)/shard_map/ppermute | solution.py:379
  28.2 1.1 %collective-permute-start.10 = (bf16[4,144,128]{2,1,0:T(8,128)(2,1)S(1)}, bf16[4,144,128]{2,1,0:T(8,128)(2,1)S(1)}, u32[]{:S(2)}, u32[]{:S(2)}) collective-permute-start(bf16[4,144,128]{2,1,0:T(8,128)(2,1)S(1)} %get-tuple-element.33), channel_id=1, source_target_pairs={{0,1},{1,0},{2,3},{3,2},{4,5},{5,4},{6,7},{7,6},{8,9},{9,8},{10,11... | collective-permute-start | bytes 442376 | tf_op jit(solution)/shard_map/ppermute | solution.py:376
  29.3 0.0 collective-permute-start.12
  29.3 2.8 %collective-permute-done.11.act_half_ref = bf16[128,384]{1,0:T(8,128)(2,1)S(1)} collective-permute-done((bf16[128,384]{1,0:T(8,128)(2,1)S(1)}, bf16[128,384]{1,0:T(8,128)(2,1)S(1)}, u32[]{:S(2)}, u32[]{:S(2)}) %collective-permute-start.11) | collective-permute-done | bytes 98336 | tf_op jit(solution)/shard_map/ppermute | solution.py:379
  32.1 0.1 collective-permute-start.13
  32.2 0.0 collective-permute-done.10.side_ref
  32.2 0.0 copy-done.6
  32.2 0.8 %select.1.after_ref.chosen_ref = bf16[64,256]{1,0:T(8,128)(2,1)S(1)} custom-call(s32[8]{0:T(128)S(1)} %copy-done.6, bf16[4,144,128]{2,1,0:T(8,128)(2,1)S(1)} %collective-permute-done.10.side_ref, bf16[528,128]{1,0:T(8,128)(2,1)S(1)} %collective-permute-done.5.refs_0_, bf16[528,128]{1,0:T(8,128)(2,1)S(1)} %collective-permute-done.6.refs_1_, ...), custom_call_target="tpu_custom_call" | custom-call | bytes 1048576 | tf_op jit(solution)/shard_map/select/pallas_call | solution.py:523
  33.0 0.0 collective-permute-done.12.act_core_ref
  33.0 0.4 collective-permute-done.13.act_both_ref
  33.4 0.0 copy-done.3
  33.4 0.8 %down.1 = bf16[8,128,128]{2,1,0:T(8,128)(2,1)S(1)} custom-call(bf16[64,256]{1,0:T(8,128)(2,1)S(1)} %select.1.after_ref.chosen_ref, s32[8]{0:T(128)S(1)} %copy-done.6, bf16[128,384]{1,0:T(8,128)(2,1)S(1)} %get-tuple-element.34.act_ref, bf16[128,384]{1,0:T(8,128)(2,1)S(1)} %collective-permute-done.11.act_half_ref, ...), custom_call_target="tpu_custom_call" | custom-call | tf_op jit(solution)/shard_map/down/pallas_call | solution.py:532
  34.2 13.6 %all_to_all.5.came_ref = bf16[8,128,128]{2,1,0:T(8,128)(2,1)S(1)} all-to-all(bf16[8,128,128]{2,1,0:T(8,128)(2,1)S(1)} %down.1), channel_id=1, replica_groups=mesh['ep'=8,'tp'=4] {'ep'}, dimensions={0} | all-to-all | bytes 524288 | tf_op jit(solution)/shard_map/all_to_all | solution.py:545
  47.8 0.8 %combine.1 = bf16[64,512]{1,0:T(8,128)(2,1)} custom-call(bf16[64,256]{1,0:T(8,128)(2,1)S(1)} %select.1.after_ref.chosen_ref, bf16[8,128,128]{2,1,0:T(8,128)(2,1)S(1)} %all_to_all.5.came_ref), custom_call_target="tpu_custom_call" | custom-call | tf_op jit(solution)/shard_map/combine/pallas_call | solution.py:546
  (6 shorter events, 0.1 us)
Async XLA Ops:
  0.0 0.9 %copy-start.9 = (bf16[1,512,128]{2,1,0:T(8,128)(2,1)S(1)}, bf16[1,512,128]{2,1,0:T(8,128)(2,1)}, u32[]{:S(2)}) copy-start(bf16[1,512,128]{2,1,0:T(8,128)(2,1)} %param.18) | copy-start | bytes 393220
  0.0 1.0 %copy-start.10 = (bf16[1,512,128]{2,1,0:T(8,128)(2,1)S(1)}, bf16[1,512,128]{2,1,0:T(8,128)(2,1)}, u32[]{:S(2)}) copy-start(bf16[1,512,128]{2,1,0:T(8,128)(2,1)} %param.19) | copy-start | bytes 393220
  0.0 1.0 %copy-start.11 = (bf16[64,512]{1,0:T(8,128)(2,1)S(1)}, bf16[64,512]{1,0:T(8,128)(2,1)}, u32[]{:S(2)}) copy-start(bf16[64,512]{1,0:T(8,128)(2,1)} %query_ref.1) | copy-start | bytes 196612
  0.0 1.0 %copy-start.12 = (bf16[64,128]{1,0:T(8,128)(2,1)S(1)}, bf16[64,128]{1,0:T(8,128)(2,1)}, u32[]{:S(2)}) copy-start(bf16[64,128]{1,0:T(8,128)(2,1)} %new_key_ref.1) | copy-start | bytes 49156
  0.0 1.0 %copy-start.13 = (bf16[64,128]{1,0:T(8,128)(2,1)S(1)}, bf16[64,128]{1,0:T(8,128)(2,1)}, u32[]{:S(2)}) copy-start(bf16[64,128]{1,0:T(8,128)(2,1)} %new_value_ref.1) | copy-start | bytes 49156
  0.0 1.6 %copy-start.4 = (bf16[64,512]{1,0:T(8,128)(2,1)S(1)}, bf16[64,512]{1,0:T(8,128)(2,1)}, u32[]{:S(2)}) copy-start(bf16[64,512]{1,0:T(8,128)(2,1)} %residual_ref.1) | copy-start | bytes 196612
  0.0 1.8 %copy-start = (bf16[512,2048]{1,0:T(8,128)(2,1)S(1)}, bf16[512,2048]{1,0:T(8,128)(2,1)}, u32[]{:S(2)}) copy-start(bf16[512,2048]{1,0:T(8,128)(2,1)} %weight_ref.1) | copy-start | bytes 6291460
  0.0 10.7 %copy-start.7 = (s32[64,2]{0,1:T(2,128)S(1)}, s32[64,2]{0,1:T(2,128)}, u32[]{:S(2)}) copy-start(s32[64,2]{0,1:T(2,128)} %param.25) | copy-start | bytes 1540
  0.1 10.7 %copy-start.8 = (f32[64,2]{0,1:T(2,128)S(1)}, f32[64,2]{0,1:T(2,128)}, u32[]{:S(2)}) copy-start(f32[64,2]{0,1:T(2,128)} %param.26) | copy-start | bytes 1540
  0.1 10.9 %copy-start.1 = (bf16[1,2048,192]{1,2,0:T(8,128)(2,1)S(1)}, bf16[1,2048,192]{1,2,0:T(8,128)(2,1)}, u32[]{:S(2)}) copy-start(bf16[1,2048,192]{1,2,0:T(8,128)(2,1)} %param.27) | copy-start | bytes 2359300
  0.1 11.4 %copy-start.2 = (bf16[1,2048,192]{1,2,0:T(8,128)(2,1)S(1)}, bf16[1,2048,192]{1,2,0:T(8,128)(2,1)}, u32[]{:S(2)}) copy-start(bf16[1,2048,192]{1,2,0:T(8,128)(2,1)} %param.28) | copy-start | bytes 2359300
  2.3 1.5 %collective-permute-start = (bf16[64,1024]{1,0:T(8,128)(2,1)S(1)}, bf16[64,1024]{1,0:T(8,128)(2,1)S(1)}, u32[]{:S(2)}, u32[]{:S(2)}) collective-permute-start(bf16[64,1024]{1,0:T(8,128)(2,1)S(1)} %get-tuple-element.21), channel_id=1, source_target_pairs={{0,1},{1,0},{2,3},{3,2},{4,5},{5,4},{6,7},{7,6},{8,9},{9,8},{10,11... | collective-permute-start | bytes 393224 | tf_op jit(solution)/shard_map/ppermute | solution.py:376
  3.9 6.7 %collective-permute-start.1 = (bf16[64,1024]{1,0:T(8,128)(2,1)S(1)}, bf16[64,1024]{1,0:T(8,128)(2,1)S(1)}, u32[]{:S(2)}, u32[]{:S(2)}) collective-permute-start(bf16[64,1024]{1,0:T(8,128)(2,1)S(1)} %get-tuple-element.23), channel_id=1, source_target_pairs={{0,2},{1,3},{2,0},{3,1},{4,6},{5,7},{6,4},{7,5},{8,10},{9,11},{10,... | collective-permute-start | bytes 393224 | tf_op jit(solution)/shard_map/ppermute | solution.py:379
  10.6 1.4 %collective-permute-start.4 = (bf16[64,1024]{1,0:T(8,128)(2,1)S(1)}, bf16[64,1024]{1,0:T(8,128)(2,1)S(1)}, u32[]{:S(2)}, u32[]{:S(2)}) collective-permute-start(bf16[64,1024]{1,0:T(8,128)(2,1)S(1)} %add_half.1.after_ref.part_ref), channel_id=1, source_target_pairs={{0,1},{1,0},{2,3},{3,2},{4,5},{5,4},{6,7},{7,6},{8,9},{9,8},{10,11... | collective-permute-start | bytes 393224 | tf_op jit(solution)/shard_map/ppermute | solution.py:376
  11.0 5.2 %collective-permute-start.2 = (bf16[192,2048]{1,0:T(8,128)(2,1)S(1)}, bf16[192,2048]{1,0:T(8,128)(2,1)S(1)}, u32[]{:S(2)}, u32[]{:S(2)}) collective-permute-start(bf16[192,2048]{1,0:T(8,128)(2,1)S(1)} %bitcast.12), channel_id=1, source_target_pairs={{0,1},{1,0},{2,3},{3,2},{4,5},{5,4},{6,7},{7,6},{8,9},{9,8},{10,11... | collective-permute-start | bytes 2359304 | tf_op jit(solution)/shard_map/ppermute | solution.py:376
  11.5 9.4 %collective-permute-start.3 = (bf16[192,2048]{1,0:T(8,128)(2,1)S(1)}, bf16[192,2048]{1,0:T(8,128)(2,1)S(1)}, u32[]{:S(2)}, u32[]{:S(2)}) collective-permute-start(bf16[192,2048]{1,0:T(8,128)(2,1)S(1)} %bitcast.14), channel_id=1, source_target_pairs={{0,1},{1,0},{2,3},{3,2},{4,5},{5,4},{6,7},{7,6},{8,9},{9,8},{10,11... | collective-permute-start | bytes 2359304 | tf_op jit(solution)/shard_map/ppermute | solution.py:376
  12.3 6.8 %collective-permute-start.8 = (bf16[272,128]{1,0:T(8,128)(2,1)S(1)}, bf16[272,128]{1,0:T(8,128)(2,1)S(1)}, u32[]{:S(2)}, u32[]{:S(2)}) collective-permute-start(bf16[272,128]{1,0:T(8,128)(2,1)S(1)} %get-tuple-element.32), channel_id=1, source_target_pairs={{0,24},{1,29},{2,26},{3,31},{4,28},{5,25},{6,30},{7,27},{8,16},{9,... | collective-permute-start | bytes 208904 | tf_op jit(solution)/shard_map/ppermute | solution.py:483
  16.2 9.7 %collective-permute-start.7 = (bf16[528,128]{1,0:T(8,128)(2,1)S(1)}, bf16[528,128]{1,0:T(8,128)(2,1)S(1)}, u32[]{:S(2)}, u32[]{:S(2)}) collective-permute-start(bf16[528,128]{1,0:T(8,128)(2,1)S(1)} %get-tuple-element.31), channel_id=1, source_target_pairs={{0,16},{1,21},{2,18},{3,23},{4,20},{5,17},{6,22},{7,19},{8,24},{9,... | collective-permute-start | bytes 405512 | tf_op jit(solution)/shard_map/ppermute | solution.py:483
  16.4 9.5 %collective-permute-start.5 = (bf16[528,128]{1,0:T(8,128)(2,1)S(1)}, bf16[528,128]{1,0:T(8,128)(2,1)S(1)}, u32[]{:S(2)}, u32[]{:S(2)}) collective-permute-start(bf16[528,128]{1,0:T(8,128)(2,1)S(1)} %get-tuple-element.29), channel_id=1, source_target_pairs={{0,0},{1,5},{2,2},{3,7},{4,4},{5,1},{6,6},{7,3},{8,8},{9,13},{10,1... | collective-permute-start | bytes 405512 | tf_op jit(solution)/shard_map/ppermute | solution.py:487
  17.1 8.8 %copy-start.5 = (f32[2048]{0:T(1024)S(1)}, f32[2048]{0:T(1024)}, u32[]{:S(2)}) copy-start(f32[2048]{0:T(1024)} %param.24) | copy-start | bytes 24580
  17.1 8.8 %collective-permute-start.6 = (bf16[528,128]{1,0:T(8,128)(2,1)S(1)}, bf16[528,128]{1,0:T(8,128)(2,1)S(1)}, u32[]{:S(2)}, u32[]{:S(2)}) collective-permute-start(bf16[528,128]{1,0:T(8,128)(2,1)S(1)} %get-tuple-element.30), channel_id=1, source_target_pairs={{0,8},{1,13},{2,10},{3,15},{4,12},{5,9},{6,14},{7,11},{8,0},{9,5},... | collective-permute-start | bytes 405512 | tf_op jit(solution)/shard_map/ppermute | solution.py:487
  19.1 6.8 %collective-permute-start.9 = (bf16[272,128]{1,0:T(8,128)(2,1)S(1)}, bf16[272,128]{1,0:T(8,128)(2,1)S(1)}, u32[]{:S(2)}, u32[]{:S(2)}) collective-permute-start(bf16[272,128]{1,0:T(8,128)(2,1)S(1)} %collective-permute-done.8.refs_3_), channel_id=1, source_target_pairs={{0,2},{1,3},{2,0},{3,1},{4,6},{5,7},{6,4},{7,5},{8,10},{9,11},{10,... | collective-permute-start | bytes 208904 | tf_op jit(solution)/shard_map/ppermute | solution.py:379
  22.1 10.2 %copy-start.6 = (s32[8]{0:T(128)S(1)}, s32[8]{0:T(128)}, u32[]{:S(2)}) copy-start(s32[8]{0:T(128)} %order_vmem.1) | copy-start | bytes 100
  22.1 11.3 %copy-start.3 = (bf16[1,768,512]{2,1,0:T(8,128)(2,1)S(1)}, bf16[1,768,512]{2,1,0:T(8,128)(2,1)}, u32[]{:S(2)}) copy-start(bf16[1,768,512]{2,1,0:T(8,128)(2,1)} %param.29) | copy-start | bytes 2359300
  26.7 5.4 %collective-permute-start.11 = (bf16[128,384]{1,0:T(8,128)(2,1)S(1)}, bf16[128,384]{1,0:T(8,128)(2,1)S(1)}, u32[]{:S(2)}, u32[]{:S(2)}) collective-permute-start(bf16[128,384]{1,0:T(8,128)(2,1)S(1)} %get-tuple-element.34.act_ref), channel_id=1, source_target_pairs={{0,2},{1,3},{2,0},{3,1},{4,6},{5,7},{6,4},{7,5},{8,10},{9,11},{10,... | collective-permute-start | bytes 294920 | tf_op jit(solution)/shard_map/ppermute | solution.py:379
  28.2 4.0 %collective-permute-start.10 = (bf16[4,144,128]{2,1,0:T(8,128)(2,1)S(1)}, bf16[4,144,128]{2,1,0:T(8,128)(2,1)S(1)}, u32[]{:S(2)}, u32[]{:S(2)}) collective-permute-start(bf16[4,144,128]{2,1,0:T(8,128)(2,1)S(1)} %get-tuple-element.33), channel_id=1, source_target_pairs={{0,1},{1,0},{2,3},{3,2},{4,5},{5,4},{6,7},{7,6},{8,9},{9,8},{10,11... | collective-permute-start | bytes 442376 | tf_op jit(solution)/shard_map/ppermute | solution.py:376
  29.3 3.7 %collective-permute-start.12 = (bf16[128,384]{1,0:T(8,128)(2,1)S(1)}, bf16[128,384]{1,0:T(8,128)(2,1)S(1)}, u32[]{:S(2)}, u32[]{:S(2)}) collective-permute-start(bf16[128,384]{1,0:T(8,128)(2,1)S(1)} %get-tuple-element.34.act_ref), channel_id=1, source_target_pairs={{0,1},{1,0},{2,3},{3,2},{4,5},{5,4},{6,7},{7,6},{8,9},{9,8},{10,11... | collective-permute-start | bytes 294920 | tf_op jit(solution)/shard_map/ppermute | solution.py:376
  32.1 1.3 %collective-permute-start.13 = (bf16[128,384]{1,0:T(8,128)(2,1)S(1)}, bf16[128,384]{1,0:T(8,128)(2,1)S(1)}, u32[]{:S(2)}, u32[]{:S(2)}) collective-permute-start(bf16[128,384]{1,0:T(8,128)(2,1)S(1)} %collective-permute-done.11.act_half_ref), channel_id=1, source_target_pairs={{0,1},{1,0},{2,3},{3,2},{4,5},{5,4},{6,7},{7,6},{8,9},{9,8},{10,11... | collective-permute-start | bytes 294920 | tf_op jit(solution)/shard_map/ppermute | solution.py:376

commit v8 on v7

--- a/solution.py
+++ b/solution.py
@@ -90,21 +90,33 @@
     context_ref[...] = jnp.concatenate(pieces, axis=1)
 
 
-def project_kernel(context_ref, residual_ref, weight_ref, keep_ref, give_ref):
+def give_kernel(context_ref, weight_ref, give_ref):
+    core = lax.axis_index("tp") % 2
+    width = context_ref.shape[1]
+    context = context_ref[...]
+    for i in range(2):
+        start = pl.multiple_of((2 * i + 1 - core) * width, width)
+        part = dot(context, weight_ref[:, pl.ds(start, width)])
+        give_ref[:, i * width : (i + 1) * width] = part.astype(BF16)
+
+
+def keep_kernel(after_ref, context_ref, residual_ref, weight_ref, keep_ref):
+    del after_ref
     tp = lax.axis_index("tp")
     half, core = tp // 2, tp % 2
-    width = residual_ref.shape[1]
+    width = context_ref.shape[1]
     context = context_ref[...]
-    for i, block in enumerate((1 - core, 3 - core, core, core + 2)):
-        start = pl.multiple_of(block * width, width)
+    for i in range(2):
+        start = pl.multiple_of((2 * i + core) * width, width)
         part = dot(context, weight_ref[:, pl.ds(start, width)])
-        columns = slice((i % 2) * width, (i % 2 + 1) * width)
-        if i < 2:
-            give_ref[:, columns] = part.astype(BF16)
-        else:
-            keep_ref[:, columns] = part + jnp.where(
-                half == i - 2, residual_ref[...].astype(F32), 0.0
-            )
+        keep_ref[:, i * width : (i + 1) * width] = part + jnp.where(
+            half == i, residual_ref[...].astype(F32), 0.0
+        )
+
+
+def step(k, peers):
+    near = peers // 2
+    return near - 1 - k if k < near else k
 
 
 def earlier_tokens(tokens):
@@ -125,9 +137,9 @@
     core = lax.axis_index("tp") % 2
     top, tokens = expert_ref.shape
     rows_each = pick_ref.shape[0] // peers
-    peer = jnp.bitwise_xor(
-        2 * lax.broadcasted_iota(jnp.int32, (peers, tokens), 0) + core, me
-    )
+    number = lax.broadcasted_iota(jnp.int32, (peers, tokens), 0)
+    near = peers // 2
+    peer = jnp.bitwise_xor(2 * jnp.where(number < near, near - 1 - number, number) + core, me)
     weights = weight_ref[...]
     mixing = (weights / jnp.sum(weights, axis=0, keepdims=True)).astype(BF16).astype(F32)
     mix_of = jnp.zeros((peers, tokens), F32)
@@ -165,7 +177,7 @@
             (got[k][got[k].shape[0] - TAGS :, :], core),
             (side_ref[k, side_ref.shape[1] - TAGS :, :], 1 - core),
         ):
-            here = order_ref[jnp.bitwise_xor(me, 2 * k + parity)] == me
+            here = order_ref[jnp.bitwise_xor(me, 2 * step(k, peers) + parity)] == me
             names = names + jnp.where(here, tags.astype(F32), 0.0)
     expert = lax.broadcasted_iota(jnp.int32, (experts, tokens), 0).astype(F32)
     named = jnp.zeros((experts, tokens), F32)
@@ -189,13 +201,15 @@
     out_ref[...] = (sum_ref[...] + came_ref[...].astype(F32)).astype(BF16)
 
 
-def gather_kernel(first, split, after_ref, part_ref, other_ref, pick_ref, tags_ref, *send_refs):
+def gather_kernel(members, split, after_ref, part_ref, other_ref, pick_ref, tags_ref, *send_refs):
     del after_ref
     tp = lax.axis_index("tp")
     mine, core = tp // 2, tp % 2
-    count = len(split)
+    count = len(members)
     rows_each = pick_ref.shape[0] // tags_ref.shape[0]
-    pick = pick_ref[first * rows_each : (first + count) * rows_each, :]
+    pick = jnp.concatenate(
+        [pick_ref[k * rows_each : (k + 1) * rows_each, :] for k in members], axis=0
+    )
     width = part_ref.shape[1] // 2
     blocks = width // LANES
     tall = blocks * rows_each
@@ -218,7 +232,7 @@
                 piece = pick[k * rows_each : (k + 1) * rows_each]
                 put(send_refs[k], dot(piece, source[:, columns]).astype(BF16), parity * tall)
     for k in range(count):
-        send_refs[k][send_refs[k].shape[0] - TAGS :, :] = tags_ref[first + k]
+        send_refs[k][send_refs[k].shape[0] - TAGS :, :] = tags_ref[members[k]]
 
 
 def stage_kernel(after_ref, gate, up, gate_pair, up_pair, out_ref, held_ref, sems):
@@ -321,7 +335,9 @@
     fetch.wait()
     for group, result in enumerate(outcomes):
         for k in range(peers):
-            request = jnp.bitwise_xor(me, 2 * k + (core if group == 0 else 1 - core))
+            request = jnp.bitwise_xor(
+                me, 2 * step(k, peers) + (core if group == 0 else 1 - core)
+            )
             place = order_ref[request]
             if group == 0:
                 start = pl.multiple_of((core if split[k] else tp) * tall, tall)
@@ -411,14 +427,23 @@
         ),
         name="attend",
     )(begun, cache_lengths, queries, new_keys, new_values, key_cache[0], value_cache[0])
-    keep, give = pl.pallas_call(
-        project_kernel,
-        out_shape=(shape((tokens, 2 * width), F32), shape((tokens, 2 * width), BF16)),
-        in_specs=[vmem()] * 3,
-        out_specs=(vmem(), vmem()),
+    give = pl.pallas_call(
+        give_kernel,
+        out_shape=shape((tokens, 2 * width), BF16),
+        in_specs=[vmem()] * 2,
+        out_specs=vmem(),
         compiler_params=params(16),
-        name="project",
-    )(context, residual, out_weight)
+        name="project_given",
+    )(context, out_weight)
+    keep = pl.pallas_call(
+        keep_kernel,
+        out_shape=shape((tokens, 2 * width), F32),
+        in_specs=[pl.BlockSpec(memory_space=pl.ANY)] + [vmem()] * 3,
+        out_specs=vmem(),
+        compiler_params=params(16),
+        cost_estimate=pl.CostEstimate(flops=0, bytes_accessed=2 * MIB, transcendentals=0),
+        name="project_kept",
+    )(give, context, residual, out_weight)
 
     summed, send = pl.pallas_call(
         add_core_kernel,
@@ -454,37 +479,38 @@
     near = peers // 2
     split = [k >= near and (k - near) % 2 == 1 for k in range(peers)]
 
-    def gather(first, last, after):
-        return pl.pallas_call(
-            functools.partial(gather_kernel, first, split[first:last]),
+    def gather(members, after):
+        sent = pl.pallas_call(
+            functools.partial(gather_kernel, members, [split[k] for k in members]),
             out_shape=[
-                shape(((2 if split[k] else 4) * tall + TAGS, LANES), BF16)
-                for k in range(first, last)
+                shape(((2 if split[k] else 4) * tall + TAGS, LANES), BF16) for k in members
             ],
             in_specs=[pl.BlockSpec(memory_space=pl.ANY)] + [vmem()] * 4,
-            out_specs=[vmem()] * (last - first),
+            out_specs=[vmem()] * len(members),
             compiler_params=params(8),
             cost_estimate=pl.CostEstimate(
-                flops=(20 * 10**9 if first else 0), bytes_accessed=MIB, transcendentals=0
+                flops=(20 * 10**9 if members[0] >= near else 0),
+                bytes_accessed=MIB,
+                transcendentals=0,
             ),
             name="gather_rows",
         )(after, part, other, pick, tags)
+        return dict(zip(members, sent))
 
     def route(k):
         return [
-            (e * tp_count + t, (e ^ (2 * k + t % 2)) * tp_count + t)
+            (e * tp_count + t, (e ^ (2 * step(k, peers) + t % 2)) * tp_count + t)
             for e in range(ep_count)
             for t in range(tp_count)
         ]
 
-    far_send = list(gather(near, peers, tags))
+    send = gather(list(reversed(range(near, peers))), tags)
     gate, up, tags = lax.optimization_barrier((gate, up, tags))
-    far = [
-        lax.ppermute(x, ("ep", "tp"), route(near + k)) for k, x in enumerate(far_send)
-    ]
     gate_pair, up_pair = swap_core(gate), swap_core(up)
-    near_send = gather(0, near, gate_pair)
-    got = [lax.ppermute(x, ("ep", "tp"), route(k)) for k, x in enumerate(near_send)] + far
+    early = near // 2
+    send.update(gather(list(range(early, near)), up_pair))
+    send.update(gather(list(range(early)), gate_pair))
+    got = [lax.ppermute(send[k], ("ep", "tp"), route(k)) for k in range(peers)]
     halves = [swap_half(got[k]) for k in range(peers) if split[k]]
 
     weights = pl.pallas_call(

time: 48.8 us -> 48.1 us (0.986)
  starting transfers between devices: 13.9 us -> 13.3 us
    ppermute x7, starting transfers between devices: 2.35 us -> 1.67 us  [swap_core(): return lax.ppermute(x, 'tp', [(i, i ^ 1) for i in range(tp_count)])]
    pallas_call x3 -> x5, Pallas kernels: 0.93 us -> 1.17 us  [the longest x3 0.57 us: gather(): pl.pallas_call(functools.partial(gather_kernel, members, [split[k] for k...]
  transfers between devices with their start and end apart: 14 -> 14, of which waited for: 7 -> 7; matrix products, arithmetic and copies ran while one was open for 0% -> 0% of each run, Pallas kernels for 5% -> 6%
where the time goes in v8:
time: 48.1 us; the launch traced here: 47.9 us
  blocking collectives  13.5 us (28%)
  starting transfers between devices  13.3 us (28%)
  waiting for transfers between devices  13.3 us (28%)
  Pallas kernels  6.25 us (13%)
  between operations  1.03 us (2%)
    all_to_all x1, blocking collectives, shards(): came = lax.all_to_all(result, 'ep', split_axis=0, concat_axis=0, tiled=True)  13.5 us
    ppermute x3, waiting for transfers between devices, swap_half(): return lax.ppermute(x, 'tp', [(i, i ^ 2) for i in range(tp_count)])  6.85 us
    ppermute x3, starting transfers between devices, swap_half(): return lax.ppermute(x, 'tp', [(i, i ^ 2) for i in range(tp_count)])  6.38 us
    ppermute x4, starting transfers between devices, shards(): got = [lax.ppermute(send[k], ('ep', 'tp'), route(k)) for k in range(peers)]  5.3 us
    ppermute x4, waiting for transfers between devices, shards(): got = [lax.ppermute(send[k], ('ep', 'tp'), route(k)) for k in range(peers)]  4.79 us
    ppermute x7, starting transfers between devices, swap_core(): return lax.ppermute(x, 'tp', [(i, i ^ 1) for i in range(tp_count)])  1.67 us
    ppermute x7, waiting for transfers between devices, swap_core(): return lax.ppermute(x, 'tp', [(i, i ^ 1) for i in range(tp_count)])  1.67 us
    pallas_call x1, Pallas kernels, shards(): pl.pallas_call(stage_kernel, out_shape=shape((gate.shape[1], 2 * units),...  1.13 us
  transfers between devices with their start and end apart: 14, of which 7 were waited for; matrix products, arithmetic and copies ran while one was open for 0% of the time, Pallas kernels for 6%

profile of v8, /device:TPU:0, one launch (start us, length us, event | category | flops | bytes accessed | tf_op | source)
XLA Modules:
  0.0 47.9 jit_solution(15618665899579432729)
XLA Ops:
  0.0 0.0 copy-start.11
  0.0 0.0 copy-start.12
  0.0 0.0 copy-start.13
  0.0 0.0 copy-start.9
  0.0 0.0 copy-start
  0.0 0.0 copy-start.4
  0.8 0.0 copy-done.11
  0.9 0.0 copy-done.12
  0.9 0.0 copy-done.13
  0.9 0.1 copy-done.9
  1.0 0.1 copy-done.10
  1.0 0.6 %attend.1.context_ref = bf16[64,512]{1,0:T(8,128)(2,1)S(1)} custom-call(f32[8,128]{1,0:T(8,128)S(1)} %begin.1.after_ref, s32[1]{0:T(128)S(6)} %copy.16.length_ref, bf16[64,512]{1,0:T(8,128)(2,1)S(1)} %copy-done.11, bf16[64,128]{1,0:T(8,128)(2,1)S(1)} %copy-done.12, bf16[64,128]{1,0:T(8,128)(2,1)S(1)} %copy-done.13, bf16[512,128]{1,0:T(8,128)(2,1)S(1)} %bitcast.20, ...), custom_call_target="tpu_custom_call" | custom-call | flops 200000000 | bytes 524288 | tf_op jit(solution)/shard_map/attend/pallas_call | solution.py:418
  1.6 0.2 copy-done
  1.8 0.3 project_given.1.after_ref
  2.1 0.5 %collective-permute-start = (bf16[64,1024]{1,0:T(8,128)(2,1)S(1)}, bf16[64,1024]{1,0:T(8,128)(2,1)S(1)}, u32[]{:S(2)}, u32[]{:S(2)}) collective-permute-start(bf16[64,1024]{1,0:T(8,128)(2,1)S(1)} %project_given.1.after_ref), channel_id=1, source_target_pairs={{0,1},{1,0},{2,3},{3,2},{4,5},{5,4},{6,7},{7,6},{8,9},{9,8},{10,11... | collective-permute-start | bytes 393224 | tf_op jit(solution)/shard_map/ppermute | solution.py:392
  2.7 0.0 copy-done.4
  2.7 0.3 project_kept.1.keep_ref
  3.0 0.7 %collective-permute-done.came_ref = bf16[64,1024]{1,0:T(8,128)(2,1)S(1)} collective-permute-done((bf16[64,1024]{1,0:T(8,128)(2,1)S(1)}, bf16[64,1024]{1,0:T(8,128)(2,1)S(1)}, u32[]{:S(2)}, u32[]{:S(2)}) %collective-permute-start) | collective-permute-done | bytes 131104 | tf_op jit(solution)/shard_map/ppermute | solution.py:392
  3.7 2.9 %collective-permute-start.1 = (bf16[64,1024]{1,0:T(8,128)(2,1)S(1)}, bf16[64,1024]{1,0:T(8,128)(2,1)S(1)}, u32[]{:S(2)}, u32[]{:S(2)}) collective-permute-start(bf16[64,1024]{1,0:T(8,128)(2,1)S(1)} %get-tuple-element.17), channel_id=1, source_target_pairs={{0,2},{1,3},{2,0},{3,1},{4,6},{5,7},{6,4},{7,5},{8,10},{9,11},{10,... | collective-permute-start | bytes 393224 | tf_op jit(solution)/shard_map/ppermute | solution.py:395
  6.6 3.8 %collective-permute-done.1.came_ref = bf16[64,1024]{1,0:T(8,128)(2,1)S(1)} collective-permute-done((bf16[64,1024]{1,0:T(8,128)(2,1)S(1)}, bf16[64,1024]{1,0:T(8,128)(2,1)S(1)}, u32[]{:S(2)}, u32[]{:S(2)}) %collective-permute-start.1) | collective-permute-done | bytes 131104 | tf_op jit(solution)/shard_map/ppermute | solution.py:395
  10.4 0.1 collective-permute-start.4
  10.5 0.0 copy-done.7
  10.5 0.0 copy-done.8
  10.5 0.3 route.1
  10.8 0.0 copy-done.1
  10.8 0.5 %collective-permute-start.2 = (bf16[192,2048]{1,0:T(8,128)(2,1)S(1)}, bf16[192,2048]{1,0:T(8,128)(2,1)S(1)}, u32[]{:S(2)}, u32[]{:S(2)}) collective-permute-start(bf16[192,2048]{1,0:T(8,128)(2,1)S(1)} %bitcast.12), channel_id=1, source_target_pairs={{0,1},{1,0},{2,3},{3,2},{4,5},{5,4},{6,7},{7,6},{8,9},{9,8},{10,11... | collective-permute-start | bytes 2359304 | tf_op jit(solution)/shard_map/ppermute | solution.py:392
  11.3 0.0 copy-done.2
  11.3 0.1 collective-permute-start.3
  11.4 0.5 %collective-permute-done.4.other_ref = bf16[64,1024]{1,0:T(8,128)(2,1)S(1)} collective-permute-done((bf16[64,1024]{1,0:T(8,128)(2,1)S(1)}, bf16[64,1024]{1,0:T(8,128)(2,1)S(1)}, u32[]{:S(2)}, u32[]{:S(2)}) %collective-permute-start.4) | collective-permute-done | bytes 131104 | tf_op jit(solution)/shard_map/ppermute | solution.py:392
  11.8 0.2 gather_rows.5
  12.1 3.9 %collective-permute-start.8 = (bf16[272,128]{1,0:T(8,128)(2,1)S(1)}, bf16[272,128]{1,0:T(8,128)(2,1)S(1)}, u32[]{:S(2)}, u32[]{:S(2)}) collective-permute-start(bf16[272,128]{1,0:T(8,128)(2,1)S(1)} %get-tuple-element.24), channel_id=1, source_target_pairs={{0,24},{1,29},{2,26},{3,31},{4,28},{5,25},{6,30},{7,27},{8,16},{9,... | collective-permute-start | bytes 208904 | tf_op jit(solution)/shard_map/ppermute | solution.py:513
  16.0 0.0 collective-permute-start.7
  16.0 0.0 collective-permute-done.2.gate_pair.after_ref
  16.0 0.2 gather_rows.3
  16.2 0.7 %collective-permute-start.5 = (bf16[528,128]{1,0:T(8,128)(2,1)S(1)}, bf16[528,128]{1,0:T(8,128)(2,1)S(1)}, u32[]{:S(2)}, u32[]{:S(2)}) collective-permute-start(bf16[528,128]{1,0:T(8,128)(2,1)S(1)} %gather_rows.3), channel_id=1, source_target_pairs={{0,8},{1,13},{2,10},{3,15},{4,12},{5,9},{6,14},{7,11},{8,0},{9,5},... | collective-permute-start | bytes 405512 | tf_op jit(solution)/shard_map/ppermute | solution.py:513
  16.9 0.0 collective-permute-done.3.up_pair.after_ref
  16.9 0.2 gather_rows.4
  17.1 0.0 copy-start.5
  17.1 0.7 %collective-permute-start.6 = (bf16[528,128]{1,0:T(8,128)(2,1)S(1)}, bf16[528,128]{1,0:T(8,128)(2,1)S(1)}, u32[]{:S(2)}, u32[]{:S(2)}) collective-permute-start(bf16[528,128]{1,0:T(8,128)(2,1)S(1)} %gather_rows.4), channel_id=1, source_target_pairs={{0,0},{1,5},{2,2},{3,7},{4,4},{5,1},{6,6},{7,3},{8,8},{9,13},{10,1... | collective-permute-start | bytes 405512 | tf_op jit(solution)/shard_map/ppermute | solution.py:513
  17.8 1.0 %collective-permute-done.8.refs_3_ = bf16[272,128]{1,0:T(8,128)(2,1)S(1)} collective-permute-done((bf16[272,128]{1,0:T(8,128)(2,1)S(1)}, bf16[272,128]{1,0:T(8,128)(2,1)S(1)}, u32[]{:S(2)}, u32[]{:S(2)}) %collective-permute-start.8) | collective-permute-done | bytes 69664 | tf_op jit(solution)/shard_map/ppermute | solution.py:513
  18.8 1.9 %collective-permute-start.9 = (bf16[272,128]{1,0:T(8,128)(2,1)S(1)}, bf16[272,128]{1,0:T(8,128)(2,1)S(1)}, u32[]{:S(2)}, u32[]{:S(2)}) collective-permute-start(bf16[272,128]{1,0:T(8,128)(2,1)S(1)} %collective-permute-done.8.refs_3_), channel_id=1, source_target_pairs={{0,2},{1,3},{2,0},{3,1},{4,6},{5,7},{6,4},{7,5},{8,10},{9,11},{10,... | collective-permute-start | bytes 208904 | tf_op jit(solution)/shard_map/ppermute | solution.py:395
  20.7 1.1 %stage.1.weight_ref = bf16[2048,768]{1,0:T(8,128)(2,1)S(1)} custom-call(bf16[4,16,128]{2,1,0:T(8,128)(2,1)S(1)} %get-tuple-element.19.after_ref.tags_ref, bf16[192,2048]{1,0:T(8,128)(2,1)S(1)} %bitcast.13, bf16[192,2048]{1,0:T(8,128)(2,1)S(1)} %bitcast.15, bf16[192,2048]{1,0:T(8,128)(2,1)S(1)} %collective-permute-done.2.gate_pair.after_ref, ...), custom_call_target="tpu_custom_call" | custom-call | bytes 6291456 | tf_op jit(solution)/shard_map/stage/pallas_call | solution.py:516
  21.8 0.0 copy-start.6
  21.9 0.0 copy-start.3
  21.9 3.7 %collective-permute-done.7.refs_2_ = bf16[528,128]{1,0:T(8,128)(2,1)S(1)} collective-permute-done((bf16[528,128]{1,0:T(8,128)(2,1)S(1)}, bf16[528,128]{1,0:T(8,128)(2,1)S(1)}, u32[]{:S(2)}, u32[]{:S(2)}) %collective-permute-start.7) | collective-permute-done | bytes 135200 | tf_op jit(solution)/shard_map/ppermute | solution.py:513
  25.6 0.0 collective-permute-done.9.refs_4_
  25.6 0.0 collective-permute-done.5.refs_0_
  25.6 0.0 collective-permute-done.6.refs_1_
  25.6 0.0 copy-done.5
  25.6 0.7 %hidden_units.1 = (bf16[128,384]{1,0:T(8,128)(2,1)S(1)}, bf16[4,144,128]{2,1,0:T(8,128)(2,1)S(1)}) custom-call(f32[16,128]{1,0:T(8,128)S(1)} %bitcast.17, bf16[2048,768]{1,0:T(8,128)(2,1)S(1)} %stage.1.weight_ref, bf16[528,128]{1,0:T(8,128)(2,1)S(1)} %collective-permute-done.5.refs_0_, bf16[528,128]{1,0:T(8,128)(2,1)S(1)} %collective-permute-done.6.refs_1_, ...), custom_call_target="tpu_custom_call" | custom-call | tf_op jit(solution)/shard_map/hidden_units/pallas_call | solution.py:532
  26.3 1.6 %collective-permute-start.11 = (bf16[128,384]{1,0:T(8,128)(2,1)S(1)}, bf16[128,384]{1,0:T(8,128)(2,1)S(1)}, u32[]{:S(2)}, u32[]{:S(2)}) collective-permute-start(bf16[128,384]{1,0:T(8,128)(2,1)S(1)} %get-tuple-element.26.act_ref), channel_id=1, source_target_pairs={{0,2},{1,3},{2,0},{3,1},{4,6},{5,7},{6,4},{7,5},{8,10},{9,11},{10,... | collective-permute-start | bytes 294920 | tf_op jit(solution)/shard_map/ppermute | solution.py:395
  27.9 0.1 collective-permute-start.10
  28.0 0.5 collective-permute-start.12
  28.4 3.0 %collective-permute-done.11.act_half_ref = bf16[128,384]{1,0:T(8,128)(2,1)S(1)} collective-permute-done((bf16[128,384]{1,0:T(8,128)(2,1)S(1)}, bf16[128,384]{1,0:T(8,128)(2,1)S(1)}, u32[]{:S(2)}, u32[]{:S(2)}) %collective-permute-start.11) | collective-permute-done | bytes 98336 | tf_op jit(solution)/shard_map/ppermute | solution.py:395
  31.5 0.0 collective-permute-start.13
  31.5 0.0 collective-permute-done.10.side_ref
  31.5 0.0 copy-done.6
  31.5 0.8 %select.1.after_ref.chosen_ref = bf16[64,256]{1,0:T(8,128)(2,1)S(1)} custom-call(s32[8]{0:T(128)S(1)} %copy-done.6, bf16[4,144,128]{2,1,0:T(8,128)(2,1)S(1)} %collective-permute-done.10.side_ref, bf16[528,128]{1,0:T(8,128)(2,1)S(1)} %collective-permute-done.5.refs_0_, bf16[528,128]{1,0:T(8,128)(2,1)S(1)} %collective-permute-done.6.refs_1_, ...), custom_call_target="tpu_custom_call" | custom-call | bytes 1048576 | tf_op jit(solution)/shard_map/select/pallas_call | solution.py:549
  32.3 0.0 collective-permute-done.12.act_core_ref
  32.3 0.5 %collective-permute-done.13.act_both_ref = bf16[128,384]{1,0:T(8,128)(2,1)S(1)} collective-permute-done((bf16[128,384]{1,0:T(8,128)(2,1)S(1)}, bf16[128,384]{1,0:T(8,128)(2,1)S(1)}, u32[]{:S(2)}, u32[]{:S(2)}) %collective-permute-start.13) | collective-permute-done | bytes 98336 | tf_op jit(solution)/shard_map/ppermute | solution.py:392
  32.8 0.0 copy-done.3
  32.8 0.8 %down.1 = bf16[8,128,128]{2,1,0:T(8,128)(2,1)S(1)} custom-call(bf16[64,256]{1,0:T(8,128)(2,1)S(1)} %select.1.after_ref.chosen_ref, s32[8]{0:T(128)S(1)} %copy-done.6, bf16[128,384]{1,0:T(8,128)(2,1)S(1)} %get-tuple-element.26.act_ref, bf16[128,384]{1,0:T(8,128)(2,1)S(1)} %collective-permute-done.11.act_half_ref, ...), custom_call_target="tpu_custom_call" | custom-call | tf_op jit(solution)/shard_map/down/pallas_call | solution.py:558
  33.5 13.5 %all_to_all.5.came_ref = bf16[8,128,128]{2,1,0:T(8,128)(2,1)S(1)} all-to-all(bf16[8,128,128]{2,1,0:T(8,128)(2,1)S(1)} %down.1), channel_id=1, replica_groups=mesh['ep'=8,'tp'=4] {'ep'}, dimensions={0} | all-to-all | bytes 524288 | tf_op jit(solution)/shard_map/all_to_all | solution.py:571
  47.1 0.8 %combine.1 = bf16[64,512]{1,0:T(8,128)(2,1)} custom-call(bf16[64,256]{1,0:T(8,128)(2,1)S(1)} %select.1.after_ref.chosen_ref, bf16[8,128,128]{2,1,0:T(8,128)(2,1)S(1)} %all_to_all.5.came_ref), custom_call_target="tpu_custom_call" | custom-call | tf_op jit(solution)/shard_map/combine/pallas_call | solution.py:572
  (8 shorter events, 0.1 us)
Async XLA Ops:
  0.0 0.8 %copy-start.11 = (bf16[64,512]{1,0:T(8,128)(2,1)S(1)}, bf16[64,512]{1,0:T(8,128)(2,1)}, u32[]{:S(2)}) copy-start(bf16[64,512]{1,0:T(8,128)(2,1)} %query_ref.1) | copy-start | bytes 196612
  0.0 0.9 %copy-start.12 = (bf16[64,128]{1,0:T(8,128)(2,1)S(1)}, bf16[64,128]{1,0:T(8,128)(2,1)}, u32[]{:S(2)}) copy-start(bf16[64,128]{1,0:T(8,128)(2,1)} %new_key_ref.1) | copy-start | bytes 49156
  0.0 0.9 %copy-start.13 = (bf16[64,128]{1,0:T(8,128)(2,1)S(1)}, bf16[64,128]{1,0:T(8,128)(2,1)}, u32[]{:S(2)}) copy-start(bf16[64,128]{1,0:T(8,128)(2,1)} %new_value_ref.1) | copy-start | bytes 49156
  0.0 1.0 %copy-start.9 = (bf16[1,512,128]{2,1,0:T(8,128)(2,1)S(1)}, bf16[1,512,128]{2,1,0:T(8,128)(2,1)}, u32[]{:S(2)}) copy-start(bf16[1,512,128]{2,1,0:T(8,128)(2,1)} %param.18) | copy-start | bytes 393220
  0.0 1.0 %copy-start.10 = (bf16[1,512,128]{2,1,0:T(8,128)(2,1)S(1)}, bf16[1,512,128]{2,1,0:T(8,128)(2,1)}, u32[]{:S(2)}) copy-start(bf16[1,512,128]{2,1,0:T(8,128)(2,1)} %param.19) | copy-start | bytes 393220
  0.0 1.8 %copy-start = (bf16[512,2048]{1,0:T(8,128)(2,1)S(1)}, bf16[512,2048]{1,0:T(8,128)(2,1)}, u32[]{:S(2)}) copy-start(bf16[512,2048]{1,0:T(8,128)(2,1)} %weight_ref.3) | copy-start | bytes 6291460
  0.0 2.6 %copy-start.4 = (bf16[64,512]{1,0:T(8,128)(2,1)S(1)}, bf16[64,512]{1,0:T(8,128)(2,1)}, u32[]{:S(2)}) copy-start(bf16[64,512]{1,0:T(8,128)(2,1)} %residual_ref.1) | copy-start | bytes 196612
  1.0 9.5 %copy-start.7 = (s32[64,2]{0,1:T(2,128)S(1)}, s32[64,2]{0,1:T(2,128)}, u32[]{:S(2)}) copy-start(s32[64,2]{0,1:T(2,128)} %param.25) | copy-start | bytes 1540
  1.0 9.5 %copy-start.8 = (f32[64,2]{0,1:T(2,128)S(1)}, f32[64,2]{0,1:T(2,128)}, u32[]{:S(2)}) copy-start(f32[64,2]{0,1:T(2,128)} %param.26) | copy-start | bytes 1540
  1.8 9.0 %copy-start.1 = (bf16[1,2048,192]{1,2,0:T(8,128)(2,1)S(1)}, bf16[1,2048,192]{1,2,0:T(8,128)(2,1)}, u32[]{:S(2)}) copy-start(bf16[1,2048,192]{1,2,0:T(8,128)(2,1)} %param.27) | copy-start | bytes 2359300
  1.8 9.5 %copy-start.2 = (bf16[1,2048,192]{1,2,0:T(8,128)(2,1)S(1)}, bf16[1,2048,192]{1,2,0:T(8,128)(2,1)}, u32[]{:S(2)}) copy-start(bf16[1,2048,192]{1,2,0:T(8,128)(2,1)} %param.28) | copy-start | bytes 2359300
  2.1 1.5 %collective-permute-start = (bf16[64,1024]{1,0:T(8,128)(2,1)S(1)}, bf16[64,1024]{1,0:T(8,128)(2,1)S(1)}, u32[]{:S(2)}, u32[]{:S(2)}) collective-permute-start(bf16[64,1024]{1,0:T(8,128)(2,1)S(1)} %project_given.1.after_ref), channel_id=1, source_target_pairs={{0,1},{1,0},{2,3},{3,2},{4,5},{5,4},{6,7},{7,6},{8,9},{9,8},{10,11... | collective-permute-start | bytes 393224 | tf_op jit(solution)/shard_map/ppermute | solution.py:392
  3.7 6.7 %collective-permute-start.1 = (bf16[64,1024]{1,0:T(8,128)(2,1)S(1)}, bf16[64,1024]{1,0:T(8,128)(2,1)S(1)}, u32[]{:S(2)}, u32[]{:S(2)}) collective-permute-start(bf16[64,1024]{1,0:T(8,128)(2,1)S(1)} %get-tuple-element.17), channel_id=1, source_target_pairs={{0,2},{1,3},{2,0},{3,1},{4,6},{5,7},{6,4},{7,5},{8,10},{9,11},{10,... | collective-permute-start | bytes 393224 | tf_op jit(solution)/shard_map/ppermute | solution.py:395
  10.4 1.4 %collective-permute-start.4 = (bf16[64,1024]{1,0:T(8,128)(2,1)S(1)}, bf16[64,1024]{1,0:T(8,128)(2,1)S(1)}, u32[]{:S(2)}, u32[]{:S(2)}) collective-permute-start(bf16[64,1024]{1,0:T(8,128)(2,1)S(1)} %add_half.1.after_ref.part_ref), channel_id=1, source_target_pairs={{0,1},{1,0},{2,3},{3,2},{4,5},{5,4},{6,7},{7,6},{8,9},{9,8},{10,11... | collective-permute-start | bytes 393224 | tf_op jit(solution)/shard_map/ppermute | solution.py:392
  10.8 5.2 %collective-permute-start.2 = (bf16[192,2048]{1,0:T(8,128)(2,1)S(1)}, bf16[192,2048]{1,0:T(8,128)(2,1)S(1)}, u32[]{:S(2)}, u32[]{:S(2)}) collective-permute-start(bf16[192,2048]{1,0:T(8,128)(2,1)S(1)} %bitcast.12), channel_id=1, source_target_pairs={{0,1},{1,0},{2,3},{3,2},{4,5},{5,4},{6,7},{7,6},{8,9},{9,8},{10,11... | collective-permute-start | bytes 2359304 | tf_op jit(solution)/shard_map/ppermute | solution.py:392
  11.3 5.6 %collective-permute-start.3 = (bf16[192,2048]{1,0:T(8,128)(2,1)S(1)}, bf16[192,2048]{1,0:T(8,128)(2,1)S(1)}, u32[]{:S(2)}, u32[]{:S(2)}) collective-permute-start(bf16[192,2048]{1,0:T(8,128)(2,1)S(1)} %bitcast.14), channel_id=1, source_target_pairs={{0,1},{1,0},{2,3},{3,2},{4,5},{5,4},{6,7},{7,6},{8,9},{9,8},{10,11... | collective-permute-start | bytes 2359304 | tf_op jit(solution)/shard_map/ppermute | solution.py:392
  12.1 6.7 %collective-permute-start.8 = (bf16[272,128]{1,0:T(8,128)(2,1)S(1)}, bf16[272,128]{1,0:T(8,128)(2,1)S(1)}, u32[]{:S(2)}, u32[]{:S(2)}) collective-permute-start(bf16[272,128]{1,0:T(8,128)(2,1)S(1)} %get-tuple-element.24), channel_id=1, source_target_pairs={{0,24},{1,29},{2,26},{3,31},{4,28},{5,25},{6,30},{7,27},{8,16},{9,... | collective-permute-start | bytes 208904 | tf_op jit(solution)/shard_map/ppermute | solution.py:513
  16.0 9.6 %collective-permute-start.7 = (bf16[528,128]{1,0:T(8,128)(2,1)S(1)}, bf16[528,128]{1,0:T(8,128)(2,1)S(1)}, u32[]{:S(2)}, u32[]{:S(2)}) collective-permute-start(bf16[528,128]{1,0:T(8,128)(2,1)S(1)} %get-tuple-element.23), channel_id=1, source_target_pairs={{0,16},{1,21},{2,18},{3,23},{4,20},{5,17},{6,22},{7,19},{8,24},{9,... | collective-permute-start | bytes 405512 | tf_op jit(solution)/shard_map/ppermute | solution.py:513
  16.2 9.4 %collective-permute-start.5 = (bf16[528,128]{1,0:T(8,128)(2,1)S(1)}, bf16[528,128]{1,0:T(8,128)(2,1)S(1)}, u32[]{:S(2)}, u32[]{:S(2)}) collective-permute-start(bf16[528,128]{1,0:T(8,128)(2,1)S(1)} %gather_rows.3), channel_id=1, source_target_pairs={{0,8},{1,13},{2,10},{3,15},{4,12},{5,9},{6,14},{7,11},{8,0},{9,5},... | collective-permute-start | bytes 405512 | tf_op jit(solution)/shard_map/ppermute | solution.py:513
  17.1 8.6 %copy-start.5 = (f32[2048]{0:T(1024)S(1)}, f32[2048]{0:T(1024)}, u32[]{:S(2)}) copy-start(f32[2048]{0:T(1024)} %param.24) | copy-start | bytes 24580
  17.1 8.5 %collective-permute-start.6 = (bf16[528,128]{1,0:T(8,128)(2,1)S(1)}, bf16[528,128]{1,0:T(8,128)(2,1)S(1)}, u32[]{:S(2)}, u32[]{:S(2)}) collective-permute-start(bf16[528,128]{1,0:T(8,128)(2,1)S(1)} %gather_rows.4), channel_id=1, source_target_pairs={{0,0},{1,5},{2,2},{3,7},{4,4},{5,1},{6,6},{7,3},{8,8},{9,13},{10,1... | collective-permute-start | bytes 405512 | tf_op jit(solution)/shard_map/ppermute | solution.py:513
  18.8 6.8 %collective-permute-start.9 = (bf16[272,128]{1,0:T(8,128)(2,1)S(1)}, bf16[272,128]{1,0:T(8,128)(2,1)S(1)}, u32[]{:S(2)}, u32[]{:S(2)}) collective-permute-start(bf16[272,128]{1,0:T(8,128)(2,1)S(1)} %collective-permute-done.8.refs_3_), channel_id=1, source_target_pairs={{0,2},{1,3},{2,0},{3,1},{4,6},{5,7},{6,4},{7,5},{8,10},{9,11},{10,... | collective-permute-start | bytes 208904 | tf_op jit(solution)/shard_map/ppermute | solution.py:395
  21.8 9.6 %copy-start.6 = (s32[8]{0:T(128)S(1)}, s32[8]{0:T(128)}, u32[]{:S(2)}) copy-start(s32[8]{0:T(128)} %order_vmem.1) | copy-start | bytes 100
  21.9 10.9 %copy-start.3 = (bf16[1,768,512]{2,1,0:T(8,128)(2,1)S(1)}, bf16[1,768,512]{2,1,0:T(8,128)(2,1)}, u32[]{:S(2)}) copy-start(bf16[1,768,512]{2,1,0:T(8,128)(2,1)} %param.29) | copy-start | bytes 2359300
  26.3 5.1 %collective-permute-start.11 = (bf16[128,384]{1,0:T(8,128)(2,1)S(1)}, bf16[128,384]{1,0:T(8,128)(2,1)S(1)}, u32[]{:S(2)}, u32[]{:S(2)}) collective-permute-start(bf16[128,384]{1,0:T(8,128)(2,1)S(1)} %get-tuple-element.26.act_ref), channel_id=1, source_target_pairs={{0,2},{1,3},{2,0},{3,1},{4,6},{5,7},{6,4},{7,5},{8,10},{9,11},{10,... | collective-permute-start | bytes 294920 | tf_op jit(solution)/shard_map/ppermute | solution.py:395
  27.9 3.6 %collective-permute-start.10 = (bf16[4,144,128]{2,1,0:T(8,128)(2,1)S(1)}, bf16[4,144,128]{2,1,0:T(8,128)(2,1)S(1)}, u32[]{:S(2)}, u32[]{:S(2)}) collective-permute-start(bf16[4,144,128]{2,1,0:T(8,128)(2,1)S(1)} %get-tuple-element.25), channel_id=1, source_target_pairs={{0,1},{1,0},{2,3},{3,2},{4,5},{5,4},{6,7},{7,6},{8,9},{9,8},{10,11... | collective-permute-start | bytes 442376 | tf_op jit(solution)/shard_map/ppermute | solution.py:392
  28.0 4.3 %collective-permute-start.12 = (bf16[128,384]{1,0:T(8,128)(2,1)S(1)}, bf16[128,384]{1,0:T(8,128)(2,1)S(1)}, u32[]{:S(2)}, u32[]{:S(2)}) collective-permute-start(bf16[128,384]{1,0:T(8,128)(2,1)S(1)} %get-tuple-element.26.act_ref), channel_id=1, source_target_pairs={{0,1},{1,0},{2,3},{3,2},{4,5},{5,4},{6,7},{7,6},{8,9},{9,8},{10,11... | collective-permute-start | bytes 294920 | tf_op jit(solution)/shard_map/ppermute | solution.py:392
  31.5 1.3 %collective-permute-start.13 = (bf16[128,384]{1,0:T(8,128)(2,1)S(1)}, bf16[128,384]{1,0:T(8,128)(2,1)S(1)}, u32[]{:S(2)}, u32[]{:S(2)}) collective-permute-start(bf16[128,384]{1,0:T(8,128)(2,1)S(1)} %collective-permute-done.11.act_half_ref), channel_id=1, source_target_pairs={{0,1},{1,0},{2,3},{3,2},{4,5},{5,4},{6,7},{7,6},{8,9},{9,8},{10,11... | collective-permute-start | bytes 294920 | tf_op jit(solution)/shard_map/ppermute | solution.py:392

commit v9 on v8

--- a/solution.py
+++ b/solution.py
@@ -116,7 +116,16 @@
 
 def step(k, peers):
     near = peers // 2
-    return near - 1 - k if k < near else k
+    if isinstance(k, int):
+        return near - 1 - k if k < near else k
+    return jnp.where(k < near, near - 1 - k, k)
+
+
+def peer_numbers(peers, tokens):
+    number = lax.broadcasted_iota(jnp.int32, (peers, tokens), 0)
+    near = peers // 2
+    steps = jnp.where(number < near, near - 1 - number, number)
+    return jnp.bitwise_xor(2 * steps + lax.axis_index("tp") % 2, lax.axis_index("ep"))
 
 
 def earlier_tokens(tokens):
@@ -133,13 +142,9 @@
 
 def route_kernel(peers, after_ref, expert_ref, weight_ref, pick_ref, tags_ref):
     del after_ref
-    me = lax.axis_index("ep")
-    core = lax.axis_index("tp") % 2
     top, tokens = expert_ref.shape
     rows_each = pick_ref.shape[0] // peers
-    number = lax.broadcasted_iota(jnp.int32, (peers, tokens), 0)
-    near = peers // 2
-    peer = jnp.bitwise_xor(2 * jnp.where(number < near, near - 1 - number, number) + core, me)
+    peer = peer_numbers(peers, tokens)
     weights = weight_ref[...]
     mixing = (weights / jnp.sum(weights, axis=0, keepdims=True)).astype(BF16).astype(F32)
     mix_of = jnp.zeros((peers, tokens), F32)
@@ -163,32 +168,64 @@
         tags_ref[k, :1, :rows_each] = dot_t(mix, pick)[:1].astype(BF16)
 
 
-def select_kernel(peers, top, order_ref, side_ref, *refs):
-    got = refs[:peers]
-    chosen_ref = refs[peers]
+def select_kernel(
+    top,
+    order_ref,
+    side_ref,
+    side_core_ref,
+    chosen_ref,
+    swap_ref,
+    rows_ref,
+    mix_ref,
+    inverse_ref,
+):
     me = lax.axis_index("ep")
     core = lax.axis_index("tp") % 2
     tokens = chosen_ref.shape[0]
-    experts = 2 * peers
-    rows_each = chosen_ref.shape[1] // experts
+    peers = side_ref.shape[0]
+    rows_each = chosen_ref.shape[1] // peers
     names = jnp.zeros((TAGS, LANES), F32)
     for k in range(peers):
-        for tags, parity in (
-            (got[k][got[k].shape[0] - TAGS :, :], core),
-            (side_ref[k, side_ref.shape[1] - TAGS :, :], 1 - core),
-        ):
+        for ref, parity in ((side_ref, core), (side_core_ref, 1 - core)):
             here = order_ref[jnp.bitwise_xor(me, 2 * step(k, peers) + parity)] == me
-            names = names + jnp.where(here, tags.astype(F32), 0.0)
-    expert = lax.broadcasted_iota(jnp.int32, (experts, tokens), 0).astype(F32)
-    named = jnp.zeros((experts, tokens), F32)
+            tags = ref[k, ref.shape[1] - TAGS :, :].astype(F32)
+            names = names + jnp.where(here, tags, 0.0)
+    expert = peer_numbers(peers, tokens).astype(F32)
+    named = jnp.zeros((peers, tokens), F32)
     for j in range(top):
         named = named + jnp.where(names[j + 1 : j + 2, :tokens] == expert, 1.0, 0.0)
     rank = slot_numbers(named, tokens)
     slot = lax.broadcasted_iota(jnp.int32, (rows_each, tokens), 0).astype(F32)
     pick = jnp.concatenate(
-        [jnp.where(rank[e : e + 1, :] == slot, 1.0, 0.0) for e in range(experts)], axis=0
+        [jnp.where(rank[k : k + 1, :] == slot, 1.0, 0.0) for k in range(peers)], axis=0
     )
     chosen_ref[...] = pick.T.astype(BF16)
+
+    def place(s, carry):
+        inverse_ref[order_ref[s]] = s
+        return carry
+
+    lax.fori_loop(0, order_ref.shape[0], place, 0)
+    height = rows_ref.shape[1]
+    diagonal = lax.broadcasted_iota(jnp.int32, (rows_each, LANES), 0) == lax.broadcasted_iota(
+        jnp.int32, (rows_each, LANES), 1
+    )
+    row = lax.broadcasted_iota(jnp.int32, (rows_each, swap_ref.shape[1]), 0)
+    column = lax.broadcasted_iota(jnp.int32, (rows_each, swap_ref.shape[1]), 1)
+    for k in range(peers):
+        offset = jnp.bitwise_xor(
+            inverse_ref[jnp.bitwise_xor(me, 2 * step(k, peers) + core)], me
+        )
+        index = step(offset // 2, peers)
+        mine = offset % 2 == core
+        block = jnp.where(mine, side_ref[index], side_core_ref[index])
+        rows_ref[k] = block[:height]
+        tags = block[height:].astype(F32)[0:1, :]
+        mix = jnp.sum(jnp.where(diagonal, tags, 0.0), axis=1, keepdims=True)
+        span = slice(k * rows_each, (k + 1) * rows_each)
+        mix_ref[span, :] = jnp.broadcast_to(mix, (rows_each, LANES))
+        base = (index + jnp.where(mine, 0, peers)) * rows_each
+        swap_ref[span, :] = jnp.where(column == base + row, 1.0, 0.0).astype(BF16)
 
 
 def add_core_kernel(keep_ref, came_ref, sum_ref, send_ref):
@@ -292,79 +329,64 @@
     gate, up = product[:, :units], product[:, units:]
     act_ref[...] = (gate / (1.0 + jnp.exp(-gate)) * up).astype(BF16)
     for k in range(peers):
-        place = 1 - core + (0 if split[k] else 2 * half)
-        start = pl.multiple_of(place * tall, tall)
-        side_ref[k, :tall, :] = got[k][pl.ds(start, tall), :]
-        side_ref[k, tall:, :] = got[k][got[k].shape[0] - TAGS :, :]
+        start = 0 if split[k] else pl.multiple_of(2 * half * tall, 2 * tall)
+        side_ref[k, : 2 * tall, :] = got[k][pl.ds(start, 2 * tall), :]
+        side_ref[k, 2 * tall :, :] = got[k][got[k].shape[0] - TAGS :, :]
 
 
 def down_kernel(
-    split,
+    members,
     rows_each,
     after_ref,
-    order_vmem,
     act_ref,
     act_half_ref,
     act_core_ref,
     act_both_ref,
     down_ref,
-    side_ref,
-    *refs,
+    down_pair_ref,
+    swap_ref,
+    rows_ref,
+    mix_ref,
+    *send_refs,
 ):
     del after_ref
-    peers = len(split)
-    got = refs[:peers]
-    out_ref, order_ref, sem = refs[peers:]
-    fetch = pltpu.make_async_copy(order_vmem, order_ref, sem)
-    fetch.start()
     tp = lax.axis_index("tp")
-    me = lax.axis_index("ep")
     half, core = tp // 2, tp % 2
     units = act_ref.shape[1]
     blocks = down_ref.shape[1] // LANES
     tall = blocks * rows_each
-    here = down_ref[pl.ds(pl.multiple_of(half * units, units), units), :]
-    there = down_ref[pl.ds(pl.multiple_of((1 - half) * units, units), units), :]
-    diagonal = lax.broadcasted_iota(jnp.int32, (rows_each, LANES), 0) == lax.broadcasted_iota(
-        jnp.int32, (rows_each, LANES), 1
-    )
-    outcomes = [
-        dot(near[...], here) + dot(far[...], there)
-        for near, far in ((act_ref, act_half_ref), (act_core_ref, act_both_ref))
-    ]
-    fetch.wait()
-    for group, result in enumerate(outcomes):
-        for k in range(peers):
-            request = jnp.bitwise_xor(
-                me, 2 * step(k, peers) + (core if group == 0 else 1 - core)
-            )
-            place = order_ref[request]
-            if group == 0:
-                start = pl.multiple_of((core if split[k] else tp) * tall, tall)
-                rows = got[k][pl.ds(start, tall), :]
-                tags = got[k][got[k].shape[0] - TAGS :, :]
-            else:
-                rows = side_ref[k, :tall, :]
-                tags = side_ref[k, tall:, :]
-            mix = jnp.sum(
-                jnp.where(diagonal, tags.astype(F32)[0:1, :], 0.0), axis=1, keepdims=True
-            )
+    spans = [slice(k * rows_each, (k + 1) * rows_each) for k in members]
+    swap = jnp.concatenate([swap_ref[span, :] for span in spans], axis=0)
+    near = jnp.concatenate([act_ref[...], act_core_ref[...]], axis=0)
+    far = jnp.concatenate([act_half_ref[...], act_both_ref[...]], axis=0)
+    near, far = dot(swap, near).astype(BF16), dot(swap, far).astype(BF16)
+    here = pl.ds(pl.multiple_of(half * units, units), units)
+    there = pl.ds(pl.multiple_of((1 - half) * units, units), units)
+    for ref, parity in ((down_ref, core), (down_pair_ref, 1 - core)):
+        result = dot(near, ref[here, :]) + dot(far, ref[there, :])
+        for i, k in enumerate(members):
+            mix = mix_ref[spans[i], :]
             for j in range(blocks):
-                piece = slice(j * rows_each, (j + 1) * rows_each)
-                value = rows[piece].astype(F32) + result[
-                    k * rows_each : (k + 1) * rows_each, j * LANES : (j + 1) * LANES
+                piece = pl.ds(
+                    pl.multiple_of(parity * tall + j * rows_each, rows_each), rows_each
+                )
+                value = rows_ref[k, piece, :].astype(F32) + result[
+                    i * rows_each : (i + 1) * rows_each, j * LANES : (j + 1) * LANES
                 ]
-                out_ref[place, piece, :] = (mix * value).astype(BF16)
-
-
-def combine_kernel(rows_each, chosen_ref, came_ref, out_ref):
+                send_refs[i][piece, :] = (mix * value).astype(BF16)
+
+
+def combine_kernel(rows_each, chosen_ref, *refs):
+    came = refs[:-2]
+    keep_ref, give_ref = refs[-2:]
+    core = lax.axis_index("tp") % 2
     chosen = chosen_ref[...]
-    experts, tall, _ = came_ref.shape
-    for j in range(tall // rows_each):
-        rows = jnp.concatenate(
-            [came_ref[e, j * rows_each : (j + 1) * rows_each, :] for e in range(experts)], axis=0
-        )
-        out_ref[:, j * LANES : (j + 1) * LANES] = dot(chosen, rows).astype(BF16)
+    tall = came[0].shape[0] // 2
+    for ref, parity in ((give_ref, 1 - core), (keep_ref, core)):
+        for j in range(tall // rows_each):
+            start = pl.multiple_of(parity * tall + j * rows_each, rows_each)
+            rows = jnp.concatenate([block[pl.ds(start, rows_each), :] for block in came], axis=0)
+            ref[:, j * LANES : (j + 1) * LANES] = dot(chosen, rows).astype(ref.dtype)
 
 
 def shards(
@@ -529,54 +551,91 @@
         name="stage",
     )(tags, gate, up, gate_pair, up_pair)
 
+    down, weights = lax.optimization_barrier((down, weights))
+    down_pair = swap_core(down)
     act, side = pl.pallas_call(
         functools.partial(hidden_units_kernel, split, rows_each),
         out_shape=(
             shape((peers * rows_each, units), BF16),
-            shape((peers, tall + TAGS, LANES), BF16),
+            shape((peers, 2 * tall + TAGS, LANES), BF16),
         ),
         in_specs=[vmem()] * (2 + peers + len(halves)),
         out_specs=(vmem(), vmem()),
         compiler_params=params(16),
+        cost_estimate=pl.CostEstimate(
+            flops=20 * 10**9, bytes_accessed=MIB, transcendentals=0
+        ),
         name="hidden_units",
     )(norm_gain.reshape(-1, LANES), weights, *got, *halves)
 
     act_half = swap_half(act)
     act_core = swap_core(act)
-    side = swap_core(side)
+    side_core = swap_core(side)
     act_both = swap_core(act_half)
 
-    chosen = pl.pallas_call(
-        functools.partial(select_kernel, peers, top),
-        out_shape=shape((tokens, ep_count * rows_each), BF16),
-        in_specs=[pl.BlockSpec(memory_space=pltpu.SMEM)] + [vmem()] * (1 + peers),
-        out_specs=vmem(),
+    chosen, swap, rows, mixes = pl.pallas_call(
+        functools.partial(select_kernel, top),
+        out_shape=(
+            shape((tokens, peers * rows_each), BF16),
+            shape((peers * rows_each, 2 * peers * rows_each), BF16),
+            shape((peers, 2 * tall, LANES), BF16),
+            shape((peers * rows_each, LANES), F32),
+        ),
+        in_specs=[pl.BlockSpec(memory_space=pltpu.SMEM)] + [vmem()] * 2,
+        out_specs=(vmem(),) * 4,
+        scratch_shapes=[pltpu.SMEM(request_order.shape, jnp.int32)],
         compiler_params=params(8),
         cost_estimate=pl.CostEstimate(flops=0, bytes_accessed=MIB, transcendentals=0),
         name="select",
-    )(request_order, side, *got)
-    result = pl.pallas_call(
-        functools.partial(down_kernel, split, rows_each),
-        out_shape=shape((ep_count, tall, LANES), BF16),
-        in_specs=[pl.BlockSpec(memory_space=pl.ANY)] + [vmem()] * (7 + peers),
-        out_specs=vmem(),
-        scratch_shapes=[
-            pltpu.SMEM(request_order.shape, jnp.int32),
-            pltpu.SemaphoreType.DMA(()),
-        ],
-        compiler_params=params(16),
-        name="down",
-    )(chosen, request_order, act, act_half, act_core, act_both, down, side, *got)
-
-    came = lax.all_to_all(result, "ep", split_axis=0, concat_axis=0, tiled=True)
+    )(request_order, side, side_core)
+
+    def results(members, after):
+        sent = pl.pallas_call(
+            functools.partial(down_kernel, members, rows_each),
+            out_shape=[shape((2 * tall, LANES), BF16)] * len(members),
+            in_specs=[pl.BlockSpec(memory_space=pl.ANY)] + [vmem()] * 9,
+            out_specs=[vmem()] * len(members),
+            compiler_params=params(16),
+            cost_estimate=pl.CostEstimate(
+                flops=(20 * 10**9 if members[0] >= near else 0),
+                bytes_accessed=MIB,
+                transcendentals=0,
+            ),
+            name="down",
+        )(
+            after,
+            act,
+            act_half,
+            act_core,
+            act_both,
+            down,
+            down_pair,
+            swap,
+            rows,
+            mixes,
+        )
+        return dict(zip(members, sent))
+
+    send = results(list(reversed(range(near, peers))), chosen)
+    send.update(results(list(range(near)), swap_core(chosen)))
+    came = [lax.ppermute(send[k], ("ep", "tp"), route(k)) for k in range(peers)]
+
+    keep, give = pl.pallas_call(
+        functools.partial(combine_kernel, rows_each),
+        out_shape=(shape((tokens, width), F32), shape((tokens, width), BF16)),
+        in_specs=[vmem()] * (1 + peers),
+        out_specs=(vmem(), vmem()),
+        compiler_params=params(8),
+        name="combine",
+    )(chosen, *came)
     return pl.pallas_call(
-        functools.partial(combine_kernel, rows_each),
+        add_half_kernel,
         out_shape=shape((tokens, width), BF16),
         in_specs=[vmem()] * 2,
         out_specs=vmem(),
-        compiler_params=params(8),
-        name="combine",
-    )(chosen, came)
+        compiler_params=params(4),
+        name="add_output",
+    )(keep, swap_core(give))
 
 
 def solution(mesh):

time: 48.1 us -> 47.1 us (0.979)
  blocking collectives: 13.5 us -> 0 us
  starting transfers between devices: 13.3 us -> 21.5 us
  waiting for transfers between devices: 13.3 us -> 17.2 us
  Pallas kernels: 6.25 us -> 6.83 us
    all_to_all x1 -> x0, blocking collectives: 13.5 us -> none  [shards(): came = lax.all_to_all(result, 'ep', split_axis=0, concat_axis=0, tiled=True)]
    ppermute x0 -> x4, waiting for transfers between devices: none -> 4.35 us  [shards(): came = [lax.ppermute(send[k], ('ep', 'tp'), route(k)) for k in range(peers)]]
    ppermute x0 -> x4, starting transfers between devices: none -> 4.28 us  [shards(): came = [lax.ppermute(send[k], ('ep', 'tp'), route(k)) for k in range(peers)]]
    ppermute x7 -> x10, starting transfers between devices: 1.67 us -> 5.67 us  [swap_core(): return lax.ppermute(x, 'tp', [(i, i ^ 1) for i in range(tp_count)])]
    ppermute x4, waiting for transfers between devices: 4.79 us -> 3.65 us  [shards(): got = [lax.ppermute(send[k], ('ep', 'tp'), route(k)) for k in range(peers)]]
    pallas_call x3 -> x5, Pallas kernels: 2.33 us -> 2.9 us  [the longest x2 1.08 us: results(): pl.pallas_call(functools.partial(down_kernel, members, rows_each), out_sh...]
    ppermute x7 -> x10, waiting for transfers between devices: 1.67 us -> 2.08 us  [swap_core(): return lax.ppermute(x, 'tp', [(i, i ^ 1) for i in range(tp_count)])]
  transfers between devices with their start and end apart: 14 -> 21, of which waited for: 7 -> 9; matrix products, arithmetic and copies ran while one was open for 0% -> 0% of each run, Pallas kernels for 6% -> 11%
where the time goes in v9:
time: 47.1 us; the launch traced here: 47 us
  starting transfers between devices  21.5 us (46%)
  waiting for transfers between devices  17.2 us (37%)
  Pallas kernels  6.83 us (15%)
  between operations  1.04 us (2%)
    ppermute x3, waiting for transfers between devices, swap_half(): return lax.ppermute(x, 'tp', [(i, i ^ 2) for i in range(tp_count)])  7.1 us
    ppermute x3, starting transfers between devices, swap_half(): return lax.ppermute(x, 'tp', [(i, i ^ 2) for i in range(tp_count)])  6.24 us
    ppermute x10, starting transfers between devices, swap_core(): return lax.ppermute(x, 'tp', [(i, i ^ 1) for i in range(tp_count)])  5.67 us
    ppermute x4, starting transfers between devices, shards(): got = [lax.ppermute(send[k], ('ep', 'tp'), route(k)) for k in range(peers)]  5.29 us
    ppermute x4, waiting for transfers between devices, shards(): came = [lax.ppermute(send[k], ('ep', 'tp'), route(k)) for k in range(peers)]  4.35 us
    ppermute x4, starting transfers between devices, shards(): came = [lax.ppermute(send[k], ('ep', 'tp'), route(k)) for k in range(peers)]  4.28 us
    ppermute x4, waiting for transfers between devices, shards(): got = [lax.ppermute(send[k], ('ep', 'tp'), route(k)) for k in range(peers)]  3.65 us
    ppermute x10, waiting for transfers between devices, swap_core(): return lax.ppermute(x, 'tp', [(i, i ^ 1) for i in range(tp_count)])  2.08 us
  transfers between devices with their start and end apart: 21, of which 9 were waited for; matrix products, arithmetic and copies ran while one was open for 0% of the time, Pallas kernels for 11%

profile of v9, /device:TPU:0, one launch (start us, length us, event | category | flops | bytes accessed | tf_op | source)
XLA Modules:
  0.0 47.0 jit_solution(5933580890413010216)
XLA Ops:
  0.0 0.0 copy-start
  0.8 0.1 copy-done.8
  0.9 0.1 copy-done.9
  1.0 0.0 copy-start.6
  1.0 0.6 %attend.1.context_ref = bf16[64,512]{1,0:T(8,128)(2,1)S(1)} custom-call(f32[8,128]{1,0:T(8,128)S(1)} %begin.1.after_ref, s32[1]{0:T(128)S(6)} %copy.16.length_ref, bf16[64,512]{1,0:T(8,128)(2,1)S(1)} %copy-done.10, bf16[64,128]{1,0:T(8,128)(2,1)S(1)} %copy-done.11, bf16[64,128]{1,0:T(8,128)(2,1)S(1)} %copy-done.12, bf16[512,128]{1,0:T(8,128)(2,1)S(1)} %bitcast.21, ...), custom_call_target="tpu_custom_call" | custom-call | flops 200000000 | bytes 524288 | tf_op jit(solution)/shard_map/attend/pallas_call | solution.py:440
  1.6 0.3 copy-done
  1.8 0.3 project_given.1.after_ref
  2.1 0.5 %collective-permute-start = (bf16[64,1024]{1,0:T(8,128)(2,1)S(1)}, bf16[64,1024]{1,0:T(8,128)(2,1)S(1)}, u32[]{:S(2)}, u32[]{:S(2)}) collective-permute-start(bf16[64,1024]{1,0:T(8,128)(2,1)S(1)} %project_given.1.after_ref), channel_id=1, source_target_pairs={{0,1},{1,0},{2,3},{3,2},{4,5},{5,4},{6,7},{7,6},{8,9},{9,8},{10,11... | collective-permute-start | bytes 393224 | tf_op jit(solution)/shard_map/ppermute | solution.py:414
  2.7 0.3 project_kept.1.keep_ref
  3.0 0.7 %collective-permute-done.came_ref = bf16[64,1024]{1,0:T(8,128)(2,1)S(1)} collective-permute-done((bf16[64,1024]{1,0:T(8,128)(2,1)S(1)}, bf16[64,1024]{1,0:T(8,128)(2,1)S(1)}, u32[]{:S(2)}, u32[]{:S(2)}) %collective-permute-start) | collective-permute-done | bytes 131104 | tf_op jit(solution)/shard_map/ppermute | solution.py:414
  3.7 2.9 %collective-permute-start.1 = (bf16[64,1024]{1,0:T(8,128)(2,1)S(1)}, bf16[64,1024]{1,0:T(8,128)(2,1)S(1)}, u32[]{:S(2)}, u32[]{:S(2)}) collective-permute-start(bf16[64,1024]{1,0:T(8,128)(2,1)S(1)} %get-tuple-element.29), channel_id=1, source_target_pairs={{0,2},{1,3},{2,0},{3,1},{4,6},{5,7},{6,4},{7,5},{8,10},{9,11},{10,... | collective-permute-start | bytes 393224 | tf_op jit(solution)/shard_map/ppermute | solution.py:417
  6.6 3.8 %collective-permute-done.1.came_ref = bf16[64,1024]{1,0:T(8,128)(2,1)S(1)} collective-permute-done((bf16[64,1024]{1,0:T(8,128)(2,1)S(1)}, bf16[64,1024]{1,0:T(8,128)(2,1)S(1)}, u32[]{:S(2)}, u32[]{:S(2)}) %collective-permute-start.1) | collective-permute-done | bytes 131104 | tf_op jit(solution)/shard_map/ppermute | solution.py:417
  10.4 0.1 collective-permute-start.4
  10.5 0.3 route.1
  10.8 0.5 %collective-permute-start.2 = (bf16[192,2048]{1,0:T(8,128)(2,1)S(1)}, bf16[192,2048]{1,0:T(8,128)(2,1)S(1)}, u32[]{:S(2)}, u32[]{:S(2)}) collective-permute-start(bf16[192,2048]{1,0:T(8,128)(2,1)S(1)} %bitcast.12), channel_id=1, source_target_pairs={{0,1},{1,0},{2,3},{3,2},{4,5},{5,4},{6,7},{7,6},{8,9},{9,8},{10,11... | collective-permute-start | bytes 2359304 | tf_op jit(solution)/shard_map/ppermute | solution.py:414
  11.3 0.1 collective-permute-start.3
  11.4 0.5 %collective-permute-done.4.other_ref = bf16[64,1024]{1,0:T(8,128)(2,1)S(1)} collective-permute-done((bf16[64,1024]{1,0:T(8,128)(2,1)S(1)}, bf16[64,1024]{1,0:T(8,128)(2,1)S(1)}, u32[]{:S(2)}, u32[]{:S(2)}) %collective-permute-start.4) | collective-permute-done | bytes 131104 | tf_op jit(solution)/shard_map/ppermute | solution.py:414
  11.9 0.2 gather_rows.5
  12.1 3.9 %collective-permute-start.8 = (bf16[272,128]{1,0:T(8,128)(2,1)S(1)}, bf16[272,128]{1,0:T(8,128)(2,1)S(1)}, u32[]{:S(2)}, u32[]{:S(2)}) collective-permute-start(bf16[272,128]{1,0:T(8,128)(2,1)S(1)} %get-tuple-element.37), channel_id=1, source_target_pairs={{0,24},{1,29},{2,26},{3,31},{4,28},{5,25},{6,30},{7,27},{8,16},{9,... | collective-permute-start | bytes 208904 | tf_op jit(solution)/shard_map/ppermute | solution.py:535
  16.0 0.0 collective-permute-start.7
  16.0 0.0 collective-permute-done.3.up_pair.after_ref
  16.0 0.2 gather_rows.4
  16.2 0.7 %collective-permute-start.6 = (bf16[528,128]{1,0:T(8,128)(2,1)S(1)}, bf16[528,128]{1,0:T(8,128)(2,1)S(1)}, u32[]{:S(2)}, u32[]{:S(2)}) collective-permute-start(bf16[528,128]{1,0:T(8,128)(2,1)S(1)} %gather_rows.4), channel_id=1, source_target_pairs={{0,0},{1,5},{2,2},{3,7},{4,4},{5,1},{6,6},{7,3},{8,8},{9,13},{10,1... | collective-permute-start | bytes 405512 | tf_op jit(solution)/shard_map/ppermute | solution.py:535
  16.9 0.0 collective-permute-done.2.gate_pair.after_ref
  16.9 0.2 gather_rows.3
  17.1 0.0 copy-start.3
  17.1 0.0 copy-start.13
  17.1 0.7 %collective-permute-start.5 = (bf16[528,128]{1,0:T(8,128)(2,1)S(1)}, bf16[528,128]{1,0:T(8,128)(2,1)S(1)}, u32[]{:S(2)}, u32[]{:S(2)}) collective-permute-start(bf16[528,128]{1,0:T(8,128)(2,1)S(1)} %gather_rows.3), channel_id=1, source_target_pairs={{0,8},{1,13},{2,10},{3,15},{4,12},{5,9},{6,14},{7,11},{8,0},{9,5},... | collective-permute-start | bytes 405512 | tf_op jit(solution)/shard_map/ppermute | solution.py:535
  17.8 1.1 %collective-permute-done.8.refs_3_ = bf16[272,128]{1,0:T(8,128)(2,1)S(1)} collective-permute-done((bf16[272,128]{1,0:T(8,128)(2,1)S(1)}, bf16[272,128]{1,0:T(8,128)(2,1)S(1)}, u32[]{:S(2)}, u32[]{:S(2)}) %collective-permute-start.8) | collective-permute-done | bytes 69664 | tf_op jit(solution)/shard_map/ppermute | solution.py:535
  18.9 1.8 %collective-permute-start.9 = (bf16[272,128]{1,0:T(8,128)(2,1)S(1)}, bf16[272,128]{1,0:T(8,128)(2,1)S(1)}, u32[]{:S(2)}, u32[]{:S(2)}) collective-permute-start(bf16[272,128]{1,0:T(8,128)(2,1)S(1)} %collective-permute-done.8.refs_3_), channel_id=1, source_target_pairs={{0,2},{1,3},{2,0},{3,1},{4,6},{5,7},{6,4},{7,5},{8,10},{9,11},{10,... | collective-permute-start | bytes 208904 | tf_op jit(solution)/shard_map/ppermute | solution.py:417
  20.7 1.1 %stage.1.weight_ref = bf16[2048,768]{1,0:T(8,128)(2,1)S(1)} custom-call(bf16[4,16,128]{2,1,0:T(8,128)(2,1)S(1)} %get-tuple-element.31.after_ref.tags_ref, bf16[192,2048]{1,0:T(8,128)(2,1)S(1)} %bitcast.13, bf16[192,2048]{1,0:T(8,128)(2,1)S(1)} %bitcast.15, bf16[192,2048]{1,0:T(8,128)(2,1)S(1)} %collective-permute-done.2.gate_pair.after_ref, ...), custom_call_target="tpu_custom_call" | custom-call | bytes 6291456 | tf_op jit(solution)/shard_map/stage/pallas_call | solution.py:538
  21.9 1.3 %collective-permute-start.15 = (bf16[768,512]{1,0:T(8,128)(2,1)S(1)}, bf16[768,512]{1,0:T(8,128)(2,1)S(1)}, u32[]{:S(2)}, u32[]{:S(2)}) collective-permute-start(bf16[768,512]{1,0:T(8,128)(2,1)S(1)} %bitcast.16), channel_id=1, source_target_pairs={{0,1},{1,0},{2,3},{3,2},{4,5},{5,4},{6,7},{7,6},{8,9},{9,8},{10,11... | collective-permute-start | bytes 2359304 | tf_op jit(solution)/shard_map/ppermute | solution.py:414
  23.2 2.5 %collective-permute-done.7.refs_2_ = bf16[528,128]{1,0:T(8,128)(2,1)S(1)} collective-permute-done((bf16[528,128]{1,0:T(8,128)(2,1)S(1)}, bf16[528,128]{1,0:T(8,128)(2,1)S(1)}, u32[]{:S(2)}, u32[]{:S(2)}) %collective-permute-start.7) | collective-permute-done | bytes 135200 | tf_op jit(solution)/shard_map/ppermute | solution.py:535
  25.7 0.0 collective-permute-done.9.refs_4_
  25.7 0.0 collective-permute-done.6.refs_1_
  25.7 0.0 collective-permute-done.5.refs_0_
  25.7 0.0 copy-start.7
  25.8 0.7 %hidden_units.1 = (bf16[128,384]{1,0:T(8,128)(2,1)S(1)}, bf16[4,272,128]{2,1,0:T(8,128)(2,1)S(1)}) custom-call(f32[16,128]{1,0:T(8,128)S(1)} %bitcast.23, bf16[2048,768]{1,0:T(8,128)(2,1)S(1)} %stage.1.weight_ref, bf16[528,128]{1,0:T(8,128)(2,1)S(1)} %collective-permute-done.5.refs_0_, bf16[528,128]{1,0:T(8,128)(2,1)S(1)} %collective-permute-done.6.refs_1_, ...), custom_call_target="tpu_custom_call" | custom-call | flops 20000000000 | bytes 1048576 | tf_op jit(solution)/shard_map/hidden_units/pallas_call | solution.py:556
  26.5 1.6 %collective-permute-start.10 = (bf16[4,272,128]{2,1,0:T(8,128)(2,1)S(1)}, bf16[4,272,128]{2,1,0:T(8,128)(2,1)S(1)}, u32[]{:S(2)}, u32[]{:S(2)}) collective-permute-start(bf16[4,272,128]{2,1,0:T(8,128)(2,1)S(1)} %get-tuple-element.38.side_ref), channel_id=1, source_target_pairs={{0,1},{1,0},{2,3},{3,2},{4,5},{5,4},{6,7},{7,6},{8,9},{9,8},{10,11... | collective-permute-start | bytes 835592 | tf_op jit(solution)/shard_map/ppermute | solution.py:414
  28.0 1.5 %collective-permute-start.12 = (bf16[128,384]{1,0:T(8,128)(2,1)S(1)}, bf16[128,384]{1,0:T(8,128)(2,1)S(1)}, u32[]{:S(2)}, u32[]{:S(2)}) collective-permute-start(bf16[128,384]{1,0:T(8,128)(2,1)S(1)} %get-tuple-element.40.act_ref), channel_id=1, source_target_pairs={{0,2},{1,3},{2,0},{3,1},{4,6},{5,7},{6,4},{7,5},{8,10},{9,11},{10,... | collective-permute-start | bytes 294920 | tf_op jit(solution)/shard_map/ppermute | solution.py:417
  29.5 0.0 collective-permute-start.13
  29.5 3.3 %collective-permute-done.12.act_half_ref = bf16[128,384]{1,0:T(8,128)(2,1)S(1)} collective-permute-done((bf16[128,384]{1,0:T(8,128)(2,1)S(1)}, bf16[128,384]{1,0:T(8,128)(2,1)S(1)}, u32[]{:S(2)}, u32[]{:S(2)}) %collective-permute-start.12) | collective-permute-done | bytes 98336 | tf_op jit(solution)/shard_map/ppermute | solution.py:417
  32.8 0.0 collective-permute-start.14
  32.8 0.0 collective-permute-done.10.side_core_ref
  32.8 1.0 %select.1 = (bf16[64,128]{1,0:T(8,128)(2,1)S(1)}, bf16[128,256]{1,0:T(8,128)(2,1)S(1)}, bf16[4,256,128]{2,1,0:T(8,128)(2,1)S(1)}, f32[128,128]{1,0:T(8,128)S(1)}) custom-call(s32[8]{0:T(128)S(1)} %copy-done.7, bf16[4,272,128]{2,1,0:T(8,128)(2,1)S(1)} %get-tuple-element.38.side_ref, bf16[4,272,128]{2,1,0:T(8,128)(2,1)S(1)} %collective-permute-done.10.side_core_ref), custom_call_target="tpu_custom_call" | custom-call | bytes 1048576 | tf_op jit(solution)/shard_map/select/pallas_call | solution.py:576
  33.8 0.5 %collective-permute-start.11 = (bf16[64,128]{1,0:T(8,128)(2,1)S(1)}, bf16[64,128]{1,0:T(8,128)(2,1)S(1)}, u32[]{:S(2)}, u32[]{:S(2)}) collective-permute-start(bf16[64,128]{1,0:T(8,128)(2,1)S(1)} %get-tuple-element.39.after_ref.chosen_ref), channel_id=1, source_target_pairs={{0,1},{1,0},{2,3},{3,2},{4,5},{5,4},{6,7},{7,6},{8,9},{9,8},{10,11... | collective-permute-start | bytes 49160 | tf_op jit(solution)/shard_map/ppermute | solution.py:414
  34.3 0.0 collective-permute-done.13.act_core_ref
  34.3 0.0 collective-permute-done.14.act_both_ref
  34.4 0.0 collective-permute-done.15.down_pair_ref
  34.4 0.5 %down.3 = (bf16[256,128]{1,0:T(8,128)(2,1)S(1)}, bf16[256,128]{1,0:T(8,128)(2,1)S(1)}) custom-call(bf16[64,128]{1,0:T(8,128)(2,1)S(1)} %get-tuple-element.39.after_ref.chosen_ref, bf16[128,384]{1,0:T(8,128)(2,1)S(1)} %get-tuple-element.40.act_ref, bf16[128,384]{1,0:T(8,128)(2,1)S(1)} %collective-permute-done.12.act_half_ref, ...), custom_call_target="tpu_custom_call" | custom-call | flops 20000000000 | bytes 1048576 | tf_op jit(solution)/shard_map/down/pallas_call | solution.py:593
  34.9 0.6 %collective-permute-start.18 = (bf16[256,128]{1,0:T(8,128)(2,1)S(1)}, bf16[256,128]{1,0:T(8,128)(2,1)S(1)}, u32[]{:S(2)}, u32[]{:S(2)}) collective-permute-start(bf16[256,128]{1,0:T(8,128)(2,1)S(1)} %get-tuple-element.47), channel_id=1, source_target_pairs={{0,16},{1,21},{2,18},{3,23},{4,20},{5,17},{6,22},{7,19},{8,24},{9,... | collective-permute-start | bytes 196616 | tf_op jit(solution)/shard_map/ppermute | solution.py:621
  35.5 2.6 %collective-permute-start.19 = (bf16[256,128]{1,0:T(8,128)(2,1)S(1)}, bf16[256,128]{1,0:T(8,128)(2,1)S(1)}, u32[]{:S(2)}, u32[]{:S(2)}) collective-permute-start(bf16[256,128]{1,0:T(8,128)(2,1)S(1)} %get-tuple-element.48), channel_id=1, source_target_pairs={{0,24},{1,29},{2,26},{3,31},{4,28},{5,25},{6,30},{7,27},{8,16},{9,... | collective-permute-start | bytes 196616 | tf_op jit(solution)/shard_map/ppermute | solution.py:621
  38.2 0.0 collective-permute-done.11.after_ref
  38.2 0.5 %down.2 = (bf16[256,128]{1,0:T(8,128)(2,1)S(1)}, bf16[256,128]{1,0:T(8,128)(2,1)S(1)}) custom-call(bf16[64,128]{1,0:T(8,128)(2,1)S(1)} %collective-permute-done.11.after_ref, bf16[128,384]{1,0:T(8,128)(2,1)S(1)} %get-tuple-element.40.act_ref, bf16[128,384]{1,0:T(8,128)(2,1)S(1)} %collective-permute-done.12.act_half_ref, ...), custom_call_target="tpu_custom_call" | custom-call | bytes 1048576 | tf_op jit(solution)/shard_map/down/pallas_call | solution.py:593
  38.7 0.4 collective-permute-start.16
  39.1 0.7 %collective-permute-start.17 = (bf16[256,128]{1,0:T(8,128)(2,1)S(1)}, bf16[256,128]{1,0:T(8,128)(2,1)S(1)}, u32[]{:S(2)}, u32[]{:S(2)}) collective-permute-start(bf16[256,128]{1,0:T(8,128)(2,1)S(1)} %get-tuple-element.46), channel_id=1, source_target_pairs={{0,0},{1,5},{2,2},{3,7},{4,4},{5,1},{6,6},{7,3},{8,8},{9,13},{10,1... | collective-permute-start | bytes 196616 | tf_op jit(solution)/shard_map/ppermute | solution.py:621
  39.7 3.2 %collective-permute-done.18.refs_2_ = bf16[256,128]{1,0:T(8,128)(2,1)S(1)} collective-permute-done((bf16[256,128]{1,0:T(8,128)(2,1)S(1)}, bf16[256,128]{1,0:T(8,128)(2,1)S(1)}, u32[]{:S(2)}, u32[]{:S(2)}) %collective-permute-start.18) | collective-permute-done | bytes 65568 | tf_op jit(solution)/shard_map/ppermute | solution.py:621
  42.9 0.0 collective-permute-done.19.refs_3_
  42.9 1.1 %collective-permute-done.16.refs_0_ = bf16[256,128]{1,0:T(8,128)(2,1)S(1)} collective-permute-done((bf16[256,128]{1,0:T(8,128)(2,1)S(1)}, bf16[256,128]{1,0:T(8,128)(2,1)S(1)}, u32[]{:S(2)}, u32[]{:S(2)}) %collective-permute-start.16) | collective-permute-done | bytes 65568 | tf_op jit(solution)/shard_map/ppermute | solution.py:621
  44.1 0.0 collective-permute-done.17.refs_1_
  44.1 0.2 combine.1
  44.3 1.1 %collective-permute-start.20 = (bf16[64,512]{1,0:T(8,128)(2,1)S(1)}, bf16[64,512]{1,0:T(8,128)(2,1)S(1)}, u32[]{:S(2)}, u32[]{:S(2)}) collective-permute-start(bf16[64,512]{1,0:T(8,128)(2,1)S(1)} %get-tuple-element.50), channel_id=1, source_target_pairs={{0,1},{1,0},{2,3},{3,2},{4,5},{5,4},{6,7},{7,6},{8,9},{9,8},{10,11... | collective-permute-start | bytes 196616 | tf_op jit(solution)/shard_map/ppermute | solution.py:414
  45.4 0.9 %collective-permute-done.20.came_ref = bf16[64,512]{1,0:T(8,128)(2,1)S(1)} collective-permute-done((bf16[64,512]{1,0:T(8,128)(2,1)S(1)}, bf16[64,512]{1,0:T(8,128)(2,1)S(1)}, u32[]{:S(2)}, u32[]{:S(2)}) %collective-permute-start.20) | collective-permute-done | bytes 65568 | tf_op jit(solution)/shard_map/ppermute | solution.py:414
  46.3 0.6 %add_output.1 = bf16[64,512]{1,0:T(8,128)(2,1)} custom-call(f32[64,512]{1,0:T(8,128)S(1)} %get-tuple-element.49.sum_ref, bf16[64,512]{1,0:T(8,128)(2,1)S(1)} %collective-permute-done.20.came_ref), custom_call_target="tpu_custom_call" | custom-call | tf_op jit(solution)/shard_map/add_output/pallas_call | solution.py:631
  (23 shorter events, 0.1 us)
Async XLA Ops:
  0.0 0.9 %copy-start.8 = (bf16[1,512,128]{2,1,0:T(8,128)(2,1)S(1)}, bf16[1,512,128]{2,1,0:T(8,128)(2,1)}, u32[]{:S(2)}) copy-start(bf16[1,512,128]{2,1,0:T(8,128)(2,1)} %param.18) | copy-start | bytes 393220
  0.0 1.0 %copy-start.9 = (bf16[1,512,128]{2,1,0:T(8,128)(2,1)S(1)}, bf16[1,512,128]{2,1,0:T(8,128)(2,1)}, u32[]{:S(2)}) copy-start(bf16[1,512,128]{2,1,0:T(8,128)(2,1)} %param.19) | copy-start | bytes 393220
  0.0 1.0 %copy-start.10 = (bf16[64,512]{1,0:T(8,128)(2,1)S(1)}, bf16[64,512]{1,0:T(8,128)(2,1)}, u32[]{:S(2)}) copy-start(bf16[64,512]{1,0:T(8,128)(2,1)} %query_ref.1) | copy-start | bytes 196612
  0.0 1.0 %copy-start.11 = (bf16[64,128]{1,0:T(8,128)(2,1)S(1)}, bf16[64,128]{1,0:T(8,128)(2,1)}, u32[]{:S(2)}) copy-start(bf16[64,128]{1,0:T(8,128)(2,1)} %new_key_ref.1) | copy-start | bytes 49156
  0.0 1.0 %copy-start.12 = (bf16[64,128]{1,0:T(8,128)(2,1)S(1)}, bf16[64,128]{1,0:T(8,128)(2,1)}, u32[]{:S(2)}) copy-start(bf16[64,128]{1,0:T(8,128)(2,1)} %new_value_ref.1) | copy-start | bytes 49156
  0.0 1.8 %copy-start = (bf16[512,2048]{1,0:T(8,128)(2,1)S(1)}, bf16[512,2048]{1,0:T(8,128)(2,1)}, u32[]{:S(2)}) copy-start(bf16[512,2048]{1,0:T(8,128)(2,1)} %weight_ref.3) | copy-start | bytes 6291460
  0.0 2.6 %copy-start.4 = (bf16[64,512]{1,0:T(8,128)(2,1)S(1)}, bf16[64,512]{1,0:T(8,128)(2,1)}, u32[]{:S(2)}) copy-start(bf16[64,512]{1,0:T(8,128)(2,1)} %residual_ref.1) | copy-start | bytes 196612
  1.0 9.5 %copy-start.5 = (s32[64,2]{0,1:T(2,128)S(1)}, s32[64,2]{0,1:T(2,128)}, u32[]{:S(2)}) copy-start(s32[64,2]{0,1:T(2,128)} %param.25) | copy-start | bytes 1540
  1.0 9.6 %copy-start.6 = (f32[64,2]{0,1:T(2,128)S(1)}, f32[64,2]{0,1:T(2,128)}, u32[]{:S(2)}) copy-start(f32[64,2]{0,1:T(2,128)} %param.26) | copy-start | bytes 1540
  1.8 9.0 %copy-start.1 = (bf16[1,2048,192]{1,2,0:T(8,128)(2,1)S(1)}, bf16[1,2048,192]{1,2,0:T(8,128)(2,1)}, u32[]{:S(2)}) copy-start(bf16[1,2048,192]{1,2,0:T(8,128)(2,1)} %param.27) | copy-start | bytes 2359300
  1.8 9.5 %copy-start.2 = (bf16[1,2048,192]{1,2,0:T(8,128)(2,1)S(1)}, bf16[1,2048,192]{1,2,0:T(8,128)(2,1)}, u32[]{:S(2)}) copy-start(bf16[1,2048,192]{1,2,0:T(8,128)(2,1)} %param.28) | copy-start | bytes 2359300
  2.1 1.5 %collective-permute-start = (bf16[64,1024]{1,0:T(8,128)(2,1)S(1)}, bf16[64,1024]{1,0:T(8,128)(2,1)S(1)}, u32[]{:S(2)}, u32[]{:S(2)}) collective-permute-start(bf16[64,1024]{1,0:T(8,128)(2,1)S(1)} %project_given.1.after_ref), channel_id=1, source_target_pairs={{0,1},{1,0},{2,3},{3,2},{4,5},{5,4},{6,7},{7,6},{8,9},{9,8},{10,11... | collective-permute-start | bytes 393224 | tf_op jit(solution)/shard_map/ppermute | solution.py:414
  3.7 6.7 %collective-permute-start.1 = (bf16[64,1024]{1,0:T(8,128)(2,1)S(1)}, bf16[64,1024]{1,0:T(8,128)(2,1)S(1)}, u32[]{:S(2)}, u32[]{:S(2)}) collective-permute-start(bf16[64,1024]{1,0:T(8,128)(2,1)S(1)} %get-tuple-element.29), channel_id=1, source_target_pairs={{0,2},{1,3},{2,0},{3,1},{4,6},{5,7},{6,4},{7,5},{8,10},{9,11},{10,... | collective-permute-start | bytes 393224 | tf_op jit(solution)/shard_map/ppermute | solution.py:417
  10.4 1.4 %collective-permute-start.4 = (bf16[64,1024]{1,0:T(8,128)(2,1)S(1)}, bf16[64,1024]{1,0:T(8,128)(2,1)S(1)}, u32[]{:S(2)}, u32[]{:S(2)}) collective-permute-start(bf16[64,1024]{1,0:T(8,128)(2,1)S(1)} %add_half.1.after_ref.part_ref), channel_id=1, source_target_pairs={{0,1},{1,0},{2,3},{3,2},{4,5},{5,4},{6,7},{7,6},{8,9},{9,8},{10,11... | collective-permute-start | bytes 393224 | tf_op jit(solution)/shard_map/ppermute | solution.py:414
  10.8 6.1 %collective-permute-start.2 = (bf16[192,2048]{1,0:T(8,128)(2,1)S(1)}, bf16[192,2048]{1,0:T(8,128)(2,1)S(1)}, u32[]{:S(2)}, u32[]{:S(2)}) collective-permute-start(bf16[192,2048]{1,0:T(8,128)(2,1)S(1)} %bitcast.12), channel_id=1, source_target_pairs={{0,1},{1,0},{2,3},{3,2},{4,5},{5,4},{6,7},{7,6},{8,9},{9,8},{10,11... | collective-permute-start | bytes 2359304 | tf_op jit(solution)/shard_map/ppermute | solution.py:414
  11.3 4.7 %collective-permute-start.3 = (bf16[192,2048]{1,0:T(8,128)(2,1)S(1)}, bf16[192,2048]{1,0:T(8,128)(2,1)S(1)}, u32[]{:S(2)}, u32[]{:S(2)}) collective-permute-start(bf16[192,2048]{1,0:T(8,128)(2,1)S(1)} %bitcast.14), channel_id=1, source_target_pairs={{0,1},{1,0},{2,3},{3,2},{4,5},{5,4},{6,7},{7,6},{8,9},{9,8},{10,11... | collective-permute-start | bytes 2359304 | tf_op jit(solution)/shard_map/ppermute | solution.py:414
  12.1 6.8 %collective-permute-start.8 = (bf16[272,128]{1,0:T(8,128)(2,1)S(1)}, bf16[272,128]{1,0:T(8,128)(2,1)S(1)}, u32[]{:S(2)}, u32[]{:S(2)}) collective-permute-start(bf16[272,128]{1,0:T(8,128)(2,1)S(1)} %get-tuple-element.37), channel_id=1, source_target_pairs={{0,24},{1,29},{2,26},{3,31},{4,28},{5,25},{6,30},{7,27},{8,16},{9,... | collective-permute-start | bytes 208904 | tf_op jit(solution)/shard_map/ppermute | solution.py:535
  16.0 9.7 %collective-permute-start.7 = (bf16[528,128]{1,0:T(8,128)(2,1)S(1)}, bf16[528,128]{1,0:T(8,128)(2,1)S(1)}, u32[]{:S(2)}, u32[]{:S(2)}) collective-permute-start(bf16[528,128]{1,0:T(8,128)(2,1)S(1)} %get-tuple-element.36), channel_id=1, source_target_pairs={{0,16},{1,21},{2,18},{3,23},{4,20},{5,17},{6,22},{7,19},{8,24},{9,... | collective-permute-start | bytes 405512 | tf_op jit(solution)/shard_map/ppermute | solution.py:535
  16.2 9.5 %collective-permute-start.6 = (bf16[528,128]{1,0:T(8,128)(2,1)S(1)}, bf16[528,128]{1,0:T(8,128)(2,1)S(1)}, u32[]{:S(2)}, u32[]{:S(2)}) collective-permute-start(bf16[528,128]{1,0:T(8,128)(2,1)S(1)} %gather_rows.4), channel_id=1, source_target_pairs={{0,0},{1,5},{2,2},{3,7},{4,4},{5,1},{6,6},{7,3},{8,8},{9,13},{10,1... | collective-permute-start | bytes 405512 | tf_op jit(solution)/shard_map/ppermute | solution.py:535
  17.1 4.8 %copy-start.3 = (bf16[1,768,512]{2,1,0:T(8,128)(2,1)S(1)}, bf16[1,768,512]{2,1,0:T(8,128)(2,1)}, u32[]{:S(2)}) copy-start(bf16[1,768,512]{2,1,0:T(8,128)(2,1)} %param.29) | copy-start | bytes 2359300
  17.1 8.7 %copy-start.13 = (f32[2048]{0:T(1024)S(1)}, f32[2048]{0:T(1024)}, u32[]{:S(2)}) copy-start(f32[2048]{0:T(1024)} %param.24) | copy-start | bytes 24580
  17.1 8.6 %collective-permute-start.5 = (bf16[528,128]{1,0:T(8,128)(2,1)S(1)}, bf16[528,128]{1,0:T(8,128)(2,1)S(1)}, u32[]{:S(2)}, u32[]{:S(2)}) collective-permute-start(bf16[528,128]{1,0:T(8,128)(2,1)S(1)} %gather_rows.3), channel_id=1, source_target_pairs={{0,8},{1,13},{2,10},{3,15},{4,12},{5,9},{6,14},{7,11},{8,0},{9,5},... | collective-permute-start | bytes 405512 | tf_op jit(solution)/shard_map/ppermute | solution.py:535
  18.9 6.8 %collective-permute-start.9 = (bf16[272,128]{1,0:T(8,128)(2,1)S(1)}, bf16[272,128]{1,0:T(8,128)(2,1)S(1)}, u32[]{:S(2)}, u32[]{:S(2)}) collective-permute-start(bf16[272,128]{1,0:T(8,128)(2,1)S(1)} %collective-permute-done.8.refs_3_), channel_id=1, source_target_pairs={{0,2},{1,3},{2,0},{3,1},{4,6},{5,7},{6,4},{7,5},{8,10},{9,11},{10,... | collective-permute-start | bytes 208904 | tf_op jit(solution)/shard_map/ppermute | solution.py:417
  21.9 12.5 %collective-permute-start.15 = (bf16[768,512]{1,0:T(8,128)(2,1)S(1)}, bf16[768,512]{1,0:T(8,128)(2,1)S(1)}, u32[]{:S(2)}, u32[]{:S(2)}) collective-permute-start(bf16[768,512]{1,0:T(8,128)(2,1)S(1)} %bitcast.16), channel_id=1, source_target_pairs={{0,1},{1,0},{2,3},{3,2},{4,5},{5,4},{6,7},{7,6},{8,9},{9,8},{10,11... | collective-permute-start | bytes 2359304 | tf_op jit(solution)/shard_map/ppermute | solution.py:414
  25.7 7.1 %copy-start.7 = (s32[8]{0:T(128)S(1)}, s32[8]{0:T(128)}, u32[]{:S(2)}) copy-start(s32[8]{0:T(128)} %order_ref.1) | copy-start | bytes 100
  26.5 6.3 %collective-permute-start.10 = (bf16[4,272,128]{2,1,0:T(8,128)(2,1)S(1)}, bf16[4,272,128]{2,1,0:T(8,128)(2,1)S(1)}, u32[]{:S(2)}, u32[]{:S(2)}) collective-permute-start(bf16[4,272,128]{2,1,0:T(8,128)(2,1)S(1)} %get-tuple-element.38.side_ref), channel_id=1, source_target_pairs={{0,1},{1,0},{2,3},{3,2},{4,5},{5,4},{6,7},{7,6},{8,9},{9,8},{10,11... | collective-permute-start | bytes 835592 | tf_op jit(solution)/shard_map/ppermute | solution.py:414
  28.0 4.8 %collective-permute-start.12 = (bf16[128,384]{1,0:T(8,128)(2,1)S(1)}, bf16[128,384]{1,0:T(8,128)(2,1)S(1)}, u32[]{:S(2)}, u32[]{:S(2)}) collective-permute-start(bf16[128,384]{1,0:T(8,128)(2,1)S(1)} %get-tuple-element.40.act_ref), channel_id=1, source_target_pairs={{0,2},{1,3},{2,0},{3,1},{4,6},{5,7},{6,4},{7,5},{8,10},{9,11},{10,... | collective-permute-start | bytes 294920 | tf_op jit(solution)/shard_map/ppermute | solution.py:417
  29.5 4.8 %collective-permute-start.13 = (bf16[128,384]{1,0:T(8,128)(2,1)S(1)}, bf16[128,384]{1,0:T(8,128)(2,1)S(1)}, u32[]{:S(2)}, u32[]{:S(2)}) collective-permute-start(bf16[128,384]{1,0:T(8,128)(2,1)S(1)} %get-tuple-element.40.act_ref), channel_id=1, source_target_pairs={{0,1},{1,0},{2,3},{3,2},{4,5},{5,4},{6,7},{7,6},{8,9},{9,8},{10,11... | collective-permute-start | bytes 294920 | tf_op jit(solution)/shard_map/ppermute | solution.py:414
  32.8 1.5 %collective-permute-start.14 = (bf16[128,384]{1,0:T(8,128)(2,1)S(1)}, bf16[128,384]{1,0:T(8,128)(2,1)S(1)}, u32[]{:S(2)}, u32[]{:S(2)}) collective-permute-start(bf16[128,384]{1,0:T(8,128)(2,1)S(1)} %collective-permute-done.12.act_half_ref), channel_id=1, source_target_pairs={{0,1},{1,0},{2,3},{3,2},{4,5},{5,4},{6,7},{7,6},{8,9},{9,8},{10,11... | collective-permute-start | bytes 294920 | tf_op jit(solution)/shard_map/ppermute | solution.py:414
  33.8 4.3 %collective-permute-start.11 = (bf16[64,128]{1,0:T(8,128)(2,1)S(1)}, bf16[64,128]{1,0:T(8,128)(2,1)S(1)}, u32[]{:S(2)}, u32[]{:S(2)}) collective-permute-start(bf16[64,128]{1,0:T(8,128)(2,1)S(1)} %get-tuple-element.39.after_ref.chosen_ref), channel_id=1, source_target_pairs={{0,1},{1,0},{2,3},{3,2},{4,5},{5,4},{6,7},{7,6},{8,9},{9,8},{10,11... | collective-permute-start | bytes 49160 | tf_op jit(solution)/shard_map/ppermute | solution.py:414
  34.9 8.0 %collective-permute-start.18 = (bf16[256,128]{1,0:T(8,128)(2,1)S(1)}, bf16[256,128]{1,0:T(8,128)(2,1)S(1)}, u32[]{:S(2)}, u32[]{:S(2)}) collective-permute-start(bf16[256,128]{1,0:T(8,128)(2,1)S(1)} %get-tuple-element.47), channel_id=1, source_target_pairs={{0,16},{1,21},{2,18},{3,23},{4,20},{5,17},{6,22},{7,19},{8,24},{9,... | collective-permute-start | bytes 196616 | tf_op jit(solution)/shard_map/ppermute | solution.py:621
  35.5 7.4 %collective-permute-start.19 = (bf16[256,128]{1,0:T(8,128)(2,1)S(1)}, bf16[256,128]{1,0:T(8,128)(2,1)S(1)}, u32[]{:S(2)}, u32[]{:S(2)}) collective-permute-start(bf16[256,128]{1,0:T(8,128)(2,1)S(1)} %get-tuple-element.48), channel_id=1, source_target_pairs={{0,24},{1,29},{2,26},{3,31},{4,28},{5,25},{6,30},{7,27},{8,16},{9,... | collective-permute-start | bytes 196616 | tf_op jit(solution)/shard_map/ppermute | solution.py:621
  38.7 5.4 %collective-permute-start.16 = (bf16[256,128]{1,0:T(8,128)(2,1)S(1)}, bf16[256,128]{1,0:T(8,128)(2,1)S(1)}, u32[]{:S(2)}, u32[]{:S(2)}) collective-permute-start(bf16[256,128]{1,0:T(8,128)(2,1)S(1)} %get-tuple-element.45), channel_id=1, source_target_pairs={{0,8},{1,13},{2,10},{3,15},{4,12},{5,9},{6,14},{7,11},{8,0},{9,5},... | collective-permute-start | bytes 196616 | tf_op jit(solution)/shard_map/ppermute | solution.py:621
  39.1 5.0 %collective-permute-start.17 = (bf16[256,128]{1,0:T(8,128)(2,1)S(1)}, bf16[256,128]{1,0:T(8,128)(2,1)S(1)}, u32[]{:S(2)}, u32[]{:S(2)}) collective-permute-start(bf16[256,128]{1,0:T(8,128)(2,1)S(1)} %get-tuple-element.46), channel_id=1, source_target_pairs={{0,0},{1,5},{2,2},{3,7},{4,4},{5,1},{6,6},{7,3},{8,8},{9,13},{10,1... | collective-permute-start | bytes 196616 | tf_op jit(solution)/shard_map/ppermute | solution.py:621
  44.3 2.0 %collective-permute-start.20 = (bf16[64,512]{1,0:T(8,128)(2,1)S(1)}, bf16[64,512]{1,0:T(8,128)(2,1)S(1)}, u32[]{:S(2)}, u32[]{:S(2)}) collective-permute-start(bf16[64,512]{1,0:T(8,128)(2,1)S(1)} %get-tuple-element.50), channel_id=1, source_target_pairs={{0,1},{1,0},{2,3},{3,2},{4,5},{5,4},{6,7},{7,6},{8,9},{9,8},{10,11... | collective-permute-start | bytes 196616 | tf_op jit(solution)/shard_map/ppermute | solution.py:414

commit v10 on v9

--- a/solution.py
+++ b/solution.py
@@ -291,9 +291,9 @@
         out_ref[columns, :] = held_ref[:, :, columns].reshape(4 * units, LANES).T
 
 
-def hidden_units_kernel(split, rows_each, gain_ref, weight_ref, *refs):
+def hidden_units_kernel(order, split, rows_each, gain_ref, weight_ref, *refs):
     peers = len(split)
-    got = refs[:peers]
+    got = [refs[order.index(k)] for k in range(peers)]
     halves = list(refs[peers:-2])
     act_ref, side_ref = refs[-2:]
     tp = lax.axis_index("tp")
@@ -376,8 +376,8 @@
                 send_refs[i][piece, :] = (mix * value).astype(BF16)
 
 
-def combine_kernel(rows_each, chosen_ref, *refs):
-    came = refs[:-2]
+def combine_kernel(order, rows_each, chosen_ref, *refs):
+    came = [refs[order.index(k)] for k in range(len(order))]
     keep_ref, give_ref = refs[-2:]
     core = lax.axis_index("tp") % 2
     chosen = chosen_ref[...]
@@ -529,9 +529,7 @@
     send = gather(list(reversed(range(near, peers))), tags)
     gate, up, tags = lax.optimization_barrier((gate, up, tags))
     gate_pair, up_pair = swap_core(gate), swap_core(up)
-    early = near // 2
-    send.update(gather(list(range(early, near)), up_pair))
-    send.update(gather(list(range(early)), gate_pair))
+    send.update(gather(list(range(near)), gate_pair))
     got = [lax.ppermute(send[k], ("ep", "tp"), route(k)) for k in range(peers)]
     halves = [swap_half(got[k]) for k in range(peers) if split[k]]
 
@@ -553,8 +551,9 @@
 
     down, weights = lax.optimization_barrier((down, weights))
     down_pair = swap_core(down)
+    arrival = [*range(near, peers), *range(near)]
     act, side = pl.pallas_call(
-        functools.partial(hidden_units_kernel, split, rows_each),
+        functools.partial(hidden_units_kernel, arrival, split, rows_each),
         out_shape=(
             shape((peers * rows_each, units), BF16),
             shape((peers, 2 * tall + TAGS, LANES), BF16),
@@ -566,7 +565,7 @@
             flops=20 * 10**9, bytes_accessed=MIB, transcendentals=0
         ),
         name="hidden_units",
-    )(norm_gain.reshape(-1, LANES), weights, *got, *halves)
+    )(norm_gain.reshape(-1, LANES), weights, *[got[k] for k in arrival], *halves)
 
     act_half = swap_half(act)
     act_core = swap_core(act)
@@ -616,12 +615,12 @@
         )
         return dict(zip(members, sent))
 
-    send = results(list(reversed(range(near, peers))), chosen)
-    send.update(results(list(range(near)), swap_core(chosen)))
-    came = [lax.ppermute(send[k], ("ep", "tp"), route(k)) for k in range(peers)]
+    order = [*range(near, peers), *range(near)]
+    send = results(list(range(peers)), chosen)
+    came = [lax.ppermute(send[k], ("ep", "tp"), route(k)) for k in order]
 
     keep, give = pl.pallas_call(
-        functools.partial(combine_kernel, rows_each),
+        functools.partial(combine_kernel, order, rows_each),
         out_shape=(shape((tokens, width), F32), shape((tokens, width), BF16)),
         in_specs=[vmem()] * (1 + peers),
         out_specs=(vmem(), vmem()),

time: 47.1 us -> 46.1 us (0.979)
  starting transfers between devices: 21.5 us -> 20 us
  waiting for transfers between devices: 17.2 us -> 18.2 us
  Pallas kernels: 6.83 us -> 6.2 us
    ppermute x10 -> x9, starting transfers between devices: 5.67 us -> 3.27 us  [swap_core(): return lax.ppermute(x, 'tp', [(i, i ^ 1) for i in range(tp_count)])]
    ppermute x4, starting transfers between devices: 4.28 us -> 5.05 us  [shards(): came = [lax.ppermute(send[k], ('ep', 'tp'), route(k)) for k in order]]
    ppermute x4, waiting for transfers between devices: 4.35 us -> 5.08 us  [shards(): came = [lax.ppermute(send[k], ('ep', 'tp'), route(k)) for k in order]]
    pallas_call x2 -> x1, Pallas kernels: 1.08 us -> 0.61 us  [results(): pl.pallas_call(functools.partial(down_kernel, members, rows_each), out_sh...]
    ppermute x10 -> x9, waiting for transfers between devices: 2.08 us -> 2.47 us  [swap_core(): return lax.ppermute(x, 'tp', [(i, i ^ 1) for i in range(tp_count)])]
  transfers between devices with their start and end apart: 21 -> 20, of which waited for: 9 -> 10; matrix products, arithmetic and copies ran while one was open for 0% -> 0% of each run, Pallas kernels for 11% -> 8%
where the time goes in v10:
time: 46.1 us; the launch traced here: 45.9 us
  starting transfers between devices  20 us (43%)
  waiting for transfers between devices  18.2 us (39%)
  Pallas kernels  6.2 us (13%)
  between operations  1 us (2%)
    ppermute x3, waiting for transfers between devices, swap_half(): return lax.ppermute(x, 'tp', [(i, i ^ 2) for i in range(tp_count)])  7.16 us
    ppermute x3, starting transfers between devices, swap_half(): return lax.ppermute(x, 'tp', [(i, i ^ 2) for i in range(tp_count)])  6.31 us
    ppermute x4, starting transfers between devices, shards(): got = [lax.ppermute(send[k], ('ep', 'tp'), route(k)) for k in range(peers)]  5.42 us
    ppermute x4, waiting for transfers between devices, shards(): came = [lax.ppermute(send[k], ('ep', 'tp'), route(k)) for k in order]  5.08 us
    ppermute x4, starting transfers between devices, shards(): came = [lax.ppermute(send[k], ('ep', 'tp'), route(k)) for k in order]  5.05 us
    ppermute x4, waiting for transfers between devices, shards(): got = [lax.ppermute(send[k], ('ep', 'tp'), route(k)) for k in range(peers)]  3.5 us
    ppermute x9, starting transfers between devices, swap_core(): return lax.ppermute(x, 'tp', [(i, i ^ 1) for i in range(tp_count)])  3.27 us
    ppermute x9, waiting for transfers between devices, swap_core(): return lax.ppermute(x, 'tp', [(i, i ^ 1) for i in range(tp_count)])  2.47 us
  transfers between devices with their start and end apart: 20, of which 10 were waited for; matrix products, arithmetic and copies ran while one was open for 0% of the time, Pallas kernels for 8%

profile of v10, /device:TPU:0, one launch (start us, length us, event | category | flops | bytes accessed | tf_op | source)
XLA Modules:
  0.0 45.9 jit_solution(10101145466764406222)
XLA Ops:
  0.0 0.0 copy-start
  0.0 0.0 copy-start.4
  0.8 0.1 copy-done.8
  0.9 0.1 copy-done.9
  1.0 0.0 copy-done.10
  1.0 0.0 copy-done.11
  1.0 0.0 copy-done.12
  1.0 0.0 copy-start.6
  1.0 0.6 %attend.1.context_ref = bf16[64,512]{1,0:T(8,128)(2,1)S(1)} custom-call(f32[8,128]{1,0:T(8,128)S(1)} %begin.1.after_ref, s32[1]{0:T(128)S(6)} %copy.16.length_ref, bf16[64,512]{1,0:T(8,128)(2,1)S(1)} %copy-done.10, bf16[64,128]{1,0:T(8,128)(2,1)S(1)} %copy-done.11, bf16[64,128]{1,0:T(8,128)(2,1)S(1)} %copy-done.12, bf16[512,128]{1,0:T(8,128)(2,1)S(1)} %bitcast.20, ...), custom_call_target="tpu_custom_call" | custom-call | flops 200000000 | bytes 524288 | tf_op jit(solution)/shard_map/attend/pallas_call | solution.py:440
  1.6 0.3 copy-done
  1.8 0.3 project_given.1.after_ref
  2.1 0.5 %collective-permute-start = (bf16[64,1024]{1,0:T(8,128)(2,1)S(1)}, bf16[64,1024]{1,0:T(8,128)(2,1)S(1)}, u32[]{:S(2)}, u32[]{:S(2)}) collective-permute-start(bf16[64,1024]{1,0:T(8,128)(2,1)S(1)} %project_given.1.after_ref), channel_id=1, source_target_pairs={{0,1},{1,0},{2,3},{3,2},{4,5},{5,4},{6,7},{7,6},{8,9},{9,8},{10,11... | collective-permute-start | bytes 393224 | tf_op jit(solution)/shard_map/ppermute | solution.py:414
  2.7 0.3 project_kept.1.keep_ref
  3.0 0.7 %collective-permute-done.came_ref = bf16[64,1024]{1,0:T(8,128)(2,1)S(1)} collective-permute-done((bf16[64,1024]{1,0:T(8,128)(2,1)S(1)}, bf16[64,1024]{1,0:T(8,128)(2,1)S(1)}, u32[]{:S(2)}, u32[]{:S(2)}) %collective-permute-start) | collective-permute-done | bytes 131104 | tf_op jit(solution)/shard_map/ppermute | solution.py:414
  3.7 2.9 %collective-permute-start.1 = (bf16[64,1024]{1,0:T(8,128)(2,1)S(1)}, bf16[64,1024]{1,0:T(8,128)(2,1)S(1)}, u32[]{:S(2)}, u32[]{:S(2)}) collective-permute-start(bf16[64,1024]{1,0:T(8,128)(2,1)S(1)} %get-tuple-element.31), channel_id=1, source_target_pairs={{0,2},{1,3},{2,0},{3,1},{4,6},{5,7},{6,4},{7,5},{8,10},{9,11},{10,... | collective-permute-start | bytes 393224 | tf_op jit(solution)/shard_map/ppermute | solution.py:417
  6.6 3.8 %collective-permute-done.1.came_ref = bf16[64,1024]{1,0:T(8,128)(2,1)S(1)} collective-permute-done((bf16[64,1024]{1,0:T(8,128)(2,1)S(1)}, bf16[64,1024]{1,0:T(8,128)(2,1)S(1)}, u32[]{:S(2)}, u32[]{:S(2)}) %collective-permute-start.1) | collective-permute-done | bytes 131104 | tf_op jit(solution)/shard_map/ppermute | solution.py:417
  10.4 0.1 collective-permute-start.4
  10.5 0.3 route.1
  10.8 0.5 %collective-permute-start.2 = (bf16[192,2048]{1,0:T(8,128)(2,1)S(1)}, bf16[192,2048]{1,0:T(8,128)(2,1)S(1)}, u32[]{:S(2)}, u32[]{:S(2)}) collective-permute-start(bf16[192,2048]{1,0:T(8,128)(2,1)S(1)} %bitcast.12), channel_id=1, source_target_pairs={{0,1},{1,0},{2,3},{3,2},{4,5},{5,4},{6,7},{7,6},{8,9},{9,8},{10,11... | collective-permute-start | bytes 2359304 | tf_op jit(solution)/shard_map/ppermute | solution.py:414
  11.3 0.0 copy-done.2
  11.3 0.1 collective-permute-start.3
  11.4 0.5 %collective-permute-done.4.other_ref = bf16[64,1024]{1,0:T(8,128)(2,1)S(1)} collective-permute-done((bf16[64,1024]{1,0:T(8,128)(2,1)S(1)}, bf16[64,1024]{1,0:T(8,128)(2,1)S(1)}, u32[]{:S(2)}, u32[]{:S(2)}) %collective-permute-start.4) | collective-permute-done | bytes 131104 | tf_op jit(solution)/shard_map/ppermute | solution.py:414
  11.9 0.2 gather_rows.2
  12.1 3.9 %collective-permute-start.6 = (bf16[272,128]{1,0:T(8,128)(2,1)S(1)}, bf16[272,128]{1,0:T(8,128)(2,1)S(1)}, u32[]{:S(2)}, u32[]{:S(2)}) collective-permute-start(bf16[272,128]{1,0:T(8,128)(2,1)S(1)} %get-tuple-element.39), channel_id=1, source_target_pairs={{0,24},{1,29},{2,26},{3,31},{4,28},{5,25},{6,30},{7,27},{8,16},{9,... | collective-permute-start | bytes 208904 | tf_op jit(solution)/shard_map/ppermute | solution.py:533
  16.0 0.0 collective-permute-start.5
  16.0 0.0 collective-permute-done.2.gate_pair.after_ref
  16.0 0.2 gather_rows.3
  16.2 0.7 %collective-permute-start.7 = (bf16[528,128]{1,0:T(8,128)(2,1)S(1)}, bf16[528,128]{1,0:T(8,128)(2,1)S(1)}, u32[]{:S(2)}, u32[]{:S(2)}) collective-permute-start(bf16[528,128]{1,0:T(8,128)(2,1)S(1)} %get-tuple-element.40), channel_id=1, source_target_pairs={{0,8},{1,13},{2,10},{3,15},{4,12},{5,9},{6,14},{7,11},{8,0},{9,5},... | collective-permute-start | bytes 405512 | tf_op jit(solution)/shard_map/ppermute | solution.py:533
  16.9 0.8 %collective-permute-start.8 = (bf16[528,128]{1,0:T(8,128)(2,1)S(1)}, bf16[528,128]{1,0:T(8,128)(2,1)S(1)}, u32[]{:S(2)}, u32[]{:S(2)}) collective-permute-start(bf16[528,128]{1,0:T(8,128)(2,1)S(1)} %get-tuple-element.41), channel_id=1, source_target_pairs={{0,0},{1,5},{2,2},{3,7},{4,4},{5,1},{6,6},{7,3},{8,8},{9,13},{10,1... | collective-permute-start | bytes 405512 | tf_op jit(solution)/shard_map/ppermute | solution.py:533
  17.7 1.1 %collective-permute-done.6.refs_1_ = bf16[272,128]{1,0:T(8,128)(2,1)S(1)} collective-permute-done((bf16[272,128]{1,0:T(8,128)(2,1)S(1)}, bf16[272,128]{1,0:T(8,128)(2,1)S(1)}, u32[]{:S(2)}, u32[]{:S(2)}) %collective-permute-start.6) | collective-permute-done | bytes 69664 | tf_op jit(solution)/shard_map/ppermute | solution.py:533
  18.8 1.9 %collective-permute-start.9 = (bf16[272,128]{1,0:T(8,128)(2,1)S(1)}, bf16[272,128]{1,0:T(8,128)(2,1)S(1)}, u32[]{:S(2)}, u32[]{:S(2)}) collective-permute-start(bf16[272,128]{1,0:T(8,128)(2,1)S(1)} %collective-permute-done.6.refs_1_), channel_id=1, source_target_pairs={{0,2},{1,3},{2,0},{3,1},{4,6},{5,7},{6,4},{7,5},{8,10},{9,11},{10,... | collective-permute-start | bytes 208904 | tf_op jit(solution)/shard_map/ppermute | solution.py:417
  20.7 0.0 collective-permute-done.3.up_pair
  20.7 1.1 %stage.1.weight_ref = bf16[2048,768]{1,0:T(8,128)(2,1)S(1)} custom-call(bf16[4,16,128]{2,1,0:T(8,128)(2,1)S(1)} %get-tuple-element.33.after_ref.tags_ref, bf16[192,2048]{1,0:T(8,128)(2,1)S(1)} %bitcast.13, bf16[192,2048]{1,0:T(8,128)(2,1)S(1)} %bitcast.15, bf16[192,2048]{1,0:T(8,128)(2,1)S(1)} %collective-permute-done.2.gate_pair.after_ref, ...), custom_call_target="tpu_custom_call" | custom-call | bytes 6291456 | tf_op jit(solution)/shard_map/stage/pallas_call | solution.py:536
  21.9 1.3 %collective-permute-start.14 = (bf16[768,512]{1,0:T(8,128)(2,1)S(1)}, bf16[768,512]{1,0:T(8,128)(2,1)S(1)}, u32[]{:S(2)}, u32[]{:S(2)}) collective-permute-start(bf16[768,512]{1,0:T(8,128)(2,1)S(1)} %bitcast.16), channel_id=1, source_target_pairs={{0,1},{1,0},{2,3},{3,2},{4,5},{5,4},{6,7},{7,6},{8,9},{9,8},{10,11... | collective-permute-start | bytes 2359304 | tf_op jit(solution)/shard_map/ppermute | solution.py:414
  23.2 2.4 %collective-permute-done.5.refs_0_ = bf16[528,128]{1,0:T(8,128)(2,1)S(1)} collective-permute-done((bf16[528,128]{1,0:T(8,128)(2,1)S(1)}, bf16[528,128]{1,0:T(8,128)(2,1)S(1)}, u32[]{:S(2)}, u32[]{:S(2)}) %collective-permute-start.5) | collective-permute-done | bytes 135200 | tf_op jit(solution)/shard_map/ppermute | solution.py:533
  25.6 0.0 collective-permute-done.9.refs_4_
  25.6 0.0 collective-permute-done.7.refs_2_
  25.6 0.0 collective-permute-done.8.refs_3_
  25.7 0.0 copy-start.7
  25.7 0.7 %hidden_units.1 = (bf16[128,384]{1,0:T(8,128)(2,1)S(1)}, bf16[4,272,128]{2,1,0:T(8,128)(2,1)S(1)}) custom-call(f32[16,128]{1,0:T(8,128)S(1)} %bitcast.22, bf16[2048,768]{1,0:T(8,128)(2,1)S(1)} %stage.1.weight_ref, bf16[528,128]{1,0:T(8,128)(2,1)S(1)} %collective-permute-done.5.refs_0_, bf16[272,128]{1,0:T(8,128)(2,1)S(1)} %collective-permute-done.6.refs_1_, ...), custom_call_target="tpu_custom_call" | custom-call | flops 20000000000 | bytes 1048576 | tf_op jit(solution)/shard_map/hidden_units/pallas_call | solution.py:555
  26.4 0.4 collective-permute-start.10
  26.8 1.5 %collective-permute-start.11 = (bf16[128,384]{1,0:T(8,128)(2,1)S(1)}, bf16[128,384]{1,0:T(8,128)(2,1)S(1)}, u32[]{:S(2)}, u32[]{:S(2)}) collective-permute-start(bf16[128,384]{1,0:T(8,128)(2,1)S(1)} %get-tuple-element.44.act_ref), channel_id=1, source_target_pairs={{0,2},{1,3},{2,0},{3,1},{4,6},{5,7},{6,4},{7,5},{8,10},{9,11},{10,... | collective-permute-start | bytes 294920 | tf_op jit(solution)/shard_map/ppermute | solution.py:417
  28.3 0.0 collective-permute-start.12
  28.3 3.4 %collective-permute-done.11.act_half_ref = bf16[128,384]{1,0:T(8,128)(2,1)S(1)} collective-permute-done((bf16[128,384]{1,0:T(8,128)(2,1)S(1)}, bf16[128,384]{1,0:T(8,128)(2,1)S(1)}, u32[]{:S(2)}, u32[]{:S(2)}) %collective-permute-start.11) | collective-permute-done | bytes 98336 | tf_op jit(solution)/shard_map/ppermute | solution.py:417
  31.7 0.0 collective-permute-start.13
  31.7 0.0 collective-permute-done.10.side_core_ref
  31.7 0.0 copy-done.7
  31.7 1.0 %select.1 = (bf16[64,128]{1,0:T(8,128)(2,1)S(1)}, bf16[128,256]{1,0:T(8,128)(2,1)S(1)}, bf16[4,256,128]{2,1,0:T(8,128)(2,1)S(1)}, f32[128,128]{1,0:T(8,128)S(1)}) custom-call(s32[8]{0:T(128)S(1)} %copy-done.7, bf16[4,272,128]{2,1,0:T(8,128)(2,1)S(1)} %get-tuple-element.42.side_ref, bf16[4,272,128]{2,1,0:T(8,128)(2,1)S(1)} %collective-permute-done.10.side_core_ref), custom_call_target="tpu_custom_call" | custom-call | bytes 1048576 | tf_op jit(solution)/shard_map/select/pallas_call | solution.py:575
  32.7 0.0 collective-permute-done.12.act_core_ref
  32.7 0.3 collective-permute-done.13.act_both_ref
  33.0 0.0 collective-permute-done.14.down_pair_ref
  33.0 0.6 %down.1 = (bf16[256,128]{1,0:T(8,128)(2,1)S(1)}, bf16[256,128]{1,0:T(8,128)(2,1)S(1)}, bf16[256,128]{1,0:T(8,128)(2,1)S(1)}, bf16[256,128]{1,0:T(8,128)(2,1)S(1)}) custom-call(bf16[64,128]{1,0:T(8,128)(2,1)S(1)} %get-tuple-element.43.after_ref.chosen_ref, bf16[128,384]{1,0:T(8,128)(2,1)S(1)} %get-tuple-element.44.act_ref, ...), custom_call_target="tpu_custom_call" | custom-call | bytes 1048576 | tf_op jit(solution)/shard_map/down/pallas_call | solution.py:592
  33.6 1.6 %collective-permute-start.15 = (bf16[256,128]{1,0:T(8,128)(2,1)S(1)}, bf16[256,128]{1,0:T(8,128)(2,1)S(1)}, u32[]{:S(2)}, u32[]{:S(2)}) collective-permute-start(bf16[256,128]{1,0:T(8,128)(2,1)S(1)} %get-tuple-element.49), channel_id=1, source_target_pairs={{0,16},{1,21},{2,18},{3,23},{4,20},{5,17},{6,22},{7,19},{8,24},{9,... | collective-permute-start | bytes 196616 | tf_op jit(solution)/shard_map/ppermute | solution.py:620
  35.2 2.8 %collective-permute-start.16 = (bf16[256,128]{1,0:T(8,128)(2,1)S(1)}, bf16[256,128]{1,0:T(8,128)(2,1)S(1)}, u32[]{:S(2)}, u32[]{:S(2)}) collective-permute-start(bf16[256,128]{1,0:T(8,128)(2,1)S(1)} %get-tuple-element.50), channel_id=1, source_target_pairs={{0,24},{1,29},{2,26},{3,31},{4,28},{5,25},{6,30},{7,27},{8,16},{9,... | collective-permute-start | bytes 196616 | tf_op jit(solution)/shard_map/ppermute | solution.py:620
  38.0 0.0 collective-permute-start.17
  38.0 0.7 %collective-permute-start.18 = (bf16[256,128]{1,0:T(8,128)(2,1)S(1)}, bf16[256,128]{1,0:T(8,128)(2,1)S(1)}, u32[]{:S(2)}, u32[]{:S(2)}) collective-permute-start(bf16[256,128]{1,0:T(8,128)(2,1)S(1)} %get-tuple-element.52), channel_id=1, source_target_pairs={{0,0},{1,5},{2,2},{3,7},{4,4},{5,1},{6,6},{7,3},{8,8},{9,13},{10,1... | collective-permute-start | bytes 196616 | tf_op jit(solution)/shard_map/ppermute | solution.py:620
  38.6 3.8 %collective-permute-done.15.refs_0_ = bf16[256,128]{1,0:T(8,128)(2,1)S(1)} collective-permute-done((bf16[256,128]{1,0:T(8,128)(2,1)S(1)}, bf16[256,128]{1,0:T(8,128)(2,1)S(1)}, u32[]{:S(2)}, u32[]{:S(2)}) %collective-permute-start.15) | collective-permute-done | bytes 65568 | tf_op jit(solution)/shard_map/ppermute | solution.py:620
  42.4 0.0 collective-permute-done.16.refs_1_
  42.4 1.3 %collective-permute-done.17.refs_2_ = bf16[256,128]{1,0:T(8,128)(2,1)S(1)} collective-permute-done((bf16[256,128]{1,0:T(8,128)(2,1)S(1)}, bf16[256,128]{1,0:T(8,128)(2,1)S(1)}, u32[]{:S(2)}, u32[]{:S(2)}) %collective-permute-start.17) | collective-permute-done | bytes 65568 | tf_op jit(solution)/shard_map/ppermute | solution.py:620
  43.7 0.0 collective-permute-done.18.refs_3_
  43.7 0.2 combine.1
  43.9 0.3 collective-permute-start.19
  44.3 1.0 %collective-permute-done.19.came_ref = bf16[64,512]{1,0:T(8,128)(2,1)S(1)} collective-permute-done((bf16[64,512]{1,0:T(8,128)(2,1)S(1)}, bf16[64,512]{1,0:T(8,128)(2,1)S(1)}, u32[]{:S(2)}, u32[]{:S(2)}) %collective-permute-start.19) | collective-permute-done | bytes 65568 | tf_op jit(solution)/shard_map/ppermute | solution.py:414
  45.2 0.6 %add_output.1 = bf16[64,512]{1,0:T(8,128)(2,1)} custom-call(f32[64,512]{1,0:T(8,128)S(1)} %get-tuple-element.53.sum_ref, bf16[64,512]{1,0:T(8,128)(2,1)S(1)} %collective-permute-done.19.came_ref), custom_call_target="tpu_custom_call" | custom-call | tf_op jit(solution)/shard_map/add_output/pallas_call | solution.py:630
  (19 shorter events, 0.1 us)
Async XLA Ops:
  0.0 0.9 %copy-start.8 = (bf16[1,512,128]{2,1,0:T(8,128)(2,1)S(1)}, bf16[1,512,128]{2,1,0:T(8,128)(2,1)}, u32[]{:S(2)}) copy-start(bf16[1,512,128]{2,1,0:T(8,128)(2,1)} %param.18) | copy-start | bytes 393220
  0.0 1.0 %copy-start.9 = (bf16[1,512,128]{2,1,0:T(8,128)(2,1)S(1)}, bf16[1,512,128]{2,1,0:T(8,128)(2,1)}, u32[]{:S(2)}) copy-start(bf16[1,512,128]{2,1,0:T(8,128)(2,1)} %param.19) | copy-start | bytes 393220
  0.0 1.0 %copy-start.10 = (bf16[64,512]{1,0:T(8,128)(2,1)S(1)}, bf16[64,512]{1,0:T(8,128)(2,1)}, u32[]{:S(2)}) copy-start(bf16[64,512]{1,0:T(8,128)(2,1)} %query_ref.1) | copy-start | bytes 196612
  0.0 1.0 %copy-start.11 = (bf16[64,128]{1,0:T(8,128)(2,1)S(1)}, bf16[64,128]{1,0:T(8,128)(2,1)}, u32[]{:S(2)}) copy-start(bf16[64,128]{1,0:T(8,128)(2,1)} %new_key_ref.1) | copy-start | bytes 49156
  0.0 1.0 %copy-start.12 = (bf16[64,128]{1,0:T(8,128)(2,1)S(1)}, bf16[64,128]{1,0:T(8,128)(2,1)}, u32[]{:S(2)}) copy-start(bf16[64,128]{1,0:T(8,128)(2,1)} %new_value_ref.1) | copy-start | bytes 49156
  0.0 1.8 %copy-start = (bf16[512,2048]{1,0:T(8,128)(2,1)S(1)}, bf16[512,2048]{1,0:T(8,128)(2,1)}, u32[]{:S(2)}) copy-start(bf16[512,2048]{1,0:T(8,128)(2,1)} %weight_ref.3) | copy-start | bytes 6291460
  0.0 2.6 %copy-start.4 = (bf16[64,512]{1,0:T(8,128)(2,1)S(1)}, bf16[64,512]{1,0:T(8,128)(2,1)}, u32[]{:S(2)}) copy-start(bf16[64,512]{1,0:T(8,128)(2,1)} %residual_ref.1) | copy-start | bytes 196612
  1.0 9.5 %copy-start.5 = (s32[64,2]{0,1:T(2,128)S(1)}, s32[64,2]{0,1:T(2,128)}, u32[]{:S(2)}) copy-start(s32[64,2]{0,1:T(2,128)} %param.25) | copy-start | bytes 1540
  1.0 9.5 %copy-start.6 = (f32[64,2]{0,1:T(2,128)S(1)}, f32[64,2]{0,1:T(2,128)}, u32[]{:S(2)}) copy-start(f32[64,2]{0,1:T(2,128)} %param.26) | copy-start | bytes 1540
  1.8 9.0 %copy-start.1 = (bf16[1,2048,192]{1,2,0:T(8,128)(2,1)S(1)}, bf16[1,2048,192]{1,2,0:T(8,128)(2,1)}, u32[]{:S(2)}) copy-start(bf16[1,2048,192]{1,2,0:T(8,128)(2,1)} %param.27) | copy-start | bytes 2359300
  1.8 9.5 %copy-start.2 = (bf16[1,2048,192]{1,2,0:T(8,128)(2,1)S(1)}, bf16[1,2048,192]{1,2,0:T(8,128)(2,1)}, u32[]{:S(2)}) copy-start(bf16[1,2048,192]{1,2,0:T(8,128)(2,1)} %param.28) | copy-start | bytes 2359300
  2.1 1.5 %collective-permute-start = (bf16[64,1024]{1,0:T(8,128)(2,1)S(1)}, bf16[64,1024]{1,0:T(8,128)(2,1)S(1)}, u32[]{:S(2)}, u32[]{:S(2)}) collective-permute-start(bf16[64,1024]{1,0:T(8,128)(2,1)S(1)} %project_given.1.after_ref), channel_id=1, source_target_pairs={{0,1},{1,0},{2,3},{3,2},{4,5},{5,4},{6,7},{7,6},{8,9},{9,8},{10,11... | collective-permute-start | bytes 393224 | tf_op jit(solution)/shard_map/ppermute | solution.py:414
  3.7 6.7 %collective-permute-start.1 = (bf16[64,1024]{1,0:T(8,128)(2,1)S(1)}, bf16[64,1024]{1,0:T(8,128)(2,1)S(1)}, u32[]{:S(2)}, u32[]{:S(2)}) collective-permute-start(bf16[64,1024]{1,0:T(8,128)(2,1)S(1)} %get-tuple-element.31), channel_id=1, source_target_pairs={{0,2},{1,3},{2,0},{3,1},{4,6},{5,7},{6,4},{7,5},{8,10},{9,11},{10,... | collective-permute-start | bytes 393224 | tf_op jit(solution)/shard_map/ppermute | solution.py:417
  10.4 1.4 %collective-permute-start.4 = (bf16[64,1024]{1,0:T(8,128)(2,1)S(1)}, bf16[64,1024]{1,0:T(8,128)(2,1)S(1)}, u32[]{:S(2)}, u32[]{:S(2)}) collective-permute-start(bf16[64,1024]{1,0:T(8,128)(2,1)S(1)} %add_half.1.after_ref.part_ref), channel_id=1, source_target_pairs={{0,1},{1,0},{2,3},{3,2},{4,5},{5,4},{6,7},{7,6},{8,9},{9,8},{10,11... | collective-permute-start | bytes 393224 | tf_op jit(solution)/shard_map/ppermute | solution.py:414
  10.8 5.2 %collective-permute-start.2 = (bf16[192,2048]{1,0:T(8,128)(2,1)S(1)}, bf16[192,2048]{1,0:T(8,128)(2,1)S(1)}, u32[]{:S(2)}, u32[]{:S(2)}) collective-permute-start(bf16[192,2048]{1,0:T(8,128)(2,1)S(1)} %bitcast.12), channel_id=1, source_target_pairs={{0,1},{1,0},{2,3},{3,2},{4,5},{5,4},{6,7},{7,6},{8,9},{9,8},{10,11... | collective-permute-start | bytes 2359304 | tf_op jit(solution)/shard_map/ppermute | solution.py:414
  11.3 9.4 %collective-permute-start.3 = (bf16[192,2048]{1,0:T(8,128)(2,1)S(1)}, bf16[192,2048]{1,0:T(8,128)(2,1)S(1)}, u32[]{:S(2)}, u32[]{:S(2)}) collective-permute-start(bf16[192,2048]{1,0:T(8,128)(2,1)S(1)} %bitcast.14), channel_id=1, source_target_pairs={{0,1},{1,0},{2,3},{3,2},{4,5},{5,4},{6,7},{7,6},{8,9},{9,8},{10,11... | collective-permute-start | bytes 2359304 | tf_op jit(solution)/shard_map/ppermute | solution.py:414
  12.1 6.7 %collective-permute-start.6 = (bf16[272,128]{1,0:T(8,128)(2,1)S(1)}, bf16[272,128]{1,0:T(8,128)(2,1)S(1)}, u32[]{:S(2)}, u32[]{:S(2)}) collective-permute-start(bf16[272,128]{1,0:T(8,128)(2,1)S(1)} %get-tuple-element.39), channel_id=1, source_target_pairs={{0,24},{1,29},{2,26},{3,31},{4,28},{5,25},{6,30},{7,27},{8,16},{9,... | collective-permute-start | bytes 208904 | tf_op jit(solution)/shard_map/ppermute | solution.py:533
  16.0 9.6 %collective-permute-start.5 = (bf16[528,128]{1,0:T(8,128)(2,1)S(1)}, bf16[528,128]{1,0:T(8,128)(2,1)S(1)}, u32[]{:S(2)}, u32[]{:S(2)}) collective-permute-start(bf16[528,128]{1,0:T(8,128)(2,1)S(1)} %get-tuple-element.38), channel_id=1, source_target_pairs={{0,16},{1,21},{2,18},{3,23},{4,20},{5,17},{6,22},{7,19},{8,24},{9,... | collective-permute-start | bytes 405512 | tf_op jit(solution)/shard_map/ppermute | solution.py:533
  16.2 9.4 %collective-permute-start.7 = (bf16[528,128]{1,0:T(8,128)(2,1)S(1)}, bf16[528,128]{1,0:T(8,128)(2,1)S(1)}, u32[]{:S(2)}, u32[]{:S(2)}) collective-permute-start(bf16[528,128]{1,0:T(8,128)(2,1)S(1)} %get-tuple-element.40), channel_id=1, source_target_pairs={{0,8},{1,13},{2,10},{3,15},{4,12},{5,9},{6,14},{7,11},{8,0},{9,5},... | collective-permute-start | bytes 405512 | tf_op jit(solution)/shard_map/ppermute | solution.py:533
  16.9 4.9 %copy-start.3 = (bf16[1,768,512]{2,1,0:T(8,128)(2,1)S(1)}, bf16[1,768,512]{2,1,0:T(8,128)(2,1)}, u32[]{:S(2)}) copy-start(bf16[1,768,512]{2,1,0:T(8,128)(2,1)} %param.29) | copy-start | bytes 2359300
  16.9 8.7 %copy-start.13 = (f32[2048]{0:T(1024)S(1)}, f32[2048]{0:T(1024)}, u32[]{:S(2)}) copy-start(f32[2048]{0:T(1024)} %param.24) | copy-start | bytes 24580
  16.9 8.7 %collective-permute-start.8 = (bf16[528,128]{1,0:T(8,128)(2,1)S(1)}, bf16[528,128]{1,0:T(8,128)(2,1)S(1)}, u32[]{:S(2)}, u32[]{:S(2)}) collective-permute-start(bf16[528,128]{1,0:T(8,128)(2,1)S(1)} %get-tuple-element.41), channel_id=1, source_target_pairs={{0,0},{1,5},{2,2},{3,7},{4,4},{5,1},{6,6},{7,3},{8,8},{9,13},{10,1... | collective-permute-start | bytes 405512 | tf_op jit(solution)/shard_map/ppermute | solution.py:533
  18.8 6.8 %collective-permute-start.9 = (bf16[272,128]{1,0:T(8,128)(2,1)S(1)}, bf16[272,128]{1,0:T(8,128)(2,1)S(1)}, u32[]{:S(2)}, u32[]{:S(2)}) collective-permute-start(bf16[272,128]{1,0:T(8,128)(2,1)S(1)} %collective-permute-done.6.refs_1_), channel_id=1, source_target_pairs={{0,2},{1,3},{2,0},{3,1},{4,6},{5,7},{6,4},{7,5},{8,10},{9,11},{10,... | collective-permute-start | bytes 208904 | tf_op jit(solution)/shard_map/ppermute | solution.py:417
  21.9 11.1 %collective-permute-start.14 = (bf16[768,512]{1,0:T(8,128)(2,1)S(1)}, bf16[768,512]{1,0:T(8,128)(2,1)S(1)}, u32[]{:S(2)}, u32[]{:S(2)}) collective-permute-start(bf16[768,512]{1,0:T(8,128)(2,1)S(1)} %bitcast.16), channel_id=1, source_target_pairs={{0,1},{1,0},{2,3},{3,2},{4,5},{5,4},{6,7},{7,6},{8,9},{9,8},{10,11... | collective-permute-start | bytes 2359304 | tf_op jit(solution)/shard_map/ppermute | solution.py:414
  25.7 6.0 %copy-start.7 = (s32[8]{0:T(128)S(1)}, s32[8]{0:T(128)}, u32[]{:S(2)}) copy-start(s32[8]{0:T(128)} %order_ref.1) | copy-start | bytes 100
  26.4 5.3 %collective-permute-start.10 = (bf16[4,272,128]{2,1,0:T(8,128)(2,1)S(1)}, bf16[4,272,128]{2,1,0:T(8,128)(2,1)S(1)}, u32[]{:S(2)}, u32[]{:S(2)}) collective-permute-start(bf16[4,272,128]{2,1,0:T(8,128)(2,1)S(1)} %get-tuple-element.42.side_ref), channel_id=1, source_target_pairs={{0,1},{1,0},{2,3},{3,2},{4,5},{5,4},{6,7},{7,6},{8,9},{9,8},{10,11... | collective-permute-start | bytes 835592 | tf_op jit(solution)/shard_map/ppermute | solution.py:414
  26.8 4.8 %collective-permute-start.11 = (bf16[128,384]{1,0:T(8,128)(2,1)S(1)}, bf16[128,384]{1,0:T(8,128)(2,1)S(1)}, u32[]{:S(2)}, u32[]{:S(2)}) collective-permute-start(bf16[128,384]{1,0:T(8,128)(2,1)S(1)} %get-tuple-element.44.act_ref), channel_id=1, source_target_pairs={{0,2},{1,3},{2,0},{3,1},{4,6},{5,7},{6,4},{7,5},{8,10},{9,11},{10,... | collective-permute-start | bytes 294920 | tf_op jit(solution)/shard_map/ppermute | solution.py:417
  28.3 4.3 %collective-permute-start.12 = (bf16[128,384]{1,0:T(8,128)(2,1)S(1)}, bf16[128,384]{1,0:T(8,128)(2,1)S(1)}, u32[]{:S(2)}, u32[]{:S(2)}) collective-permute-start(bf16[128,384]{1,0:T(8,128)(2,1)S(1)} %get-tuple-element.44.act_ref), channel_id=1, source_target_pairs={{0,1},{1,0},{2,3},{3,2},{4,5},{5,4},{6,7},{7,6},{8,9},{9,8},{10,11... | collective-permute-start | bytes 294920 | tf_op jit(solution)/shard_map/ppermute | solution.py:414
  31.7 1.3 %collective-permute-start.13 = (bf16[128,384]{1,0:T(8,128)(2,1)S(1)}, bf16[128,384]{1,0:T(8,128)(2,1)S(1)}, u32[]{:S(2)}, u32[]{:S(2)}) collective-permute-start(bf16[128,384]{1,0:T(8,128)(2,1)S(1)} %collective-permute-done.11.act_half_ref), channel_id=1, source_target_pairs={{0,1},{1,0},{2,3},{3,2},{4,5},{5,4},{6,7},{7,6},{8,9},{9,8},{10,11... | collective-permute-start | bytes 294920 | tf_op jit(solution)/shard_map/ppermute | solution.py:414
  33.6 8.8 %collective-permute-start.15 = (bf16[256,128]{1,0:T(8,128)(2,1)S(1)}, bf16[256,128]{1,0:T(8,128)(2,1)S(1)}, u32[]{:S(2)}, u32[]{:S(2)}) collective-permute-start(bf16[256,128]{1,0:T(8,128)(2,1)S(1)} %get-tuple-element.49), channel_id=1, source_target_pairs={{0,16},{1,21},{2,18},{3,23},{4,20},{5,17},{6,22},{7,19},{8,24},{9,... | collective-permute-start | bytes 196616 | tf_op jit(solution)/shard_map/ppermute | solution.py:620
  35.2 7.2 %collective-permute-start.16 = (bf16[256,128]{1,0:T(8,128)(2,1)S(1)}, bf16[256,128]{1,0:T(8,128)(2,1)S(1)}, u32[]{:S(2)}, u32[]{:S(2)}) collective-permute-start(bf16[256,128]{1,0:T(8,128)(2,1)S(1)} %get-tuple-element.50), channel_id=1, source_target_pairs={{0,24},{1,29},{2,26},{3,31},{4,28},{5,25},{6,30},{7,27},{8,16},{9,... | collective-permute-start | bytes 196616 | tf_op jit(solution)/shard_map/ppermute | solution.py:620
  38.0 5.7 %collective-permute-start.17 = (bf16[256,128]{1,0:T(8,128)(2,1)S(1)}, bf16[256,128]{1,0:T(8,128)(2,1)S(1)}, u32[]{:S(2)}, u32[]{:S(2)}) collective-permute-start(bf16[256,128]{1,0:T(8,128)(2,1)S(1)} %get-tuple-element.51), channel_id=1, source_target_pairs={{0,8},{1,13},{2,10},{3,15},{4,12},{5,9},{6,14},{7,11},{8,0},{9,5},... | collective-permute-start | bytes 196616 | tf_op jit(solution)/shard_map/ppermute | solution.py:620
  38.0 5.7 %collective-permute-start.18 = (bf16[256,128]{1,0:T(8,128)(2,1)S(1)}, bf16[256,128]{1,0:T(8,128)(2,1)S(1)}, u32[]{:S(2)}, u32[]{:S(2)}) collective-permute-start(bf16[256,128]{1,0:T(8,128)(2,1)S(1)} %get-tuple-element.52), channel_id=1, source_target_pairs={{0,0},{1,5},{2,2},{3,7},{4,4},{5,1},{6,6},{7,3},{8,8},{9,13},{10,1... | collective-permute-start | bytes 196616 | tf_op jit(solution)/shard_map/ppermute | solution.py:620
  43.9 1.3 %collective-permute-start.19 = (bf16[64,512]{1,0:T(8,128)(2,1)S(1)}, bf16[64,512]{1,0:T(8,128)(2,1)S(1)}, u32[]{:S(2)}, u32[]{:S(2)}) collective-permute-start(bf16[64,512]{1,0:T(8,128)(2,1)S(1)} %get-tuple-element.54), channel_id=1, source_target_pairs={{0,1},{1,0},{2,3},{3,2},{4,5},{5,4},{6,7},{7,6},{8,9},{9,8},{10,11... | collective-permute-start | bytes 196616 | tf_op jit(solution)/shard_map/ppermute | solution.py:414

commit v11 on v10

--- a/solution.py
+++ b/solution.py
@@ -163,9 +163,9 @@
     for k in range(peers):
         pick = jnp.where(rank[k : k + 1, :] == slot, 1.0, 0.0).astype(BF16)
         pick_ref[k * rows_each : (k + 1) * rows_each, :] = pick
-        tags_ref[k, :, :tokens] = names.astype(BF16)
         mix = jnp.where(line == 0, mix_of[k : k + 1, :], 0.0).astype(BF16)
-        tags_ref[k, :1, :rows_each] = dot_t(mix, pick)[:1].astype(BF16)
+        every = jnp.concatenate([pick, jnp.zeros((tokens - rows_each, tokens), BF16)], axis=0)
+        tags_ref[k, :, :tokens] = (names + dot_t(mix, every)).astype(BF16)
 
 
 def select_kernel(

time: 46.1 us -> 46.1 us (level)
  no operation moved by 1% of the time
where the time goes in v11:
time: 46.1 us; the launch traced here: 45.9 us
  starting transfers between devices  20.1 us (44%)
  waiting for transfers between devices  18.2 us (39%)
  Pallas kernels  6.21 us (13%)
  between operations  1 us (2%)
    ppermute x3, waiting for transfers between devices, swap_half(): return lax.ppermute(x, 'tp', [(i, i ^ 2) for i in range(tp_count)])  7.16 us
    ppermute x3, starting transfers between devices, swap_half(): return lax.ppermute(x, 'tp', [(i, i ^ 2) for i in range(tp_count)])  6.31 us
    ppermute x4, starting transfers between devices, shards(): got = [lax.ppermute(send[k], ('ep', 'tp'), route(k)) for k in range(peers)]  5.42 us
    ppermute x4, waiting for transfers between devices, shards(): came = [lax.ppermute(send[k], ('ep', 'tp'), route(k)) for k in order]  5.08 us
    ppermute x4, starting transfers between devices, shards(): came = [lax.ppermute(send[k], ('ep', 'tp'), route(k)) for k in order]  5.05 us
    ppermute x4, waiting for transfers between devices, shards(): got = [lax.ppermute(send[k], ('ep', 'tp'), route(k)) for k in range(peers)]  3.5 us
    ppermute x9, starting transfers between devices, swap_core(): return lax.ppermute(x, 'tp', [(i, i ^ 1) for i in range(tp_count)])  3.31 us
    ppermute x9, waiting for transfers between devices, swap_core(): return lax.ppermute(x, 'tp', [(i, i ^ 1) for i in range(tp_count)])  2.43 us
  transfers between devices with their start and end apart: 20, of which 10 were waited for; matrix products, arithmetic and copies ran while one was open for 0% of the time, Pallas kernels for 8%

profile of v11, /device:TPU:0, one launch (start us, length us, event | category | flops | bytes accessed | tf_op | source)
XLA Modules:
  0.0 45.9 jit_solution(12255654063710158484)
XLA Ops:
  0.0 0.0 copy-start
  0.0 0.0 copy-start.4
  0.8 0.1 copy-done.8
  0.9 0.1 copy-done.9
  1.0 0.0 copy-done.10
  1.0 0.0 copy-done.11
  1.0 0.0 copy-done.12
  1.0 0.0 copy-start.6
  1.0 0.6 %attend.1.context_ref = bf16[64,512]{1,0:T(8,128)(2,1)S(1)} custom-call(f32[8,128]{1,0:T(8,128)S(1)} %begin.1.after_ref, s32[1]{0:T(128)S(6)} %copy.16.length_ref, bf16[64,512]{1,0:T(8,128)(2,1)S(1)} %copy-done.10, bf16[64,128]{1,0:T(8,128)(2,1)S(1)} %copy-done.11, bf16[64,128]{1,0:T(8,128)(2,1)S(1)} %copy-done.12, bf16[512,128]{1,0:T(8,128)(2,1)S(1)} %bitcast.20, ...), custom_call_target="tpu_custom_call" | custom-call | flops 200000000 | bytes 524288 | tf_op jit(solution)/shard_map/attend/pallas_call | solution.py:440
  1.6 0.3 copy-done
  1.8 0.3 project_given.1.after_ref
  2.1 0.5 %collective-permute-start = (bf16[64,1024]{1,0:T(8,128)(2,1)S(1)}, bf16[64,1024]{1,0:T(8,128)(2,1)S(1)}, u32[]{:S(2)}, u32[]{:S(2)}) collective-permute-start(bf16[64,1024]{1,0:T(8,128)(2,1)S(1)} %project_given.1.after_ref), channel_id=1, source_target_pairs={{0,1},{1,0},{2,3},{3,2},{4,5},{5,4},{6,7},{7,6},{8,9},{9,8},{10,11... | collective-permute-start | bytes 393224 | tf_op jit(solution)/shard_map/ppermute | solution.py:414
  2.7 0.3 project_kept.1.keep_ref
  3.0 0.7 %collective-permute-done.came_ref = bf16[64,1024]{1,0:T(8,128)(2,1)S(1)} collective-permute-done((bf16[64,1024]{1,0:T(8,128)(2,1)S(1)}, bf16[64,1024]{1,0:T(8,128)(2,1)S(1)}, u32[]{:S(2)}, u32[]{:S(2)}) %collective-permute-start) | collective-permute-done | bytes 131104 | tf_op jit(solution)/shard_map/ppermute | solution.py:414
  3.7 2.9 %collective-permute-start.1 = (bf16[64,1024]{1,0:T(8,128)(2,1)S(1)}, bf16[64,1024]{1,0:T(8,128)(2,1)S(1)}, u32[]{:S(2)}, u32[]{:S(2)}) collective-permute-start(bf16[64,1024]{1,0:T(8,128)(2,1)S(1)} %get-tuple-element.31), channel_id=1, source_target_pairs={{0,2},{1,3},{2,0},{3,1},{4,6},{5,7},{6,4},{7,5},{8,10},{9,11},{10,... | collective-permute-start | bytes 393224 | tf_op jit(solution)/shard_map/ppermute | solution.py:417
  6.6 3.8 %collective-permute-done.1.came_ref = bf16[64,1024]{1,0:T(8,128)(2,1)S(1)} collective-permute-done((bf16[64,1024]{1,0:T(8,128)(2,1)S(1)}, bf16[64,1024]{1,0:T(8,128)(2,1)S(1)}, u32[]{:S(2)}, u32[]{:S(2)}) %collective-permute-start.1) | collective-permute-done | bytes 131104 | tf_op jit(solution)/shard_map/ppermute | solution.py:417
  10.4 0.1 collective-permute-start.4
  10.5 0.3 route.1
  10.8 0.5 %collective-permute-start.2 = (bf16[192,2048]{1,0:T(8,128)(2,1)S(1)}, bf16[192,2048]{1,0:T(8,128)(2,1)S(1)}, u32[]{:S(2)}, u32[]{:S(2)}) collective-permute-start(bf16[192,2048]{1,0:T(8,128)(2,1)S(1)} %bitcast.12), channel_id=1, source_target_pairs={{0,1},{1,0},{2,3},{3,2},{4,5},{5,4},{6,7},{7,6},{8,9},{9,8},{10,11... | collective-permute-start | bytes 2359304 | tf_op jit(solution)/shard_map/ppermute | solution.py:414
  11.3 0.0 copy-done.2
  11.3 0.1 collective-permute-start.3
  11.4 0.4 collective-permute-done.4.other_ref
  11.9 0.2 gather_rows.2
  12.1 3.9 %collective-permute-start.6 = (bf16[272,128]{1,0:T(8,128)(2,1)S(1)}, bf16[272,128]{1,0:T(8,128)(2,1)S(1)}, u32[]{:S(2)}, u32[]{:S(2)}) collective-permute-start(bf16[272,128]{1,0:T(8,128)(2,1)S(1)} %get-tuple-element.39), channel_id=1, source_target_pairs={{0,24},{1,29},{2,26},{3,31},{4,28},{5,25},{6,30},{7,27},{8,16},{9,... | collective-permute-start | bytes 208904 | tf_op jit(solution)/shard_map/ppermute | solution.py:533
  16.0 0.0 collective-permute-start.5
  16.0 0.0 collective-permute-done.2.gate_pair.after_ref
  16.0 0.2 gather_rows.3
  16.2 0.7 %collective-permute-start.7 = (bf16[528,128]{1,0:T(8,128)(2,1)S(1)}, bf16[528,128]{1,0:T(8,128)(2,1)S(1)}, u32[]{:S(2)}, u32[]{:S(2)}) collective-permute-start(bf16[528,128]{1,0:T(8,128)(2,1)S(1)} %get-tuple-element.40), channel_id=1, source_target_pairs={{0,8},{1,13},{2,10},{3,15},{4,12},{5,9},{6,14},{7,11},{8,0},{9,5},... | collective-permute-start | bytes 405512 | tf_op jit(solution)/shard_map/ppermute | solution.py:533
  16.9 0.8 %collective-permute-start.8 = (bf16[528,128]{1,0:T(8,128)(2,1)S(1)}, bf16[528,128]{1,0:T(8,128)(2,1)S(1)}, u32[]{:S(2)}, u32[]{:S(2)}) collective-permute-start(bf16[528,128]{1,0:T(8,128)(2,1)S(1)} %get-tuple-element.41), channel_id=1, source_target_pairs={{0,0},{1,5},{2,2},{3,7},{4,4},{5,1},{6,6},{7,3},{8,8},{9,13},{10,1... | collective-permute-start | bytes 405512 | tf_op jit(solution)/shard_map/ppermute | solution.py:533
  17.7 1.1 %collective-permute-done.6.refs_1_ = bf16[272,128]{1,0:T(8,128)(2,1)S(1)} collective-permute-done((bf16[272,128]{1,0:T(8,128)(2,1)S(1)}, bf16[272,128]{1,0:T(8,128)(2,1)S(1)}, u32[]{:S(2)}, u32[]{:S(2)}) %collective-permute-start.6) | collective-permute-done | bytes 69664 | tf_op jit(solution)/shard_map/ppermute | solution.py:533
  18.8 1.9 %collective-permute-start.9 = (bf16[272,128]{1,0:T(8,128)(2,1)S(1)}, bf16[272,128]{1,0:T(8,128)(2,1)S(1)}, u32[]{:S(2)}, u32[]{:S(2)}) collective-permute-start(bf16[272,128]{1,0:T(8,128)(2,1)S(1)} %collective-permute-done.6.refs_1_), channel_id=1, source_target_pairs={{0,2},{1,3},{2,0},{3,1},{4,6},{5,7},{6,4},{7,5},{8,10},{9,11},{10,... | collective-permute-start | bytes 208904 | tf_op jit(solution)/shard_map/ppermute | solution.py:417
  20.7 0.0 collective-permute-done.3.up_pair
  20.7 1.1 %stage.1.weight_ref = bf16[2048,768]{1,0:T(8,128)(2,1)S(1)} custom-call(bf16[4,16,128]{2,1,0:T(8,128)(2,1)S(1)} %get-tuple-element.33.after_ref.tags_ref, bf16[192,2048]{1,0:T(8,128)(2,1)S(1)} %bitcast.13, bf16[192,2048]{1,0:T(8,128)(2,1)S(1)} %bitcast.15, bf16[192,2048]{1,0:T(8,128)(2,1)S(1)} %collective-permute-done.2.gate_pair.after_ref, ...), custom_call_target="tpu_custom_call" | custom-call | bytes 6291456 | tf_op jit(solution)/shard_map/stage/pallas_call | solution.py:536
  21.9 1.3 %collective-permute-start.14 = (bf16[768,512]{1,0:T(8,128)(2,1)S(1)}, bf16[768,512]{1,0:T(8,128)(2,1)S(1)}, u32[]{:S(2)}, u32[]{:S(2)}) collective-permute-start(bf16[768,512]{1,0:T(8,128)(2,1)S(1)} %bitcast.16), channel_id=1, source_target_pairs={{0,1},{1,0},{2,3},{3,2},{4,5},{5,4},{6,7},{7,6},{8,9},{9,8},{10,11... | collective-permute-start | bytes 2359304 | tf_op jit(solution)/shard_map/ppermute | solution.py:414
  23.2 2.4 %collective-permute-done.5.refs_0_ = bf16[528,128]{1,0:T(8,128)(2,1)S(1)} collective-permute-done((bf16[528,128]{1,0:T(8,128)(2,1)S(1)}, bf16[528,128]{1,0:T(8,128)(2,1)S(1)}, u32[]{:S(2)}, u32[]{:S(2)}) %collective-permute-start.5) | collective-permute-done | bytes 135200 | tf_op jit(solution)/shard_map/ppermute | solution.py:533
  25.6 0.0 collective-permute-done.9.refs_4_
  25.6 0.0 collective-permute-done.7.refs_2_
  25.6 0.0 collective-permute-done.8.refs_3_
  25.7 0.0 copy-start.7
  25.7 0.7 %hidden_units.1 = (bf16[128,384]{1,0:T(8,128)(2,1)S(1)}, bf16[4,272,128]{2,1,0:T(8,128)(2,1)S(1)}) custom-call(f32[16,128]{1,0:T(8,128)S(1)} %bitcast.22, bf16[2048,768]{1,0:T(8,128)(2,1)S(1)} %stage.1.weight_ref, bf16[528,128]{1,0:T(8,128)(2,1)S(1)} %collective-permute-done.5.refs_0_, bf16[272,128]{1,0:T(8,128)(2,1)S(1)} %collective-permute-done.6.refs_1_, ...), custom_call_target="tpu_custom_call" | custom-call | flops 20000000000 | bytes 1048576 | tf_op jit(solution)/shard_map/hidden_units/pallas_call | solution.py:555
  26.4 0.4 collective-permute-start.10
  26.8 1.5 %collective-permute-start.11 = (bf16[128,384]{1,0:T(8,128)(2,1)S(1)}, bf16[128,384]{1,0:T(8,128)(2,1)S(1)}, u32[]{:S(2)}, u32[]{:S(2)}) collective-permute-start(bf16[128,384]{1,0:T(8,128)(2,1)S(1)} %get-tuple-element.44.act_ref), channel_id=1, source_target_pairs={{0,2},{1,3},{2,0},{3,1},{4,6},{5,7},{6,4},{7,5},{8,10},{9,11},{10,... | collective-permute-start | bytes 294920 | tf_op jit(solution)/shard_map/ppermute | solution.py:417
  28.3 0.0 collective-permute-start.12
  28.3 3.4 %collective-permute-done.11.act_half_ref = bf16[128,384]{1,0:T(8,128)(2,1)S(1)} collective-permute-done((bf16[128,384]{1,0:T(8,128)(2,1)S(1)}, bf16[128,384]{1,0:T(8,128)(2,1)S(1)}, u32[]{:S(2)}, u32[]{:S(2)}) %collective-permute-start.11) | collective-permute-done | bytes 98336 | tf_op jit(solution)/shard_map/ppermute | solution.py:417
  31.7 0.0 collective-permute-start.13
  31.7 0.0 collective-permute-done.10.side_core_ref
  31.7 0.0 copy-done.7
  31.7 1.0 %select.1 = (bf16[64,128]{1,0:T(8,128)(2,1)S(1)}, bf16[128,256]{1,0:T(8,128)(2,1)S(1)}, bf16[4,256,128]{2,1,0:T(8,128)(2,1)S(1)}, f32[128,128]{1,0:T(8,128)S(1)}) custom-call(s32[8]{0:T(128)S(1)} %copy-done.7, bf16[4,272,128]{2,1,0:T(8,128)(2,1)S(1)} %get-tuple-element.42.side_ref, bf16[4,272,128]{2,1,0:T(8,128)(2,1)S(1)} %collective-permute-done.10.side_core_ref), custom_call_target="tpu_custom_call" | custom-call | bytes 1048576 | tf_op jit(solution)/shard_map/select/pallas_call | solution.py:575
  32.7 0.0 collective-permute-done.12.act_core_ref
  32.7 0.3 collective-permute-done.13.act_both_ref
  33.0 0.0 collective-permute-done.14.down_pair_ref
  33.0 0.6 %down.1 = (bf16[256,128]{1,0:T(8,128)(2,1)S(1)}, bf16[256,128]{1,0:T(8,128)(2,1)S(1)}, bf16[256,128]{1,0:T(8,128)(2,1)S(1)}, bf16[256,128]{1,0:T(8,128)(2,1)S(1)}) custom-call(bf16[64,128]{1,0:T(8,128)(2,1)S(1)} %get-tuple-element.43.after_ref.chosen_ref, bf16[128,384]{1,0:T(8,128)(2,1)S(1)} %get-tuple-element.44.act_ref, ...), custom_call_target="tpu_custom_call" | custom-call | bytes 1048576 | tf_op jit(solution)/shard_map/down/pallas_call | solution.py:592
  33.6 1.6 %collective-permute-start.15 = (bf16[256,128]{1,0:T(8,128)(2,1)S(1)}, bf16[256,128]{1,0:T(8,128)(2,1)S(1)}, u32[]{:S(2)}, u32[]{:S(2)}) collective-permute-start(bf16[256,128]{1,0:T(8,128)(2,1)S(1)} %get-tuple-element.49), channel_id=1, source_target_pairs={{0,16},{1,21},{2,18},{3,23},{4,20},{5,17},{6,22},{7,19},{8,24},{9,... | collective-permute-start | bytes 196616 | tf_op jit(solution)/shard_map/ppermute | solution.py:620
  35.2 2.8 %collective-permute-start.16 = (bf16[256,128]{1,0:T(8,128)(2,1)S(1)}, bf16[256,128]{1,0:T(8,128)(2,1)S(1)}, u32[]{:S(2)}, u32[]{:S(2)}) collective-permute-start(bf16[256,128]{1,0:T(8,128)(2,1)S(1)} %get-tuple-element.50), channel_id=1, source_target_pairs={{0,24},{1,29},{2,26},{3,31},{4,28},{5,25},{6,30},{7,27},{8,16},{9,... | collective-permute-start | bytes 196616 | tf_op jit(solution)/shard_map/ppermute | solution.py:620
  38.0 0.0 collective-permute-start.17
  38.0 0.7 %collective-permute-start.18 = (bf16[256,128]{1,0:T(8,128)(2,1)S(1)}, bf16[256,128]{1,0:T(8,128)(2,1)S(1)}, u32[]{:S(2)}, u32[]{:S(2)}) collective-permute-start(bf16[256,128]{1,0:T(8,128)(2,1)S(1)} %get-tuple-element.52), channel_id=1, source_target_pairs={{0,0},{1,5},{2,2},{3,7},{4,4},{5,1},{6,6},{7,3},{8,8},{9,13},{10,1... | collective-permute-start | bytes 196616 | tf_op jit(solution)/shard_map/ppermute | solution.py:620
  38.6 3.8 %collective-permute-done.15.refs_0_ = bf16[256,128]{1,0:T(8,128)(2,1)S(1)} collective-permute-done((bf16[256,128]{1,0:T(8,128)(2,1)S(1)}, bf16[256,128]{1,0:T(8,128)(2,1)S(1)}, u32[]{:S(2)}, u32[]{:S(2)}) %collective-permute-start.15) | collective-permute-done | bytes 65568 | tf_op jit(solution)/shard_map/ppermute | solution.py:620
  42.4 0.0 collective-permute-done.16.refs_1_
  42.4 1.3 %collective-permute-done.17.refs_2_ = bf16[256,128]{1,0:T(8,128)(2,1)S(1)} collective-permute-done((bf16[256,128]{1,0:T(8,128)(2,1)S(1)}, bf16[256,128]{1,0:T(8,128)(2,1)S(1)}, u32[]{:S(2)}, u32[]{:S(2)}) %collective-permute-start.17) | collective-permute-done | bytes 65568 | tf_op jit(solution)/shard_map/ppermute | solution.py:620
  43.7 0.0 collective-permute-done.18.refs_3_
  43.7 0.2 combine.1
  43.9 0.3 collective-permute-start.19
  44.3 1.0 %collective-permute-done.19.came_ref = bf16[64,512]{1,0:T(8,128)(2,1)S(1)} collective-permute-done((bf16[64,512]{1,0:T(8,128)(2,1)S(1)}, bf16[64,512]{1,0:T(8,128)(2,1)S(1)}, u32[]{:S(2)}, u32[]{:S(2)}) %collective-permute-start.19) | collective-permute-done | bytes 65568 | tf_op jit(solution)/shard_map/ppermute | solution.py:414
  45.2 0.6 %add_output.1 = bf16[64,512]{1,0:T(8,128)(2,1)} custom-call(f32[64,512]{1,0:T(8,128)S(1)} %get-tuple-element.53.sum_ref, bf16[64,512]{1,0:T(8,128)(2,1)S(1)} %collective-permute-done.19.came_ref), custom_call_target="tpu_custom_call" | custom-call | tf_op jit(solution)/shard_map/add_output/pallas_call | solution.py:630
  (19 shorter events, 0.1 us)
Async XLA Ops:
  0.0 0.9 %copy-start.8 = (bf16[1,512,128]{2,1,0:T(8,128)(2,1)S(1)}, bf16[1,512,128]{2,1,0:T(8,128)(2,1)}, u32[]{:S(2)}) copy-start(bf16[1,512,128]{2,1,0:T(8,128)(2,1)} %param.18) | copy-start | bytes 393220
  0.0 1.0 %copy-start.9 = (bf16[1,512,128]{2,1,0:T(8,128)(2,1)S(1)}, bf16[1,512,128]{2,1,0:T(8,128)(2,1)}, u32[]{:S(2)}) copy-start(bf16[1,512,128]{2,1,0:T(8,128)(2,1)} %param.19) | copy-start | bytes 393220
  0.0 1.0 %copy-start.10 = (bf16[64,512]{1,0:T(8,128)(2,1)S(1)}, bf16[64,512]{1,0:T(8,128)(2,1)}, u32[]{:S(2)}) copy-start(bf16[64,512]{1,0:T(8,128)(2,1)} %query_ref.1) | copy-start | bytes 196612
  0.0 1.0 %copy-start.11 = (bf16[64,128]{1,0:T(8,128)(2,1)S(1)}, bf16[64,128]{1,0:T(8,128)(2,1)}, u32[]{:S(2)}) copy-start(bf16[64,128]{1,0:T(8,128)(2,1)} %new_key_ref.1) | copy-start | bytes 49156
  0.0 1.0 %copy-start.12 = (bf16[64,128]{1,0:T(8,128)(2,1)S(1)}, bf16[64,128]{1,0:T(8,128)(2,1)}, u32[]{:S(2)}) copy-start(bf16[64,128]{1,0:T(8,128)(2,1)} %new_value_ref.1) | copy-start | bytes 49156
  0.0 1.8 %copy-start = (bf16[512,2048]{1,0:T(8,128)(2,1)S(1)}, bf16[512,2048]{1,0:T(8,128)(2,1)}, u32[]{:S(2)}) copy-start(bf16[512,2048]{1,0:T(8,128)(2,1)} %weight_ref.3) | copy-start | bytes 6291460
  0.0 2.6 %copy-start.4 = (bf16[64,512]{1,0:T(8,128)(2,1)S(1)}, bf16[64,512]{1,0:T(8,128)(2,1)}, u32[]{:S(2)}) copy-start(bf16[64,512]{1,0:T(8,128)(2,1)} %residual_ref.1) | copy-start | bytes 196612
  1.0 9.5 %copy-start.5 = (s32[64,2]{0,1:T(2,128)S(1)}, s32[64,2]{0,1:T(2,128)}, u32[]{:S(2)}) copy-start(s32[64,2]{0,1:T(2,128)} %param.25) | copy-start | bytes 1540
  1.0 9.5 %copy-start.6 = (f32[64,2]{0,1:T(2,128)S(1)}, f32[64,2]{0,1:T(2,128)}, u32[]{:S(2)}) copy-start(f32[64,2]{0,1:T(2,128)} %param.26) | copy-start | bytes 1540
  1.8 9.0 %copy-start.1 = (bf16[1,2048,192]{1,2,0:T(8,128)(2,1)S(1)}, bf16[1,2048,192]{1,2,0:T(8,128)(2,1)}, u32[]{:S(2)}) copy-start(bf16[1,2048,192]{1,2,0:T(8,128)(2,1)} %param.27) | copy-start | bytes 2359300
  1.8 9.5 %copy-start.2 = (bf16[1,2048,192]{1,2,0:T(8,128)(2,1)S(1)}, bf16[1,2048,192]{1,2,0:T(8,128)(2,1)}, u32[]{:S(2)}) copy-start(bf16[1,2048,192]{1,2,0:T(8,128)(2,1)} %param.28) | copy-start | bytes 2359300
  2.1 1.5 %collective-permute-start = (bf16[64,1024]{1,0:T(8,128)(2,1)S(1)}, bf16[64,1024]{1,0:T(8,128)(2,1)S(1)}, u32[]{:S(2)}, u32[]{:S(2)}) collective-permute-start(bf16[64,1024]{1,0:T(8,128)(2,1)S(1)} %project_given.1.after_ref), channel_id=1, source_target_pairs={{0,1},{1,0},{2,3},{3,2},{4,5},{5,4},{6,7},{7,6},{8,9},{9,8},{10,11... | collective-permute-start | bytes 393224 | tf_op jit(solution)/shard_map/ppermute | solution.py:414
  3.7 6.7 %collective-permute-start.1 = (bf16[64,1024]{1,0:T(8,128)(2,1)S(1)}, bf16[64,1024]{1,0:T(8,128)(2,1)S(1)}, u32[]{:S(2)}, u32[]{:S(2)}) collective-permute-start(bf16[64,1024]{1,0:T(8,128)(2,1)S(1)} %get-tuple-element.31), channel_id=1, source_target_pairs={{0,2},{1,3},{2,0},{3,1},{4,6},{5,7},{6,4},{7,5},{8,10},{9,11},{10,... | collective-permute-start | bytes 393224 | tf_op jit(solution)/shard_map/ppermute | solution.py:417
  10.4 1.4 %collective-permute-start.4 = (bf16[64,1024]{1,0:T(8,128)(2,1)S(1)}, bf16[64,1024]{1,0:T(8,128)(2,1)S(1)}, u32[]{:S(2)}, u32[]{:S(2)}) collective-permute-start(bf16[64,1024]{1,0:T(8,128)(2,1)S(1)} %add_half.1.after_ref.part_ref), channel_id=1, source_target_pairs={{0,1},{1,0},{2,3},{3,2},{4,5},{5,4},{6,7},{7,6},{8,9},{9,8},{10,11... | collective-permute-start | bytes 393224 | tf_op jit(solution)/shard_map/ppermute | solution.py:414
  10.8 5.2 %collective-permute-start.2 = (bf16[192,2048]{1,0:T(8,128)(2,1)S(1)}, bf16[192,2048]{1,0:T(8,128)(2,1)S(1)}, u32[]{:S(2)}, u32[]{:S(2)}) collective-permute-start(bf16[192,2048]{1,0:T(8,128)(2,1)S(1)} %bitcast.12), channel_id=1, source_target_pairs={{0,1},{1,0},{2,3},{3,2},{4,5},{5,4},{6,7},{7,6},{8,9},{9,8},{10,11... | collective-permute-start | bytes 2359304 | tf_op jit(solution)/shard_map/ppermute | solution.py:414
  11.3 9.4 %collective-permute-start.3 = (bf16[192,2048]{1,0:T(8,128)(2,1)S(1)}, bf16[192,2048]{1,0:T(8,128)(2,1)S(1)}, u32[]{:S(2)}, u32[]{:S(2)}) collective-permute-start(bf16[192,2048]{1,0:T(8,128)(2,1)S(1)} %bitcast.14), channel_id=1, source_target_pairs={{0,1},{1,0},{2,3},{3,2},{4,5},{5,4},{6,7},{7,6},{8,9},{9,8},{10,11... | collective-permute-start | bytes 2359304 | tf_op jit(solution)/shard_map/ppermute | solution.py:414
  12.1 6.7 %collective-permute-start.6 = (bf16[272,128]{1,0:T(8,128)(2,1)S(1)}, bf16[272,128]{1,0:T(8,128)(2,1)S(1)}, u32[]{:S(2)}, u32[]{:S(2)}) collective-permute-start(bf16[272,128]{1,0:T(8,128)(2,1)S(1)} %get-tuple-element.39), channel_id=1, source_target_pairs={{0,24},{1,29},{2,26},{3,31},{4,28},{5,25},{6,30},{7,27},{8,16},{9,... | collective-permute-start | bytes 208904 | tf_op jit(solution)/shard_map/ppermute | solution.py:533
  16.0 9.6 %collective-permute-start.5 = (bf16[528,128]{1,0:T(8,128)(2,1)S(1)}, bf16[528,128]{1,0:T(8,128)(2,1)S(1)}, u32[]{:S(2)}, u32[]{:S(2)}) collective-permute-start(bf16[528,128]{1,0:T(8,128)(2,1)S(1)} %get-tuple-element.38), channel_id=1, source_target_pairs={{0,16},{1,21},{2,18},{3,23},{4,20},{5,17},{6,22},{7,19},{8,24},{9,... | collective-permute-start | bytes 405512 | tf_op jit(solution)/shard_map/ppermute | solution.py:533
  16.2 9.4 %collective-permute-start.7 = (bf16[528,128]{1,0:T(8,128)(2,1)S(1)}, bf16[528,128]{1,0:T(8,128)(2,1)S(1)}, u32[]{:S(2)}, u32[]{:S(2)}) collective-permute-start(bf16[528,128]{1,0:T(8,128)(2,1)S(1)} %get-tuple-element.40), channel_id=1, source_target_pairs={{0,8},{1,13},{2,10},{3,15},{4,12},{5,9},{6,14},{7,11},{8,0},{9,5},... | collective-permute-start | bytes 405512 | tf_op jit(solution)/shard_map/ppermute | solution.py:533
  16.9 4.9 %copy-start.3 = (bf16[1,768,512]{2,1,0:T(8,128)(2,1)S(1)}, bf16[1,768,512]{2,1,0:T(8,128)(2,1)}, u32[]{:S(2)}) copy-start(bf16[1,768,512]{2,1,0:T(8,128)(2,1)} %param.29) | copy-start | bytes 2359300
  16.9 8.7 %copy-start.13 = (f32[2048]{0:T(1024)S(1)}, f32[2048]{0:T(1024)}, u32[]{:S(2)}) copy-start(f32[2048]{0:T(1024)} %param.24) | copy-start | bytes 24580
  16.9 8.7 %collective-permute-start.8 = (bf16[528,128]{1,0:T(8,128)(2,1)S(1)}, bf16[528,128]{1,0:T(8,128)(2,1)S(1)}, u32[]{:S(2)}, u32[]{:S(2)}) collective-permute-start(bf16[528,128]{1,0:T(8,128)(2,1)S(1)} %get-tuple-element.41), channel_id=1, source_target_pairs={{0,0},{1,5},{2,2},{3,7},{4,4},{5,1},{6,6},{7,3},{8,8},{9,13},{10,1... | collective-permute-start | bytes 405512 | tf_op jit(solution)/shard_map/ppermute | solution.py:533
  18.8 6.8 %collective-permute-start.9 = (bf16[272,128]{1,0:T(8,128)(2,1)S(1)}, bf16[272,128]{1,0:T(8,128)(2,1)S(1)}, u32[]{:S(2)}, u32[]{:S(2)}) collective-permute-start(bf16[272,128]{1,0:T(8,128)(2,1)S(1)} %collective-permute-done.6.refs_1_), channel_id=1, source_target_pairs={{0,2},{1,3},{2,0},{3,1},{4,6},{5,7},{6,4},{7,5},{8,10},{9,11},{10,... | collective-permute-start | bytes 208904 | tf_op jit(solution)/shard_map/ppermute | solution.py:417
  21.9 11.1 %collective-permute-start.14 = (bf16[768,512]{1,0:T(8,128)(2,1)S(1)}, bf16[768,512]{1,0:T(8,128)(2,1)S(1)}, u32[]{:S(2)}, u32[]{:S(2)}) collective-permute-start(bf16[768,512]{1,0:T(8,128)(2,1)S(1)} %bitcast.16), channel_id=1, source_target_pairs={{0,1},{1,0},{2,3},{3,2},{4,5},{5,4},{6,7},{7,6},{8,9},{9,8},{10,11... | collective-permute-start | bytes 2359304 | tf_op jit(solution)/shard_map/ppermute | solution.py:414
  25.7 6.0 %copy-start.7 = (s32[8]{0:T(128)S(1)}, s32[8]{0:T(128)}, u32[]{:S(2)}) copy-start(s32[8]{0:T(128)} %order_ref.1) | copy-start | bytes 100
  26.4 5.3 %collective-permute-start.10 = (bf16[4,272,128]{2,1,0:T(8,128)(2,1)S(1)}, bf16[4,272,128]{2,1,0:T(8,128)(2,1)S(1)}, u32[]{:S(2)}, u32[]{:S(2)}) collective-permute-start(bf16[4,272,128]{2,1,0:T(8,128)(2,1)S(1)} %get-tuple-element.42.side_ref), channel_id=1, source_target_pairs={{0,1},{1,0},{2,3},{3,2},{4,5},{5,4},{6,7},{7,6},{8,9},{9,8},{10,11... | collective-permute-start | bytes 835592 | tf_op jit(solution)/shard_map/ppermute | solution.py:414
  26.8 4.8 %collective-permute-start.11 = (bf16[128,384]{1,0:T(8,128)(2,1)S(1)}, bf16[128,384]{1,0:T(8,128)(2,1)S(1)}, u32[]{:S(2)}, u32[]{:S(2)}) collective-permute-start(bf16[128,384]{1,0:T(8,128)(2,1)S(1)} %get-tuple-element.44.act_ref), channel_id=1, source_target_pairs={{0,2},{1,3},{2,0},{3,1},{4,6},{5,7},{6,4},{7,5},{8,10},{9,11},{10,... | collective-permute-start | bytes 294920 | tf_op jit(solution)/shard_map/ppermute | solution.py:417
  28.3 4.3 %collective-permute-start.12 = (bf16[128,384]{1,0:T(8,128)(2,1)S(1)}, bf16[128,384]{1,0:T(8,128)(2,1)S(1)}, u32[]{:S(2)}, u32[]{:S(2)}) collective-permute-start(bf16[128,384]{1,0:T(8,128)(2,1)S(1)} %get-tuple-element.44.act_ref), channel_id=1, source_target_pairs={{0,1},{1,0},{2,3},{3,2},{4,5},{5,4},{6,7},{7,6},{8,9},{9,8},{10,11... | collective-permute-start | bytes 294920 | tf_op jit(solution)/shard_map/ppermute | solution.py:414
  31.7 1.3 %collective-permute-start.13 = (bf16[128,384]{1,0:T(8,128)(2,1)S(1)}, bf16[128,384]{1,0:T(8,128)(2,1)S(1)}, u32[]{:S(2)}, u32[]{:S(2)}) collective-permute-start(bf16[128,384]{1,0:T(8,128)(2,1)S(1)} %collective-permute-done.11.act_half_ref), channel_id=1, source_target_pairs={{0,1},{1,0},{2,3},{3,2},{4,5},{5,4},{6,7},{7,6},{8,9},{9,8},{10,11... | collective-permute-start | bytes 294920 | tf_op jit(solution)/shard_map/ppermute | solution.py:414
  33.6 8.8 %collective-permute-start.15 = (bf16[256,128]{1,0:T(8,128)(2,1)S(1)}, bf16[256,128]{1,0:T(8,128)(2,1)S(1)}, u32[]{:S(2)}, u32[]{:S(2)}) collective-permute-start(bf16[256,128]{1,0:T(8,128)(2,1)S(1)} %get-tuple-element.49), channel_id=1, source_target_pairs={{0,16},{1,21},{2,18},{3,23},{4,20},{5,17},{6,22},{7,19},{8,24},{9,... | collective-permute-start | bytes 196616 | tf_op jit(solution)/shard_map/ppermute | solution.py:620
  35.2 7.2 %collective-permute-start.16 = (bf16[256,128]{1,0:T(8,128)(2,1)S(1)}, bf16[256,128]{1,0:T(8,128)(2,1)S(1)}, u32[]{:S(2)}, u32[]{:S(2)}) collective-permute-start(bf16[256,128]{1,0:T(8,128)(2,1)S(1)} %get-tuple-element.50), channel_id=1, source_target_pairs={{0,24},{1,29},{2,26},{3,31},{4,28},{5,25},{6,30},{7,27},{8,16},{9,... | collective-permute-start | bytes 196616 | tf_op jit(solution)/shard_map/ppermute | solution.py:620
  38.0 5.7 %collective-permute-start.17 = (bf16[256,128]{1,0:T(8,128)(2,1)S(1)}, bf16[256,128]{1,0:T(8,128)(2,1)S(1)}, u32[]{:S(2)}, u32[]{:S(2)}) collective-permute-start(bf16[256,128]{1,0:T(8,128)(2,1)S(1)} %get-tuple-element.51), channel_id=1, source_target_pairs={{0,8},{1,13},{2,10},{3,15},{4,12},{5,9},{6,14},{7,11},{8,0},{9,5},... | collective-permute-start | bytes 196616 | tf_op jit(solution)/shard_map/ppermute | solution.py:620
  38.0 5.7 %collective-permute-start.18 = (bf16[256,128]{1,0:T(8,128)(2,1)S(1)}, bf16[256,128]{1,0:T(8,128)(2,1)S(1)}, u32[]{:S(2)}, u32[]{:S(2)}) collective-permute-start(bf16[256,128]{1,0:T(8,128)(2,1)S(1)} %get-tuple-element.52), channel_id=1, source_target_pairs={{0,0},{1,5},{2,2},{3,7},{4,4},{5,1},{6,6},{7,3},{8,8},{9,13},{10,1... | collective-permute-start | bytes 196616 | tf_op jit(solution)/shard_map/ppermute | solution.py:620
  43.9 1.3 %collective-permute-start.19 = (bf16[64,512]{1,0:T(8,128)(2,1)S(1)}, bf16[64,512]{1,0:T(8,128)(2,1)S(1)}, u32[]{:S(2)}, u32[]{:S(2)}) collective-permute-start(bf16[64,512]{1,0:T(8,128)(2,1)S(1)} %get-tuple-element.54), channel_id=1, source_target_pairs={{0,1},{1,0},{2,3},{3,2},{4,5},{5,4},{6,7},{7,6},{8,9},{9,8},{10,11... | collective-permute-start | bytes 196616 | tf_op jit(solution)/shard_map/ppermute | solution.py:414

commit v12 on v11

--- a/solution.py
+++ b/solution.py
@@ -378,6 +378,8 @@
 
 def combine_kernel(order, rows_each, chosen_ref, *refs):
     came = [refs[order.index(k)] for k in range(len(order))]
+    own_ref = refs[len(order)]
+    nearest = len(order) // 2 - 1
     keep_ref, give_ref = refs[-2:]
     core = lax.axis_index("tp") % 2
     chosen = chosen_ref[...]
@@ -385,7 +387,10 @@
     for ref, parity in ((give_ref, 1 - core), (keep_ref, core)):
         for j in range(tall // rows_each):
             start = pl.multiple_of(parity * tall + j * rows_each, rows_each)
-            rows = jnp.concatenate([block[pl.ds(start, rows_each), :] for block in came], axis=0)
+            pieces = [block[pl.ds(start, rows_each), :] for block in came]
+            own = own_ref[pl.ds(start, rows_each), :]
+            pieces[nearest] = jnp.where(core == 0, own, pieces[nearest])
+            rows = jnp.concatenate(pieces, axis=0)
             ref[:, j * LANES : (j + 1) * LANES] = dot(chosen, rows).astype(ref.dtype)
 
 
@@ -519,11 +524,12 @@
         )(after, part, other, pick, tags)
         return dict(zip(members, sent))
 
-    def route(k):
+    def route(k, own=True):
         return [
             (e * tp_count + t, (e ^ (2 * step(k, peers) + t % 2)) * tp_count + t)
             for e in range(ep_count)
             for t in range(tp_count)
+            if own or step(k, peers) or t % 2
         ]
 
     send = gather(list(reversed(range(near, peers))), tags)
@@ -584,7 +590,7 @@
         out_specs=(vmem(),) * 4,
         scratch_shapes=[pltpu.SMEM(request_order.shape, jnp.int32)],
         compiler_params=params(8),
-        cost_estimate=pl.CostEstimate(flops=0, bytes_accessed=MIB, transcendentals=0),
+        cost_estimate=pl.CostEstimate(flops=10 * 10**9, bytes_accessed=MIB, transcendentals=0),
         name="select",
     )(request_order, side, side_core)
 
@@ -617,16 +623,16 @@
 
     order = [*range(near, peers), *range(near)]
     send = results(list(range(peers)), chosen)
-    came = [lax.ppermute(send[k], ("ep", "tp"), route(k)) for k in order]
+    came = [lax.ppermute(send[k], ("ep", "tp"), route(k, False)) for k in order]
 
     keep, give = pl.pallas_call(
         functools.partial(combine_kernel, order, rows_each),
         out_shape=(shape((tokens, width), F32), shape((tokens, width), BF16)),
-        in_specs=[vmem()] * (1 + peers),
+        in_specs=[vmem()] * (2 + peers),
         out_specs=(vmem(), vmem()),
         compiler_params=params(8),
         name="combine",
-    )(chosen, *came)
+    )(chosen, *came, send[near - 1])
     return pl.pallas_call(
         add_half_kernel,
         out_shape=shape((tokens, width), BF16),

time: 46.1 us -> 46.1 us (level)
  starting transfers between devices: 20.1 us -> 19.3 us
  waiting for transfers between devices: 18.2 us -> 19 us
    ppermute x4, waiting for transfers between devices: 3.5 us -> 4.86 us  [shards(): got = [lax.ppermute(send[k], ('ep', 'tp'), route(k)) for k in range(peers)]]
    ppermute x9, starting transfers between devices: 3.31 us -> 2.48 us  [swap_core(): return lax.ppermute(x, 'tp', [(i, i ^ 1) for i in range(tp_count)])]
    ppermute x3, waiting for transfers between devices: 7.16 us -> 6.65 us  [swap_half(): return lax.ppermute(x, 'tp', [(i, i ^ 2) for i in range(tp_count)])]
  transfers between devices with their start and end apart: 20 -> 20, of which waited for: 10 -> 10; matrix products, arithmetic and copies ran while one was open for 0% -> 0% of each run, Pallas kernels for 8% -> 7%
where the time goes in v12:
time: 46.1 us; the launch traced here: 45.9 us
  starting transfers between devices  19.3 us (42%)
  waiting for transfers between devices  19 us (41%)
  Pallas kernels  6.19 us (13%)
  between operations  1 us (2%)
    ppermute x3, waiting for transfers between devices, swap_half(): return lax.ppermute(x, 'tp', [(i, i ^ 2) for i in range(tp_count)])  6.65 us
    ppermute x3, starting transfers between devices, swap_half(): return lax.ppermute(x, 'tp', [(i, i ^ 2) for i in range(tp_count)])  6.31 us
    ppermute x4, starting transfers between devices, shards(): got = [lax.ppermute(send[k], ('ep', 'tp'), route(k)) for k in range(peers)]  5.42 us
    ppermute x4, waiting for transfers between devices, shards(): came = [lax.ppermute(send[k], ('ep', 'tp'), route(k, False)) for k in order]  5.08 us
    ppermute x4, starting transfers between devices, shards(): came = [lax.ppermute(send[k], ('ep', 'tp'), route(k, False)) for k in order]  5.06 us
    ppermute x4, waiting for transfers between devices, shards(): got = [lax.ppermute(send[k], ('ep', 'tp'), route(k)) for k in range(peers)]  4.86 us
    ppermute x9, starting transfers between devices, swap_core(): return lax.ppermute(x, 'tp', [(i, i ^ 1) for i in range(tp_count)])  2.48 us
    ppermute x9, waiting for transfers between devices, swap_core(): return lax.ppermute(x, 'tp', [(i, i ^ 1) for i in range(tp_count)])  2.42 us
  transfers between devices with their start and end apart: 20, of which 10 were waited for; matrix products, arithmetic and copies ran while one was open for 0% of the time, Pallas kernels for 7%

profile of v12, /device:TPU:0, one launch (start us, length us, event | category | flops | bytes accessed | tf_op | source)
XLA Modules:
  0.0 45.9 jit_solution(16562846593345492157)
XLA Ops:
  0.0 0.0 copy-start
  0.0 0.0 copy-start.4
  0.8 0.1 copy-done.7
  0.9 0.1 copy-done.8
  1.0 0.0 copy-done.9
  1.0 0.0 copy-done.10
  1.0 0.0 copy-done.11
  1.0 0.0 copy-start.6
  1.0 0.6 %attend.1.context_ref = bf16[64,512]{1,0:T(8,128)(2,1)S(1)} custom-call(f32[8,128]{1,0:T(8,128)S(1)} %begin.1.after_ref, s32[1]{0:T(128)S(6)} %copy.16.length_ref, bf16[64,512]{1,0:T(8,128)(2,1)S(1)} %copy-done.9, bf16[64,128]{1,0:T(8,128)(2,1)S(1)} %copy-done.10, bf16[64,128]{1,0:T(8,128)(2,1)S(1)} %copy-done.11, bf16[512,128]{1,0:T(8,128)(2,1)S(1)} %bitcast.20, ...), custom_call_target="tpu_custom_call" | custom-call | flops 200000000 | bytes 524288 | tf_op jit(solution)/shard_map/attend/pallas_call | solution.py:445
  1.6 0.3 copy-done
  1.8 0.3 project_given.1.after_ref
  2.1 0.5 %collective-permute-start = (bf16[64,1024]{1,0:T(8,128)(2,1)S(1)}, bf16[64,1024]{1,0:T(8,128)(2,1)S(1)}, u32[]{:S(2)}, u32[]{:S(2)}) collective-permute-start(bf16[64,1024]{1,0:T(8,128)(2,1)S(1)} %project_given.1.after_ref), channel_id=1, source_target_pairs={{0,1},{1,0},{2,3},{3,2},{4,5},{5,4},{6,7},{7,6},{8,9},{9,8},{10,11... | collective-permute-start | bytes 393224 | tf_op jit(solution)/shard_map/ppermute | solution.py:419
  2.7 0.0 copy-done.4
  2.7 0.3 project_kept.1.keep_ref
  3.0 0.7 %collective-permute-done.came_ref = bf16[64,1024]{1,0:T(8,128)(2,1)S(1)} collective-permute-done((bf16[64,1024]{1,0:T(8,128)(2,1)S(1)}, bf16[64,1024]{1,0:T(8,128)(2,1)S(1)}, u32[]{:S(2)}, u32[]{:S(2)}) %collective-permute-start) | collective-permute-done | bytes 131104 | tf_op jit(solution)/shard_map/ppermute | solution.py:419
  3.7 2.9 %collective-permute-start.1 = (bf16[64,1024]{1,0:T(8,128)(2,1)S(1)}, bf16[64,1024]{1,0:T(8,128)(2,1)S(1)}, u32[]{:S(2)}, u32[]{:S(2)}) collective-permute-start(bf16[64,1024]{1,0:T(8,128)(2,1)S(1)} %get-tuple-element.31), channel_id=1, source_target_pairs={{0,2},{1,3},{2,0},{3,1},{4,6},{5,7},{6,4},{7,5},{8,10},{9,11},{10,... | collective-permute-start | bytes 393224 | tf_op jit(solution)/shard_map/ppermute | solution.py:422
  6.6 3.8 %collective-permute-done.1.came_ref = bf16[64,1024]{1,0:T(8,128)(2,1)S(1)} collective-permute-done((bf16[64,1024]{1,0:T(8,128)(2,1)S(1)}, bf16[64,1024]{1,0:T(8,128)(2,1)S(1)}, u32[]{:S(2)}, u32[]{:S(2)}) %collective-permute-start.1) | collective-permute-done | bytes 131104 | tf_op jit(solution)/shard_map/ppermute | solution.py:422
  10.4 0.1 collective-permute-start.4
  10.5 0.3 route.1
  10.8 0.5 %collective-permute-start.2 = (bf16[192,2048]{1,0:T(8,128)(2,1)S(1)}, bf16[192,2048]{1,0:T(8,128)(2,1)S(1)}, u32[]{:S(2)}, u32[]{:S(2)}) collective-permute-start(bf16[192,2048]{1,0:T(8,128)(2,1)S(1)} %bitcast.12), channel_id=1, source_target_pairs={{0,1},{1,0},{2,3},{3,2},{4,5},{5,4},{6,7},{7,6},{8,9},{9,8},{10,11... | collective-permute-start | bytes 2359304 | tf_op jit(solution)/shard_map/ppermute | solution.py:419
  11.3 0.1 collective-permute-start.3
  11.4 0.4 collective-permute-done.4.other_ref
  11.9 0.2 gather_rows.2
  12.1 3.9 %collective-permute-start.6 = (bf16[272,128]{1,0:T(8,128)(2,1)S(1)}, bf16[272,128]{1,0:T(8,128)(2,1)S(1)}, u32[]{:S(2)}, u32[]{:S(2)}) collective-permute-start(bf16[272,128]{1,0:T(8,128)(2,1)S(1)} %get-tuple-element.39), channel_id=1, source_target_pairs={{0,24},{1,29},{2,26},{3,31},{4,28},{5,25},{6,30},{7,27},{8,16},{9,... | collective-permute-start | bytes 208904 | tf_op jit(solution)/shard_map/ppermute | solution.py:539
  16.0 0.0 collective-permute-start.5
  16.0 0.0 collective-permute-done.2.gate_pair.after_ref
  16.0 0.2 gather_rows.3
  16.2 0.7 %collective-permute-start.7 = (bf16[528,128]{1,0:T(8,128)(2,1)S(1)}, bf16[528,128]{1,0:T(8,128)(2,1)S(1)}, u32[]{:S(2)}, u32[]{:S(2)}) collective-permute-start(bf16[528,128]{1,0:T(8,128)(2,1)S(1)} %get-tuple-element.40), channel_id=1, source_target_pairs={{0,8},{1,13},{2,10},{3,15},{4,12},{5,9},{6,14},{7,11},{8,0},{9,5},... | collective-permute-start | bytes 405512 | tf_op jit(solution)/shard_map/ppermute | solution.py:539
  16.9 0.8 %collective-permute-start.8 = (bf16[528,128]{1,0:T(8,128)(2,1)S(1)}, bf16[528,128]{1,0:T(8,128)(2,1)S(1)}, u32[]{:S(2)}, u32[]{:S(2)}) collective-permute-start(bf16[528,128]{1,0:T(8,128)(2,1)S(1)} %get-tuple-element.41), channel_id=1, source_target_pairs={{0,0},{1,5},{2,2},{3,7},{4,4},{5,1},{6,6},{7,3},{8,8},{9,13},{10,1... | collective-permute-start | bytes 405512 | tf_op jit(solution)/shard_map/ppermute | solution.py:539
  17.7 1.1 %collective-permute-done.6.refs_1_ = bf16[272,128]{1,0:T(8,128)(2,1)S(1)} collective-permute-done((bf16[272,128]{1,0:T(8,128)(2,1)S(1)}, bf16[272,128]{1,0:T(8,128)(2,1)S(1)}, u32[]{:S(2)}, u32[]{:S(2)}) %collective-permute-start.6) | collective-permute-done | bytes 69664 | tf_op jit(solution)/shard_map/ppermute | solution.py:539
  18.8 1.9 %collective-permute-start.9 = (bf16[272,128]{1,0:T(8,128)(2,1)S(1)}, bf16[272,128]{1,0:T(8,128)(2,1)S(1)}, u32[]{:S(2)}, u32[]{:S(2)}) collective-permute-start(bf16[272,128]{1,0:T(8,128)(2,1)S(1)} %collective-permute-done.6.refs_1_), channel_id=1, source_target_pairs={{0,2},{1,3},{2,0},{3,1},{4,6},{5,7},{6,4},{7,5},{8,10},{9,11},{10,... | collective-permute-start | bytes 208904 | tf_op jit(solution)/shard_map/ppermute | solution.py:422
  20.7 0.0 collective-permute-done.3.up_pair
  20.7 1.1 %stage.1.weight_ref = bf16[2048,768]{1,0:T(8,128)(2,1)S(1)} custom-call(bf16[4,16,128]{2,1,0:T(8,128)(2,1)S(1)} %get-tuple-element.33.after_ref.tags_ref, bf16[192,2048]{1,0:T(8,128)(2,1)S(1)} %bitcast.13, bf16[192,2048]{1,0:T(8,128)(2,1)S(1)} %bitcast.15, bf16[192,2048]{1,0:T(8,128)(2,1)S(1)} %collective-permute-done.2.gate_pair.after_ref, ...), custom_call_target="tpu_custom_call" | custom-call | bytes 6291456 | tf_op jit(solution)/shard_map/stage/pallas_call | solution.py:542
  21.9 3.8 %collective-permute-done.5.refs_0_ = bf16[528,128]{1,0:T(8,128)(2,1)S(1)} collective-permute-done((bf16[528,128]{1,0:T(8,128)(2,1)S(1)}, bf16[528,128]{1,0:T(8,128)(2,1)S(1)}, u32[]{:S(2)}, u32[]{:S(2)}) %collective-permute-start.5) | collective-permute-done | bytes 135200 | tf_op jit(solution)/shard_map/ppermute | solution.py:539
  25.6 0.0 collective-permute-done.9.refs_4_
  25.6 0.0 collective-permute-done.7.refs_2_
  25.6 0.0 collective-permute-done.8.refs_3_
  25.7 0.0 copy-start.3
  25.7 0.0 copy-start.13
  25.7 0.7 %hidden_units.1 = (bf16[128,384]{1,0:T(8,128)(2,1)S(1)}, bf16[4,272,128]{2,1,0:T(8,128)(2,1)S(1)}) custom-call(f32[16,128]{1,0:T(8,128)S(1)} %bitcast.22, bf16[2048,768]{1,0:T(8,128)(2,1)S(1)} %stage.1.weight_ref, bf16[528,128]{1,0:T(8,128)(2,1)S(1)} %collective-permute-done.5.refs_0_, bf16[272,128]{1,0:T(8,128)(2,1)S(1)} %collective-permute-done.6.refs_1_, ...), custom_call_target="tpu_custom_call" | custom-call | flops 20000000000 | bytes 1048576 | tf_op jit(solution)/shard_map/hidden_units/pallas_call | solution.py:561
  26.4 0.4 collective-permute-start.10
  26.8 1.5 %collective-permute-start.11 = (bf16[128,384]{1,0:T(8,128)(2,1)S(1)}, bf16[128,384]{1,0:T(8,128)(2,1)S(1)}, u32[]{:S(2)}, u32[]{:S(2)}) collective-permute-start(bf16[128,384]{1,0:T(8,128)(2,1)S(1)} %get-tuple-element.44.act_ref), channel_id=1, source_target_pairs={{0,2},{1,3},{2,0},{3,1},{4,6},{5,7},{6,4},{7,5},{8,10},{9,11},{10,... | collective-permute-start | bytes 294920 | tf_op jit(solution)/shard_map/ppermute | solution.py:422
  28.3 0.0 collective-permute-start.14
  28.3 0.5 %collective-permute-start.12 = (bf16[128,384]{1,0:T(8,128)(2,1)S(1)}, bf16[128,384]{1,0:T(8,128)(2,1)S(1)}, u32[]{:S(2)}, u32[]{:S(2)}) collective-permute-start(bf16[128,384]{1,0:T(8,128)(2,1)S(1)} %get-tuple-element.44.act_ref), channel_id=1, source_target_pairs={{0,1},{1,0},{2,3},{3,2},{4,5},{5,4},{6,7},{7,6},{8,9},{9,8},{10,11... | collective-permute-start | bytes 294920 | tf_op jit(solution)/shard_map/ppermute | solution.py:419
  28.8 2.8 %collective-permute-done.11.act_half_ref = bf16[128,384]{1,0:T(8,128)(2,1)S(1)} collective-permute-done((bf16[128,384]{1,0:T(8,128)(2,1)S(1)}, bf16[128,384]{1,0:T(8,128)(2,1)S(1)}, u32[]{:S(2)}, u32[]{:S(2)}) %collective-permute-start.11) | collective-permute-done | bytes 98336 | tf_op jit(solution)/shard_map/ppermute | solution.py:422
  31.7 0.0 collective-permute-start.13
  31.7 0.0 collective-permute-done.10.side_core_ref
  31.7 1.0 %select.1 = (bf16[64,128]{1,0:T(8,128)(2,1)S(1)}, bf16[128,256]{1,0:T(8,128)(2,1)S(1)}, bf16[4,256,128]{2,1,0:T(8,128)(2,1)S(1)}, f32[128,128]{1,0:T(8,128)S(1)}) custom-call(s32[8]{0:T(128)S(1)} %copy-done.13, bf16[4,272,128]{2,1,0:T(8,128)(2,1)S(1)} %get-tuple-element.42.side_ref, bf16[4,272,128]{2,1,0:T(8,128)(2,1)S(1)} %collective-permute-done.10.side_core_ref), custom_call_target="tpu_custom_call" | custom-call | flops 10000000000 | bytes 1048576 | tf_op jit(solution)/shard_map/select/pallas_call | solution.py:581
  32.7 0.0 collective-permute-done.12.act_core_ref
  32.7 0.3 collective-permute-done.13.act_both_ref
  33.0 0.0 collective-permute-done.14.down_pair_ref
  33.0 0.6 %down.1 = (bf16[256,128]{1,0:T(8,128)(2,1)S(1)}, bf16[256,128]{1,0:T(8,128)(2,1)S(1)}, bf16[256,128]{1,0:T(8,128)(2,1)S(1)}, bf16[256,128]{1,0:T(8,128)(2,1)S(1)}) custom-call(bf16[64,128]{1,0:T(8,128)(2,1)S(1)} %get-tuple-element.43.after_ref.chosen_ref, bf16[128,384]{1,0:T(8,128)(2,1)S(1)} %get-tuple-element.44.act_ref, ...), custom_call_target="tpu_custom_call" | custom-call | bytes 1048576 | tf_op jit(solution)/shard_map/down/pallas_call | solution.py:598
  33.6 1.5 %collective-permute-start.15 = (bf16[256,128]{1,0:T(8,128)(2,1)S(1)}, bf16[256,128]{1,0:T(8,128)(2,1)S(1)}, u32[]{:S(2)}, u32[]{:S(2)}) collective-permute-start(bf16[256,128]{1,0:T(8,128)(2,1)S(1)} %get-tuple-element.49), channel_id=1, source_target_pairs={{0,16},{1,21},{2,18},{3,23},{4,20},{5,17},{6,22},{7,19},{8,24},{9,... | collective-permute-start | bytes 196616 | tf_op jit(solution)/shard_map/ppermute | solution.py:626
  35.1 2.9 %collective-permute-start.16 = (bf16[256,128]{1,0:T(8,128)(2,1)S(1)}, bf16[256,128]{1,0:T(8,128)(2,1)S(1)}, u32[]{:S(2)}, u32[]{:S(2)}) collective-permute-start(bf16[256,128]{1,0:T(8,128)(2,1)S(1)} %get-tuple-element.50), channel_id=1, source_target_pairs={{0,24},{1,29},{2,26},{3,31},{4,28},{5,25},{6,30},{7,27},{8,16},{9,... | collective-permute-start | bytes 196616 | tf_op jit(solution)/shard_map/ppermute | solution.py:626
  38.0 0.0 collective-permute-start.17
  38.0 0.7 %collective-permute-start.18 = (bf16[256,128]{1,0:T(8,128)(2,1)S(1)}, bf16[256,128]{1,0:T(8,128)(2,1)S(1)}, u32[]{:S(2)}, u32[]{:S(2)}) collective-permute-start(bf16[256,128]{1,0:T(8,128)(2,1)S(1)} %get-tuple-element.52.refs_4_), channel_id=1, source_target_pairs={{1,5},{3,7},{5,1},{7,3},{9,13},{11,15},{13,9},{15,11},{17,21},{19,... | collective-permute-start | bytes 196616 | tf_op jit(solution)/shard_map/ppermute | solution.py:626
  38.7 3.8 %collective-permute-done.15.refs_0_ = bf16[256,128]{1,0:T(8,128)(2,1)S(1)} collective-permute-done((bf16[256,128]{1,0:T(8,128)(2,1)S(1)}, bf16[256,128]{1,0:T(8,128)(2,1)S(1)}, u32[]{:S(2)}, u32[]{:S(2)}) %collective-permute-start.15) | collective-permute-done | bytes 65568 | tf_op jit(solution)/shard_map/ppermute | solution.py:626
  42.4 0.0 collective-permute-done.16.refs_1_
  42.4 1.3 %collective-permute-done.17.refs_2_ = bf16[256,128]{1,0:T(8,128)(2,1)S(1)} collective-permute-done((bf16[256,128]{1,0:T(8,128)(2,1)S(1)}, bf16[256,128]{1,0:T(8,128)(2,1)S(1)}, u32[]{:S(2)}, u32[]{:S(2)}) %collective-permute-start.17) | collective-permute-done | bytes 65568 | tf_op jit(solution)/shard_map/ppermute | solution.py:626
  43.7 0.0 collective-permute-done.18.refs_3_
  43.7 0.2 combine.1
  43.9 0.3 collective-permute-start.19
  44.3 1.0 %collective-permute-done.19.came_ref = bf16[64,512]{1,0:T(8,128)(2,1)S(1)} collective-permute-done((bf16[64,512]{1,0:T(8,128)(2,1)S(1)}, bf16[64,512]{1,0:T(8,128)(2,1)S(1)}, u32[]{:S(2)}, u32[]{:S(2)}) %collective-permute-start.19) | collective-permute-done | bytes 65568 | tf_op jit(solution)/shard_map/ppermute | solution.py:419
  45.3 0.6 %add_output.1 = bf16[64,512]{1,0:T(8,128)(2,1)} custom-call(f32[64,512]{1,0:T(8,128)S(1)} %get-tuple-element.53.sum_ref, bf16[64,512]{1,0:T(8,128)(2,1)S(1)} %collective-permute-done.19.came_ref), custom_call_target="tpu_custom_call" | custom-call | tf_op jit(solution)/shard_map/add_output/pallas_call | solution.py:636
  (19 shorter events, 0.1 us)
Async XLA Ops:
  0.0 0.9 %copy-start.7 = (bf16[1,512,128]{2,1,0:T(8,128)(2,1)S(1)}, bf16[1,512,128]{2,1,0:T(8,128)(2,1)}, u32[]{:S(2)}) copy-start(bf16[1,512,128]{2,1,0:T(8,128)(2,1)} %param.18) | copy-start | bytes 393220
  0.0 1.0 %copy-start.8 = (bf16[1,512,128]{2,1,0:T(8,128)(2,1)S(1)}, bf16[1,512,128]{2,1,0:T(8,128)(2,1)}, u32[]{:S(2)}) copy-start(bf16[1,512,128]{2,1,0:T(8,128)(2,1)} %param.19) | copy-start | bytes 393220
  0.0 1.0 %copy-start.9 = (bf16[64,512]{1,0:T(8,128)(2,1)S(1)}, bf16[64,512]{1,0:T(8,128)(2,1)}, u32[]{:S(2)}) copy-start(bf16[64,512]{1,0:T(8,128)(2,1)} %query_ref.1) | copy-start | bytes 196612
  0.0 1.0 %copy-start.10 = (bf16[64,128]{1,0:T(8,128)(2,1)S(1)}, bf16[64,128]{1,0:T(8,128)(2,1)}, u32[]{:S(2)}) copy-start(bf16[64,128]{1,0:T(8,128)(2,1)} %new_key_ref.1) | copy-start | bytes 49156
  0.0 1.0 %copy-start.11 = (bf16[64,128]{1,0:T(8,128)(2,1)S(1)}, bf16[64,128]{1,0:T(8,128)(2,1)}, u32[]{:S(2)}) copy-start(bf16[64,128]{1,0:T(8,128)(2,1)} %new_value_ref.1) | copy-start | bytes 49156
  0.0 1.8 %copy-start = (bf16[512,2048]{1,0:T(8,128)(2,1)S(1)}, bf16[512,2048]{1,0:T(8,128)(2,1)}, u32[]{:S(2)}) copy-start(bf16[512,2048]{1,0:T(8,128)(2,1)} %weight_ref.3) | copy-start | bytes 6291460
  0.0 2.6 %copy-start.4 = (bf16[64,512]{1,0:T(8,128)(2,1)S(1)}, bf16[64,512]{1,0:T(8,128)(2,1)}, u32[]{:S(2)}) copy-start(bf16[64,512]{1,0:T(8,128)(2,1)} %residual_ref.1) | copy-start | bytes 196612
  1.0 9.5 %copy-start.5 = (s32[64,2]{0,1:T(2,128)S(1)}, s32[64,2]{0,1:T(2,128)}, u32[]{:S(2)}) copy-start(s32[64,2]{0,1:T(2,128)} %param.25) | copy-start | bytes 1540
  1.0 9.5 %copy-start.6 = (f32[64,2]{0,1:T(2,128)S(1)}, f32[64,2]{0,1:T(2,128)}, u32[]{:S(2)}) copy-start(f32[64,2]{0,1:T(2,128)} %param.26) | copy-start | bytes 1540
  1.8 9.0 %copy-start.1 = (bf16[1,2048,192]{1,2,0:T(8,128)(2,1)S(1)}, bf16[1,2048,192]{1,2,0:T(8,128)(2,1)}, u32[]{:S(2)}) copy-start(bf16[1,2048,192]{1,2,0:T(8,128)(2,1)} %param.27) | copy-start | bytes 2359300
  1.8 9.5 %copy-start.2 = (bf16[1,2048,192]{1,2,0:T(8,128)(2,1)S(1)}, bf16[1,2048,192]{1,2,0:T(8,128)(2,1)}, u32[]{:S(2)}) copy-start(bf16[1,2048,192]{1,2,0:T(8,128)(2,1)} %param.28) | copy-start | bytes 2359300
  2.1 1.5 %collective-permute-start = (bf16[64,1024]{1,0:T(8,128)(2,1)S(1)}, bf16[64,1024]{1,0:T(8,128)(2,1)S(1)}, u32[]{:S(2)}, u32[]{:S(2)}) collective-permute-start(bf16[64,1024]{1,0:T(8,128)(2,1)S(1)} %project_given.1.after_ref), channel_id=1, source_target_pairs={{0,1},{1,0},{2,3},{3,2},{4,5},{5,4},{6,7},{7,6},{8,9},{9,8},{10,11... | collective-permute-start | bytes 393224 | tf_op jit(solution)/shard_map/ppermute | solution.py:419
  3.7 6.7 %collective-permute-start.1 = (bf16[64,1024]{1,0:T(8,128)(2,1)S(1)}, bf16[64,1024]{1,0:T(8,128)(2,1)S(1)}, u32[]{:S(2)}, u32[]{:S(2)}) collective-permute-start(bf16[64,1024]{1,0:T(8,128)(2,1)S(1)} %get-tuple-element.31), channel_id=1, source_target_pairs={{0,2},{1,3},{2,0},{3,1},{4,6},{5,7},{6,4},{7,5},{8,10},{9,11},{10,... | collective-permute-start | bytes 393224 | tf_op jit(solution)/shard_map/ppermute | solution.py:422
  10.4 1.4 %collective-permute-start.4 = (bf16[64,1024]{1,0:T(8,128)(2,1)S(1)}, bf16[64,1024]{1,0:T(8,128)(2,1)S(1)}, u32[]{:S(2)}, u32[]{:S(2)}) collective-permute-start(bf16[64,1024]{1,0:T(8,128)(2,1)S(1)} %add_half.1.after_ref.part_ref), channel_id=1, source_target_pairs={{0,1},{1,0},{2,3},{3,2},{4,5},{5,4},{6,7},{7,6},{8,9},{9,8},{10,11... | collective-permute-start | bytes 393224 | tf_op jit(solution)/shard_map/ppermute | solution.py:419
  10.8 5.2 %collective-permute-start.2 = (bf16[192,2048]{1,0:T(8,128)(2,1)S(1)}, bf16[192,2048]{1,0:T(8,128)(2,1)S(1)}, u32[]{:S(2)}, u32[]{:S(2)}) collective-permute-start(bf16[192,2048]{1,0:T(8,128)(2,1)S(1)} %bitcast.12), channel_id=1, source_target_pairs={{0,1},{1,0},{2,3},{3,2},{4,5},{5,4},{6,7},{7,6},{8,9},{9,8},{10,11... | collective-permute-start | bytes 2359304 | tf_op jit(solution)/shard_map/ppermute | solution.py:419
  11.3 9.4 %collective-permute-start.3 = (bf16[192,2048]{1,0:T(8,128)(2,1)S(1)}, bf16[192,2048]{1,0:T(8,128)(2,1)S(1)}, u32[]{:S(2)}, u32[]{:S(2)}) collective-permute-start(bf16[192,2048]{1,0:T(8,128)(2,1)S(1)} %bitcast.14), channel_id=1, source_target_pairs={{0,1},{1,0},{2,3},{3,2},{4,5},{5,4},{6,7},{7,6},{8,9},{9,8},{10,11... | collective-permute-start | bytes 2359304 | tf_op jit(solution)/shard_map/ppermute | solution.py:419
  12.1 6.7 %collective-permute-start.6 = (bf16[272,128]{1,0:T(8,128)(2,1)S(1)}, bf16[272,128]{1,0:T(8,128)(2,1)S(1)}, u32[]{:S(2)}, u32[]{:S(2)}) collective-permute-start(bf16[272,128]{1,0:T(8,128)(2,1)S(1)} %get-tuple-element.39), channel_id=1, source_target_pairs={{0,24},{1,29},{2,26},{3,31},{4,28},{5,25},{6,30},{7,27},{8,16},{9,... | collective-permute-start | bytes 208904 | tf_op jit(solution)/shard_map/ppermute | solution.py:539
  16.0 9.6 %collective-permute-start.5 = (bf16[528,128]{1,0:T(8,128)(2,1)S(1)}, bf16[528,128]{1,0:T(8,128)(2,1)S(1)}, u32[]{:S(2)}, u32[]{:S(2)}) collective-permute-start(bf16[528,128]{1,0:T(8,128)(2,1)S(1)} %get-tuple-element.38), channel_id=1, source_target_pairs={{0,16},{1,21},{2,18},{3,23},{4,20},{5,17},{6,22},{7,19},{8,24},{9,... | collective-permute-start | bytes 405512 | tf_op jit(solution)/shard_map/ppermute | solution.py:539
  16.2 9.4 %collective-permute-start.7 = (bf16[528,128]{1,0:T(8,128)(2,1)S(1)}, bf16[528,128]{1,0:T(8,128)(2,1)S(1)}, u32[]{:S(2)}, u32[]{:S(2)}) collective-permute-start(bf16[528,128]{1,0:T(8,128)(2,1)S(1)} %get-tuple-element.40), channel_id=1, source_target_pairs={{0,8},{1,13},{2,10},{3,15},{4,12},{5,9},{6,14},{7,11},{8,0},{9,5},... | collective-permute-start | bytes 405512 | tf_op jit(solution)/shard_map/ppermute | solution.py:539
  16.9 8.7 %copy-start.12 = (f32[2048]{0:T(1024)S(1)}, f32[2048]{0:T(1024)}, u32[]{:S(2)}) copy-start(f32[2048]{0:T(1024)} %param.24) | copy-start | bytes 24580
  16.9 8.7 %collective-permute-start.8 = (bf16[528,128]{1,0:T(8,128)(2,1)S(1)}, bf16[528,128]{1,0:T(8,128)(2,1)S(1)}, u32[]{:S(2)}, u32[]{:S(2)}) collective-permute-start(bf16[528,128]{1,0:T(8,128)(2,1)S(1)} %get-tuple-element.41), channel_id=1, source_target_pairs={{0,0},{1,5},{2,2},{3,7},{4,4},{5,1},{6,6},{7,3},{8,8},{9,13},{10,1... | collective-permute-start | bytes 405512 | tf_op jit(solution)/shard_map/ppermute | solution.py:539
  18.8 6.8 %collective-permute-start.9 = (bf16[272,128]{1,0:T(8,128)(2,1)S(1)}, bf16[272,128]{1,0:T(8,128)(2,1)S(1)}, u32[]{:S(2)}, u32[]{:S(2)}) collective-permute-start(bf16[272,128]{1,0:T(8,128)(2,1)S(1)} %collective-permute-done.6.refs_1_), channel_id=1, source_target_pairs={{0,2},{1,3},{2,0},{3,1},{4,6},{5,7},{6,4},{7,5},{8,10},{9,11},{10,... | collective-permute-start | bytes 208904 | tf_op jit(solution)/shard_map/ppermute | solution.py:422
  25.7 2.7 %copy-start.3 = (bf16[1,768,512]{2,1,0:T(8,128)(2,1)S(1)}, bf16[1,768,512]{2,1,0:T(8,128)(2,1)}, u32[]{:S(2)}) copy-start(bf16[1,768,512]{2,1,0:T(8,128)(2,1)} %param.29) | copy-start | bytes 2359300
  25.7 6.0 %copy-start.13 = (s32[8]{0:T(128)S(1)}, s32[8]{0:T(128)}, u32[]{:S(2)}) copy-start(s32[8]{0:T(128)} %order_ref.1) | copy-start | bytes 100
  26.4 5.3 %collective-permute-start.10 = (bf16[4,272,128]{2,1,0:T(8,128)(2,1)S(1)}, bf16[4,272,128]{2,1,0:T(8,128)(2,1)S(1)}, u32[]{:S(2)}, u32[]{:S(2)}) collective-permute-start(bf16[4,272,128]{2,1,0:T(8,128)(2,1)S(1)} %get-tuple-element.42.side_ref), channel_id=1, source_target_pairs={{0,1},{1,0},{2,3},{3,2},{4,5},{5,4},{6,7},{7,6},{8,9},{9,8},{10,11... | collective-permute-start | bytes 835592 | tf_op jit(solution)/shard_map/ppermute | solution.py:419
  26.8 4.8 %collective-permute-start.11 = (bf16[128,384]{1,0:T(8,128)(2,1)S(1)}, bf16[128,384]{1,0:T(8,128)(2,1)S(1)}, u32[]{:S(2)}, u32[]{:S(2)}) collective-permute-start(bf16[128,384]{1,0:T(8,128)(2,1)S(1)} %get-tuple-element.44.act_ref), channel_id=1, source_target_pairs={{0,2},{1,3},{2,0},{3,1},{4,6},{5,7},{6,4},{7,5},{8,10},{9,11},{10,... | collective-permute-start | bytes 294920 | tf_op jit(solution)/shard_map/ppermute | solution.py:422
  28.3 4.7 %collective-permute-start.14 = (bf16[768,512]{1,0:T(8,128)(2,1)S(1)}, bf16[768,512]{1,0:T(8,128)(2,1)S(1)}, u32[]{:S(2)}, u32[]{:S(2)}) collective-permute-start(bf16[768,512]{1,0:T(8,128)(2,1)S(1)} %bitcast.16), channel_id=1, source_target_pairs={{0,1},{1,0},{2,3},{3,2},{4,5},{5,4},{6,7},{7,6},{8,9},{9,8},{10,11... | collective-permute-start | bytes 2359304 | tf_op jit(solution)/shard_map/ppermute | solution.py:419
  28.3 4.3 %collective-permute-start.12 = (bf16[128,384]{1,0:T(8,128)(2,1)S(1)}, bf16[128,384]{1,0:T(8,128)(2,1)S(1)}, u32[]{:S(2)}, u32[]{:S(2)}) collective-permute-start(bf16[128,384]{1,0:T(8,128)(2,1)S(1)} %get-tuple-element.44.act_ref), channel_id=1, source_target_pairs={{0,1},{1,0},{2,3},{3,2},{4,5},{5,4},{6,7},{7,6},{8,9},{9,8},{10,11... | collective-permute-start | bytes 294920 | tf_op jit(solution)/shard_map/ppermute | solution.py:419
  31.7 1.3 %collective-permute-start.13 = (bf16[128,384]{1,0:T(8,128)(2,1)S(1)}, bf16[128,384]{1,0:T(8,128)(2,1)S(1)}, u32[]{:S(2)}, u32[]{:S(2)}) collective-permute-start(bf16[128,384]{1,0:T(8,128)(2,1)S(1)} %collective-permute-done.11.act_half_ref), channel_id=1, source_target_pairs={{0,1},{1,0},{2,3},{3,2},{4,5},{5,4},{6,7},{7,6},{8,9},{9,8},{10,11... | collective-permute-start | bytes 294920 | tf_op jit(solution)/shard_map/ppermute | solution.py:419
  33.6 8.8 %collective-permute-start.15 = (bf16[256,128]{1,0:T(8,128)(2,1)S(1)}, bf16[256,128]{1,0:T(8,128)(2,1)S(1)}, u32[]{:S(2)}, u32[]{:S(2)}) collective-permute-start(bf16[256,128]{1,0:T(8,128)(2,1)S(1)} %get-tuple-element.49), channel_id=1, source_target_pairs={{0,16},{1,21},{2,18},{3,23},{4,20},{5,17},{6,22},{7,19},{8,24},{9,... | collective-permute-start | bytes 196616 | tf_op jit(solution)/shard_map/ppermute | solution.py:626
  35.1 7.3 %collective-permute-start.16 = (bf16[256,128]{1,0:T(8,128)(2,1)S(1)}, bf16[256,128]{1,0:T(8,128)(2,1)S(1)}, u32[]{:S(2)}, u32[]{:S(2)}) collective-permute-start(bf16[256,128]{1,0:T(8,128)(2,1)S(1)} %get-tuple-element.50), channel_id=1, source_target_pairs={{0,24},{1,29},{2,26},{3,31},{4,28},{5,25},{6,30},{7,27},{8,16},{9,... | collective-permute-start | bytes 196616 | tf_op jit(solution)/shard_map/ppermute | solution.py:626
  38.0 5.7 %collective-permute-start.17 = (bf16[256,128]{1,0:T(8,128)(2,1)S(1)}, bf16[256,128]{1,0:T(8,128)(2,1)S(1)}, u32[]{:S(2)}, u32[]{:S(2)}) collective-permute-start(bf16[256,128]{1,0:T(8,128)(2,1)S(1)} %get-tuple-element.51), channel_id=1, source_target_pairs={{0,8},{1,13},{2,10},{3,15},{4,12},{5,9},{6,14},{7,11},{8,0},{9,5},... | collective-permute-start | bytes 196616 | tf_op jit(solution)/shard_map/ppermute | solution.py:626
  38.0 5.7 %collective-permute-start.18 = (bf16[256,128]{1,0:T(8,128)(2,1)S(1)}, bf16[256,128]{1,0:T(8,128)(2,1)S(1)}, u32[]{:S(2)}, u32[]{:S(2)}) collective-permute-start(bf16[256,128]{1,0:T(8,128)(2,1)S(1)} %get-tuple-element.52.refs_4_), channel_id=1, source_target_pairs={{1,5},{3,7},{5,1},{7,3},{9,13},{11,15},{13,9},{15,11},{17,21},{19,... | collective-permute-start | bytes 196616 | tf_op jit(solution)/shard_map/ppermute | solution.py:626
  43.9 1.3 %collective-permute-start.19 = (bf16[64,512]{1,0:T(8,128)(2,1)S(1)}, bf16[64,512]{1,0:T(8,128)(2,1)S(1)}, u32[]{:S(2)}, u32[]{:S(2)}) collective-permute-start(bf16[64,512]{1,0:T(8,128)(2,1)S(1)} %get-tuple-element.54), channel_id=1, source_target_pairs={{0,1},{1,0},{2,3},{3,2},{4,5},{5,4},{6,7},{7,6},{8,9},{9,8},{10,11... | collective-permute-start | bytes 196616 | tf_op jit(solution)/shard_map/ppermute | solution.py:419

commit v13 on v12

--- a/solution.py
+++ b/solution.py
@@ -294,7 +294,8 @@
 def hidden_units_kernel(order, split, rows_each, gain_ref, weight_ref, *refs):
     peers = len(split)
     got = [refs[order.index(k)] for k in range(peers)]
-    halves = list(refs[peers:-2])
+    halves, own_ref = list(refs[peers:-3]), refs[-3]
+    nearest = peers // 2 - 1
     act_ref, side_ref = refs[-2:]
     tp = lax.axis_index("tp")
     half, core = tp // 2, tp % 2
@@ -310,6 +311,8 @@
             rows = jnp.concatenate([low, high], axis=0)
         else:
             rows = ref[: 4 * tall, :]
+            if ref is got[nearest]:
+                rows = jnp.where(core == 0, own_ref[: 4 * tall, :], rows)
         columns.append([rows[j * rows_each : (j + 1) * rows_each] for j in range(blocks)])
     parts = [
         jnp.concatenate([column[j] for column in columns], axis=0).astype(F32)
@@ -330,8 +333,13 @@
     act_ref[...] = (gate / (1.0 + jnp.exp(-gate)) * up).astype(BF16)
     for k in range(peers):
         start = 0 if split[k] else pl.multiple_of(2 * half * tall, 2 * tall)
-        side_ref[k, : 2 * tall, :] = got[k][pl.ds(start, 2 * tall), :]
-        side_ref[k, 2 * tall :, :] = got[k][got[k].shape[0] - TAGS :, :]
+        rows = got[k][pl.ds(start, 2 * tall), :]
+        tags = got[k][got[k].shape[0] - TAGS :, :]
+        if k == nearest:
+            rows = jnp.where(core == 0, own_ref[pl.ds(start, 2 * tall), :], rows)
+            tags = jnp.where(core == 0, own_ref[4 * tall :, :], tags)
+        side_ref[k, : 2 * tall, :] = rows
+        side_ref[k, 2 * tall :, :] = tags
 
 
 def down_kernel(
@@ -536,7 +544,7 @@
     gate, up, tags = lax.optimization_barrier((gate, up, tags))
     gate_pair, up_pair = swap_core(gate), swap_core(up)
     send.update(gather(list(range(near)), gate_pair))
-    got = [lax.ppermute(send[k], ("ep", "tp"), route(k)) for k in range(peers)]
+    got = [lax.ppermute(send[k], ("ep", "tp"), route(k, False)) for k in range(peers)]
     halves = [swap_half(got[k]) for k in range(peers) if split[k]]
 
     weights = pl.pallas_call(
@@ -564,14 +572,14 @@
             shape((peers * rows_each, units), BF16),
             shape((peers, 2 * tall + TAGS, LANES), BF16),
         ),
-        in_specs=[vmem()] * (2 + peers + len(halves)),
+        in_specs=[vmem()] * (3 + peers + len(halves)),
         out_specs=(vmem(), vmem()),
         compiler_params=params(16),
         cost_estimate=pl.CostEstimate(
             flops=20 * 10**9, bytes_accessed=MIB, transcendentals=0
         ),
         name="hidden_units",
-    )(norm_gain.reshape(-1, LANES), weights, *[got[k] for k in arrival], *halves)
+    )(norm_gain.reshape(-1, LANES), weights, *[got[k] for k in arrival], *halves, send[near - 1])
 
     act_half = swap_half(act)
     act_core = swap_core(act)

time: 46.1 us -> 46.8 us (1.015)
    ppermute x9, starting transfers between devices: 2.48 us -> 3.86 us  [swap_core(): return lax.ppermute(x, 'tp', [(i, i ^ 1) for i in range(tp_count)])]
    ppermute x4, starting transfers between devices: 5.06 us -> 4.21 us  [shards(): came = [lax.ppermute(send[k], ('ep', 'tp'), route(k, False)) for k in order]]
where the time goes in v13:
time: 46.8 us; the launch traced here: 46.6 us
  starting transfers between devices  19.7 us (42%)
  waiting for transfers between devices  19.2 us (41%)
  Pallas kernels  6.26 us (13%)
  between operations  1.01 us (2%)
    ppermute x3, waiting for transfers between devices, swap_half(): return lax.ppermute(x, 'tp', [(i, i ^ 2) for i in range(tp_count)])  6.59 us
    ppermute x3, starting transfers between devices, swap_half(): return lax.ppermute(x, 'tp', [(i, i ^ 2) for i in range(tp_count)])  6.3 us
    ppermute x4, starting transfers between devices, shards(): lax.ppermute(send[k], ('ep', 'tp'), route(k, False))  5.3 us
    ppermute x4, waiting for transfers between devices, shards(): came = [lax.ppermute(send[k], ('ep', 'tp'), route(k, False)) for k in order]  5.22 us
    ppermute x4, waiting for transfers between devices, shards(): lax.ppermute(send[k], ('ep', 'tp'), route(k, False))  5.07 us
    ppermute x4, starting transfers between devices, shards(): came = [lax.ppermute(send[k], ('ep', 'tp'), route(k, False)) for k in order]  4.21 us
    ppermute x9, starting transfers between devices, swap_core(): return lax.ppermute(x, 'tp', [(i, i ^ 1) for i in range(tp_count)])  3.86 us
    ppermute x9, waiting for transfers between devices, swap_core(): return lax.ppermute(x, 'tp', [(i, i ^ 1) for i in range(tp_count)])  2.34 us
  transfers between devices with their start and end apart: 20, of which 10 were waited for; matrix products, arithmetic and copies ran while one was open for 0% of the time, Pallas kernels for 7%

profile of v13, /device:TPU:0, one launch (start us, length us, event | category | flops | bytes accessed | tf_op | source)
XLA Modules:
  0.0 46.6 jit_solution(14166367690641837369)
XLA Ops:
  0.0 0.0 copy-start
  0.0 0.0 copy-start.4
  0.8 0.1 copy-done.7
  0.9 0.1 copy-done.8
  1.0 0.0 copy-done.9
  1.0 0.0 copy-done.10
  1.0 0.0 copy-start.6
  1.0 0.6 %attend.1.context_ref = bf16[64,512]{1,0:T(8,128)(2,1)S(1)} custom-call(f32[8,128]{1,0:T(8,128)S(1)} %begin.1.after_ref, s32[1]{0:T(128)S(6)} %copy.16.length_ref, bf16[64,512]{1,0:T(8,128)(2,1)S(1)} %copy-done.9, bf16[64,128]{1,0:T(8,128)(2,1)S(1)} %copy-done.10, bf16[64,128]{1,0:T(8,128)(2,1)S(1)} %copy-done.11, bf16[512,128]{1,0:T(8,128)(2,1)S(1)} %bitcast.20, ...), custom_call_target="tpu_custom_call" | custom-call | flops 200000000 | bytes 524288 | tf_op jit(solution)/shard_map/attend/pallas_call | solution.py:453
  1.6 0.3 copy-done
  1.8 0.3 project_given.1.after_ref
  2.1 0.5 %collective-permute-start = (bf16[64,1024]{1,0:T(8,128)(2,1)S(1)}, bf16[64,1024]{1,0:T(8,128)(2,1)S(1)}, u32[]{:S(2)}, u32[]{:S(2)}) collective-permute-start(bf16[64,1024]{1,0:T(8,128)(2,1)S(1)} %project_given.1.after_ref), channel_id=1, source_target_pairs={{0,1},{1,0},{2,3},{3,2},{4,5},{5,4},{6,7},{7,6},{8,9},{9,8},{10,11... | collective-permute-start | bytes 393224 | tf_op jit(solution)/shard_map/ppermute | solution.py:427
  2.7 0.3 project_kept.1.keep_ref
  3.0 0.7 %collective-permute-done.came_ref = bf16[64,1024]{1,0:T(8,128)(2,1)S(1)} collective-permute-done((bf16[64,1024]{1,0:T(8,128)(2,1)S(1)}, bf16[64,1024]{1,0:T(8,128)(2,1)S(1)}, u32[]{:S(2)}, u32[]{:S(2)}) %collective-permute-start) | collective-permute-done | bytes 131104 | tf_op jit(solution)/shard_map/ppermute | solution.py:427
  3.7 2.9 %collective-permute-start.1 = (bf16[64,1024]{1,0:T(8,128)(2,1)S(1)}, bf16[64,1024]{1,0:T(8,128)(2,1)S(1)}, u32[]{:S(2)}, u32[]{:S(2)}) collective-permute-start(bf16[64,1024]{1,0:T(8,128)(2,1)S(1)} %get-tuple-element.31), channel_id=1, source_target_pairs={{0,2},{1,3},{2,0},{3,1},{4,6},{5,7},{6,4},{7,5},{8,10},{9,11},{10,... | collective-permute-start | bytes 393224 | tf_op jit(solution)/shard_map/ppermute | solution.py:430
  6.6 3.8 %collective-permute-done.1.came_ref = bf16[64,1024]{1,0:T(8,128)(2,1)S(1)} collective-permute-done((bf16[64,1024]{1,0:T(8,128)(2,1)S(1)}, bf16[64,1024]{1,0:T(8,128)(2,1)S(1)}, u32[]{:S(2)}, u32[]{:S(2)}) %collective-permute-start.1) | collective-permute-done | bytes 131104 | tf_op jit(solution)/shard_map/ppermute | solution.py:430
  10.4 0.1 collective-permute-start.4
  10.5 0.3 route.1
  10.8 0.5 %collective-permute-start.2 = (bf16[192,2048]{1,0:T(8,128)(2,1)S(1)}, bf16[192,2048]{1,0:T(8,128)(2,1)S(1)}, u32[]{:S(2)}, u32[]{:S(2)}) collective-permute-start(bf16[192,2048]{1,0:T(8,128)(2,1)S(1)} %bitcast.12), channel_id=1, source_target_pairs={{0,1},{1,0},{2,3},{3,2},{4,5},{5,4},{6,7},{7,6},{8,9},{9,8},{10,11... | collective-permute-start | bytes 2359304 | tf_op jit(solution)/shard_map/ppermute | solution.py:427
  11.3 0.0 copy-done.2
  11.3 0.1 collective-permute-start.3
  11.4 0.4 collective-permute-done.4.other_ref
  11.9 0.2 gather_rows.2
  12.1 3.9 %collective-permute-start.6 = (bf16[272,128]{1,0:T(8,128)(2,1)S(1)}, bf16[272,128]{1,0:T(8,128)(2,1)S(1)}, u32[]{:S(2)}, u32[]{:S(2)}) collective-permute-start(bf16[272,128]{1,0:T(8,128)(2,1)S(1)} %get-tuple-element.39), channel_id=1, source_target_pairs={{0,24},{1,29},{2,26},{3,31},{4,28},{5,25},{6,30},{7,27},{8,16},{9,... | collective-permute-start | bytes 208904 | tf_op jit(solution)/shard_map/ppermute | solution.py:547
  16.0 0.0 collective-permute-start.5
  16.0 0.0 collective-permute-done.2.gate_pair.after_ref
  16.0 0.2 gather_rows.3
  16.2 0.7 %collective-permute-start.8 = (bf16[528,128]{1,0:T(8,128)(2,1)S(1)}, bf16[528,128]{1,0:T(8,128)(2,1)S(1)}, u32[]{:S(2)}, u32[]{:S(2)}) collective-permute-start(bf16[528,128]{1,0:T(8,128)(2,1)S(1)} %get-tuple-element.41.refs_5_), channel_id=1, source_target_pairs={{1,5},{3,7},{5,1},{7,3},{9,13},{11,15},{13,9},{15,11},{17,21},{19,... | collective-permute-start | bytes 405512 | tf_op jit(solution)/shard_map/ppermute | solution.py:547
  16.9 0.0 copy-start.12
  16.9 0.7 %collective-permute-start.7 = (bf16[528,128]{1,0:T(8,128)(2,1)S(1)}, bf16[528,128]{1,0:T(8,128)(2,1)S(1)}, u32[]{:S(2)}, u32[]{:S(2)}) collective-permute-start(bf16[528,128]{1,0:T(8,128)(2,1)S(1)} %get-tuple-element.40), channel_id=1, source_target_pairs={{0,8},{1,13},{2,10},{3,15},{4,12},{5,9},{6,14},{7,11},{8,0},{9,5},... | collective-permute-start | bytes 405512 | tf_op jit(solution)/shard_map/ppermute | solution.py:547
  17.6 1.2 %collective-permute-done.6.refs_1_ = bf16[272,128]{1,0:T(8,128)(2,1)S(1)} collective-permute-done((bf16[272,128]{1,0:T(8,128)(2,1)S(1)}, bf16[272,128]{1,0:T(8,128)(2,1)S(1)}, u32[]{:S(2)}, u32[]{:S(2)}) %collective-permute-start.6) | collective-permute-done | bytes 69664 | tf_op jit(solution)/shard_map/ppermute | solution.py:547
  18.8 1.9 %collective-permute-start.9 = (bf16[272,128]{1,0:T(8,128)(2,1)S(1)}, bf16[272,128]{1,0:T(8,128)(2,1)S(1)}, u32[]{:S(2)}, u32[]{:S(2)}) collective-permute-start(bf16[272,128]{1,0:T(8,128)(2,1)S(1)} %collective-permute-done.6.refs_1_), channel_id=1, source_target_pairs={{0,2},{1,3},{2,0},{3,1},{4,6},{5,7},{6,4},{7,5},{8,10},{9,11},{10,... | collective-permute-start | bytes 208904 | tf_op jit(solution)/shard_map/ppermute | solution.py:430
  20.7 0.0 collective-permute-done.3.up_pair
  20.7 1.1 %stage.1.weight_ref = bf16[2048,768]{1,0:T(8,128)(2,1)S(1)} custom-call(bf16[4,16,128]{2,1,0:T(8,128)(2,1)S(1)} %get-tuple-element.33.after_ref.tags_ref, bf16[192,2048]{1,0:T(8,128)(2,1)S(1)} %bitcast.13, bf16[192,2048]{1,0:T(8,128)(2,1)S(1)} %bitcast.15, bf16[192,2048]{1,0:T(8,128)(2,1)S(1)} %collective-permute-done.2.gate_pair.after_ref, ...), custom_call_target="tpu_custom_call" | custom-call | bytes 6291456 | tf_op jit(solution)/shard_map/stage/pallas_call | solution.py:550
  21.9 3.9 %collective-permute-done.5.refs_0_ = bf16[528,128]{1,0:T(8,128)(2,1)S(1)} collective-permute-done((bf16[528,128]{1,0:T(8,128)(2,1)S(1)}, bf16[528,128]{1,0:T(8,128)(2,1)S(1)}, u32[]{:S(2)}, u32[]{:S(2)}) %collective-permute-start.5) | collective-permute-done | bytes 135200 | tf_op jit(solution)/shard_map/ppermute | solution.py:547
  25.7 0.0 collective-permute-done.9.refs_4_
  25.7 0.0 collective-permute-done.8.refs_3_
  25.7 0.0 collective-permute-done.7.refs_2_
  25.8 0.0 copy-start.3
  25.8 0.0 copy-start.13
  25.8 0.8 %hidden_units.1 = (bf16[128,384]{1,0:T(8,128)(2,1)S(1)}, bf16[4,272,128]{2,1,0:T(8,128)(2,1)S(1)}) custom-call(f32[16,128]{1,0:T(8,128)S(1)} %bitcast.22, bf16[2048,768]{1,0:T(8,128)(2,1)S(1)} %stage.1.weight_ref, bf16[528,128]{1,0:T(8,128)(2,1)S(1)} %collective-permute-done.5.refs_0_, bf16[272,128]{1,0:T(8,128)(2,1)S(1)} %collective-permute-done.6.refs_1_, ...), custom_call_target="tpu_custom_call" | custom-call | flops 20000000000 | bytes 1048576 | tf_op jit(solution)/shard_map/hidden_units/pallas_call | solution.py:569
  26.6 1.4 %collective-permute-start.10 = (bf16[4,272,128]{2,1,0:T(8,128)(2,1)S(1)}, bf16[4,272,128]{2,1,0:T(8,128)(2,1)S(1)}, u32[]{:S(2)}, u32[]{:S(2)}) collective-permute-start(bf16[4,272,128]{2,1,0:T(8,128)(2,1)S(1)} %get-tuple-element.42.side_ref), channel_id=1, source_target_pairs={{0,1},{1,0},{2,3},{3,2},{4,5},{5,4},{6,7},{7,6},{8,9},{9,8},{10,11... | collective-permute-start | bytes 835592 | tf_op jit(solution)/shard_map/ppermute | solution.py:427
  27.9 1.5 %collective-permute-start.11 = (bf16[128,384]{1,0:T(8,128)(2,1)S(1)}, bf16[128,384]{1,0:T(8,128)(2,1)S(1)}, u32[]{:S(2)}, u32[]{:S(2)}) collective-permute-start(bf16[128,384]{1,0:T(8,128)(2,1)S(1)} %get-tuple-element.44.act_ref), channel_id=1, source_target_pairs={{0,2},{1,3},{2,0},{3,1},{4,6},{5,7},{6,4},{7,5},{8,10},{9,11},{10,... | collective-permute-start | bytes 294920 | tf_op jit(solution)/shard_map/ppermute | solution.py:430
  29.4 0.0 collective-permute-start.14
  29.4 0.5 %collective-permute-start.12 = (bf16[128,384]{1,0:T(8,128)(2,1)S(1)}, bf16[128,384]{1,0:T(8,128)(2,1)S(1)}, u32[]{:S(2)}, u32[]{:S(2)}) collective-permute-start(bf16[128,384]{1,0:T(8,128)(2,1)S(1)} %get-tuple-element.44.act_ref), channel_id=1, source_target_pairs={{0,1},{1,0},{2,3},{3,2},{4,5},{5,4},{6,7},{7,6},{8,9},{9,8},{10,11... | collective-permute-start | bytes 294920 | tf_op jit(solution)/shard_map/ppermute | solution.py:427
  30.0 2.8 %collective-permute-done.11.act_half_ref = bf16[128,384]{1,0:T(8,128)(2,1)S(1)} collective-permute-done((bf16[128,384]{1,0:T(8,128)(2,1)S(1)}, bf16[128,384]{1,0:T(8,128)(2,1)S(1)}, u32[]{:S(2)}, u32[]{:S(2)}) %collective-permute-start.11) | collective-permute-done | bytes 98336 | tf_op jit(solution)/shard_map/ppermute | solution.py:430
  32.7 0.0 collective-permute-start.13
  32.7 0.0 collective-permute-done.10.side_core_ref
  32.7 1.0 %select.1 = (bf16[64,128]{1,0:T(8,128)(2,1)S(1)}, bf16[128,256]{1,0:T(8,128)(2,1)S(1)}, bf16[4,256,128]{2,1,0:T(8,128)(2,1)S(1)}, f32[128,128]{1,0:T(8,128)S(1)}) custom-call(s32[8]{0:T(128)S(1)} %copy-done.13, bf16[4,272,128]{2,1,0:T(8,128)(2,1)S(1)} %get-tuple-element.42.side_ref, bf16[4,272,128]{2,1,0:T(8,128)(2,1)S(1)} %collective-permute-done.10.side_core_ref), custom_call_target="tpu_custom_call" | custom-call | flops 10000000000 | bytes 1048576 | tf_op jit(solution)/shard_map/select/pallas_call | solution.py:589
  33.7 0.0 collective-permute-done.12.act_core_ref
  33.7 0.3 collective-permute-done.13.act_both_ref
  34.0 0.0 collective-permute-done.14.down_pair_ref
  34.0 0.6 %down.1 = (bf16[256,128]{1,0:T(8,128)(2,1)S(1)}, bf16[256,128]{1,0:T(8,128)(2,1)S(1)}, bf16[256,128]{1,0:T(8,128)(2,1)S(1)}, bf16[256,128]{1,0:T(8,128)(2,1)S(1)}) custom-call(bf16[64,128]{1,0:T(8,128)(2,1)S(1)} %get-tuple-element.43.after_ref.chosen_ref, bf16[128,384]{1,0:T(8,128)(2,1)S(1)} %get-tuple-element.44.act_ref, ...), custom_call_target="tpu_custom_call" | custom-call | bytes 1048576 | tf_op jit(solution)/shard_map/down/pallas_call | solution.py:606
  34.6 0.6 %collective-permute-start.15 = (bf16[256,128]{1,0:T(8,128)(2,1)S(1)}, bf16[256,128]{1,0:T(8,128)(2,1)S(1)}, u32[]{:S(2)}, u32[]{:S(2)}) collective-permute-start(bf16[256,128]{1,0:T(8,128)(2,1)S(1)} %get-tuple-element.49), channel_id=1, source_target_pairs={{0,16},{1,21},{2,18},{3,23},{4,20},{5,17},{6,22},{7,19},{8,24},{9,... | collective-permute-start | bytes 196616 | tf_op jit(solution)/shard_map/ppermute | solution.py:634
  35.2 2.8 %collective-permute-start.16 = (bf16[256,128]{1,0:T(8,128)(2,1)S(1)}, bf16[256,128]{1,0:T(8,128)(2,1)S(1)}, u32[]{:S(2)}, u32[]{:S(2)}) collective-permute-start(bf16[256,128]{1,0:T(8,128)(2,1)S(1)} %get-tuple-element.50), channel_id=1, source_target_pairs={{0,24},{1,29},{2,26},{3,31},{4,28},{5,25},{6,30},{7,27},{8,16},{9,... | collective-permute-start | bytes 196616 | tf_op jit(solution)/shard_map/ppermute | solution.py:634
  38.1 0.1 collective-permute-start.17
  38.2 0.7 %collective-permute-start.18 = (bf16[256,128]{1,0:T(8,128)(2,1)S(1)}, bf16[256,128]{1,0:T(8,128)(2,1)S(1)}, u32[]{:S(2)}, u32[]{:S(2)}) collective-permute-start(bf16[256,128]{1,0:T(8,128)(2,1)S(1)} %get-tuple-element.52.refs_4_), channel_id=1, source_target_pairs={{1,5},{3,7},{5,1},{7,3},{9,13},{11,15},{13,9},{15,11},{17,21},{19,... | collective-permute-start | bytes 196616 | tf_op jit(solution)/shard_map/ppermute | solution.py:634
  38.9 3.9 %collective-permute-done.15.refs_0_ = bf16[256,128]{1,0:T(8,128)(2,1)S(1)} collective-permute-done((bf16[256,128]{1,0:T(8,128)(2,1)S(1)}, bf16[256,128]{1,0:T(8,128)(2,1)S(1)}, u32[]{:S(2)}, u32[]{:S(2)}) %collective-permute-start.15) | collective-permute-done | bytes 65568 | tf_op jit(solution)/shard_map/ppermute | solution.py:634
  42.8 0.0 collective-permute-done.16.refs_1_
  42.8 1.3 %collective-permute-done.17.refs_2_ = bf16[256,128]{1,0:T(8,128)(2,1)S(1)} collective-permute-done((bf16[256,128]{1,0:T(8,128)(2,1)S(1)}, bf16[256,128]{1,0:T(8,128)(2,1)S(1)}, u32[]{:S(2)}, u32[]{:S(2)}) %collective-permute-start.17) | collective-permute-done | bytes 65568 | tf_op jit(solution)/shard_map/ppermute | solution.py:634
  44.1 0.0 collective-permute-done.18.refs_3_
  44.1 0.2 combine.1
  44.3 0.8 %collective-permute-start.19 = (bf16[64,512]{1,0:T(8,128)(2,1)S(1)}, bf16[64,512]{1,0:T(8,128)(2,1)S(1)}, u32[]{:S(2)}, u32[]{:S(2)}) collective-permute-start(bf16[64,512]{1,0:T(8,128)(2,1)S(1)} %get-tuple-element.54), channel_id=1, source_target_pairs={{0,1},{1,0},{2,3},{3,2},{4,5},{5,4},{6,7},{7,6},{8,9},{9,8},{10,11... | collective-permute-start | bytes 196616 | tf_op jit(solution)/shard_map/ppermute | solution.py:427
  45.1 0.9 %collective-permute-done.19.came_ref = bf16[64,512]{1,0:T(8,128)(2,1)S(1)} collective-permute-done((bf16[64,512]{1,0:T(8,128)(2,1)S(1)}, bf16[64,512]{1,0:T(8,128)(2,1)S(1)}, u32[]{:S(2)}, u32[]{:S(2)}) %collective-permute-start.19) | collective-permute-done | bytes 65568 | tf_op jit(solution)/shard_map/ppermute | solution.py:427
  46.0 0.6 %add_output.1 = bf16[64,512]{1,0:T(8,128)(2,1)} custom-call(f32[64,512]{1,0:T(8,128)S(1)} %get-tuple-element.53.sum_ref, bf16[64,512]{1,0:T(8,128)(2,1)S(1)} %collective-permute-done.19.came_ref), custom_call_target="tpu_custom_call" | custom-call | tf_op jit(solution)/shard_map/add_output/pallas_call | solution.py:644
  (19 shorter events, 0.1 us)
Async XLA Ops:
  0.0 0.9 %copy-start.7 = (bf16[1,512,128]{2,1,0:T(8,128)(2,1)S(1)}, bf16[1,512,128]{2,1,0:T(8,128)(2,1)}, u32[]{:S(2)}) copy-start(bf16[1,512,128]{2,1,0:T(8,128)(2,1)} %param.18) | copy-start | bytes 393220
  0.0 1.0 %copy-start.8 = (bf16[1,512,128]{2,1,0:T(8,128)(2,1)S(1)}, bf16[1,512,128]{2,1,0:T(8,128)(2,1)}, u32[]{:S(2)}) copy-start(bf16[1,512,128]{2,1,0:T(8,128)(2,1)} %param.19) | copy-start | bytes 393220
  0.0 1.0 %copy-start.9 = (bf16[64,512]{1,0:T(8,128)(2,1)S(1)}, bf16[64,512]{1,0:T(8,128)(2,1)}, u32[]{:S(2)}) copy-start(bf16[64,512]{1,0:T(8,128)(2,1)} %query_ref.1) | copy-start | bytes 196612
  0.0 1.0 %copy-start.10 = (bf16[64,128]{1,0:T(8,128)(2,1)S(1)}, bf16[64,128]{1,0:T(8,128)(2,1)}, u32[]{:S(2)}) copy-start(bf16[64,128]{1,0:T(8,128)(2,1)} %new_key_ref.1) | copy-start | bytes 49156
  0.0 1.0 %copy-start.11 = (bf16[64,128]{1,0:T(8,128)(2,1)S(1)}, bf16[64,128]{1,0:T(8,128)(2,1)}, u32[]{:S(2)}) copy-start(bf16[64,128]{1,0:T(8,128)(2,1)} %new_value_ref.1) | copy-start | bytes 49156
  0.0 1.8 %copy-start = (bf16[512,2048]{1,0:T(8,128)(2,1)S(1)}, bf16[512,2048]{1,0:T(8,128)(2,1)}, u32[]{:S(2)}) copy-start(bf16[512,2048]{1,0:T(8,128)(2,1)} %weight_ref.3) | copy-start | bytes 6291460
  0.0 2.6 %copy-start.4 = (bf16[64,512]{1,0:T(8,128)(2,1)S(1)}, bf16[64,512]{1,0:T(8,128)(2,1)}, u32[]{:S(2)}) copy-start(bf16[64,512]{1,0:T(8,128)(2,1)} %residual_ref.1) | copy-start | bytes 196612
  1.0 9.5 %copy-start.5 = (s32[64,2]{0,1:T(2,128)S(1)}, s32[64,2]{0,1:T(2,128)}, u32[]{:S(2)}) copy-start(s32[64,2]{0,1:T(2,128)} %param.25) | copy-start | bytes 1540
  1.0 9.5 %copy-start.6 = (f32[64,2]{0,1:T(2,128)S(1)}, f32[64,2]{0,1:T(2,128)}, u32[]{:S(2)}) copy-start(f32[64,2]{0,1:T(2,128)} %param.26) | copy-start | bytes 1540
  1.8 9.0 %copy-start.1 = (bf16[1,2048,192]{1,2,0:T(8,128)(2,1)S(1)}, bf16[1,2048,192]{1,2,0:T(8,128)(2,1)}, u32[]{:S(2)}) copy-start(bf16[1,2048,192]{1,2,0:T(8,128)(2,1)} %param.27) | copy-start | bytes 2359300
  1.8 9.5 %copy-start.2 = (bf16[1,2048,192]{1,2,0:T(8,128)(2,1)S(1)}, bf16[1,2048,192]{1,2,0:T(8,128)(2,1)}, u32[]{:S(2)}) copy-start(bf16[1,2048,192]{1,2,0:T(8,128)(2,1)} %param.28) | copy-start | bytes 2359300
  2.1 1.5 %collective-permute-start = (bf16[64,1024]{1,0:T(8,128)(2,1)S(1)}, bf16[64,1024]{1,0:T(8,128)(2,1)S(1)}, u32[]{:S(2)}, u32[]{:S(2)}) collective-permute-start(bf16[64,1024]{1,0:T(8,128)(2,1)S(1)} %project_given.1.after_ref), channel_id=1, source_target_pairs={{0,1},{1,0},{2,3},{3,2},{4,5},{5,4},{6,7},{7,6},{8,9},{9,8},{10,11... | collective-permute-start | bytes 393224 | tf_op jit(solution)/shard_map/ppermute | solution.py:427
  3.7 6.7 %collective-permute-start.1 = (bf16[64,1024]{1,0:T(8,128)(2,1)S(1)}, bf16[64,1024]{1,0:T(8,128)(2,1)S(1)}, u32[]{:S(2)}, u32[]{:S(2)}) collective-permute-start(bf16[64,1024]{1,0:T(8,128)(2,1)S(1)} %get-tuple-element.31), channel_id=1, source_target_pairs={{0,2},{1,3},{2,0},{3,1},{4,6},{5,7},{6,4},{7,5},{8,10},{9,11},{10,... | collective-permute-start | bytes 393224 | tf_op jit(solution)/shard_map/ppermute | solution.py:430
  10.4 1.4 %collective-permute-start.4 = (bf16[64,1024]{1,0:T(8,128)(2,1)S(1)}, bf16[64,1024]{1,0:T(8,128)(2,1)S(1)}, u32[]{:S(2)}, u32[]{:S(2)}) collective-permute-start(bf16[64,1024]{1,0:T(8,128)(2,1)S(1)} %add_half.1.after_ref.part_ref), channel_id=1, source_target_pairs={{0,1},{1,0},{2,3},{3,2},{4,5},{5,4},{6,7},{7,6},{8,9},{9,8},{10,11... | collective-permute-start | bytes 393224 | tf_op jit(solution)/shard_map/ppermute | solution.py:427
  10.8 5.2 %collective-permute-start.2 = (bf16[192,2048]{1,0:T(8,128)(2,1)S(1)}, bf16[192,2048]{1,0:T(8,128)(2,1)S(1)}, u32[]{:S(2)}, u32[]{:S(2)}) collective-permute-start(bf16[192,2048]{1,0:T(8,128)(2,1)S(1)} %bitcast.12), channel_id=1, source_target_pairs={{0,1},{1,0},{2,3},{3,2},{4,5},{5,4},{6,7},{7,6},{8,9},{9,8},{10,11... | collective-permute-start | bytes 2359304 | tf_op jit(solution)/shard_map/ppermute | solution.py:427
  11.3 9.4 %collective-permute-start.3 = (bf16[192,2048]{1,0:T(8,128)(2,1)S(1)}, bf16[192,2048]{1,0:T(8,128)(2,1)S(1)}, u32[]{:S(2)}, u32[]{:S(2)}) collective-permute-start(bf16[192,2048]{1,0:T(8,128)(2,1)S(1)} %bitcast.14), channel_id=1, source_target_pairs={{0,1},{1,0},{2,3},{3,2},{4,5},{5,4},{6,7},{7,6},{8,9},{9,8},{10,11... | collective-permute-start | bytes 2359304 | tf_op jit(solution)/shard_map/ppermute | solution.py:427
  12.1 6.7 %collective-permute-start.6 = (bf16[272,128]{1,0:T(8,128)(2,1)S(1)}, bf16[272,128]{1,0:T(8,128)(2,1)S(1)}, u32[]{:S(2)}, u32[]{:S(2)}) collective-permute-start(bf16[272,128]{1,0:T(8,128)(2,1)S(1)} %get-tuple-element.39), channel_id=1, source_target_pairs={{0,24},{1,29},{2,26},{3,31},{4,28},{5,25},{6,30},{7,27},{8,16},{9,... | collective-permute-start | bytes 208904 | tf_op jit(solution)/shard_map/ppermute | solution.py:547
  16.0 9.7 %collective-permute-start.5 = (bf16[528,128]{1,0:T(8,128)(2,1)S(1)}, bf16[528,128]{1,0:T(8,128)(2,1)S(1)}, u32[]{:S(2)}, u32[]{:S(2)}) collective-permute-start(bf16[528,128]{1,0:T(8,128)(2,1)S(1)} %get-tuple-element.38), channel_id=1, source_target_pairs={{0,16},{1,21},{2,18},{3,23},{4,20},{5,17},{6,22},{7,19},{8,24},{9,... | collective-permute-start | bytes 405512 | tf_op jit(solution)/shard_map/ppermute | solution.py:547
  16.2 9.5 %collective-permute-start.8 = (bf16[528,128]{1,0:T(8,128)(2,1)S(1)}, bf16[528,128]{1,0:T(8,128)(2,1)S(1)}, u32[]{:S(2)}, u32[]{:S(2)}) collective-permute-start(bf16[528,128]{1,0:T(8,128)(2,1)S(1)} %get-tuple-element.41.refs_5_), channel_id=1, source_target_pairs={{1,5},{3,7},{5,1},{7,3},{9,13},{11,15},{13,9},{15,11},{17,21},{19,... | collective-permute-start | bytes 405512 | tf_op jit(solution)/shard_map/ppermute | solution.py:547
  16.9 8.8 %copy-start.12 = (f32[2048]{0:T(1024)S(1)}, f32[2048]{0:T(1024)}, u32[]{:S(2)}) copy-start(f32[2048]{0:T(1024)} %param.24) | copy-start | bytes 24580
  16.9 8.8 %collective-permute-start.7 = (bf16[528,128]{1,0:T(8,128)(2,1)S(1)}, bf16[528,128]{1,0:T(8,128)(2,1)S(1)}, u32[]{:S(2)}, u32[]{:S(2)}) collective-permute-start(bf16[528,128]{1,0:T(8,128)(2,1)S(1)} %get-tuple-element.40), channel_id=1, source_target_pairs={{0,8},{1,13},{2,10},{3,15},{4,12},{5,9},{6,14},{7,11},{8,0},{9,5},... | collective-permute-start | bytes 405512 | tf_op jit(solution)/shard_map/ppermute | solution.py:547
  18.8 6.9 %collective-permute-start.9 = (bf16[272,128]{1,0:T(8,128)(2,1)S(1)}, bf16[272,128]{1,0:T(8,128)(2,1)S(1)}, u32[]{:S(2)}, u32[]{:S(2)}) collective-permute-start(bf16[272,128]{1,0:T(8,128)(2,1)S(1)} %collective-permute-done.6.refs_1_), channel_id=1, source_target_pairs={{0,2},{1,3},{2,0},{3,1},{4,6},{5,7},{6,4},{7,5},{8,10},{9,11},{10,... | collective-permute-start | bytes 208904 | tf_op jit(solution)/shard_map/ppermute | solution.py:430
  25.8 3.7 %copy-start.3 = (bf16[1,768,512]{2,1,0:T(8,128)(2,1)S(1)}, bf16[1,768,512]{2,1,0:T(8,128)(2,1)}, u32[]{:S(2)}) copy-start(bf16[1,768,512]{2,1,0:T(8,128)(2,1)} %param.29) | copy-start | bytes 2359300
  25.8 7.0 %copy-start.13 = (s32[8]{0:T(128)S(1)}, s32[8]{0:T(128)}, u32[]{:S(2)}) copy-start(s32[8]{0:T(128)} %order_ref.1) | copy-start | bytes 100
  26.6 6.2 %collective-permute-start.10 = (bf16[4,272,128]{2,1,0:T(8,128)(2,1)S(1)}, bf16[4,272,128]{2,1,0:T(8,128)(2,1)S(1)}, u32[]{:S(2)}, u32[]{:S(2)}) collective-permute-start(bf16[4,272,128]{2,1,0:T(8,128)(2,1)S(1)} %get-tuple-element.42.side_ref), channel_id=1, source_target_pairs={{0,1},{1,0},{2,3},{3,2},{4,5},{5,4},{6,7},{7,6},{8,9},{9,8},{10,11... | collective-permute-start | bytes 835592 | tf_op jit(solution)/shard_map/ppermute | solution.py:427
  27.9 4.8 %collective-permute-start.11 = (bf16[128,384]{1,0:T(8,128)(2,1)S(1)}, bf16[128,384]{1,0:T(8,128)(2,1)S(1)}, u32[]{:S(2)}, u32[]{:S(2)}) collective-permute-start(bf16[128,384]{1,0:T(8,128)(2,1)S(1)} %get-tuple-element.44.act_ref), channel_id=1, source_target_pairs={{0,2},{1,3},{2,0},{3,1},{4,6},{5,7},{6,4},{7,5},{8,10},{9,11},{10,... | collective-permute-start | bytes 294920 | tf_op jit(solution)/shard_map/ppermute | solution.py:430
  29.4 4.6 %collective-permute-start.14 = (bf16[768,512]{1,0:T(8,128)(2,1)S(1)}, bf16[768,512]{1,0:T(8,128)(2,1)S(1)}, u32[]{:S(2)}, u32[]{:S(2)}) collective-permute-start(bf16[768,512]{1,0:T(8,128)(2,1)S(1)} %bitcast.16), channel_id=1, source_target_pairs={{0,1},{1,0},{2,3},{3,2},{4,5},{5,4},{6,7},{7,6},{8,9},{9,8},{10,11... | collective-permute-start | bytes 2359304 | tf_op jit(solution)/shard_map/ppermute | solution.py:427
  29.4 4.3 %collective-permute-start.12 = (bf16[128,384]{1,0:T(8,128)(2,1)S(1)}, bf16[128,384]{1,0:T(8,128)(2,1)S(1)}, u32[]{:S(2)}, u32[]{:S(2)}) collective-permute-start(bf16[128,384]{1,0:T(8,128)(2,1)S(1)} %get-tuple-element.44.act_ref), channel_id=1, source_target_pairs={{0,1},{1,0},{2,3},{3,2},{4,5},{5,4},{6,7},{7,6},{8,9},{9,8},{10,11... | collective-permute-start | bytes 294920 | tf_op jit(solution)/shard_map/ppermute | solution.py:427
  32.7 1.3 %collective-permute-start.13 = (bf16[128,384]{1,0:T(8,128)(2,1)S(1)}, bf16[128,384]{1,0:T(8,128)(2,1)S(1)}, u32[]{:S(2)}, u32[]{:S(2)}) collective-permute-start(bf16[128,384]{1,0:T(8,128)(2,1)S(1)} %collective-permute-done.11.act_half_ref), channel_id=1, source_target_pairs={{0,1},{1,0},{2,3},{3,2},{4,5},{5,4},{6,7},{7,6},{8,9},{9,8},{10,11... | collective-permute-start | bytes 294920 | tf_op jit(solution)/shard_map/ppermute | solution.py:427
  34.6 8.1 %collective-permute-start.15 = (bf16[256,128]{1,0:T(8,128)(2,1)S(1)}, bf16[256,128]{1,0:T(8,128)(2,1)S(1)}, u32[]{:S(2)}, u32[]{:S(2)}) collective-permute-start(bf16[256,128]{1,0:T(8,128)(2,1)S(1)} %get-tuple-element.49), channel_id=1, source_target_pairs={{0,16},{1,21},{2,18},{3,23},{4,20},{5,17},{6,22},{7,19},{8,24},{9,... | collective-permute-start | bytes 196616 | tf_op jit(solution)/shard_map/ppermute | solution.py:634
  35.2 7.5 %collective-permute-start.16 = (bf16[256,128]{1,0:T(8,128)(2,1)S(1)}, bf16[256,128]{1,0:T(8,128)(2,1)S(1)}, u32[]{:S(2)}, u32[]{:S(2)}) collective-permute-start(bf16[256,128]{1,0:T(8,128)(2,1)S(1)} %get-tuple-element.50), channel_id=1, source_target_pairs={{0,24},{1,29},{2,26},{3,31},{4,28},{5,25},{6,30},{7,27},{8,16},{9,... | collective-permute-start | bytes 196616 | tf_op jit(solution)/shard_map/ppermute | solution.py:634
  38.1 6.0 %collective-permute-start.17 = (bf16[256,128]{1,0:T(8,128)(2,1)S(1)}, bf16[256,128]{1,0:T(8,128)(2,1)S(1)}, u32[]{:S(2)}, u32[]{:S(2)}) collective-permute-start(bf16[256,128]{1,0:T(8,128)(2,1)S(1)} %get-tuple-element.51), channel_id=1, source_target_pairs={{0,8},{1,13},{2,10},{3,15},{4,12},{5,9},{6,14},{7,11},{8,0},{9,5},... | collective-permute-start | bytes 196616 | tf_op jit(solution)/shard_map/ppermute | solution.py:634
  38.2 5.9 %collective-permute-start.18 = (bf16[256,128]{1,0:T(8,128)(2,1)S(1)}, bf16[256,128]{1,0:T(8,128)(2,1)S(1)}, u32[]{:S(2)}, u32[]{:S(2)}) collective-permute-start(bf16[256,128]{1,0:T(8,128)(2,1)S(1)} %get-tuple-element.52.refs_4_), channel_id=1, source_target_pairs={{1,5},{3,7},{5,1},{7,3},{9,13},{11,15},{13,9},{15,11},{17,21},{19,... | collective-permute-start | bytes 196616 | tf_op jit(solution)/shard_map/ppermute | solution.py:634
  44.3 1.7 %collective-permute-start.19 = (bf16[64,512]{1,0:T(8,128)(2,1)S(1)}, bf16[64,512]{1,0:T(8,128)(2,1)S(1)}, u32[]{:S(2)}, u32[]{:S(2)}) collective-permute-start(bf16[64,512]{1,0:T(8,128)(2,1)S(1)} %get-tuple-element.54), channel_id=1, source_target_pairs={{0,1},{1,0},{2,3},{3,2},{4,5},{5,4},{6,7},{7,6},{8,9},{9,8},{10,11... | collective-permute-start | bytes 196616 | tf_op jit(solution)/shard_map/ppermute | solution.py:427
